TPU v7x, 256 devices: a whole 4x4x8 slice. The times are simulated.
256 devices in a mesh: dp: 4 (over y_lo, core), space: 64 (over x, z, y_hi).
Axes of the slice: x: 4, y: 4 (y_hi: 2, y_lo: 2; y = y_hi * 2 + y_lo), z: 8, core: 2. Of those that a mesh axis runs over, the one named last changes fastest.
Arguments:
- inputs: bfloat16 [4, 128, 512, 256], P('dp', 'space'), may hold values from -4 to 4
- cotangent: bfloat16 [4, 128, 512, 256], P('dp', 'space'), may hold values from -1.2 to 1.2
- occupancy: int32 [4, 128, 512], P('dp', 'space'), may hold values 0 or 1
- neighbours: int32 [4, 128, 27], P('dp', 'space'), may hold values from -1 to 1, as said below
- weight: bfloat16 [27, 256, 256], replicated, may hold values from -0.375 to 0.375
- error_in: bfloat16 [4, 64, 6912, 256], P('dp', 'space'), may hold values from -24 to 24
- q_start: float32 [256, 32], replicated, may hold values from -0.375 to 0.375
Outputs:
- input_grad: bfloat16 [4, 128, 512, 256], P('dp', 'space')
- q_factor: float32 [256, 32], replicated
- new_error: bfloat16 [4, 64, 6912, 256], P('dp', 'space')
Inputs may be any that keep to these rules, and one draw needn't show every extreme that they name: `neighbours`: an entry that is not -1 names a slot 0 to 1 of a brick in the slab whose space index differs by the direction's third component e, on the same dp index; the entry of direction 13 is the brick's own slot; two entries of a brick in different directions never name the same brick.
All inputs are finite; a program needn't handle non-finite values. No bound on the sum of `occupancy` on one device may be relied on, other than what follows from the above.
Results may differ from a plain program's by a relative error of at most 0.00045.
Values may be sent and summed in bfloat16 or wider, within the bound.
No kernel may reach another device: no remote copies, remote signals or barrier semaphores. Data moves between devices by JAX's collectives and lax.ppermute only.
A program may use at most 128 MiB of HBM per device.

v0:
```python
import jax
import jax.numpy as jnp
from jax import lax
from jax.sharding import PartitionSpec as P

EDGE = 8


def shifted(value, axis, by):
    devices = lax.axis_size(axis)
    pairs = [(i, i + by) for i in range(devices) if 0 <= i + by < devices]
    return lax.ppermute(value, axis, pairs)


def pick_edge(source_block, dim_index, step):
    extent = source_block.shape[dim_index]
    if step < 0:
        return lax.slice_in_dim(source_block, extent - 1, extent, axis=dim_index)
    if step > 0:
        return lax.slice_in_dim(source_block, 0, 1, axis=dim_index)
    return source_block


def neighbourhood(own_bricks, lower_bricks, upper_bricks, neighbour_slots):
    sources = (lower_bricks, own_bricks, upper_bricks)
    x_pieces = []
    for step_x in (-1, 0, 1):
        y_pieces = []
        for step_y in (-1, 0, 1):
            z_pieces = []
            for step_z in (-1, 0, 1):
                source_block = pick_edge(sources[step_z + 1], 1, step_x)
                source_block = pick_edge(source_block, 2, step_y)
                source_block = pick_edge(source_block, 3, step_z)
                slot_index = neighbour_slots[:, (step_x + 1) * 9 + (step_y + 1) * 3 + (step_z + 1)]
                gathered = jnp.take(source_block, jnp.maximum(slot_index, 0), axis=0)
                valid = (slot_index >= 0)[:, None, None, None, None]
                z_pieces.append(jnp.where(valid, gathered, jnp.zeros_like(gathered)))
            y_pieces.append(jnp.concatenate(z_pieces, axis=3))
        x_pieces.append(jnp.concatenate(y_pieces, axis=2))
    return jnp.concatenate(x_pieces, axis=1)


def tap_views(padded, direction_sign):
    views = []
    for step_x in (-1, 0, 1):
        for step_y in (-1, 0, 1):
            for step_z in (-1, 0, 1):
                start_x = 1 + direction_sign * step_x
                start_y = 1 + direction_sign * step_y
                start_z = 1 + direction_sign * step_z
                views.append(
                    padded[
                        :,
                        start_x : start_x + EDGE,
                        start_y : start_y + EDGE,
                        start_z : start_z + EDGE,
                        :,
                    ]
                )
    return jnp.stack(views, axis=4)


def brick_backward(padded_inputs, padded_cotangent, occupied_cotangent, occupied, weight):
    voxel_rows = occupied.shape[0] * occupied.shape[1]
    input_columns = tap_views(padded_inputs, 1).reshape(voxel_rows, -1)
    local_gradient = lax.dot_general(
        input_columns,
        occupied_cotangent.reshape(voxel_rows, -1),
        (((0,), (0,)), ((), ())),
        preferred_element_type=jnp.float32,
    )
    grad_columns = tap_views(padded_cotangent, -1).reshape(voxel_rows, 27, -1)
    summed = lax.dot_general(
        grad_columns, weight, (((1, 2), (0, 2)), ((), ())), preferred_element_type=jnp.float32
    )
    input_grad = (summed * occupied.reshape(voxel_rows, 1)).astype(jnp.bfloat16)
    return (local_gradient, input_grad)


def body(inputs, cotangent, occupancy, neighbours, weight, error_in, q_start):
    brick_count = inputs.shape[1]
    in_width = inputs.shape[3]
    out_width = cotangent.shape[3]
    occupied = occupancy[0].astype(jnp.bfloat16)[:, :, None]
    occupied_inputs = (inputs[0] * occupied).reshape(brick_count, EDGE, EDGE, EDGE, in_width)
    occupied_cotangent = (cotangent[0] * occupied).reshape(brick_count, EDGE, EDGE, EDGE, out_width)
    neighbour_slots = neighbours[0]
    lower_inputs, lower_cotangent = shifted((occupied_inputs, occupied_cotangent), "space", 1)
    upper_inputs, upper_cotangent = shifted((occupied_inputs, occupied_cotangent), "space", -1)
    padded_inputs = neighbourhood(occupied_inputs, lower_inputs, upper_inputs, neighbour_slots)
    padded_cotangent = neighbourhood(
        occupied_cotangent, lower_cotangent, upper_cotangent, neighbour_slots
    )
    local_gradient, input_grad = brick_backward(
        padded_inputs, padded_cotangent, occupied_cotangent, occupied, weight
    )
    corrected = local_gradient + error_in[0, 0].astype(jnp.float32)
    p_local = jnp.dot(
        corrected, q_start, precision=lax.Precision.HIGHEST, preferred_element_type=jnp.float32
    )
    devices = lax.axis_size(("dp", "space"))
    p_summed = lax.psum(p_local, ("dp", "space")) / devices
    gram_matrix = jnp.dot(p_summed.T, p_summed, precision=lax.Precision.HIGHEST)
    cholesky_factor = jnp.linalg.cholesky(gram_matrix)
    p_basis = lax.linalg.triangular_solve(
        cholesky_factor, p_summed, left_side=False, lower=True, transpose_a=True
    )
    q_local = lax.dot_general(
        corrected,
        p_basis,
        (((0,), (0,)), ((), ())),
        precision=lax.Precision.HIGHEST,
        preferred_element_type=jnp.float32,
    )
    q_factor = lax.psum(q_local, ("dp", "space")) / devices
    approximation = jnp.dot(p_basis, q_factor.T, precision=lax.Precision.HIGHEST)
    new_error = (corrected - approximation).astype(jnp.bfloat16)
    return (input_grad.reshape(1, brick_count, -1, in_width), q_factor, new_error[None, None])


def solution(mesh):
    in_specs = (
        P("dp", "space", None, None),
        P("dp", "space", None, None),
        P("dp", "space", None),
        P("dp", "space", None),
        P(),
        P("dp", "space", None, None),
        P(),
    )
    out_specs = (P("dp", "space", None, None), P(), P("dp", "space", None, None))
    return jax.shard_map(body, mesh=mesh, in_specs=in_specs, out_specs=out_specs, check_vma=False)
```

profile of v0, /device:TPU:1, one launch (start us, length us, event | category | flops | bytes accessed | tf_op | source)
XLA Modules:
  0.0 699.4 jit_solution(16967134328860178509)
XLA Ops:
  10.9 2.8 copy_multiply_fusion
  15.0 7.1 %collective-permute-start = (bf16[2,8,8,8,256]{4,1,0,3,2:T(8,128)(2,1)}, bf16[2,8,8,8,256]{4,1,0,3,2:T(8,128)(2,1)}, u32[]{:S(2)}, u32[]{:S(2)}) collective-permute-start(bf16[2,8,8,8,256]{4,1,0,3,2:T(8,128)(2,1)} %get-tuple-element.146), channel_id=1, source_target_pairs={{0,1},{1,2},{2,3},{3,4},{4,5},{5,6},{6,7},{7,8},{8,9},{9,10},{10,1... | collective-permute-start | bytes 1572872 | tf_op jit(solution)/shard_map/ppermute | solution.py:12
  23.3 6.4 collective-permute-start.2
  29.8 2.4 compare_reduce_fusion.9
  32.2 2.3 maximum_reduce_fusion.8
  42.7 2.2 fusion.79
  45.9 2.2 fusion.85
  95.7 2.1 gather_fusion.13
  104.3 2.1 gather_fusion.31
  116.5 2.1 gather_fusion.7
  122.4 2.6 gather_fusion.40
  124.9 2.6 gather_fusion.4
  136.2 2.1 gather_fusion.1
  165.8 2.4 select_select_fusion
  219.7 2.1 gather_fusion.41
  221.8 2.1 gather_fusion.5
  231.4 2.1 gather_fusion.3
  249.4 2.8 pad_maximum_fusion.4
  252.2 2.8 maximum_maximum_fusion.4
  258.9 2.5 fusion.72
  293.7 2.8 fusion.71
  306.7 5.9 convolution_add_fusion
  312.6 2.8 copy-done.1
  315.4 7.5 %fusion.87 = f32[6912,32]{0,1:T(8,128)} fusion(f32[6912,256]{1,0:T(8,128)S(1)} %convolution_add_fusion, f32[256,32]{0,1:T(8,128)S(1)} %copy-done.51), kind=kOutput, calls=%fused_computation.488 | convolution fusion | flops 679477248 | bytes 7995392 | tf_op jit(solution)/shard_map/dot_general | solution.py:99
  348.2 9.9 %fusion.3 = bf16[1024,256]{1,0:T(8,128)(2,1)} fusion(bf16[1024,27,256]{2,0,1:T(8,128)(2,1)} %constant_dynamic-update-slice_fusion, bf16[27,256,256]{2,1,0:T(8,128)(2,1)S(1)} %copy-done, f32[1024]{0:T(1024)S(1)} %bitcast.557), kind=kOutput, calls=%fused_computation.64 | convolution fusion | flops 3624402944 | bytes 18223104 | tf_op jit(solution)/shard_map/dot_general | solution.py:74
  358.2 225.1 %all-reduce.2.cloned.1.call-done = f32[6912,32]{0,1:T(8,128)} async-done(((f32[6912,32]{0,1:T(8,128)}), f32[6912,32]{0,1:T(8,128)}) %all-reduce.2.cloned.1.call-update) | async-done | bytes 884752 | tf_op jit(solution)/shard_map/psum | solution.py:103
  583.3 2.3 fusion.6
  587.7 3.6 cholesky.16
  593.2 3.2 custom-call.6
  599.4 6.5 fusion.88
  605.9 76.4 %psum.15 = f32[256,32]{0,1:T(8,128)} all-reduce(f32[256,32]{0,1:T(8,128)} %fusion.88), channel_id=1, replica_groups=mesh['dp'=4,'space'=64] {'dp','space'}, use_global_device_ids=true, to_apply=%region_3.12 | all-reduce | flops 8192 | bytes 65536 | tf_op jit(solution)/shard_map/psum | solution.py:116
  683.0 9.3 %fusion.1 = bf16[1,1,6912,256]{3,2,1,0:T(8,128)(2,1)} fusion(f32[6912,256]{1,0:T(8,128)} %copy-done.1, f32[6912,32]{0,1:T(8,128)} %copy-done.5, f32[256,32]{0,1:T(8,128)S(1)} %broadcast_multiply_fusion.1), kind=kOutput, calls=%fused_computation.57 | convolution fusion | flops 683016192 | bytes 11534336 | tf_op jit(solution)/shard_map/dot_general | solution.py:117
  (536 shorter events, 272.2 us)
Async XLA Ops:
  7.2 341.1 %copy-start = (bf16[27,256,256]{2,1,0:T(8,128)(2,1)S(1)}, bf16[27,256,256]{2,1,0:T(8,128)(2,1)}, u32[]{:S(2)}) copy-start(bf16[27,256,256]{2,1,0:T(8,128)(2,1)} %param.27) | copy-start | bytes 10616836
  7.2 40.8 %copy-start.8 = (s32[1,2,27]{2,1,0:T(2,128)S(1)}, s32[1,2,27]{2,1,0:T(2,128)}, u32[]{:S(2)}) copy-start(s32[1,2,27]{2,1,0:T(2,128)} %param.26) | copy-start | bytes 652
  7.2 576.1 %all-reduce.2.cloned.1.call-start = ((), (), s32[]{:S(2)}) async-start(), calls=%async_computation | async-start | bytes 1769472 | tf_op jit(solution)/shard_map/psum | solution.py:103
  8.7 50.4 %copy-start.75 = (bf16[1,2,512]{2,1,0:T(2,128)(2,1)}, bf16[1,2,512]{2,1,0:T(2,128)(2,1)S(1)}, u32[]{:S(2)}) copy-start(bf16[1,2,512]{2,1,0:T(2,128)(2,1)S(1)} %get-tuple-element.66) | copy-start | bytes 6148
  13.7 160.3 %collective-permute-start.1 = (bf16[2,8,8,8,256]{4,1,0,3,2:T(8,128)(2,1)}, bf16[2,8,8,8,256]{4,1,0,3,2:T(8,128)(2,1)}, u32[]{:S(2)}, u32[]{:S(2)}) collective-permute-start(bf16[2,8,8,8,256]{4,1,0,3,2:T(8,128)(2,1)} %get-tuple-element.146), channel_id=1, source_target_pairs={{1,0},{2,1},{3,2},{4,3},{5,4},{6,5},{7,6},{8,7},{9,8},{10,9},{11,1... | collective-permute-start | bytes 1572872 | tf_op jit(solution)/shard_map/ppermute | solution.py:12
  15.0 162.9 %collective-permute-start = (bf16[2,8,8,8,256]{4,1,0,3,2:T(8,128)(2,1)}, bf16[2,8,8,8,256]{4,1,0,3,2:T(8,128)(2,1)}, u32[]{:S(2)}, u32[]{:S(2)}) collective-permute-start(bf16[2,8,8,8,256]{4,1,0,3,2:T(8,128)(2,1)} %get-tuple-element.146), channel_id=1, source_target_pairs={{0,1},{1,2},{2,3},{3,4},{4,5},{5,6},{6,7},{7,8},{8,9},{9,10},{10,1... | collective-permute-start | bytes 1572872 | tf_op jit(solution)/shard_map/ppermute | solution.py:12
  22.0 150.5 %collective-permute-start.3 = (bf16[2,8,8,8,256]{4,1,0,3,2:T(8,128)(2,1)}, bf16[2,8,8,8,256]{4,1,0,3,2:T(8,128)(2,1)}, u32[]{:S(2)}, u32[]{:S(2)}) collective-permute-start(bf16[2,8,8,8,256]{4,1,0,3,2:T(8,128)(2,1)} %get-tuple-element.145), channel_id=1, source_target_pairs={{1,0},{2,1},{3,2},{4,3},{5,4},{6,5},{7,6},{8,7},{9,8},{10,9},{11,1... | collective-permute-start | bytes 1572872 | tf_op jit(solution)/shard_map/ppermute | solution.py:12
  23.3 155.9 %collective-permute-start.2 = (bf16[2,8,8,8,256]{4,1,0,3,2:T(8,128)(2,1)}, bf16[2,8,8,8,256]{4,1,0,3,2:T(8,128)(2,1)}, u32[]{:S(2)}, u32[]{:S(2)}) collective-permute-start(bf16[2,8,8,8,256]{4,1,0,3,2:T(8,128)(2,1)} %get-tuple-element.145), channel_id=1, source_target_pairs={{0,1},{1,2},{2,3},{3,4},{4,5},{5,6},{6,7},{7,8},{8,9},{9,10},{10,1... | collective-permute-start | bytes 1572872 | tf_op jit(solution)/shard_map/ppermute | solution.py:12
  59.7 92.6 %copy-start.50 = (bf16[2,1,1,8,256]{4,1,0,3,2:T(2,128)(2,1)S(1)}, bf16[2,1,1,8,256]{4,1,0,3,2:T(2,128)(2,1)}, u32[]{:S(2)}) copy-start(bf16[2,1,1,8,256]{4,1,0,3,2:T(2,128)(2,1)} %get-tuple-element.102) | copy-start | bytes 24580
  152.9 16.1 %copy-start.63 = (bf16[2,8,256]{2,1,0:T(8,128)(2,1)S(1)}, bf16[2,8,256]{2,1,0:T(8,128)(2,1)}, u32[]{:S(2)}) copy-start(bf16[2,8,256]{2,1,0:T(8,128)(2,1)} %gather_fusion.52) | copy-start | bytes 24580
  152.9 16.1 %copy-start.64 = (bf16[2,8,256]{2,1,0:T(8,128)(2,1)S(1)}, bf16[2,8,256]{2,1,0:T(8,128)(2,1)}, u32[]{:S(2)}) copy-start(bf16[2,8,256]{2,1,0:T(8,128)(2,1)} %gather_fusion.16) | copy-start | bytes 24580
  156.8 12.1 %copy-start.65 = (bf16[2,8,256]{2,1,0:T(8,128)(2,1)S(1)}, bf16[2,8,256]{2,1,0:T(8,128)(2,1)}, u32[]{:S(2)}) copy-start(bf16[2,8,256]{2,1,0:T(8,128)(2,1)} %gather_fusion.10) | copy-start | bytes 24580
  156.8 12.1 %copy-start.66 = (bf16[2,8,256]{2,1,0:T(8,128)(2,1)S(1)}, bf16[2,8,256]{2,1,0:T(8,128)(2,1)}, u32[]{:S(2)}) copy-start(bf16[2,8,256]{2,1,0:T(8,128)(2,1)} %gather_fusion.46) | copy-start | bytes 24580
  156.9 12.1 %copy-start.95 = (pred[2]{0:T(512)(128)(4,1)S(1)}, pred[2]{0:T(512)(128)(4,1)}, u32[]{:S(2)}) copy-start(pred[2]{0:T(512)(128)(4,1)} %get-tuple-element.40) | copy-start | bytes 10
  156.9 12.8 %copy-start.43 = (bf16[2,8,8,256]{3,2,1,0:T(8,128)(2,1)S(1)}, bf16[2,8,8,256]{3,2,1,0:T(8,128)(2,1)}, u32[]{:S(2)}) copy-start(bf16[2,8,8,256]{3,2,1,0:T(8,128)(2,1)} %gather_fusion.49) | copy-start | bytes 196612
  156.9 12.8 %copy-start.44 = (bf16[2,8,8,256]{3,2,1,0:T(8,128)(2,1)S(1)}, bf16[2,8,8,256]{3,2,1,0:T(8,128)(2,1)}, u32[]{:S(2)}) copy-start(bf16[2,8,8,256]{3,2,1,0:T(8,128)(2,1)} %gather_fusion.13) | copy-start | bytes 196612
  156.9 12.8 %copy-start.45 = (bf16[2,8,8,256]{3,2,1,0:T(8,128)(2,1)S(1)}, bf16[2,8,8,256]{3,2,1,0:T(8,128)(2,1)}, u32[]{:S(2)}) copy-start(bf16[2,8,8,256]{3,2,1,0:T(8,128)(2,1)} %gather_fusion.22) | copy-start | bytes 196612
  156.9 12.8 %copy-start.46 = (bf16[2,8,8,256]{3,2,1,0:T(8,128)(2,1)S(1)}, bf16[2,8,8,256]{3,2,1,0:T(8,128)(2,1)}, u32[]{:S(2)}) copy-start(bf16[2,8,8,256]{3,2,1,0:T(8,128)(2,1)} %gather_fusion.31) | copy-start | bytes 196612
  156.9 12.8 %copy-start.103 = (pred[2]{0:T(512)(128)(4,1)S(1)}, pred[2]{0:T(512)(128)(4,1)}, u32[]{:S(2)}) copy-start(pred[2]{0:T(512)(128)(4,1)} %get-tuple-element.35) | copy-start | bytes 10
  156.9 12.8 %copy-start.104 = (pred[2]{0:T(512)(128)(4,1)S(1)}, pred[2]{0:T(512)(128)(4,1)}, u32[]{:S(2)}) copy-start(pred[2]{0:T(512)(128)(4,1)} %get-tuple-element.43) | copy-start | bytes 10
  157.0 12.8 %copy-start.116 = (pred[2]{0:T(512)(128)(4,1)S(1)}, pred[2]{0:T(512)(128)(4,1)}, u32[]{:S(2)}) copy-start(pred[2]{0:T(512)(128)(4,1)} %compare_and_fusion.13) | copy-start | bytes 10
  157.0 12.8 %copy-start.117 = (pred[2]{0:T(512)(128)(4,1)S(1)}, pred[2]{0:T(512)(128)(4,1)}, u32[]{:S(2)}) copy-start(pred[2]{0:T(512)(128)(4,1)} %compare_and_fusion.4) | copy-start | bytes 10
  157.0 13.6 %copy-start.67 = (bf16[2,8,256]{2,1,0:T(8,128)(2,1)S(1)}, bf16[2,8,256]{2,1,0:T(8,128)(2,1)}, u32[]{:S(2)}) copy-start(bf16[2,8,256]{2,1,0:T(8,128)(2,1)} %gather_fusion.34) | copy-start | bytes 24580
  157.0 13.6 %copy-start.68 = (bf16[2,8,256]{2,1,0:T(8,128)(2,1)S(1)}, bf16[2,8,256]{2,1,0:T(8,128)(2,1)}, u32[]{:S(2)}) copy-start(bf16[2,8,256]{2,1,0:T(8,128)(2,1)} %gather_fusion.25) | copy-start | bytes 24580
  157.0 13.6 %copy-start.69 = (bf16[2,8,256]{2,1,0:T(8,128)(2,1)S(1)}, bf16[2,8,256]{2,1,0:T(8,128)(2,1)}, u32[]{:S(2)}) copy-start(bf16[2,8,256]{2,1,0:T(8,128)(2,1)} %gather_fusion.19) | copy-start | bytes 24580
  157.0 13.6 %copy-start.70 = (bf16[2,8,256]{2,1,0:T(8,128)(2,1)S(1)}, bf16[2,8,256]{2,1,0:T(8,128)(2,1)}, u32[]{:S(2)}) copy-start(bf16[2,8,256]{2,1,0:T(8,128)(2,1)} %gather_fusion.28) | copy-start | bytes 24580
  157.0 13.6 %copy-start.93 = (pred[2]{0:T(512)(128)(4,1)S(1)}, pred[2]{0:T(512)(128)(4,1)}, u32[]{:S(2)}) copy-start(pred[2]{0:T(512)(128)(4,1)} %get-tuple-element.32) | copy-start | bytes 10
  157.0 13.6 %copy-start.94 = (pred[2]{0:T(512)(128)(4,1)S(1)}, pred[2]{0:T(512)(128)(4,1)}, u32[]{:S(2)}) copy-start(pred[2]{0:T(512)(128)(4,1)} %get-tuple-element.38) | copy-start | bytes 10
  157.0 13.6 %copy-start.110 = (pred[2]{0:T(512)(128)(4,1)S(1)}, pred[2]{0:T(512)(128)(4,1)}, u32[]{:S(2)}) copy-start(pred[2]{0:T(512)(128)(4,1)} %compare_and_fusion.1) | copy-start | bytes 10
  157.0 13.6 %copy-start.111 = (pred[2]{0:T(512)(128)(4,1)S(1)}, pred[2]{0:T(512)(128)(4,1)}, u32[]{:S(2)}) copy-start(pred[2]{0:T(512)(128)(4,1)} %compare_and_fusion.7) | copy-start | bytes 10
  157.1 14.3 %copy-start.107 = (s32[2]{0:T(128)S(1)}, s32[2]{0:T(128)}, u32[]{:S(2)}) copy-start(s32[2]{0:T(128)} %get-tuple-element.6) | copy-start | bytes 28
  262.2 29.4 %copy-start.56 = (bf16[2,1,1,8,256]{4,3,2,1,0:T(8,128)(2,1)S(1)}, bf16[2,1,1,8,256]{4,3,2,1,0:T(8,128)(2,1)}, u32[]{:S(2)}) copy-start(bf16[2,1,1,8,256]{4,3,2,1,0:T(8,128)(2,1)} %get-tuple-element.180) | copy-start | bytes 24580
  (91 other events, 590.5 us)
Sparse Core Ops, SparseCore 0:
  323.0 260.2 all-reduce.1
where the time goes:
time: 712 us; the launch traced here: 699 us
  waiting for transfers between devices  225 us (32%)
  local copies, waits for them, and re-layouts  209 us (29%)
  other arithmetic  113 us (16%)
  blocking collectives  76.4 us (11%)
  matrix products  43.5 us (6%)
  starting transfers between devices  16.1 us (2%)
  between operations  16 us (2%)
    psum x1, waiting for transfers between devices, body(): p_summed = lax.psum(p_local, ('dp', 'space')) / devices  225 us
    gather x54, local copies, waits for them, and re-layouts, neighbourhood(): gathered = jnp.take(source_block, jnp.maximum(slot_index, 0), axis=0)  91.2 us
    psum x1, blocking collectives, body(): q_factor = lax.psum(q_local, ('dp', 'space')) / devices  76.4 us
    unnamed x303, local copies, waits for them, and re-layouts  40.2 us
    gather x27, other arithmetic  30.6 us
    slice x17, local copies, waits for them, and re-layouts, pick_edge(): return lax.slice_in_dim(source_block, extent - 1, extent, axis=dim_index)  20.8 us
    select_n x18, other arithmetic, neighbourhood(): z_pieces.append(jnp.where(valid, gathered, jnp.zeros_like(gathered)))  20.2 us
    another operation x17, local copies, waits for them, and re-layouts, neighbourhood(): gathered = jnp.take(source_block, jnp.maximum(slot_index, 0), axis=0)  18.9 us
  transfers between devices with their start and end apart: 5, of which 1 were waited for; matrix products, arithmetic and copies ran while one was open for 26% of the time, Pallas kernels for 0%

commit v1 on v0

v1 whole, which is shorter than its diff:
```python
import jax
import jax.numpy as jnp
from jax import lax
from jax.experimental import pallas as pl
from jax.experimental.pallas import tpu as pltpu
from jax.sharding import PartitionSpec as P

EDGE = 8
PLANE = EDGE * EDGE
F32 = jnp.float32
BF16 = jnp.bfloat16
NT = (((1,), (1,)), ((), ()))
NN = (((1,), (0,)), ((), ()))
STEPS = (-1, 0, 1)


def split(value):
    high = value.astype(BF16)
    low = (value - high.astype(F32)).astype(BF16)
    return high, low


def source_rows(slots, step_x, step_y, step_z, along):
    shape = (128, 1) if along == 0 else (1, 128)
    place = lax.broadcasted_iota(jnp.int32, shape, along)
    brick = place // PLANE
    y = (place // EDGE) % EDGE + step_y
    z = place % EDGE + step_z
    wrapped_y = y % EDGE
    wrapped_z = z % EDGE
    rows = jnp.full(shape, -1, jnp.int32)
    for side_y in sorted({0, step_y}):
        in_y = (y < 0) if side_y < 0 else (y >= EDGE) if side_y > 0 else (y >= 0) & (y < EDGE)
        for side_z in sorted({0, step_z}):
            in_z = (z < 0) if side_z < 0 else (z >= EDGE) if side_z > 0 else (z >= 0) & (z < EDGE)
            if side_z == 0:
                offset = wrapped_y * EDGE + wrapped_z
                first, stride = 0, PLANE
            else:
                offset = wrapped_y
                first, stride = (128 if side_z < 0 else 144), EDGE
            for which in (0, 1):
                slot = slots[which, (step_x + 1) * 9 + (side_y + 1) * 3 + side_z + 1]
                base = jnp.where(slot < 0, -4096, slot * stride + first)
                rows = jnp.where(in_y & in_z & (brick == which), base + offset, rows)
    return rows


def one_hot(rows, along):
    shape = (128, 256) if along == 0 else (256, 128)
    places = lax.broadcasted_iota(jnp.int32, shape, 1 - along)
    return jnp.where(places == rows, 1.0, 0.0).astype(BF16)


def own_plane(field, mask, plane):
    rows = jnp.concatenate(
        [field[0, plane * PLANE : (plane + 1) * PLANE, :], field[1, plane * PLANE : (plane + 1) * PLANE, :]],
        axis=0,
    )
    return rows * mask[:, plane : plane + 1]


def source_plane(field, mask, lower, upper, plane):
    own = own_plane(field, mask, plane)
    return jnp.concatenate(
        [own, lower[plane], upper[plane], jnp.zeros((96, own.shape[1]), BF16)], axis=0
    )


def groups():
    return [(step_y, step_z) for step_y in STEPS for step_z in STEPS]


def coordinates():
    dp, space = lax.axis_index("dp"), lax.axis_index("space")
    return dp % 2, space // 16, (space % 2) * 2 + dp // 2, (space // 2) % 8


def place_of(tap, y):
    return ((tap // 7) ^ y) * 7 + tap % 7


def put_factor(mine, other, tap, value):
    core, x, y, _ = coordinates()
    place = place_of(tap, y)
    halves = value[:, :128], value[:, 128:]
    kept = jnp.where(core == 0, halves[0], halves[1])
    sent = jnp.where(core == 0, halves[1], halves[0])
    for block in range(4):
        rows = slice(block * 8, block * 8 + 8)
        mine[block ^ x, place] = kept[rows]
        other[block ^ x, place] = sent[rows]


def get_factor(mine, other, tap):
    core, x, y, _ = coordinates()
    place = place_of(tap, y)
    own = jnp.concatenate([mine[block ^ x, place] for block in range(4)], axis=0)
    rest = jnp.concatenate([other[block ^ x, place] for block in range(4)], axis=0)
    both = jnp.concatenate(
        [jnp.where(core == 0, own, rest), jnp.where(core == 0, rest, own)], axis=1
    )
    return both * (1.0 / 256.0)


def gradient_kernel(slots, field, cotangent, occupancy, lower, upper, start, error, corrected, mine, other, views, own, start_split):
    group = pl.program_id(0)

    @pl.when(group == 0)
    def _():
        mask = occupancy[...].T.astype(BF16)
        high, low = split(start[...].T)
        start_split[0:32, :] = high
        start_split[32:64, :] = low
        sources = []
        for plane in range(EDGE):
            own[plane * 128 : (plane + 1) * 128, :] = own_plane(cotangent, mask, plane)
            sources.append(source_plane(field, mask, lower, upper, plane).T)
        inner = jnp.concatenate(sources, axis=0)
        for first in range(0, 9, 2):
            pair = groups()[first : first + 2]
            for step_x, left, where in ((-1, sources[7], 0), (0, inner, 1), (1, sources[0], 9)):
                picks = jnp.concatenate(
                    [one_hot(source_rows(slots, step_x, y, z, 1), 1) for y, z in pair], axis=1
                )
                found = lax.dot_general(left, picks, NN, preferred_element_type=F32).astype(BF16)
                for member in range(len(pair)):
                    for block in range(left.shape[0] // 256):
                        views[first + member, :, (where + block) * 128 : (where + block + 1) * 128] = found[
                            block * 256 : (block + 1) * 256, member * 128 : (member + 1) * 128
                        ]

    for tap_x in range(3):
        columns = views[group, :, tap_x * 128 : tap_x * 128 + 1024]
        total = lax.dot_general(columns, own[...], NN, preferred_element_type=F32)
        total = total + error[tap_x, 0].astype(F32)
        corrected[tap_x, 0] = total
        high, low = split(total)
        both = lax.dot_general(start_split[...], high, NT, preferred_element_type=F32)
        rest = lax.dot_general(start_split[0:32, :], low, NT, preferred_element_type=F32)
        put_factor(mine, other, tap_x * 9 + group, both[0:32] + both[32:64] + rest)

    @pl.when(group == 8)
    def _():
        put_factor(mine, other, 27, jnp.zeros((32, 256), F32))


def local_gradient(slots, field, cotangent, occupancy, lower, upper, start, error):
    whole = lambda *shape: pl.BlockSpec(shape, lambda group: (0,) * len(shape))
    taps = lambda *shape: pl.BlockSpec((3, 1) + shape, lambda group: (0, group, 0, 0))
    return pl.pallas_call(
        gradient_kernel,
        grid=(9,),
        in_specs=[
            pl.BlockSpec(memory_space=pltpu.SMEM),
            whole(2, 512, 256),
            whole(2, 512, 256),
            whole(8, 128),
            whole(8, 16, 256),
            whole(8, 16, 256),
            whole(256, 32),
            taps(256, 256),
        ],
        out_specs=[taps(256, 256), whole(4, 28, 8, 128), whole(4, 28, 8, 128)],
        out_shape=[
            jax.ShapeDtypeStruct((3, 9, 256, 256), F32),
            jax.ShapeDtypeStruct((4, 28, 8, 128), F32),
            jax.ShapeDtypeStruct((4, 28, 8, 128), F32),
        ],
        scratch_shapes=[
            pltpu.VMEM((9, 256, 1280), BF16),
            pltpu.VMEM((1024, 256), BF16),
            pltpu.VMEM((64, 256), BF16),
        ],
        compiler_params=pltpu.CompilerParams(vmem_limit_bytes=48 * 1024 * 1024),
        cost_estimate=pl.CostEstimate(flops=6 * 10**9, bytes_accessed=14 * 10**6, transcendentals=0),
        name="local_gradient",
    )(slots, field, cotangent, occupancy, lower, upper, start, error)


def input_kernel(slots, cotangent, occupancy, lower, upper, weight, grad, views, mask_rows, total):
    group = pl.program_id(0)

    @pl.when(group == 0)
    def _():
        mask_rows[...] = occupancy[...].T
        mask = mask_rows[...].astype(BF16)
        sources = [source_plane(cotangent, mask, lower, upper, plane) for plane in range(EDGE)]
        for first in range(9):
            y, z = groups()[first]
            picks = [one_hot(source_rows(slots, step_x, y, z, 0), 0) for step_x in STEPS]
            for plane in range(-1, EDGE + 1):
                side = -1 if plane < 0 else 1 if plane >= EDGE else 0
                found = lax.dot_general(
                    picks[side + 1], sources[plane % EDGE], NN, preferred_element_type=F32
                )
                views[first, (plane + 1) * 128 : (plane + 2) * 128, :] = found.astype(BF16)
        total[...] = jnp.zeros_like(total)

    columns = jnp.concatenate(
        [views[8 - group, (2 - tap_x) * 128 : (2 - tap_x) * 128 + 1024, :] for tap_x in range(3)], axis=1
    )
    weights = jnp.concatenate([weight[tap_x, 0] for tap_x in range(3)], axis=1)
    total[...] += lax.dot_general(columns, weights, NT, preferred_element_type=F32)

    @pl.when(group == 8)
    def _():
        for plane in range(EDGE):
            rows = total[plane * 128 : (plane + 1) * 128, :] * mask_rows[:, plane : plane + 1]
            for brick in (0, 1):
                grad[brick, plane * PLANE : (plane + 1) * PLANE, :] = rows[
                    brick * PLANE : (brick + 1) * PLANE
                ].astype(BF16)


def input_gradient(slots, cotangent, occupancy, lower, upper, weight):
    whole = lambda *shape: pl.BlockSpec(shape, lambda group: (0,) * len(shape))
    taps = lambda *shape: pl.BlockSpec((3, 1) + shape, lambda group: (0, group, 0, 0))
    return pl.pallas_call(
        input_kernel,
        grid=(9,),
        in_specs=[
            pl.BlockSpec(memory_space=pltpu.SMEM),
            whole(2, 512, 256),
            whole(8, 128),
            whole(8, 16, 256),
            whole(8, 16, 256),
            taps(256, 256),
        ],
        out_specs=whole(2, 512, 256),
        out_shape=jax.ShapeDtypeStruct((2, 512, 256), BF16),
        scratch_shapes=[
            pltpu.VMEM((9, 1280, 256), BF16),
            pltpu.VMEM((128, 8), F32),
            pltpu.VMEM((1024, 256), F32),
        ],
        compiler_params=pltpu.CompilerParams(vmem_limit_bytes=48 * 1024 * 1024),
        cost_estimate=pl.CostEstimate(flops=6 * 10**9, bytes_accessed=6 * 10**6, transcendentals=0),
        name="input_gradient",
    )(slots, cotangent, occupancy, lower, upper, weight)


def right_kernel(mine, other, corrected, right, gram):
    step = pl.program_id(0)

    @pl.when(step == 0)
    def _():
        right[...] = jnp.zeros_like(right)
        gram[...] = jnp.zeros_like(gram)

    left = jnp.concatenate([get_factor(mine, other, step * 3 + tap) for tap in range(3)], axis=1)
    gram[...] += lax.dot_general(left, left, NT, precision=lax.Precision.HIGHEST, preferred_element_type=F32)
    left_high, left_low = split(left)
    high, low = split(corrected[...].reshape(768, 256))
    both = lax.dot_general(
        jnp.concatenate([left_high, left_low], axis=0), high, NN, preferred_element_type=F32
    )
    rest = lax.dot_general(left_high, low, NN, preferred_element_type=F32)
    right[...] += both[0:32] + both[32:64] + rest


def right_product(mine, other, corrected):
    blocks = lambda *shape: pl.BlockSpec((3,) + shape, lambda step: (step, 0, 0))
    whole = lambda *shape: pl.BlockSpec(shape, lambda step: (0,) * len(shape))
    return pl.pallas_call(
        right_kernel,
        grid=(9,),
        in_specs=[whole(4, 28, 8, 128), whole(4, 28, 8, 128), blocks(256, 256)],
        out_specs=[whole(32, 256), whole(32, 32)],
        out_shape=[jax.ShapeDtypeStruct((32, 256), F32), jax.ShapeDtypeStruct((32, 32), F32)],
        compiler_params=pltpu.CompilerParams(vmem_limit_bytes=32 * 1024 * 1024),
        name="right_product",
    )(mine, other, corrected)


def inverse_kernel(gram, inverse):
    places = lax.broadcasted_iota(jnp.int32, (32, 32), 0)
    columns = lax.broadcasted_iota(jnp.int32, (32, 32), 1)
    work = gram[...]
    made = jnp.where(places == columns, 1.0, 0.0).astype(F32)
    row_index = lax.broadcasted_iota(jnp.int32, (32, 1), 0)
    for step in range(32):
        scale = 1.0 / jnp.sqrt(work[step : step + 1, step : step + 1])
        work_row = work[step : step + 1, :] * scale
        made_row = made[step : step + 1, :] * scale
        column = work[:, step : step + 1] * scale
        later = jnp.where(row_index > step, column, 0.0)
        here = row_index == step
        work = jnp.where(here, work_row, work - later * work_row)
        made = jnp.where(here, made_row, made - later * made_row)
    inverse[...] = made


def inverse_factor(gram):
    return pl.pallas_call(
        inverse_kernel, out_shape=jax.ShapeDtypeStruct((32, 32), F32), name="inverse_factor"
    )(gram)


def error_kernel(mine, other, corrected, right, inverse, new_error, q_factor, basis):
    step = pl.program_id(0)

    @pl.when(step == 0)
    def _():
        q_rows = lax.dot_general(
            inverse[...], right[...], NN, precision=lax.Precision.HIGHEST, preferred_element_type=F32
        ) * (1.0 / 256.0)
        q_factor[...] = q_rows.T
        back = lax.dot_general(
            inverse[...].T, q_rows, NN, precision=lax.Precision.HIGHEST, preferred_element_type=F32
        )
        high, low = split(back)
        basis[0:32, :] = high
        basis[32:64, :] = high
        basis[64:96, :] = low
        basis[96:128, :] = jnp.zeros((32, 256), BF16)

    for tap in range(3):
        high, low = split(get_factor(mine, other, step * 3 + tap))
        left = jnp.concatenate([high, low, high, jnp.zeros((32, 256), BF16)], axis=0).T
        product = lax.dot_general(left, basis[...], NN, preferred_element_type=F32)
        new_error[tap] = (corrected[tap] - product).astype(BF16)


def remaining_error(mine, other, corrected, right, inverse):
    blocks = lambda *shape: pl.BlockSpec((3,) + shape, lambda step: (step, 0, 0))
    whole = lambda *shape: pl.BlockSpec(shape, lambda step: (0,) * len(shape))
    return pl.pallas_call(
        error_kernel,
        grid=(9,),
        in_specs=[whole(4, 28, 8, 128), whole(4, 28, 8, 128), blocks(256, 256), whole(32, 256), whole(32, 32)],
        out_specs=[blocks(256, 256), whole(256, 32)],
        out_shape=[jax.ShapeDtypeStruct((27, 256, 256), BF16), jax.ShapeDtypeStruct((256, 32), F32)],
        scratch_shapes=[pltpu.VMEM((128, 256), BF16)],
        compiler_params=pltpu.CompilerParams(vmem_limit_bytes=32 * 1024 * 1024),
        name="remaining_error",
    )(mine, other, corrected, right, inverse)


def face(field, occupied, at):
    chosen = field.reshape(2, EDGE, EDGE, EDGE, -1)[:, :, :, at, :]
    kept = occupied.reshape(2, EDGE, EDGE, EDGE)[:, :, :, at].astype(BF16)
    return (chosen * kept[..., None]).transpose(1, 0, 2, 3).reshape(EDGE, 2 * EDGE, -1)


def shifted(value, by):
    devices = lax.axis_size("space")
    return lax.ppermute(value, "space", [(i, i + by) for i in range(devices) if 0 <= i + by < devices])


def partners(core=0, x=0, y=0, z=0):
    def place(at_core, at_x, at_y, at_z):
        return (at_y % 2 * 2 + at_core) * 64 + (at_x * 8 + at_z) * 2 + at_y // 2

    return [
        (place(c, i, j, l), place(c ^ core, i ^ x, j ^ y, l ^ z))
        for c in range(2)
        for i in range(4)
        for j in range(4)
        for l in range(8)
    ]


def swapped(value, **bits):
    return lax.ppermute(value, ("dp", "space"), partners(**bits))


def added(values):
    return (values[0] + values[1]) + (values[2] + values[3])


def summed_among(value, steps):
    return added([value] + [swapped(value, **bits) for bits in steps])


ALONG_X = [dict(x=1), dict(x=2), dict(x=3)]
ALONG_Y = [dict(y=1), dict(y=2), dict(y=3)]
ALONG_Z = [dict(z=2), dict(z=4), dict(z=6)]
CORE_AND_Z = [dict(core=1), dict(z=1), dict(core=1, z=1)]


def factor_sum(mine, other):
    part = mine + swapped(other, core=1)
    part = added([part[0]] + [swapped(part[k], x=k) for k in (1, 2, 3)])
    part = part.reshape(4, 7, 8, 128)
    part = added([part[0]] + [swapped(part[k], y=k) for k in (1, 2, 3)])
    part = summed_among(part, ALONG_Z)
    part = part + swapped(part, z=1)
    part = jnp.concatenate([part] + [swapped(part, **bits) for bits in ALONG_Y], axis=0)
    part = jnp.stack([part] + [swapped(part, **bits) for bits in ALONG_X], axis=0)
    return part, swapped(part, core=1)


def right_sum(value):
    for steps in (CORE_AND_Z, ALONG_X, ALONG_Y, ALONG_Z):
        value = summed_among(value, steps)
    return value


def body(inputs, cotangent, occupancy, neighbours, weight, error_in, q_start):
    field, gradient, occupied, slots = inputs[0], cotangent[0], occupancy[0], neighbours[0]
    mask = occupied.reshape(2, EDGE, PLANE).transpose(1, 0, 2).reshape(EDGE, 2 * PLANE).astype(F32)
    lower_field = shifted(face(field, occupied, EDGE - 1), 1)
    upper_field = shifted(face(field, occupied, 0), -1)
    lower_gradient = shifted(face(gradient, occupied, EDGE - 1), 1)
    upper_gradient = shifted(face(gradient, occupied, 0), -1)
    corrected, mine, other = local_gradient(
        slots, field, gradient, mask, lower_field, upper_field, q_start, error_in.reshape(3, 9, 256, 256)
    )
    corrected = corrected.reshape(27, 256, 256)
    mine, other = factor_sum(mine, other)
    input_grad = input_gradient(
        slots, gradient, mask, lower_gradient, upper_gradient, weight.reshape(3, 9, 256, 256)
    )
    right, gram = right_product(mine, other, corrected)
    right = right_sum(right)
    inverse = inverse_factor(gram)
    new_error, q_factor = remaining_error(mine, other, corrected, right, inverse)
    return (input_grad[None], q_factor, new_error.reshape(1, 1, 6912, 256))


def solution(mesh):
    in_specs = (
        P("dp", "space", None, None),
        P("dp", "space", None, None),
        P("dp", "space", None),
        P("dp", "space", None),
        P(),
        P("dp", "space", None, None),
        P(),
    )
    out_specs = (P("dp", "space", None, None), P(), P("dp", "space", None, None))
    return jax.shard_map(body, mesh=mesh, in_specs=in_specs, out_specs=out_specs, check_vma=False)
```

time: 712 us -> 168 us (0.24)
  the two profiles are of different devices: /device:TPU:1 before, /device:TPU:10 now
where the time goes in v1:
time: 168 us; the launch traced here: 167 us
  starting transfers between devices  65 us (39%)
  waiting for transfers between devices  42.9 us (26%)
  Pallas kernels  41.1 us (24%)
  local copies, waits for them, and re-layouts  15.8 us (9%)
    ppermute x30, starting transfers between devices, swapped(): return lax.ppermute(value, ('dp', 'space'), partners(**bits))  40.1 us
    ppermute x30, waiting for transfers between devices, swapped(): return lax.ppermute(value, ('dp', 'space'), partners(**bits))  32.3 us
    ppermute x4, starting transfers between devices, shifted(): lax.ppermute(value, 'space', [(i, i + by) for i in range(devices) if 0 <=...  25 us
    pallas_call x1, Pallas kernels, local_gradient(): pl.pallas_call(gradient_kernel, grid=(9,), in_specs=[pl.BlockSpec(memory_...  17.9 us
    unnamed x20, local copies, waits for them, and re-layouts  13 us
    ppermute x4, waiting for transfers between devices, shifted(): lax.ppermute(value, 'space', [(i, i + by) for i in range(devices) if 0 <=...  10.5 us
    pallas_call x1, Pallas kernels, input_gradient(): pl.pallas_call(input_kernel, grid=(9,), in_specs=[pl.BlockSpec(memory_spa...  9.76 us
    pallas_call x1, Pallas kernels, remaining_error(): pl.pallas_call(error_kernel, grid=(9,), in_specs=[whole(4, 28, 8, 128), w...  5.64 us
  transfers between devices with their start and end apart: 34, of which 21 were waited for; matrix products, arithmetic and copies ran while one was open for 1% of the time, Pallas kernels for 8%

profile of v1, /device:TPU:10, one launch (start us, length us, event | category | flops | bytes accessed | tf_op | source)
XLA Modules:
  0.0 166.9 jit_solution(2752068394872169255)
XLA Ops:
  1.8 2.1 %fusion.12 = (bf16[2,8,8,1,256]{4,3,2,1,0:T(2,128)(2,1)S(1)}, bf16[2,8,8,1,256]{4,3,2,1,0:T(2,128)(2,1)S(1)}, bf16[2,8,8,1,256]{4,3,2,1,0:T(2,128)(2,1)S(1)}, bf16[2,8,8,1,256]{4,3,2,1,0:T(2,128)(2,1)S(1)}) fusion(bf16[2,8,8,8,256]{4,3,2,1,0:T(8,128)(2,1)} %bitcast.74, bf16[2,8,8,8,256]{4,3,2,1,0:T(8,128)(2,1)} %bitcast.76), kind=kLoop, calls=%fused_computation.29 | loop fusion | bytes 524288 | tf_op jit(solution)/shard_map/slice | solution.py:341
  4.0 9.5 %collective-permute-start.3 = (bf16[8,16,256]{2,1,0:T(8,128)(2,1)S(1)}, bf16[8,16,256]{2,1,0:T(8,128)(2,1)S(1)}, u32[]{:S(2)}, u32[]{:S(2)}) collective-permute-start(bf16[8,16,256]{2,1,0:T(8,128)(2,1)S(1)} %get-tuple-element.40), channel_id=1, source_target_pairs={{1,0},{2,1},{3,2},{4,3},{5,4},{6,5},{7,6},{8,7},{9,8},{10,9},{11,1... | collective-permute-start | bytes 196616 | tf_op jit(solution)/shard_map/ppermute | solution.py:348
  13.7 1.9 %collective-permute-start.2 = (bf16[8,16,256]{2,1,0:T(8,128)(2,1)S(1)}, bf16[8,16,256]{2,1,0:T(8,128)(2,1)S(1)}, u32[]{:S(2)}, u32[]{:S(2)}) collective-permute-start(bf16[8,16,256]{2,1,0:T(8,128)(2,1)S(1)} %get-tuple-element.42), channel_id=1, source_target_pairs={{0,1},{1,2},{2,3},{3,4},{4,5},{5,6},{6,7},{7,8},{8,9},{9,10},{10,1... | collective-permute-start | bytes 196616 | tf_op jit(solution)/shard_map/ppermute | solution.py:348
  16.7 7.7 %collective-permute-done.2.lower = bf16[8,16,256]{2,1,0:T(8,128)(2,1)S(1)} collective-permute-done((bf16[8,16,256]{2,1,0:T(8,128)(2,1)S(1)}, bf16[8,16,256]{2,1,0:T(8,128)(2,1)S(1)}, u32[]{:S(2)}, u32[]{:S(2)}) %collective-permute-start.2) | collective-permute-done | bytes 65568 | tf_op jit(solution)/shard_map/ppermute | solution.py:348
  26.5 2.0 %copy-done.6 = bf16[1,1,6912,256]{3,2,1,0:T(8,128)(2,1)S(1)} copy-done((bf16[1,1,6912,256]{3,2,1,0:T(8,128)(2,1)S(1)}, bf16[1,1,6912,256]{3,2,1,0:T(8,128)(2,1)}, u32[]{:S(2)}) %copy-start.6) | copy-done | bytes 3538968
  29.1 17.9 %local_gradient.1 = (f32[3,9,256,256]{3,2,1,0:T(8,128)}, f32[4,28,8,128]{3,2,1,0:T(8,128)S(1)}, f32[4,28,8,128]{3,2,1,0:T(8,128)S(1)}) custom-call(s32[2,27]{1,0:T(2,128)S(1)} %bitcast.81, bf16[2,512,256]{2,1,0:T(8,128)(2,1)S(1)} %bitcast.75, bf16[2,512,256]{2,1,0:T(8,128)(2,1)S(1)} %bitcast.77, f32[8,128]{1,0:T(8,128)S(1)} %convert_element_type.18.occupancy, ...), custom_call_target="tpu_custom_call" | custom-call | flops 6000000000 | bytes 14000000 | tf_op jit(solution)/shard_map/local_gradient/pallas_call | solution.py:151
  47.0 1.8 %collective-permute-done.4 = f32[4,28,8,128]{3,2,1,0:T(8,128)S(1)} collective-permute-done((f32[4,28,8,128]{3,2,1,0:T(8,128)S(1)}, f32[4,28,8,128]{3,2,1,0:T(8,128)S(1)}, u32[]{:S(2)}, u32[]{:S(2)}) %collective-permute-start.4) | collective-permute-done | bytes 458784 | tf_op jit(solution)/shard_map/ppermute | solution.py:365
  49.0 2.9 %collective-permute-start.6 = (f32[28,8,128]{2,1,0:T(8,128)S(1)}, f32[28,8,128]{2,1,0:T(8,128)S(1)}, u32[]{:S(2)}, u32[]{:S(2)}) collective-permute-start(f32[28,8,128]{2,1,0:T(8,128)S(1)} %get-tuple-element.31), channel_id=1, source_target_pairs={{0,32},{2,34},{4,36},{6,38},{8,40},{10,42},{12,44},{14,46},{128,16... | collective-permute-start | bytes 344072 | tf_op jit(solution)/shard_map/ppermute | solution.py:365
  54.2 3.5 %collective-permute-done.6 = f32[28,8,128]{2,1,0:T(8,128)S(1)} collective-permute-done((f32[28,8,128]{2,1,0:T(8,128)S(1)}, f32[28,8,128]{2,1,0:T(8,128)S(1)}, u32[]{:S(2)}, u32[]{:S(2)}) %collective-permute-start.6) | collective-permute-done | bytes 114720 | tf_op jit(solution)/shard_map/ppermute | solution.py:365
  60.7 2.0 %collective-permute-start.9 = (f32[7,8,128]{2,1,0:T(8,128)S(1)}, f32[7,8,128]{2,1,0:T(8,128)S(1)}, u32[]{:S(2)}, u32[]{:S(2)}) collective-permute-start(f32[7,8,128]{2,1,0:T(8,128)S(1)} %get-tuple-element.36), channel_id=1, source_target_pairs={{0,1},{2,3},{4,5},{6,7},{8,9},{10,11},{12,13},{14,15},{128,129},{1... | collective-permute-start | bytes 86024 | tf_op jit(solution)/shard_map/ppermute | solution.py:365
  63.2 2.9 %collective-permute-done.9 = f32[7,8,128]{2,1,0:T(8,128)S(1)} collective-permute-done((f32[7,8,128]{2,1,0:T(8,128)S(1)}, f32[7,8,128]{2,1,0:T(8,128)S(1)}, u32[]{:S(2)}, u32[]{:S(2)}) %collective-permute-start.9) | collective-permute-done | bytes 28704 | tf_op jit(solution)/shard_map/ppermute | solution.py:365
  67.9 4.8 %collective-permute-start.13 = (f32[7,8,128]{2,1,0:T(8,128)S(1)}, f32[7,8,128]{2,1,0:T(8,128)S(1)}, u32[]{:S(2)}, u32[]{:S(2)}) collective-permute-start(f32[7,8,128]{2,1,0:T(8,128)S(1)} %fusion.10), channel_id=1, source_target_pairs={{0,12},{2,14},{4,8},{6,10},{8,4},{10,6},{12,0},{14,2},{128,140},{1... | collective-permute-start | bytes 86024 | tf_op jit(solution)/shard_map/ppermute | solution.py:365
  76.6 2.2 %collective-permute-done.14 = f32[7,8,128]{2,1,0:T(8,128)S(1)} collective-permute-done((f32[7,8,128]{2,1,0:T(8,128)S(1)}, f32[7,8,128]{2,1,0:T(8,128)S(1)}, u32[]{:S(2)}, u32[]{:S(2)}) %collective-permute-start.14) | collective-permute-done | bytes 28704 | tf_op jit(solution)/shard_map/ppermute | solution.py:365
  80.1 2.6 %collective-permute-start.16 = (f32[7,8,128]{2,1,0:T(8,128)S(1)}, f32[7,8,128]{2,1,0:T(8,128)S(1)}, u32[]{:S(2)}, u32[]{:S(2)}) collective-permute-start(f32[7,8,128]{2,1,0:T(8,128)S(1)} %add.79), channel_id=1, source_target_pairs={{0,1},{2,3},{4,5},{6,7},{8,9},{10,11},{12,13},{14,15},{128,129},{1... | collective-permute-start | bytes 86024 | tf_op jit(solution)/shard_map/ppermute | solution.py:365
  82.8 2.8 %collective-permute-done.16 = f32[7,8,128]{2,1,0:T(8,128)S(1)} collective-permute-done((f32[7,8,128]{2,1,0:T(8,128)S(1)}, f32[7,8,128]{2,1,0:T(8,128)S(1)}, u32[]{:S(2)}, u32[]{:S(2)}) %collective-permute-start.16) | collective-permute-done | bytes 28704 | tf_op jit(solution)/shard_map/ppermute | solution.py:365
  86.6 3.1 %collective-permute-start.18 = (f32[28,8,128]{2,1,0:T(8,128)S(1)}, f32[28,8,128]{2,1,0:T(8,128)S(1)}, u32[]{:S(2)}, u32[]{:S(2)}) collective-permute-start(f32[28,8,128]{2,1,0:T(8,128)S(1)} %get-tuple-element.34), channel_id=1, source_target_pairs={{0,16},{2,18},{4,20},{6,22},{8,24},{10,26},{12,28},{14,30},{128,14... | collective-permute-start | bytes 344072 | tf_op jit(solution)/shard_map/ppermute | solution.py:365
  92.5 3.5 %collective-permute-done.19 = f32[28,8,128]{2,1,0:T(8,128)S(1)} collective-permute-done((f32[28,8,128]{2,1,0:T(8,128)S(1)}, f32[28,8,128]{2,1,0:T(8,128)S(1)}, u32[]{:S(2)}, u32[]{:S(2)}) %collective-permute-start.19) | collective-permute-done | bytes 114720 | tf_op jit(solution)/shard_map/ppermute | solution.py:365
  96.2 1.8 %collective-permute-done.21.other = f32[4,28,8,128]{3,2,1,0:T(8,128)S(1)} collective-permute-done((f32[4,28,8,128]{3,2,1,0:T(8,128)S(1)}, f32[4,28,8,128]{3,2,1,0:T(8,128)S(1)}, u32[]{:S(2)}, u32[]{:S(2)}) %collective-permute-start.21) | collective-permute-done | bytes 458784 | tf_op jit(solution)/shard_map/ppermute | solution.py:365
  98.0 3.0 %copy-done = f32[3,9,256,256]{3,2,1,0:T(8,128)S(1)} copy-done((f32[3,9,256,256]{3,2,1,0:T(8,128)S(1)}, f32[3,9,256,256]{3,2,1,0:T(8,128)}, u32[]{:S(2)}) %copy-start) | copy-done | bytes 7077912
  101.0 3.5 %right_product.1 = (f32[32,256]{1,0:T(8,128)S(1)}, f32[32,32]{1,0:T(8,128)S(1)}) custom-call(f32[4,28,8,128]{3,2,1,0:T(8,128)S(1)} %pad_maximum_fusion.mine, f32[4,28,8,128]{3,2,1,0:T(8,128)S(1)} %collective-permute-done.21.other, f32[27,256,256]{2,1,0:T(8,128)S(1)} %bitcast.72), custom_call_target="tpu_custom_call" | custom-call | tf_op jit(solution)/shard_map/right_product/pallas_call | solution.py:265
  106.4 2.3 %collective-permute-done.23 = f32[32,256]{1,0:T(8,128)S(1)} collective-permute-done((f32[32,256]{1,0:T(8,128)S(1)}, f32[32,256]{1,0:T(8,128)S(1)}, u32[]{:S(2)}, u32[]{:S(2)}) %collective-permute-start.23) | collective-permute-done | bytes 32800 | tf_op jit(solution)/shard_map/ppermute | solution.py:365
  110.3 1.9 %collective-permute-start.26 = (f32[32,256]{1,0:T(8,128)S(1)}, f32[32,256]{1,0:T(8,128)S(1)}, u32[]{:S(2)}, u32[]{:S(2)}) collective-permute-start(f32[32,256]{1,0:T(8,128)S(1)} %add_add_fusion.3), channel_id=1, source_target_pairs={{0,32},{2,34},{4,36},{6,38},{8,40},{10,42},{12,44},{14,46},{128,16... | collective-permute-start | bytes 98312 | tf_op jit(solution)/shard_map/ppermute | solution.py:365
  112.8 3.0 %collective-permute-done.26 = f32[32,256]{1,0:T(8,128)S(1)} collective-permute-done((f32[32,256]{1,0:T(8,128)S(1)}, f32[32,256]{1,0:T(8,128)S(1)}, u32[]{:S(2)}, u32[]{:S(2)}) %collective-permute-start.26) | collective-permute-done | bytes 32800 | tf_op jit(solution)/shard_map/ppermute | solution.py:365
  116.1 2.0 %collective-permute-start.28 = (f32[32,256]{1,0:T(8,128)S(1)}, f32[32,256]{1,0:T(8,128)S(1)}, u32[]{:S(2)}, u32[]{:S(2)}) collective-permute-start(f32[32,256]{1,0:T(8,128)S(1)} %add_add_fusion.2), channel_id=1, source_target_pairs={{0,128},{2,130},{4,132},{6,134},{8,136},{10,138},{12,140},{14,142}... | collective-permute-start | bytes 98312 | tf_op jit(solution)/shard_map/ppermute | solution.py:365
  119.7 11.7 %collective-permute-start.1 = (bf16[8,16,256]{2,1,0:T(8,128)(2,1)S(1)}, bf16[8,16,256]{2,1,0:T(8,128)(2,1)S(1)}, u32[]{:S(2)}, u32[]{:S(2)}) collective-permute-start(bf16[8,16,256]{2,1,0:T(8,128)(2,1)S(1)} %get-tuple-element.41), channel_id=1, source_target_pairs={{1,0},{2,1},{3,2},{4,3},{5,4},{6,5},{7,6},{8,7},{9,8},{10,9},{11,1... | collective-permute-start | bytes 196616 | tf_op jit(solution)/shard_map/ppermute | solution.py:348
  131.4 1.9 %collective-permute-start = (bf16[8,16,256]{2,1,0:T(8,128)(2,1)S(1)}, bf16[8,16,256]{2,1,0:T(8,128)(2,1)S(1)}, u32[]{:S(2)}, u32[]{:S(2)}) collective-permute-start(bf16[8,16,256]{2,1,0:T(8,128)(2,1)S(1)} %get-tuple-element.43), channel_id=1, source_target_pairs={{0,1},{1,2},{2,3},{3,4},{4,5},{5,6},{6,7},{7,8},{8,9},{9,10},{10,1... | collective-permute-start | bytes 196616 | tf_op jit(solution)/shard_map/ppermute | solution.py:348
  133.5 6.4 %collective-permute-start.33 = (f32[32,256]{1,0:T(8,128)S(1)}, f32[32,256]{1,0:T(8,128)S(1)}, u32[]{:S(2)}, u32[]{:S(2)}) collective-permute-start(f32[32,256]{1,0:T(8,128)S(1)} %add_add_fusion.1), channel_id=1, source_target_pairs={{0,12},{2,14},{4,8},{6,10},{8,4},{10,6},{12,0},{14,2},{128,140},{1... | collective-permute-start | bytes 98312 | tf_op jit(solution)/shard_map/ppermute | solution.py:365
  139.9 2.8 %collective-permute-done.lower = bf16[8,16,256]{2,1,0:T(8,128)(2,1)S(1)} collective-permute-done((bf16[8,16,256]{2,1,0:T(8,128)(2,1)S(1)}, bf16[8,16,256]{2,1,0:T(8,128)(2,1)S(1)}, u32[]{:S(2)}, u32[]{:S(2)}) %collective-permute-start) | collective-permute-done | bytes 65568 | tf_op jit(solution)/shard_map/ppermute | solution.py:348
  142.7 9.8 %input_gradient.1 = bf16[2,512,256]{2,1,0:T(8,128)(2,1)} custom-call(s32[2,27]{1,0:T(2,128)S(1)} %bitcast.82, bf16[2,512,256]{2,1,0:T(8,128)(2,1)S(1)} %bitcast.78, f32[8,128]{1,0:T(8,128)S(1)} %convert_element_type.18.occupancy, bf16[8,16,256]{2,1,0:T(8,128)(2,1)S(1)} %collective-permute-done.lower, bf16[8,16,256]{2,1,0:T(8,128)(2,1)S(1)} %collective-permute-done.1.upper, ...), custom_call_target="tpu_custom_call" | custom-call | flops 6000000000 | bytes 6000000 | tf_op jit(solution)/shard_map/input_gradient/pallas_call | solution.py:219
  152.5 4.3 %inverse_factor.1.inverse = f32[32,32]{1,0:T(8,128)} custom-call(f32[32,32]{1,0:T(8,128)} %copy-done.5), custom_call_target="tpu_custom_call" | custom-call | tf_op jit(solution)/shard_map/inverse_factor/pallas_call | solution.py:295
  156.9 3.0 %copy-done.1 = f32[3,9,256,256]{3,2,1,0:T(8,128)S(1)} copy-done((f32[3,9,256,256]{3,2,1,0:T(8,128)S(1)}, f32[3,9,256,256]{3,2,1,0:T(8,128)}, u32[]{:S(2)}) %copy-start.1) | copy-done | bytes 7077912
  160.6 5.6 %remaining_error.1 = (bf16[27,256,256]{2,1,0:T(8,128)(2,1)}, f32[256,32]{1,0:T(8,128)S(1)}) custom-call(f32[4,28,8,128]{3,2,1,0:T(8,128)S(1)} %pad_maximum_fusion.mine, f32[4,28,8,128]{3,2,1,0:T(8,128)S(1)} %collective-permute-done.21.other, f32[27,256,256]{2,1,0:T(8,128)S(1)} %bitcast.73, f32[32,256]{1,0:T(8,128)S(1)} %add_add_fusion.right, ...), custom_call_target="tpu_custom_call" | custom-call | tf_op jit(solution)/shard_map/remaining_error/pallas_call | solution.py:328
  (85 shorter events, 29.9 us)
Async XLA Ops:
  4.0 12.7 %collective-permute-start.3 = (bf16[8,16,256]{2,1,0:T(8,128)(2,1)S(1)}, bf16[8,16,256]{2,1,0:T(8,128)(2,1)S(1)}, u32[]{:S(2)}, u32[]{:S(2)}) collective-permute-start(bf16[8,16,256]{2,1,0:T(8,128)(2,1)S(1)} %get-tuple-element.40), channel_id=1, source_target_pairs={{1,0},{2,1},{3,2},{4,3},{5,4},{6,5},{7,6},{8,7},{9,8},{10,9},{11,1... | collective-permute-start | bytes 196616 | tf_op jit(solution)/shard_map/ppermute | solution.py:348
  13.7 10.7 %collective-permute-start.2 = (bf16[8,16,256]{2,1,0:T(8,128)(2,1)S(1)}, bf16[8,16,256]{2,1,0:T(8,128)(2,1)S(1)}, u32[]{:S(2)}, u32[]{:S(2)}) collective-permute-start(bf16[8,16,256]{2,1,0:T(8,128)(2,1)S(1)} %get-tuple-element.42), channel_id=1, source_target_pairs={{0,1},{1,2},{2,3},{3,4},{4,5},{5,6},{6,7},{7,8},{8,9},{9,10},{10,1... | collective-permute-start | bytes 196616 | tf_op jit(solution)/shard_map/ppermute | solution.py:348
  48.9 5.3 %collective-permute-start.5 = (f32[28,8,128]{2,1,0:T(8,128)S(1)}, f32[28,8,128]{2,1,0:T(8,128)S(1)}, u32[]{:S(2)}, u32[]{:S(2)}) collective-permute-start(f32[28,8,128]{2,1,0:T(8,128)S(1)} %get-tuple-element.32), channel_id=1, source_target_pairs={{0,16},{2,18},{4,20},{6,22},{8,24},{10,26},{12,28},{14,30},{128,14... | collective-permute-start | bytes 344072 | tf_op jit(solution)/shard_map/ppermute | solution.py:365
  49.0 8.7 %collective-permute-start.6 = (f32[28,8,128]{2,1,0:T(8,128)S(1)}, f32[28,8,128]{2,1,0:T(8,128)S(1)}, u32[]{:S(2)}, u32[]{:S(2)}) collective-permute-start(f32[28,8,128]{2,1,0:T(8,128)S(1)} %get-tuple-element.31), channel_id=1, source_target_pairs={{0,32},{2,34},{4,36},{6,38},{8,40},{10,42},{12,44},{14,46},{128,16... | collective-permute-start | bytes 344072 | tf_op jit(solution)/shard_map/ppermute | solution.py:365
  52.0 7.1 %collective-permute-start.7 = (f32[28,8,128]{2,1,0:T(8,128)S(1)}, f32[28,8,128]{2,1,0:T(8,128)S(1)}, u32[]{:S(2)}, u32[]{:S(2)}) collective-permute-start(f32[28,8,128]{2,1,0:T(8,128)S(1)} %get-tuple-element.30), channel_id=1, source_target_pairs={{0,48},{2,50},{4,52},{6,54},{8,56},{10,58},{12,60},{14,62},{128,17... | collective-permute-start | bytes 344072 | tf_op jit(solution)/shard_map/ppermute | solution.py:365
  59.1 4.0 %collective-permute-start.10 = (f32[7,8,128]{2,1,0:T(8,128)S(1)}, f32[7,8,128]{2,1,0:T(8,128)S(1)}, u32[]{:S(2)}, u32[]{:S(2)}) collective-permute-start(f32[7,8,128]{2,1,0:T(8,128)S(1)} %get-tuple-element.35), channel_id=1, source_target_pairs={{0,129},{2,131},{4,133},{6,135},{8,137},{10,139},{12,141},{14,143}... | collective-permute-start | bytes 86024 | tf_op jit(solution)/shard_map/ppermute | solution.py:365
  59.2 4.0 %collective-permute-start.8 = (f32[7,8,128]{2,1,0:T(8,128)S(1)}, f32[7,8,128]{2,1,0:T(8,128)S(1)}, u32[]{:S(2)}, u32[]{:S(2)}) collective-permute-start(f32[7,8,128]{2,1,0:T(8,128)S(1)} %get-tuple-element.37), channel_id=1, source_target_pairs={{0,128},{2,130},{4,132},{6,134},{8,136},{10,138},{12,140},{14,142}... | collective-permute-start | bytes 86024 | tf_op jit(solution)/shard_map/ppermute | solution.py:365
  60.7 5.4 %collective-permute-start.9 = (f32[7,8,128]{2,1,0:T(8,128)S(1)}, f32[7,8,128]{2,1,0:T(8,128)S(1)}, u32[]{:S(2)}, u32[]{:S(2)}) collective-permute-start(f32[7,8,128]{2,1,0:T(8,128)S(1)} %get-tuple-element.36), channel_id=1, source_target_pairs={{0,1},{2,3},{4,5},{6,7},{8,9},{10,11},{12,13},{14,15},{128,129},{1... | collective-permute-start | bytes 86024 | tf_op jit(solution)/shard_map/ppermute | solution.py:365
  66.0 6.6 %collective-permute-start.11 = (f32[7,8,128]{2,1,0:T(8,128)S(1)}, f32[7,8,128]{2,1,0:T(8,128)S(1)}, u32[]{:S(2)}, u32[]{:S(2)}) collective-permute-start(f32[7,8,128]{2,1,0:T(8,128)S(1)} %fusion.10), channel_id=1, source_target_pairs={{0,4},{2,6},{4,0},{6,2},{8,12},{10,14},{12,8},{14,10},{128,132},{1... | collective-permute-start | bytes 86024 | tf_op jit(solution)/shard_map/ppermute | solution.py:365
  66.1 7.9 %collective-permute-start.12 = (f32[7,8,128]{2,1,0:T(8,128)S(1)}, f32[7,8,128]{2,1,0:T(8,128)S(1)}, u32[]{:S(2)}, u32[]{:S(2)}) collective-permute-start(f32[7,8,128]{2,1,0:T(8,128)S(1)} %fusion.10), channel_id=1, source_target_pairs={{0,8},{2,10},{4,12},{6,14},{8,0},{10,2},{12,4},{14,6},{128,136},{1... | collective-permute-start | bytes 86024 | tf_op jit(solution)/shard_map/ppermute | solution.py:365
  67.9 7.0 %collective-permute-start.13 = (f32[7,8,128]{2,1,0:T(8,128)S(1)}, f32[7,8,128]{2,1,0:T(8,128)S(1)}, u32[]{:S(2)}, u32[]{:S(2)}) collective-permute-start(f32[7,8,128]{2,1,0:T(8,128)S(1)} %fusion.10), channel_id=1, source_target_pairs={{0,12},{2,14},{4,8},{6,10},{8,4},{10,6},{12,0},{14,2},{128,140},{1... | collective-permute-start | bytes 86024 | tf_op jit(solution)/shard_map/ppermute | solution.py:365
  74.9 4.0 %collective-permute-start.14 = (f32[7,8,128]{2,1,0:T(8,128)S(1)}, f32[7,8,128]{2,1,0:T(8,128)S(1)}, u32[]{:S(2)}, u32[]{:S(2)}) collective-permute-start(f32[7,8,128]{2,1,0:T(8,128)S(1)} %add_add_fusion.4), channel_id=1, source_target_pairs={{0,2},{2,0},{4,6},{6,4},{8,10},{10,8},{12,14},{14,12},{128,130},{1... | collective-permute-start | bytes 86024 | tf_op jit(solution)/shard_map/ppermute | solution.py:365
  78.9 3.9 %collective-permute-start.15 = (f32[7,8,128]{2,1,0:T(8,128)S(1)}, f32[7,8,128]{2,1,0:T(8,128)S(1)}, u32[]{:S(2)}, u32[]{:S(2)}) collective-permute-start(f32[7,8,128]{2,1,0:T(8,128)S(1)} %add.79), channel_id=1, source_target_pairs={{0,128},{2,130},{4,132},{6,134},{8,136},{10,138},{12,140},{14,142}... | collective-permute-start | bytes 86024 | tf_op jit(solution)/shard_map/ppermute | solution.py:365
  80.1 5.4 %collective-permute-start.16 = (f32[7,8,128]{2,1,0:T(8,128)S(1)}, f32[7,8,128]{2,1,0:T(8,128)S(1)}, u32[]{:S(2)}, u32[]{:S(2)}) collective-permute-start(f32[7,8,128]{2,1,0:T(8,128)S(1)} %add.79), channel_id=1, source_target_pairs={{0,1},{2,3},{4,5},{6,7},{8,9},{10,11},{12,13},{14,15},{128,129},{1... | collective-permute-start | bytes 86024 | tf_op jit(solution)/shard_map/ppermute | solution.py:365
  82.8 3.9 %collective-permute-start.17 = (f32[7,8,128]{2,1,0:T(8,128)S(1)}, f32[7,8,128]{2,1,0:T(8,128)S(1)}, u32[]{:S(2)}, u32[]{:S(2)}) collective-permute-start(f32[7,8,128]{2,1,0:T(8,128)S(1)} %add.79), channel_id=1, source_target_pairs={{0,129},{2,131},{4,133},{6,135},{8,137},{10,139},{12,141},{14,143}... | collective-permute-start | bytes 86024 | tf_op jit(solution)/shard_map/ppermute | solution.py:365
  86.6 5.9 %collective-permute-start.18 = (f32[28,8,128]{2,1,0:T(8,128)S(1)}, f32[28,8,128]{2,1,0:T(8,128)S(1)}, u32[]{:S(2)}, u32[]{:S(2)}) collective-permute-start(f32[28,8,128]{2,1,0:T(8,128)S(1)} %get-tuple-element.34), channel_id=1, source_target_pairs={{0,16},{2,18},{4,20},{6,22},{8,24},{10,26},{12,28},{14,30},{128,14... | collective-permute-start | bytes 344072 | tf_op jit(solution)/shard_map/ppermute | solution.py:365
  89.7 6.3 %collective-permute-start.19 = (f32[28,8,128]{2,1,0:T(8,128)S(1)}, f32[28,8,128]{2,1,0:T(8,128)S(1)}, u32[]{:S(2)}, u32[]{:S(2)}) collective-permute-start(f32[28,8,128]{2,1,0:T(8,128)S(1)} %get-tuple-element.34), channel_id=1, source_target_pairs={{0,32},{2,34},{4,36},{6,38},{8,40},{10,42},{12,44},{14,46},{128,16... | collective-permute-start | bytes 344072 | tf_op jit(solution)/shard_map/ppermute | solution.py:365
  89.7 6.3 %collective-permute-start.20 = (f32[28,8,128]{2,1,0:T(8,128)S(1)}, f32[28,8,128]{2,1,0:T(8,128)S(1)}, u32[]{:S(2)}, u32[]{:S(2)}) collective-permute-start(f32[28,8,128]{2,1,0:T(8,128)S(1)} %get-tuple-element.34), channel_id=1, source_target_pairs={{0,48},{2,50},{4,52},{6,54},{8,56},{10,58},{12,60},{14,62},{128,17... | collective-permute-start | bytes 344072 | tf_op jit(solution)/shard_map/ppermute | solution.py:365
  104.5 2.0 %collective-permute-start.22 = (f32[32,256]{1,0:T(8,128)S(1)}, f32[32,256]{1,0:T(8,128)S(1)}, u32[]{:S(2)}, u32[]{:S(2)}) collective-permute-start(f32[32,256]{1,0:T(8,128)S(1)} %get-tuple-element.13), channel_id=1, source_target_pairs={{0,64},{2,66},{4,68},{6,70},{8,72},{10,74},{12,76},{14,78},{128,19... | collective-permute-start | bytes 98312 | tf_op jit(solution)/shard_map/ppermute | solution.py:365
  104.7 4.0 %collective-permute-start.23 = (f32[32,256]{1,0:T(8,128)S(1)}, f32[32,256]{1,0:T(8,128)S(1)}, u32[]{:S(2)}, u32[]{:S(2)}) collective-permute-start(f32[32,256]{1,0:T(8,128)S(1)} %get-tuple-element.13), channel_id=1, source_target_pairs={{0,2},{2,0},{4,6},{6,4},{8,10},{10,8},{12,14},{14,12},{128,130},{1... | collective-permute-start | bytes 98312 | tf_op jit(solution)/shard_map/ppermute | solution.py:365
  104.7 4.0 %collective-permute-start.24 = (f32[32,256]{1,0:T(8,128)S(1)}, f32[32,256]{1,0:T(8,128)S(1)}, u32[]{:S(2)}, u32[]{:S(2)}) collective-permute-start(f32[32,256]{1,0:T(8,128)S(1)} %get-tuple-element.13), channel_id=1, source_target_pairs={{0,66},{2,64},{4,70},{6,68},{8,74},{10,72},{12,78},{14,76},{128,19... | collective-permute-start | bytes 98312 | tf_op jit(solution)/shard_map/ppermute | solution.py:365
  108.8 4.0 %collective-permute-start.25 = (f32[32,256]{1,0:T(8,128)S(1)}, f32[32,256]{1,0:T(8,128)S(1)}, u32[]{:S(2)}, u32[]{:S(2)}) collective-permute-start(f32[32,256]{1,0:T(8,128)S(1)} %add_add_fusion.3), channel_id=1, source_target_pairs={{0,16},{2,18},{4,20},{6,22},{8,24},{10,26},{12,28},{14,30},{128,14... | collective-permute-start | bytes 98312 | tf_op jit(solution)/shard_map/ppermute | solution.py:365
  110.3 5.4 %collective-permute-start.26 = (f32[32,256]{1,0:T(8,128)S(1)}, f32[32,256]{1,0:T(8,128)S(1)}, u32[]{:S(2)}, u32[]{:S(2)}) collective-permute-start(f32[32,256]{1,0:T(8,128)S(1)} %add_add_fusion.3), channel_id=1, source_target_pairs={{0,32},{2,34},{4,36},{6,38},{8,40},{10,42},{12,44},{14,46},{128,16... | collective-permute-start | bytes 98312 | tf_op jit(solution)/shard_map/ppermute | solution.py:365
  112.2 3.9 %collective-permute-start.27 = (f32[32,256]{1,0:T(8,128)S(1)}, f32[32,256]{1,0:T(8,128)S(1)}, u32[]{:S(2)}, u32[]{:S(2)}) collective-permute-start(f32[32,256]{1,0:T(8,128)S(1)} %add_add_fusion.3), channel_id=1, source_target_pairs={{0,48},{2,50},{4,52},{6,54},{8,56},{10,58},{12,60},{14,62},{128,17... | collective-permute-start | bytes 98312 | tf_op jit(solution)/shard_map/ppermute | solution.py:365
  116.1 17.2 %collective-permute-start.28 = (f32[32,256]{1,0:T(8,128)S(1)}, f32[32,256]{1,0:T(8,128)S(1)}, u32[]{:S(2)}, u32[]{:S(2)}) collective-permute-start(f32[32,256]{1,0:T(8,128)S(1)} %add_add_fusion.2), channel_id=1, source_target_pairs={{0,128},{2,130},{4,132},{6,134},{8,136},{10,138},{12,140},{14,142}... | collective-permute-start | bytes 98312 | tf_op jit(solution)/shard_map/ppermute | solution.py:365
  118.1 15.2 %collective-permute-start.29 = (f32[32,256]{1,0:T(8,128)S(1)}, f32[32,256]{1,0:T(8,128)S(1)}, u32[]{:S(2)}, u32[]{:S(2)}) collective-permute-start(f32[32,256]{1,0:T(8,128)S(1)} %add_add_fusion.2), channel_id=1, source_target_pairs={{0,1},{2,3},{4,5},{6,7},{8,9},{10,11},{12,13},{14,15},{128,129},{1... | collective-permute-start | bytes 98312 | tf_op jit(solution)/shard_map/ppermute | solution.py:365
  118.5 14.8 %collective-permute-start.30 = (f32[32,256]{1,0:T(8,128)S(1)}, f32[32,256]{1,0:T(8,128)S(1)}, u32[]{:S(2)}, u32[]{:S(2)}) collective-permute-start(f32[32,256]{1,0:T(8,128)S(1)} %add_add_fusion.2), channel_id=1, source_target_pairs={{0,129},{2,131},{4,133},{6,135},{8,137},{10,139},{12,141},{14,143}... | collective-permute-start | bytes 98312 | tf_op jit(solution)/shard_map/ppermute | solution.py:365
  119.7 20.2 %collective-permute-start.1 = (bf16[8,16,256]{2,1,0:T(8,128)(2,1)S(1)}, bf16[8,16,256]{2,1,0:T(8,128)(2,1)S(1)}, u32[]{:S(2)}, u32[]{:S(2)}) collective-permute-start(bf16[8,16,256]{2,1,0:T(8,128)(2,1)S(1)} %get-tuple-element.41), channel_id=1, source_target_pairs={{1,0},{2,1},{3,2},{4,3},{5,4},{6,5},{7,6},{8,7},{9,8},{10,9},{11,1... | collective-permute-start | bytes 196616 | tf_op jit(solution)/shard_map/ppermute | solution.py:348
  131.4 11.4 %collective-permute-start = (bf16[8,16,256]{2,1,0:T(8,128)(2,1)S(1)}, bf16[8,16,256]{2,1,0:T(8,128)(2,1)S(1)}, u32[]{:S(2)}, u32[]{:S(2)}) collective-permute-start(bf16[8,16,256]{2,1,0:T(8,128)(2,1)S(1)} %get-tuple-element.43), channel_id=1, source_target_pairs={{0,1},{1,2},{2,3},{3,4},{4,5},{5,6},{6,7},{7,8},{8,9},{9,10},{10,1... | collective-permute-start | bytes 196616 | tf_op jit(solution)/shard_map/ppermute | solution.py:348
  133.3 23.5 %collective-permute-start.31 = (f32[32,256]{1,0:T(8,128)S(1)}, f32[32,256]{1,0:T(8,128)S(1)}, u32[]{:S(2)}, u32[]{:S(2)}) collective-permute-start(f32[32,256]{1,0:T(8,128)S(1)} %add_add_fusion.1), channel_id=1, source_target_pairs={{0,4},{2,6},{4,0},{6,2},{8,12},{10,14},{12,8},{14,10},{128,132},{1... | collective-permute-start | bytes 98312 | tf_op jit(solution)/shard_map/ppermute | solution.py:365
  133.4 23.4 %collective-permute-start.32 = (f32[32,256]{1,0:T(8,128)S(1)}, f32[32,256]{1,0:T(8,128)S(1)}, u32[]{:S(2)}, u32[]{:S(2)}) collective-permute-start(f32[32,256]{1,0:T(8,128)S(1)} %add_add_fusion.1), channel_id=1, source_target_pairs={{0,8},{2,10},{4,12},{6,14},{8,0},{10,2},{12,4},{14,6},{128,136},{1... | collective-permute-start | bytes 98312 | tf_op jit(solution)/shard_map/ppermute | solution.py:365
  133.5 23.3 %collective-permute-start.33 = (f32[32,256]{1,0:T(8,128)S(1)}, f32[32,256]{1,0:T(8,128)S(1)}, u32[]{:S(2)}, u32[]{:S(2)}) collective-permute-start(f32[32,256]{1,0:T(8,128)S(1)} %add_add_fusion.1), channel_id=1, source_target_pairs={{0,12},{2,14},{4,8},{6,10},{8,4},{10,6},{12,0},{14,2},{128,140},{1... | collective-permute-start | bytes 98312 | tf_op jit(solution)/shard_map/ppermute | solution.py:365
  (11 other events, 61.3 us)

commit v2 on v1

v2 whole, which is shorter than its diff:
```python
import functools

import jax
import jax.numpy as jnp
from jax import lax
from jax.experimental import pallas as pl
from jax.experimental.pallas import tpu as pltpu
from jax.sharding import PartitionSpec as P

EDGE = 8
PLANE = EDGE * EDGE
F32 = jnp.float32
BF16 = jnp.bfloat16
NT = (((1,), (1,)), ((), ()))
NN = (((1,), (0,)), ((), ()))
TN = (((0,), (0,)), ((), ()))
STEPS = (-1, 0, 1)
MIB = 1024 * 1024


def split(value):
    high = value.astype(BF16)
    low = (value - high.astype(F32)).astype(BF16)
    return high, low


def source_rows(slots, step_x, step_y, step_z, along):
    shape = (128, 1) if along == 0 else (1, 128)
    place = lax.broadcasted_iota(jnp.int32, shape, along)
    brick = place // PLANE
    y = (place // EDGE) % EDGE + step_y
    z = place % EDGE + step_z
    wrapped_y = y % EDGE
    wrapped_z = z % EDGE
    rows = jnp.full(shape, -1, jnp.int32)
    for side_y in sorted({0, step_y}):
        in_y = (y < 0) if side_y < 0 else (y >= EDGE) if side_y > 0 else (y >= 0) & (y < EDGE)
        for side_z in sorted({0, step_z}):
            in_z = (z < 0) if side_z < 0 else (z >= EDGE) if side_z > 0 else (z >= 0) & (z < EDGE)
            if side_z == 0:
                offset = wrapped_y * EDGE + wrapped_z
                first, stride = 0, PLANE
            else:
                offset = wrapped_y
                first, stride = (128 if side_z < 0 else 144), EDGE
            for which in (0, 1):
                slot = slots[which, (step_x + 1) * 9 + (side_y + 1) * 3 + side_z + 1]
                base = jnp.where(slot < 0, -4096, slot * stride + first)
                rows = jnp.where(in_y & in_z & (brick == which), base + offset, rows)
    return rows


def one_hot(rows, along, depth):
    shape = (128, depth) if along == 0 else (depth, 128)
    places = lax.broadcasted_iota(jnp.int32, shape, 1 - along)
    return jnp.where(places == rows, 1.0, 0.0).astype(BF16)


def own_plane(field, mask, plane):
    rows = jnp.concatenate([field[b, plane * PLANE : (plane + 1) * PLANE, :] for b in (0, 1)], axis=0)
    return rows * mask[:, plane : plane + 1]


def with_faces(own, lower, upper, plane):
    rest = jnp.zeros((96, own.shape[1]), BF16)
    return jnp.concatenate([own, lower[0, plane], upper[0, plane], rest], axis=0)


def coordinates():
    dp, space = lax.axis_index("dp"), lax.axis_index("space")
    return dp % 2, space // 16, (space % 2) * 2 + dp // 2, (space // 2) % 8


def place_of(tap, y):
    return ((tap // 7) ^ y) * 7 + tap % 7


def put_factor(mine, other, tap, value):
    core, x, y, _ = coordinates()
    place = place_of(tap, y)
    halves = value[:, :128], value[:, 128:]
    kept = jnp.where(core == 0, halves[0], halves[1])
    sent = jnp.where(core == 0, halves[1], halves[0])
    for block in range(4):
        rows = slice(block * 8, block * 8 + 8)
        mine[block ^ x, place] = kept[rows]
        other[block ^ x, place] = sent[rows]


def get_factor(mine, other, tap):
    core, x, y, _ = coordinates()
    place = place_of(tap, y)
    own = jnp.concatenate([mine[block ^ x, place] for block in range(4)], axis=0)
    rest = jnp.concatenate([other[block ^ x, place] for block in range(4)], axis=0)
    both = jnp.concatenate([jnp.where(core == 0, own, rest), jnp.where(core == 0, rest, own)], axis=1)
    return both * (1.0 / 256.0)


def whole(*shape):
    return pl.BlockSpec(shape, lambda *step: (0,) * len(shape))


def faces_kernel(field, cotangent, occupancy, up, down):
    mask = occupancy[...].T.astype(BF16)
    row = lax.broadcasted_iota(jnp.int32, (32, 128), 0)
    place = lax.broadcasted_iota(jnp.int32, (32, 128), 1)
    wanted = jnp.where(row < 16, row * EDGE + EDGE - 1, (row - 16) * EDGE)
    picks = jnp.where(place == wanted, 1.0, 0.0).astype(BF16)
    for which, source in enumerate((field, cotangent)):
        for plane in range(EDGE):
            found = lax.dot_general(picks, own_plane(source, mask, plane), NN, preferred_element_type=F32)
            up[which, plane] = found[:16].astype(BF16)
            down[which, plane] = found[16:].astype(BF16)


def brick_faces(field, cotangent, occupancy):
    shape = jax.ShapeDtypeStruct((2, EDGE, 16, 256), BF16)
    return pl.pallas_call(faces_kernel, out_shape=[shape, shape], compiler_params=SMALL, name="brick_faces")(
        in_hbm(field), in_hbm(cotangent), occupancy
    )


def gradient_kernel(sides, *refs):
    count = 3 * len(sides)
    faces = sides != (0,)
    slots, field, cotangent, occupancy, start, error = refs[:6]
    refs = refs[6:]
    if faces:
        lower, upper, _, mine_before, other_before = refs[:5]
        refs = refs[5:]
    corrected, mine, other, views, own, start_split, kept_high, kept_low = refs
    step = pl.program_id(0)

    @pl.when(step == 0)
    def _():
        mask = occupancy[...].T.astype(BF16)
        high, low = split(start[...])
        start_split[0:32, :] = high
        start_split[32:64, :] = low
        depth = 256 if faces else 128
        sources = []
        for plane in range(EDGE):
            own[plane * 128 : (plane + 1) * 128, :] = own_plane(cotangent, mask, plane)
            source = own_plane(field, mask, plane)
            if faces:
                source = with_faces(source, lower, upper, plane)
            sources.append(source.T)
        inner = jnp.concatenate(sources, axis=0)
        groups = [(y, z) for y in STEPS for z in sides]
        for first in range(0, count, 2):
            pair = groups[first : first + 2]
            for step_x, left, where in ((-1, sources[7], 0), (0, inner, 1), (1, sources[0], 9)):
                picks = jnp.concatenate(
                    [one_hot(source_rows(slots, step_x, y, z, 1), 1, depth) for y, z in pair], axis=1
                )
                found = lax.dot_general(left, picks, NN, preferred_element_type=F32).astype(BF16)
                for member in range(len(pair)):
                    for block in range(left.shape[0] // 256):
                        views[first + member, :, (where + block) * 128 : (where + block + 1) * 128] = found[
                            block * 256 : (block + 1) * 256, member * 128 : (member + 1) * 128
                        ]
        if faces:
            mine[...] = mine_before[...]
            other[...] = other_before[...]

    def product():
        columns = jnp.concatenate([views[step, :, k * 128 : k * 128 + 1024] for k in range(3)], axis=0)
        total = lax.dot_general(columns, own[...], NN, preferred_element_type=F32)
        total = total + error[:, 0, 0].astype(F32).reshape(768, 256)
        corrected[:, 0, 0] = total.reshape(3, 256, 256)
        return split(total)

    def keep(parts):
        kept_high[...], kept_low[...] = parts

    def factor():
        both = lax.dot_general(start_split[...], kept_high[...], NT, preferred_element_type=F32)
        rest = lax.dot_general(start_split[0:32, :], kept_low[...], NT, preferred_element_type=F32)
        return both[0:32] + both[32:64] + rest

    def put(made):
        before = step - 1
        if faces:
            group = before // 2 * 3 + before % 2 * 2
        else:
            group = before * 3 + 1
        for tap_x in range(3):
            put_factor(mine, other, tap_x * 9 + group, made[:, tap_x * 256 : tap_x * 256 + 256])

    @pl.when(step == 0)
    def _():
        keep(product())

    @pl.when((step > 0) & (step < count))
    def _():
        made = factor()
        parts = product()
        put(made)
        keep(parts)

    @pl.when(step == count)
    def _():
        put(factor())
        if not faces:
            put_factor(mine, other, 27, jnp.zeros((32, 256), F32))


def local_gradient(sides, slots, field, cotangent, occupancy, start, error, *more):
    count = 3 * len(sides)
    faces = sides != (0,)

    def at(step):
        group = jnp.minimum(step, count - 1)
        return (0, group // 2, group % 2 * 2, 0, 0) if faces else (0, group, 1, 0, 0)

    taps = pl.BlockSpec((3, 1, 1, 256, 256), at)
    piece = whole(4, 28, 8, 128)
    face = whole(1, EDGE, 16, 256)
    in_specs = [
        pl.BlockSpec(memory_space=pltpu.SMEM),
        whole(2, 512, 256),
        whole(2, 512, 256),
        whole(8, 128),
        whole(32, 256),
        taps,
    ]
    if faces:
        in_specs += [face, face, pl.BlockSpec(memory_space=pl.ANY), piece, piece]
    return pl.pallas_call(
        functools.partial(gradient_kernel, sides),
        grid=(count + 1,),
        in_specs=in_specs,
        out_specs=[taps, piece, piece],
        out_shape=[
            CORRECTED,
            jax.ShapeDtypeStruct((4, 28, 8, 128), F32),
            jax.ShapeDtypeStruct((4, 28, 8, 128), F32),
        ],
        input_output_aliases={8: 0} if faces else {},
        scratch_shapes=[
            pltpu.VMEM((count, 256, 1280), BF16),
            pltpu.VMEM((1024, 256), BF16),
            pltpu.VMEM((64, 256), BF16),
            pltpu.VMEM((768, 256), BF16),
            pltpu.VMEM((768, 256), BF16),
        ],
        compiler_params=pltpu.CompilerParams(vmem_limit_bytes=GRAD_LIMIT),
        cost_estimate=pl.CostEstimate(
            flops=count * 6 * 10**8, bytes_accessed=count * 15 * 10**5, transcendentals=0
        ),
        name="gradient_with_faces" if faces else "gradient_own",
    )(slots, field, cotangent, occupancy, start, error, *more)


def input_kernel(side, last, *refs):
    slots, cotangent, occupancy, weight = refs[:4]
    refs = refs[4:]
    if side:
        face, total_before = refs[:2]
        refs = refs[2:]
    result, views, total = refs[-3:]
    step = pl.program_id(0)

    @pl.when(step == 0)
    def _():
        mask = occupancy[...].T.astype(BF16)
        sources = [own_plane(cotangent, mask, plane) for plane in range(EDGE)]
        if side:
            sources = [with_faces(own, face, face, plane) for plane, own in enumerate(sources)]
        for index, y in enumerate(STEPS):
            picks = [one_hot(source_rows(slots, x, y, -side, 0), 0, 256 if side else 128) for x in STEPS]
            for plane in range(-1, EDGE + 1):
                which = 0 if plane < 0 else 2 if plane >= EDGE else 1
                found = lax.dot_general(picks[which], sources[plane % EDGE], NN, preferred_element_type=F32)
                views[index, (plane + 1) * 128 : (plane + 2) * 128, :] = found.astype(BF16)
        total[...] = total_before[...] if side else jnp.zeros_like(total)

    columns = jnp.concatenate(
        [views[2 - step, (2 - tap_x) * 128 : (2 - tap_x) * 128 + 1024, :] for tap_x in range(3)], axis=1
    )
    weights = jnp.concatenate([weight[tap_x, 0, 0] for tap_x in range(3)], axis=1)
    total[...] += lax.dot_general(columns, weights, NT, preferred_element_type=F32)

    @pl.when(step == 2)
    def _():
        if not last:
            result[...] = total[...]
            return
        mask = occupancy[...].T
        for plane in range(EDGE):
            rows = total[plane * 128 : (plane + 1) * 128, :] * mask[:, plane : plane + 1]
            for brick in (0, 1):
                result[brick, plane * PLANE : (plane + 1) * PLANE, :] = rows[
                    brick * PLANE : (brick + 1) * PLANE
                ].astype(BF16)


def input_gradient(side, last, slots, cotangent, occupancy, weight, *more, tie=None):
    in_specs = [
        pl.BlockSpec(memory_space=pltpu.SMEM),
        whole(2, 512, 256),
        whole(8, 128),
        pl.BlockSpec((3, 1, 1, 256, 256), lambda step: (0, step, side + 1, 0, 0)),
    ]
    if side:
        in_specs += [pl.BlockSpec((1, EDGE, 16, 256), lambda step: (1, 0, 0, 0)), whole(1024, 256)]
    if tie is not None:
        in_specs += [pl.BlockSpec(memory_space=pl.ANY)]
        more += (tie,)
    if last:
        shape, spec = jax.ShapeDtypeStruct((2, 512, 256), BF16), whole(2, 512, 256)
    else:
        shape, spec = jax.ShapeDtypeStruct((1024, 256), F32), whole(1024, 256)
    return pl.pallas_call(
        functools.partial(input_kernel, side, last),
        grid=(3,),
        in_specs=in_specs,
        out_specs=spec,
        out_shape=shape,
        scratch_shapes=[pltpu.VMEM((3, 1280, 256), BF16), pltpu.VMEM((1024, 256), F32)],
        compiler_params=pltpu.CompilerParams(vmem_limit_bytes=INPUT_LIMIT),
        cost_estimate=pl.CostEstimate(flops=2 * 10**9, bytes_accessed=4 * 10**6, transcendentals=0),
        name=("input_own", "input_above", "input_below")[side],
    )(slots, cotangent, occupancy, weight, *more)


def right_kernel(mine, other, corrected, right):
    step = pl.program_id(0)

    @pl.when(step == 0)
    def _():
        right[...] = jnp.zeros_like(right)

    left = jnp.concatenate([get_factor(mine, other, step * 3 + tap) for tap in range(3)], axis=1)
    left_high, left_low = split(left)
    high, low = split(corrected[...].reshape(768, 256))
    both = lax.dot_general(jnp.concatenate([left_high, left_low], axis=0), high, NN, preferred_element_type=F32)
    rest = lax.dot_general(left_high, low, NN, preferred_element_type=F32)
    right[...] += both[0:32] + both[32:64] + rest


def blocks(*shape):
    return pl.BlockSpec((3,) + shape, lambda step: (step, 0, 0))


def right_product(mine, other, corrected):
    return pl.pallas_call(
        right_kernel,
        grid=(9,),
        in_specs=[whole(4, 28, 8, 128), whole(4, 28, 8, 128), blocks(256, 256)],
        out_specs=whole(32, 256),
        out_shape=jax.ShapeDtypeStruct((32, 256), F32),
        compiler_params=pltpu.CompilerParams(vmem_limit_bytes=LATE_LIMIT),
        name="right_product",
    )(mine, other, in_vmem(corrected))


def eliminate(first, work, made):
    places = lax.broadcasted_iota(jnp.int32, (32, 1), 0)
    for step in range(first, first + 16):
        scale = 1.0 / jnp.sqrt(work[step : step + 1, step : step + 1])
        work_row = work[step : step + 1, :] * scale
        made_row = made[step : step + 1, :] * scale
        column = work[:, step : step + 1] * scale
        later = jnp.where(places > step, column, 0.0)
        here = places == step
        work = jnp.where(here, work_row, work - later * work_row)
        made = jnp.where(here, made_row, made - later * made_row)
    return work, made


def first_half_kernel(mine, other, work, made):
    gram = jnp.zeros((32, 32), F32)
    for step in range(9):
        left = jnp.concatenate([get_factor(mine, other, step * 3 + tap) for tap in range(3)], axis=1)
        gram += lax.dot_general(left, left, NT, precision=lax.Precision.HIGHEST, preferred_element_type=F32)
    row = lax.broadcasted_iota(jnp.int32, (32, 32), 0)
    column = lax.broadcasted_iota(jnp.int32, (32, 32), 1)
    work[...], made[...] = eliminate(0, gram, jnp.where(row == column, 1.0, 0.0).astype(F32))


def second_half_kernel(work, made, inverse):
    inverse[...] = eliminate(16, work[...], made[...])[1]


SQUARE = jax.ShapeDtypeStruct((32, 32), F32)


def half_inverse(mine, other):
    return pl.pallas_call(first_half_kernel, out_shape=[SQUARE, SQUARE], compiler_params=SMALL, name="half_inverse")(
        mine, other
    )


def whole_inverse(work, made, tie=None):
    def kernel(work, made, *refs):
        second_half_kernel(work, made, refs[-1])

    more = () if tie is None else (tie,)
    vmem = pl.BlockSpec(memory_space=pltpu.VMEM)
    return pl.pallas_call(
        kernel,
        in_specs=[vmem, vmem] + [pl.BlockSpec(memory_space=pl.ANY)] * len(more),
        out_specs=vmem,
        out_shape=SQUARE,
        compiler_params=SMALL,
        name="whole_inverse",
    )(work, made, *more)


def error_kernel(mine, other, corrected, right, inverse, new_error, q_rows, basis):
    step = pl.program_id(0)

    @pl.when(step == 0)
    def _():
        rows = lax.dot_general(
            inverse[...], right[...], NN, precision=lax.Precision.HIGHEST, preferred_element_type=F32
        ) * (1.0 / 256.0)
        q_rows[...] = rows
        back = lax.dot_general(
            inverse[...].T, rows, NN, precision=lax.Precision.HIGHEST, preferred_element_type=F32
        )
        high, low = split(back)
        basis[0:32, :] = high
        basis[32:64, :] = high
        basis[64:96, :] = low
        basis[96:128, :] = jnp.zeros((32, 256), BF16)

    high, low = split(jnp.concatenate([get_factor(mine, other, step * 3 + tap) for tap in range(3)], axis=1))
    left = jnp.concatenate([high, low, high, jnp.zeros((32, 768), BF16)], axis=0)
    product = lax.dot_general(left, basis[...], TN, preferred_element_type=F32)
    new_error[...] = (corrected[...] - product.reshape(3, 256, 256)).astype(BF16)


def remaining_error(mine, other, corrected, right, inverse):
    return pl.pallas_call(
        error_kernel,
        grid=(9,),
        in_specs=[whole(4, 28, 8, 128), whole(4, 28, 8, 128), blocks(256, 256), whole(32, 256), whole(32, 32)],
        out_specs=[blocks(256, 256), whole(32, 256)],
        out_shape=[jax.ShapeDtypeStruct((27, 256, 256), BF16), jax.ShapeDtypeStruct((32, 256), F32)],
        scratch_shapes=[pltpu.VMEM((128, 256), BF16)],
        compiler_params=pltpu.CompilerParams(vmem_limit_bytes=LATE_LIMIT),
        name="remaining_error",
    )(mine, other, in_vmem(corrected), right, inverse)


CORRECTED = pltpu.VMEM((3, 3, 3, 256, 256), F32)
GRAD_LIMIT = 32 * MIB
INPUT_LIMIT = 24 * MIB
LATE_LIMIT = 24 * MIB
SMALL = pltpu.CompilerParams(vmem_limit_bytes=12 * MIB)


def in_vmem(value):
    return pltpu.with_memory_space_constraint(value, pltpu.VMEM)


def in_hbm(value):
    return pltpu.with_memory_space_constraint(value, pltpu.HBM)


def shifted(value, by):
    devices = lax.axis_size("space")
    return lax.ppermute(value, "space", [(i, i + by) for i in range(devices) if 0 <= i + by < devices])


def partners(core=0, x=0, y=0, z=0):
    def place(at_core, at_x, at_y, at_z):
        return (at_y % 2 * 2 + at_core) * 64 + (at_x * 8 + at_z) * 2 + at_y // 2

    return [
        (place(c, i, j, l), place(c ^ core, i ^ x, j ^ y, l ^ z))
        for c in range(2)
        for i in range(4)
        for j in range(4)
        for l in range(8)
    ]


def swapped(value, **bits):
    return lax.ppermute(value, ("dp", "space"), partners(**bits))


def added(values):
    return (values[0] + values[1]) + (values[2] + values[3])


def summed_among(value, steps):
    return added([value] + [swapped(value, **bits) for bits in steps])


ALONG_X = [dict(x=1), dict(x=2), dict(x=3)]
ALONG_Y = [dict(y=1), dict(y=2), dict(y=3)]
ALONG_Z = [dict(z=2), dict(z=4), dict(z=6)]
CORE_AND_Z = [dict(core=1), dict(z=1), dict(core=1, z=1)]


def body(inputs, cotangent, occupancy, neighbours, weight, error_in, q_start):
    field, gradient, occupied, slots = inputs[0], cotangent[0], occupancy[0], neighbours[0]
    mask = occupied.reshape(2, EDGE, PLANE).transpose(1, 0, 2).reshape(EDGE, 2 * PLANE).astype(F32)
    weight = weight.reshape(3, 3, 3, 256, 256)
    up, down = brick_faces(field, gradient, mask)
    lower, upper = shifted(up, 1), shifted(down, -1)
    fixed = (slots, in_hbm(field), in_hbm(gradient), mask, q_start.T, in_hbm(error_in.reshape(3, 3, 3, 256, 256)))
    corrected, mine, other = local_gradient((0,), *fixed)
    corrected, mine, other = local_gradient((-1, 1), *fixed, lower, upper, in_vmem(corrected), mine, other)
    corrected = corrected.reshape(27, 256, 256)

    part = mine + swapped(other, core=1)
    arrived = [swapped(part[k], x=k) for k in (1, 2, 3)]
    total = input_gradient(0, False, slots, gradient, mask, weight, tie=part)
    part, total = lax.optimization_barrier((added([part[0]] + arrived), total))
    part = part.reshape(4, 7, 8, 128)
    part = added([part[0]] + [swapped(part[k], y=k) for k in (1, 2, 3)])
    arrived = [swapped(part, **bits) for bits in ALONG_Z]
    total = input_gradient(-1, False, slots, gradient, mask, weight, upper, total, tie=part)
    part, total = lax.optimization_barrier((added([part] + arrived), total))
    part = part + swapped(part, z=1)
    part = jnp.concatenate([part] + [swapped(part, **bits) for bits in ALONG_Y], axis=0)
    arrived = [swapped(part, **bits) for bits in ALONG_X]
    input_grad = input_gradient(1, True, slots, gradient, mask, weight, lower, total, tie=part)
    mine, input_grad = lax.optimization_barrier((jnp.stack([part] + arrived, axis=0), input_grad))
    other = swapped(mine, core=1)

    right = right_product(mine, other, corrected)
    arrived = [swapped(right, **bits) for bits in CORE_AND_Z]
    halves = half_inverse(mine, other)
    right, *halves = lax.optimization_barrier((added([right] + arrived), *halves))
    arrived = [swapped(right, **bits) for bits in ALONG_X]
    inverse = whole_inverse(*halves, tie=right)
    right, inverse = lax.optimization_barrier((added([right] + arrived), inverse))
    right = summed_among(summed_among(right, ALONG_Y), ALONG_Z)
    new_error, q_rows = remaining_error(mine, other, corrected, right, inverse)
    return (input_grad[None], q_rows.T, new_error.reshape(1, 1, 6912, 256))


def solution(mesh):
    in_specs = (
        P("dp", "space", None, None),
        P("dp", "space", None, None),
        P("dp", "space", None),
        P("dp", "space", None),
        P(),
        P("dp", "space", None, None),
        P(),
    )
    out_specs = (P("dp", "space", None, None), P(), P("dp", "space", None, None))
    return jax.shard_map(body, mesh=mesh, in_specs=in_specs, out_specs=out_specs, check_vma=False)
```

time: 168 us -> 124 us (0.74)
  the two profiles are of different devices: /device:TPU:10 before, /device:TPU:8 now
where the time goes in v2:
time: 124 us
  starting transfers between devices  52.8 us (43%)
  Pallas kernels  40.9 us (33%)
  waiting for transfers between devices  26.7 us (22%)
  local copies, waits for them, and re-layouts  1.65 us (1%)
    ppermute x30, starting transfers between devices, swapped(): return lax.ppermute(value, ('dp', 'space'), partners(**bits))  47.3 us
    ppermute x30, waiting for transfers between devices, swapped(): return lax.ppermute(value, ('dp', 'space'), partners(**bits))  26.7 us
    pallas_call x2, Pallas kernels, local_gradient(): pl.pallas_call(functools.partial(gradient_kernel, sides), grid=(count + 1...  15.7 us
    pallas_call x3, Pallas kernels, input_gradient(): pl.pallas_call(functools.partial(input_kernel, side, last), grid=(3,), in...  11.6 us
    pallas_call x1, Pallas kernels, remaining_error(): pl.pallas_call(error_kernel, grid=(9,), in_specs=[whole(4, 28, 8, 128), w...  5.74 us
    ppermute x2, starting transfers between devices, shifted(): lax.ppermute(value, 'space', [(i, i + by) for i in range(devices) if 0 <=...  5.5 us
  transfers between devices with their start and end apart: 32, of which 16 were waited for; matrix products, arithmetic and copies ran while one was open for 0% of the time, Pallas kernels for 17%

profile of v2, /device:TPU:8, one launch (start us, length us, event | category | flops | bytes accessed | tf_op | source)
XLA Modules:
  0.0 123.8 jit_solution(6825374521073777787)
XLA Ops:
  1.5 1.7 %brick_faces.1 = (bf16[2,8,16,256]{3,2,1,0:T(8,128)(2,1)S(1)}, bf16[2,8,16,256]{3,2,1,0:T(8,128)(2,1)S(1)}) custom-call(bf16[2,512,256]{2,1,0:T(8,128)(2,1)} %bitcast.48, bf16[2,512,256]{2,1,0:T(8,128)(2,1)} %bitcast.32, f32[8,128]{1,0:T(8,128)S(1)} %convert_element_type.12.occupancy.refs_3_.refs_2_), custom_call_target="tpu_custom_call" | custom-call | tf_op jit(solution)/shard_map/brick_faces/pallas_call | solution.py:118
  3.2 4.2 %collective-permute-start = (bf16[2,8,16,256]{3,2,1,0:T(8,128)(2,1)S(1)}, bf16[2,8,16,256]{3,2,1,0:T(8,128)(2,1)S(1)}, u32[]{:S(2)}, u32[]{:S(2)}) collective-permute-start(bf16[2,8,16,256]{3,2,1,0:T(8,128)(2,1)S(1)} %get-tuple-element.26), channel_id=1, source_target_pairs={{0,1},{1,2},{2,3},{3,4},{4,5},{5,6},{6,7},{7,8},{8,9},{9,10},{10,1... | collective-permute-start | bytes 393224 | tf_op jit(solution)/shard_map/ppermute | solution.py:465
  10.1 5.9 %gradient_own.1 = (f32[3,3,3,256,256]{4,3,2,1,0:T(8,128)S(1)}, f32[4,28,8,128]{3,2,1,0:T(8,128)S(1)}, f32[4,28,8,128]{3,2,1,0:T(8,128)S(1)}) custom-call(s32[2,27]{1,0:T(2,128)S(1)} %bitcast.43, bf16[2,512,256]{2,1,0:T(8,128)(2,1)} %bitcast.49, bf16[2,512,256]{2,1,0:T(8,128)(2,1)} %bitcast.33, f32[8,128]{1,0:T(8,128)S(1)} %convert_element_type.12.occupancy.refs_3_.refs_2_, ...), custom_call_target="tpu_custom_call" | custom-call | flops 1800000000 | bytes 4500000 | tf_op jit(solution)/shard_map/gradient_own/pallas_call | solution.py:229
  16.1 9.8 %gradient_with_faces.1 = (f32[3,3,3,256,256]{4,3,2,1,0:T(8,128)S(1)}, f32[4,28,8,128]{3,2,1,0:T(8,128)S(1)}, f32[4,28,8,128]{3,2,1,0:T(8,128)S(1)}) custom-call(s32[2,27]{1,0:T(2,128)S(1)} %bitcast.44, bf16[2,512,256]{2,1,0:T(8,128)(2,1)} %bitcast.50, bf16[2,512,256]{2,1,0:T(8,128)(2,1)} %bitcast.34, ...), custom_call_target="tpu_custom_call", output_to_operand_aliasing={{0}: (8, {})} | custom-call | flops 3600000000 | bytes 9000000 | tf_op jit(solution)/shard_map/gradient_with_faces/pallas_call | solution.py:229
  26.0 1.8 %collective-permute-done.2 = f32[4,28,8,128]{3,2,1,0:T(8,128)S(1)} collective-permute-done((f32[4,28,8,128]{3,2,1,0:T(8,128)S(1)}, f32[4,28,8,128]{3,2,1,0:T(8,128)S(1)}, u32[]{:S(2)}, u32[]{:S(2)}) %collective-permute-start.2) | collective-permute-done | bytes 458784 | tf_op jit(solution)/shard_map/ppermute | solution.py:482
  27.8 9.0 %collective-permute-start.5 = (f32[28,8,128]{2,1,0:T(8,128)S(1)}, f32[28,8,128]{2,1,0:T(8,128)S(1)}, u32[]{:S(2)}, u32[]{:S(2)}) collective-permute-start(f32[28,8,128]{2,1,0:T(8,128)S(1)} %get-tuple-element.49), channel_id=1, source_target_pairs={{0,48},{2,50},{4,52},{6,54},{8,56},{10,58},{12,60},{14,62},{128,17... | collective-permute-start | bytes 344072 | tf_op jit(solution)/shard_map/ppermute | solution.py:482
  37.8 3.4 %input_own.1.refs_5_ = f32[1024,256]{1,0:T(8,128)S(1)} custom-call(s32[2,27]{1,0:T(2,128)S(1)} %bitcast.45, bf16[2,512,256]{2,1,0:T(8,128)(2,1)S(1)} %bitcast.35, f32[8,128]{1,0:T(8,128)S(1)} %convert_element_type.12.occupancy.refs_3_.refs_2_, bf16[3,3,3,256,256]{4,3,2,1,0:T(8,128)(2,1)S(1)} %bitcast.38, f32[4,28,8,128]{3,2,1,0:T(8,128)S(1)} %add.69.refs_4_), custom_call_target="tpu_custom_call" | custom-call | flops 2000000000 | bytes 4000000 | tf_op jit(solution)/shard_map/input_own/pallas_call | solution.py:314
  42.1 2.3 %collective-permute-done.4 = f32[28,8,128]{2,1,0:T(8,128)S(1)} collective-permute-done((f32[28,8,128]{2,1,0:T(8,128)S(1)}, f32[28,8,128]{2,1,0:T(8,128)S(1)}, u32[]{:S(2)}, u32[]{:S(2)}) %collective-permute-start.4) | collective-permute-done | bytes 114720 | tf_op jit(solution)/shard_map/ppermute | solution.py:482
  45.9 2.7 %collective-permute-start.7 = (f32[7,8,128]{2,1,0:T(8,128)S(1)}, f32[7,8,128]{2,1,0:T(8,128)S(1)}, u32[]{:S(2)}, u32[]{:S(2)}) collective-permute-start(f32[7,8,128]{2,1,0:T(8,128)S(1)} %get-tuple-element.56), channel_id=1, source_target_pairs={{0,1},{2,3},{4,5},{6,7},{8,9},{10,11},{12,13},{14,15},{128,129},{1... | collective-permute-start | bytes 86024 | tf_op jit(solution)/shard_map/ppermute | solution.py:482
  49.8 1.5 %collective-permute-done.7 = f32[7,8,128]{2,1,0:T(8,128)S(1)} collective-permute-done((f32[7,8,128]{2,1,0:T(8,128)S(1)}, f32[7,8,128]{2,1,0:T(8,128)S(1)}, u32[]{:S(2)}, u32[]{:S(2)}) %collective-permute-start.7) | collective-permute-done | bytes 28704 | tf_op jit(solution)/shard_map/ppermute | solution.py:482
  51.3 3.7 %collective-permute-start.11 = (f32[7,8,128]{2,1,0:T(8,128)S(1)}, f32[7,8,128]{2,1,0:T(8,128)S(1)}, u32[]{:S(2)}, u32[]{:S(2)}) collective-permute-start(f32[7,8,128]{2,1,0:T(8,128)S(1)} %add_add_fusion.5.refs_6_), channel_id=1, source_target_pairs={{0,12},{2,14},{4,8},{6,10},{8,4},{10,6},{12,0},{14,2},{128,140},{1... | collective-permute-start | bytes 86024 | tf_op jit(solution)/shard_map/ppermute | solution.py:482
  56.0 2.0 %collective-permute-start.9 = (f32[7,8,128]{2,1,0:T(8,128)S(1)}, f32[7,8,128]{2,1,0:T(8,128)S(1)}, u32[]{:S(2)}, u32[]{:S(2)}) collective-permute-start(f32[7,8,128]{2,1,0:T(8,128)S(1)} %add_add_fusion.5.refs_6_), channel_id=1, source_target_pairs={{0,4},{2,6},{4,0},{6,2},{8,12},{10,14},{12,8},{14,10},{128,132},{1... | collective-permute-start | bytes 86024 | tf_op jit(solution)/shard_map/ppermute | solution.py:482
  58.0 3.6 %input_below.1.refs_5_ = f32[1024,256]{1,0:T(8,128)S(1)} custom-call(s32[2,27]{1,0:T(2,128)S(1)} %bitcast.46, bf16[2,512,256]{2,1,0:T(8,128)(2,1)S(1)} %bitcast.36, f32[8,128]{1,0:T(8,128)S(1)} %convert_element_type.12.occupancy.refs_3_.refs_2_, bf16[3,3,3,256,256]{4,3,2,1,0:T(8,128)(2,1)S(1)} %bitcast.39, ...), custom_call_target="tpu_custom_call" | custom-call | flops 2000000000 | bytes 4000000 | tf_op jit(solution)/shard_map/input_below/pallas_call | solution.py:314
  61.6 1.6 %collective-permute-done.10 = f32[7,8,128]{2,1,0:T(8,128)S(1)} collective-permute-done((f32[7,8,128]{2,1,0:T(8,128)S(1)}, f32[7,8,128]{2,1,0:T(8,128)S(1)}, u32[]{:S(2)}, u32[]{:S(2)}) %collective-permute-start.10) | collective-permute-done | bytes 28704 | tf_op jit(solution)/shard_map/ppermute | solution.py:482
  64.0 3.1 %collective-permute-done.12 = f32[7,8,128]{2,1,0:T(8,128)S(1)} collective-permute-done((f32[7,8,128]{2,1,0:T(8,128)S(1)}, f32[7,8,128]{2,1,0:T(8,128)S(1)}, u32[]{:S(2)}, u32[]{:S(2)}) %collective-permute-start.12) | collective-permute-done | bytes 28704 | tf_op jit(solution)/shard_map/ppermute | solution.py:482
  67.7 2.6 %collective-permute-start.14 = (f32[7,8,128]{2,1,0:T(8,128)S(1)}, f32[7,8,128]{2,1,0:T(8,128)S(1)}, u32[]{:S(2)}, u32[]{:S(2)}) collective-permute-start(f32[7,8,128]{2,1,0:T(8,128)S(1)} %add.79), channel_id=1, source_target_pairs={{0,1},{2,3},{4,5},{6,7},{8,9},{10,11},{12,13},{14,15},{128,129},{1... | collective-permute-start | bytes 86024 | tf_op jit(solution)/shard_map/ppermute | solution.py:482
  71.3 1.8 %collective-permute-done.14 = f32[7,8,128]{2,1,0:T(8,128)S(1)} collective-permute-done((f32[7,8,128]{2,1,0:T(8,128)S(1)}, f32[7,8,128]{2,1,0:T(8,128)S(1)}, u32[]{:S(2)}, u32[]{:S(2)}) %collective-permute-start.14) | collective-permute-done | bytes 28704 | tf_op jit(solution)/shard_map/ppermute | solution.py:482
  74.2 1.9 %collective-permute-start.18 = (f32[28,8,128]{2,1,0:T(8,128)S(1)}, f32[28,8,128]{2,1,0:T(8,128)S(1)}, u32[]{:S(2)}, u32[]{:S(2)}) collective-permute-start(f32[28,8,128]{2,1,0:T(8,128)S(1)} %get-tuple-element.53.refs_6_), channel_id=1, source_target_pairs={{0,48},{2,50},{4,52},{6,54},{8,56},{10,58},{12,60},{14,62},{128,17... | collective-permute-start | bytes 344072 | tf_op jit(solution)/shard_map/ppermute | solution.py:482
  76.9 1.5 %collective-permute-start.16 = (f32[28,8,128]{2,1,0:T(8,128)S(1)}, f32[28,8,128]{2,1,0:T(8,128)S(1)}, u32[]{:S(2)}, u32[]{:S(2)}) collective-permute-start(f32[28,8,128]{2,1,0:T(8,128)S(1)} %get-tuple-element.53.refs_6_), channel_id=1, source_target_pairs={{0,16},{2,18},{4,20},{6,22},{8,24},{10,26},{12,28},{14,30},{128,14... | collective-permute-start | bytes 344072 | tf_op jit(solution)/shard_map/ppermute | solution.py:482
  78.4 4.6 %input_above.1 = bf16[2,512,256]{2,1,0:T(8,128)(2,1)} custom-call(s32[2,27]{1,0:T(2,128)S(1)} %bitcast.47, bf16[2,512,256]{2,1,0:T(8,128)(2,1)S(1)} %bitcast.37, f32[8,128]{1,0:T(8,128)S(1)} %convert_element_type.12.occupancy.refs_3_.refs_2_, bf16[3,3,3,256,256]{4,3,2,1,0:T(8,128)(2,1)S(1)} %bitcast.40, ...), custom_call_target="tpu_custom_call" | custom-call | flops 2000000000 | bytes 4000000 | tf_op jit(solution)/shard_map/input_above/pallas_call | solution.py:314
  83.1 1.8 %collective-permute-done.19.other = f32[4,28,8,128]{3,2,1,0:T(8,128)S(1)} collective-permute-done((f32[4,28,8,128]{3,2,1,0:T(8,128)S(1)}, f32[4,28,8,128]{3,2,1,0:T(8,128)S(1)}, u32[]{:S(2)}, u32[]{:S(2)}) %collective-permute-start.19) | collective-permute-done | bytes 458784 | tf_op jit(solution)/shard_map/ppermute | solution.py:482
  84.9 2.4 %right_product.1 = f32[32,256]{1,0:T(8,128)S(1)} custom-call(f32[4,28,8,128]{3,2,1,0:T(8,128)S(1)} %pad_maximum_fusion.mine, f32[4,28,8,128]{3,2,1,0:T(8,128)S(1)} %collective-permute-done.19.other, f32[27,256,256]{2,1,0:T(8,128)S(1)} %bitcast.30), custom_call_target="tpu_custom_call" | custom-call | tf_op jit(solution)/shard_map/right_product/pallas_call | solution.py:347
  89.3 2.4 %half_inverse.1 = (f32[32,32]{1,0:T(8,128)S(1)}, f32[32,32]{1,0:T(8,128)S(1)}) custom-call(f32[4,28,8,128]{3,2,1,0:T(8,128)S(1)} %pad_maximum_fusion.mine, f32[4,28,8,128]{3,2,1,0:T(8,128)S(1)} %collective-permute-done.19.other), custom_call_target="tpu_custom_call" | custom-call | tf_op jit(solution)/shard_map/half_inverse/pallas_call | solution.py:390
  92.1 2.2 %collective-permute-start.25 = (f32[32,256]{1,0:T(8,128)S(1)}, f32[32,256]{1,0:T(8,128)S(1)}, u32[]{:S(2)}, u32[]{:S(2)}) collective-permute-start(f32[32,256]{1,0:T(8,128)S(1)} %add_add_fusion.3.refs_0_), channel_id=1, source_target_pairs={{0,48},{2,50},{4,52},{6,54},{8,56},{10,58},{12,60},{14,62},{128,17... | collective-permute-start | bytes 98312 | tf_op jit(solution)/shard_map/ppermute | solution.py:482
  96.5 1.4 %whole_inverse.1.inverse = f32[32,32]{1,0:T(8,128)S(1)} custom-call(f32[32,32]{1,0:T(8,128)S(1)} %get-tuple-element.43.work, f32[32,32]{1,0:T(8,128)S(1)} %get-tuple-element.44.made, f32[32,256]{1,0:T(8,128)S(1)} %add_add_fusion.3.refs_0_), custom_call_target="tpu_custom_call" | custom-call | tf_op jit(solution)/shard_map/whole_inverse/pallas_call | solution.py:401
  97.9 1.8 %collective-permute-done.24 = f32[32,256]{1,0:T(8,128)S(1)} collective-permute-done((f32[32,256]{1,0:T(8,128)S(1)}, f32[32,256]{1,0:T(8,128)S(1)}, u32[]{:S(2)}, u32[]{:S(2)}) %collective-permute-start.24) | collective-permute-done | bytes 32800 | tf_op jit(solution)/shard_map/ppermute | solution.py:482
  101.1 2.1 %collective-permute-start.27 = (f32[32,256]{1,0:T(8,128)S(1)}, f32[32,256]{1,0:T(8,128)S(1)}, u32[]{:S(2)}, u32[]{:S(2)}) collective-permute-start(f32[32,256]{1,0:T(8,128)S(1)} %add_add_fusion.2), channel_id=1, source_target_pairs={{0,1},{2,3},{4,5},{6,7},{8,9},{10,11},{12,13},{14,15},{128,129},{1... | collective-permute-start | bytes 98312 | tf_op jit(solution)/shard_map/ppermute | solution.py:482
  104.0 2.5 %collective-permute-done.27 = f32[32,256]{1,0:T(8,128)S(1)} collective-permute-done((f32[32,256]{1,0:T(8,128)S(1)}, f32[32,256]{1,0:T(8,128)S(1)}, u32[]{:S(2)}, u32[]{:S(2)}) %collective-permute-start.27) | collective-permute-done | bytes 32800 | tf_op jit(solution)/shard_map/ppermute | solution.py:482
  107.2 3.0 %collective-permute-start.31 = (f32[32,256]{1,0:T(8,128)S(1)}, f32[32,256]{1,0:T(8,128)S(1)}, u32[]{:S(2)}, u32[]{:S(2)}) collective-permute-start(f32[32,256]{1,0:T(8,128)S(1)} %add_add_fusion.1), channel_id=1, source_target_pairs={{0,12},{2,14},{4,8},{6,10},{8,4},{10,6},{12,0},{14,2},{128,140},{1... | collective-permute-start | bytes 98312 | tf_op jit(solution)/shard_map/ppermute | solution.py:482
  110.2 3.0 %collective-permute-start.30 = (f32[32,256]{1,0:T(8,128)S(1)}, f32[32,256]{1,0:T(8,128)S(1)}, u32[]{:S(2)}, u32[]{:S(2)}) collective-permute-start(f32[32,256]{1,0:T(8,128)S(1)} %add_add_fusion.1), channel_id=1, source_target_pairs={{0,8},{2,10},{4,12},{6,14},{8,0},{10,2},{12,4},{14,6},{128,136},{1... | collective-permute-start | bytes 98312 | tf_op jit(solution)/shard_map/ppermute | solution.py:482
  113.7 4.3 %collective-permute-done.30 = f32[32,256]{1,0:T(8,128)S(1)} collective-permute-done((f32[32,256]{1,0:T(8,128)S(1)}, f32[32,256]{1,0:T(8,128)S(1)}, u32[]{:S(2)}, u32[]{:S(2)}) %collective-permute-start.30) | collective-permute-done | bytes 32800 | tf_op jit(solution)/shard_map/ppermute | solution.py:482
  118.0 5.7 %remaining_error.1 = (bf16[27,256,256]{2,1,0:T(8,128)(2,1)}, f32[32,256]{1,0:T(8,128)}) custom-call(f32[4,28,8,128]{3,2,1,0:T(8,128)S(1)} %pad_maximum_fusion.mine, f32[4,28,8,128]{3,2,1,0:T(8,128)S(1)} %collective-permute-done.19.other, f32[27,256,256]{2,1,0:T(8,128)S(1)} %bitcast.31, f32[32,256]{1,0:T(8,128)S(1)} %add_add_fusion.right, ...), custom_call_target="tpu_custom_call" | custom-call | tf_op jit(solution)/shard_map/remaining_error/pallas_call | solution.py:436
  (67 shorter events, 21.5 us)
Async XLA Ops:
  3.2 12.9 %collective-permute-start = (bf16[2,8,16,256]{3,2,1,0:T(8,128)(2,1)S(1)}, bf16[2,8,16,256]{3,2,1,0:T(8,128)(2,1)S(1)}, u32[]{:S(2)}, u32[]{:S(2)}) collective-permute-start(bf16[2,8,16,256]{3,2,1,0:T(8,128)(2,1)S(1)} %get-tuple-element.26), channel_id=1, source_target_pairs={{0,1},{1,2},{2,3},{3,4},{4,5},{5,6},{6,7},{7,8},{8,9},{9,10},{10,1... | collective-permute-start | bytes 393224 | tf_op jit(solution)/shard_map/ppermute | solution.py:465
  7.4 8.7 %collective-permute-start.1 = (bf16[2,8,16,256]{3,2,1,0:T(8,128)(2,1)S(1)}, bf16[2,8,16,256]{3,2,1,0:T(8,128)(2,1)S(1)}, u32[]{:S(2)}, u32[]{:S(2)}) collective-permute-start(bf16[2,8,16,256]{3,2,1,0:T(8,128)(2,1)S(1)} %get-tuple-element.27), channel_id=1, source_target_pairs={{1,0},{2,1},{3,2},{4,3},{5,4},{6,5},{7,6},{8,7},{9,8},{10,9},{11,1... | collective-permute-start | bytes 393224 | tf_op jit(solution)/shard_map/ppermute | solution.py:465
  25.9 1.9 %collective-permute-start.2 = (f32[4,28,8,128]{3,2,1,0:T(8,128)S(1)}, f32[4,28,8,128]{3,2,1,0:T(8,128)S(1)}, u32[]{:S(2)}, u32[]{:S(2)}) collective-permute-start(f32[4,28,8,128]{3,2,1,0:T(8,128)S(1)} %get-tuple-element.32), channel_id=1, source_target_pairs={{0,64},{2,66},{4,68},{6,70},{8,72},{10,74},{12,76},{14,78},{128,19... | collective-permute-start | bytes 1376264 | tf_op jit(solution)/shard_map/ppermute | solution.py:482
  27.8 14.2 %collective-permute-start.5 = (f32[28,8,128]{2,1,0:T(8,128)S(1)}, f32[28,8,128]{2,1,0:T(8,128)S(1)}, u32[]{:S(2)}, u32[]{:S(2)}) collective-permute-start(f32[28,8,128]{2,1,0:T(8,128)S(1)} %get-tuple-element.49), channel_id=1, source_target_pairs={{0,48},{2,50},{4,52},{6,54},{8,56},{10,58},{12,60},{14,62},{128,17... | collective-permute-start | bytes 344072 | tf_op jit(solution)/shard_map/ppermute | solution.py:482
  36.9 7.5 %collective-permute-start.4 = (f32[28,8,128]{2,1,0:T(8,128)S(1)}, f32[28,8,128]{2,1,0:T(8,128)S(1)}, u32[]{:S(2)}, u32[]{:S(2)}) collective-permute-start(f32[28,8,128]{2,1,0:T(8,128)S(1)} %get-tuple-element.50), channel_id=1, source_target_pairs={{0,32},{2,34},{4,36},{6,38},{8,40},{10,42},{12,44},{14,46},{128,16... | collective-permute-start | bytes 344072 | tf_op jit(solution)/shard_map/ppermute | solution.py:482
  37.4 7.0 %collective-permute-start.3 = (f32[28,8,128]{2,1,0:T(8,128)S(1)}, f32[28,8,128]{2,1,0:T(8,128)S(1)}, u32[]{:S(2)}, u32[]{:S(2)}) collective-permute-start(f32[28,8,128]{2,1,0:T(8,128)S(1)} %get-tuple-element.51), channel_id=1, source_target_pairs={{0,16},{2,18},{4,20},{6,22},{8,24},{10,26},{12,28},{14,30},{128,14... | collective-permute-start | bytes 344072 | tf_op jit(solution)/shard_map/ppermute | solution.py:482
  44.5 4.2 %collective-permute-start.6 = (f32[7,8,128]{2,1,0:T(8,128)S(1)}, f32[7,8,128]{2,1,0:T(8,128)S(1)}, u32[]{:S(2)}, u32[]{:S(2)}) collective-permute-start(f32[7,8,128]{2,1,0:T(8,128)S(1)} %get-tuple-element.54), channel_id=1, source_target_pairs={{0,128},{2,130},{4,132},{6,134},{8,136},{10,138},{12,140},{14,142}... | collective-permute-start | bytes 86024 | tf_op jit(solution)/shard_map/ppermute | solution.py:482
  45.9 3.9 %collective-permute-start.8 = (f32[7,8,128]{2,1,0:T(8,128)S(1)}, f32[7,8,128]{2,1,0:T(8,128)S(1)}, u32[]{:S(2)}, u32[]{:S(2)}) collective-permute-start(f32[7,8,128]{2,1,0:T(8,128)S(1)} %get-tuple-element.55), channel_id=1, source_target_pairs={{0,129},{2,131},{4,133},{6,135},{8,137},{10,139},{12,141},{14,143}... | collective-permute-start | bytes 86024 | tf_op jit(solution)/shard_map/ppermute | solution.py:482
  45.9 5.4 %collective-permute-start.7 = (f32[7,8,128]{2,1,0:T(8,128)S(1)}, f32[7,8,128]{2,1,0:T(8,128)S(1)}, u32[]{:S(2)}, u32[]{:S(2)}) collective-permute-start(f32[7,8,128]{2,1,0:T(8,128)S(1)} %get-tuple-element.56), channel_id=1, source_target_pairs={{0,1},{2,3},{4,5},{6,7},{8,9},{10,11},{12,13},{14,15},{128,129},{1... | collective-permute-start | bytes 86024 | tf_op jit(solution)/shard_map/ppermute | solution.py:482
  51.3 10.4 %collective-permute-start.11 = (f32[7,8,128]{2,1,0:T(8,128)S(1)}, f32[7,8,128]{2,1,0:T(8,128)S(1)}, u32[]{:S(2)}, u32[]{:S(2)}) collective-permute-start(f32[7,8,128]{2,1,0:T(8,128)S(1)} %add_add_fusion.5.refs_6_), channel_id=1, source_target_pairs={{0,12},{2,14},{4,8},{6,10},{8,4},{10,6},{12,0},{14,2},{128,140},{1... | collective-permute-start | bytes 86024 | tf_op jit(solution)/shard_map/ppermute | solution.py:482
  55.0 8.2 %collective-permute-start.10 = (f32[7,8,128]{2,1,0:T(8,128)S(1)}, f32[7,8,128]{2,1,0:T(8,128)S(1)}, u32[]{:S(2)}, u32[]{:S(2)}) collective-permute-start(f32[7,8,128]{2,1,0:T(8,128)S(1)} %add_add_fusion.5.refs_6_), channel_id=1, source_target_pairs={{0,8},{2,10},{4,12},{6,14},{8,0},{10,2},{12,4},{14,6},{128,136},{1... | collective-permute-start | bytes 86024 | tf_op jit(solution)/shard_map/ppermute | solution.py:482
  56.0 7.2 %collective-permute-start.9 = (f32[7,8,128]{2,1,0:T(8,128)S(1)}, f32[7,8,128]{2,1,0:T(8,128)S(1)}, u32[]{:S(2)}, u32[]{:S(2)}) collective-permute-start(f32[7,8,128]{2,1,0:T(8,128)S(1)} %add_add_fusion.5.refs_6_), channel_id=1, source_target_pairs={{0,4},{2,6},{4,0},{6,2},{8,12},{10,14},{12,8},{14,10},{128,132},{1... | collective-permute-start | bytes 86024 | tf_op jit(solution)/shard_map/ppermute | solution.py:482
  63.2 4.0 %collective-permute-start.12 = (f32[7,8,128]{2,1,0:T(8,128)S(1)}, f32[7,8,128]{2,1,0:T(8,128)S(1)}, u32[]{:S(2)}, u32[]{:S(2)}) collective-permute-start(f32[7,8,128]{2,1,0:T(8,128)S(1)} %add_add_fusion.4), channel_id=1, source_target_pairs={{0,2},{2,0},{4,6},{6,4},{8,10},{10,8},{12,14},{14,12},{128,130},{1... | collective-permute-start | bytes 86024 | tf_op jit(solution)/shard_map/ppermute | solution.py:482
  67.2 4.1 %collective-permute-start.15 = (f32[7,8,128]{2,1,0:T(8,128)S(1)}, f32[7,8,128]{2,1,0:T(8,128)S(1)}, u32[]{:S(2)}, u32[]{:S(2)}) collective-permute-start(f32[7,8,128]{2,1,0:T(8,128)S(1)} %add.79), channel_id=1, source_target_pairs={{0,129},{2,131},{4,133},{6,135},{8,137},{10,139},{12,141},{14,143}... | collective-permute-start | bytes 86024 | tf_op jit(solution)/shard_map/ppermute | solution.py:482
  67.7 5.4 %collective-permute-start.14 = (f32[7,8,128]{2,1,0:T(8,128)S(1)}, f32[7,8,128]{2,1,0:T(8,128)S(1)}, u32[]{:S(2)}, u32[]{:S(2)}) collective-permute-start(f32[7,8,128]{2,1,0:T(8,128)S(1)} %add.79), channel_id=1, source_target_pairs={{0,1},{2,3},{4,5},{6,7},{8,9},{10,11},{12,13},{14,15},{128,129},{1... | collective-permute-start | bytes 86024 | tf_op jit(solution)/shard_map/ppermute | solution.py:482
  70.3 3.9 %collective-permute-start.13 = (f32[7,8,128]{2,1,0:T(8,128)S(1)}, f32[7,8,128]{2,1,0:T(8,128)S(1)}, u32[]{:S(2)}, u32[]{:S(2)}) collective-permute-start(f32[7,8,128]{2,1,0:T(8,128)S(1)} %add.79), channel_id=1, source_target_pairs={{0,128},{2,130},{4,132},{6,134},{8,136},{10,138},{12,140},{14,142}... | collective-permute-start | bytes 86024 | tf_op jit(solution)/shard_map/ppermute | solution.py:482
  74.2 8.8 %collective-permute-start.18 = (f32[28,8,128]{2,1,0:T(8,128)S(1)}, f32[28,8,128]{2,1,0:T(8,128)S(1)}, u32[]{:S(2)}, u32[]{:S(2)}) collective-permute-start(f32[28,8,128]{2,1,0:T(8,128)S(1)} %get-tuple-element.53.refs_6_), channel_id=1, source_target_pairs={{0,48},{2,50},{4,52},{6,54},{8,56},{10,58},{12,60},{14,62},{128,17... | collective-permute-start | bytes 344072 | tf_op jit(solution)/shard_map/ppermute | solution.py:482
  76.1 6.9 %collective-permute-start.17 = (f32[28,8,128]{2,1,0:T(8,128)S(1)}, f32[28,8,128]{2,1,0:T(8,128)S(1)}, u32[]{:S(2)}, u32[]{:S(2)}) collective-permute-start(f32[28,8,128]{2,1,0:T(8,128)S(1)} %get-tuple-element.53.refs_6_), channel_id=1, source_target_pairs={{0,32},{2,34},{4,36},{6,38},{8,40},{10,42},{12,44},{14,46},{128,16... | collective-permute-start | bytes 344072 | tf_op jit(solution)/shard_map/ppermute | solution.py:482
  76.9 6.1 %collective-permute-start.16 = (f32[28,8,128]{2,1,0:T(8,128)S(1)}, f32[28,8,128]{2,1,0:T(8,128)S(1)}, u32[]{:S(2)}, u32[]{:S(2)}) collective-permute-start(f32[28,8,128]{2,1,0:T(8,128)S(1)} %get-tuple-element.53.refs_6_), channel_id=1, source_target_pairs={{0,16},{2,18},{4,20},{6,22},{8,24},{10,26},{12,28},{14,30},{128,14... | collective-permute-start | bytes 344072 | tf_op jit(solution)/shard_map/ppermute | solution.py:482
  83.0 1.9 %collective-permute-start.19 = (f32[4,28,8,128]{3,2,1,0:T(8,128)S(1)}, f32[4,28,8,128]{3,2,1,0:T(8,128)S(1)}, u32[]{:S(2)}, u32[]{:S(2)}) collective-permute-start(f32[4,28,8,128]{3,2,1,0:T(8,128)S(1)} %pad_maximum_fusion.mine), channel_id=1, source_target_pairs={{0,64},{2,66},{4,68},{6,70},{8,72},{10,74},{12,76},{14,78},{128,19... | collective-permute-start | bytes 1376264 | tf_op jit(solution)/shard_map/ppermute | solution.py:482
  87.4 4.3 %collective-permute-start.22 = (f32[32,256]{1,0:T(8,128)S(1)}, f32[32,256]{1,0:T(8,128)S(1)}, u32[]{:S(2)}, u32[]{:S(2)}) collective-permute-start(f32[32,256]{1,0:T(8,128)S(1)} %right_product.1), channel_id=1, source_target_pairs={{0,66},{2,64},{4,70},{6,68},{8,74},{10,72},{12,78},{14,76},{128,19... | collective-permute-start | bytes 98312 | tf_op jit(solution)/shard_map/ppermute | solution.py:482
  88.1 3.9 %collective-permute-start.21 = (f32[32,256]{1,0:T(8,128)S(1)}, f32[32,256]{1,0:T(8,128)S(1)}, u32[]{:S(2)}, u32[]{:S(2)}) collective-permute-start(f32[32,256]{1,0:T(8,128)S(1)} %right_product.1), channel_id=1, source_target_pairs={{0,2},{2,0},{4,6},{6,4},{8,10},{10,8},{12,14},{14,12},{128,130},{1... | collective-permute-start | bytes 98312 | tf_op jit(solution)/shard_map/ppermute | solution.py:482
  89.2 2.8 %collective-permute-start.20 = (f32[32,256]{1,0:T(8,128)S(1)}, f32[32,256]{1,0:T(8,128)S(1)}, u32[]{:S(2)}, u32[]{:S(2)}) collective-permute-start(f32[32,256]{1,0:T(8,128)S(1)} %right_product.1), channel_id=1, source_target_pairs={{0,64},{2,66},{4,68},{6,70},{8,72},{10,74},{12,76},{14,78},{128,19... | collective-permute-start | bytes 98312 | tf_op jit(solution)/shard_map/ppermute | solution.py:482
  92.1 5.9 %collective-permute-start.25 = (f32[32,256]{1,0:T(8,128)S(1)}, f32[32,256]{1,0:T(8,128)S(1)}, u32[]{:S(2)}, u32[]{:S(2)}) collective-permute-start(f32[32,256]{1,0:T(8,128)S(1)} %add_add_fusion.3.refs_0_), channel_id=1, source_target_pairs={{0,48},{2,50},{4,52},{6,54},{8,56},{10,58},{12,60},{14,62},{128,17... | collective-permute-start | bytes 98312 | tf_op jit(solution)/shard_map/ppermute | solution.py:482
  94.2 5.4 %collective-permute-start.24 = (f32[32,256]{1,0:T(8,128)S(1)}, f32[32,256]{1,0:T(8,128)S(1)}, u32[]{:S(2)}, u32[]{:S(2)}) collective-permute-start(f32[32,256]{1,0:T(8,128)S(1)} %add_add_fusion.3.refs_0_), channel_id=1, source_target_pairs={{0,32},{2,34},{4,36},{6,38},{8,40},{10,42},{12,44},{14,46},{128,16... | collective-permute-start | bytes 98312 | tf_op jit(solution)/shard_map/ppermute | solution.py:482
  95.1 4.6 %collective-permute-start.23 = (f32[32,256]{1,0:T(8,128)S(1)}, f32[32,256]{1,0:T(8,128)S(1)}, u32[]{:S(2)}, u32[]{:S(2)}) collective-permute-start(f32[32,256]{1,0:T(8,128)S(1)} %add_add_fusion.3.refs_0_), channel_id=1, source_target_pairs={{0,16},{2,18},{4,20},{6,22},{8,24},{10,26},{12,28},{14,30},{128,14... | collective-permute-start | bytes 98312 | tf_op jit(solution)/shard_map/ppermute | solution.py:482
  99.7 4.4 %collective-permute-start.28 = (f32[32,256]{1,0:T(8,128)S(1)}, f32[32,256]{1,0:T(8,128)S(1)}, u32[]{:S(2)}, u32[]{:S(2)}) collective-permute-start(f32[32,256]{1,0:T(8,128)S(1)} %add_add_fusion.2), channel_id=1, source_target_pairs={{0,129},{2,131},{4,133},{6,135},{8,137},{10,139},{12,141},{14,143}... | collective-permute-start | bytes 98312 | tf_op jit(solution)/shard_map/ppermute | solution.py:482
  101.1 5.4 %collective-permute-start.27 = (f32[32,256]{1,0:T(8,128)S(1)}, f32[32,256]{1,0:T(8,128)S(1)}, u32[]{:S(2)}, u32[]{:S(2)}) collective-permute-start(f32[32,256]{1,0:T(8,128)S(1)} %add_add_fusion.2), channel_id=1, source_target_pairs={{0,1},{2,3},{4,5},{6,7},{8,9},{10,11},{12,13},{14,15},{128,129},{1... | collective-permute-start | bytes 98312 | tf_op jit(solution)/shard_map/ppermute | solution.py:482
  103.2 3.9 %collective-permute-start.26 = (f32[32,256]{1,0:T(8,128)S(1)}, f32[32,256]{1,0:T(8,128)S(1)}, u32[]{:S(2)}, u32[]{:S(2)}) collective-permute-start(f32[32,256]{1,0:T(8,128)S(1)} %add_add_fusion.2), channel_id=1, source_target_pairs={{0,128},{2,130},{4,132},{6,134},{8,136},{10,138},{12,140},{14,142}... | collective-permute-start | bytes 98312 | tf_op jit(solution)/shard_map/ppermute | solution.py:482
  107.2 6.6 %collective-permute-start.31 = (f32[32,256]{1,0:T(8,128)S(1)}, f32[32,256]{1,0:T(8,128)S(1)}, u32[]{:S(2)}, u32[]{:S(2)}) collective-permute-start(f32[32,256]{1,0:T(8,128)S(1)} %add_add_fusion.1), channel_id=1, source_target_pairs={{0,12},{2,14},{4,8},{6,10},{8,4},{10,6},{12,0},{14,2},{128,140},{1... | collective-permute-start | bytes 98312 | tf_op jit(solution)/shard_map/ppermute | solution.py:482
  110.2 7.8 %collective-permute-start.30 = (f32[32,256]{1,0:T(8,128)S(1)}, f32[32,256]{1,0:T(8,128)S(1)}, u32[]{:S(2)}, u32[]{:S(2)}) collective-permute-start(f32[32,256]{1,0:T(8,128)S(1)} %add_add_fusion.1), channel_id=1, source_target_pairs={{0,8},{2,10},{4,12},{6,14},{8,0},{10,2},{12,4},{14,6},{128,136},{1... | collective-permute-start | bytes 98312 | tf_op jit(solution)/shard_map/ppermute | solution.py:482
  113.2 4.8 %collective-permute-start.29 = (f32[32,256]{1,0:T(8,128)S(1)}, f32[32,256]{1,0:T(8,128)S(1)}, u32[]{:S(2)}, u32[]{:S(2)}) collective-permute-start(f32[32,256]{1,0:T(8,128)S(1)} %add_add_fusion.1), channel_id=1, source_target_pairs={{0,4},{2,6},{4,0},{6,2},{8,12},{10,14},{12,8},{14,10},{128,132},{1... | collective-permute-start | bytes 98312 | tf_op jit(solution)/shard_map/ppermute | solution.py:482
  (4 other events, 45.0 us)

commit v3 on v2

--- a/solution.py
+++ b/solution.py
@@ -56,9 +56,14 @@
     return jnp.where(places == rows, 1.0, 0.0).astype(BF16)
 
 
+def voxel_mask(occupancy):
+    padded = jnp.concatenate([occupancy[...].astype(F32), jnp.zeros((6, 512), F32)], axis=0)
+    return padded.T
+
+
 def own_plane(field, mask, plane):
-    rows = jnp.concatenate([field[b, plane * PLANE : (plane + 1) * PLANE, :] for b in (0, 1)], axis=0)
-    return rows * mask[:, plane : plane + 1]
+    rows = slice(plane * PLANE, (plane + 1) * PLANE)
+    return jnp.concatenate([field[b, rows, :] * mask[rows, b : b + 1] for b in (0, 1)], axis=0)
 
 
 def with_faces(own, lower, upper, plane):
@@ -101,7 +106,7 @@
 
 
 def faces_kernel(field, cotangent, occupancy, up, down):
-    mask = occupancy[...].T.astype(BF16)
+    mask = voxel_mask(occupancy).astype(BF16)
     row = lax.broadcasted_iota(jnp.int32, (32, 128), 0)
     place = lax.broadcasted_iota(jnp.int32, (32, 128), 1)
     wanted = jnp.where(row < 16, row * EDGE + EDGE - 1, (row - 16) * EDGE)
@@ -120,36 +125,48 @@
     )
 
 
-def gradient_kernel(sides, *refs):
-    count = 3 * len(sides)
+def gradient_kernel(sides, width, *refs):
     faces = sides != (0,)
     slots, field, cotangent, occupancy, start, error = refs[:6]
     refs = refs[6:]
     if faces:
         lower, upper, _, mine_before, other_before = refs[:5]
         refs = refs[5:]
-    corrected, mine, other, views, own, start_split, kept_high, kept_low = refs
+    corrected, mine, other, views, sources, own, start_parts = refs
     step = pl.program_id(0)
+    depth = 256 if faces else 128
+    shares = 3 // width
+    side = step // shares * 2 - 1 if faces else 0
 
     @pl.when(step == 0)
     def _():
-        mask = occupancy[...].T.astype(BF16)
-        high, low = split(start[...])
-        start_split[0:32, :] = high
-        start_split[32:64, :] = low
-        depth = 256 if faces else 128
-        sources = []
+        mask = voxel_mask(occupancy).astype(BF16)
+        high, low = split(start[...].T)
+        none = jnp.zeros((256, 32), BF16)
+        start_parts[0:256, :] = jnp.concatenate([high, low, none, none], axis=1)
+        start_parts[256:512, :] = jnp.concatenate([high, none, none, none], axis=1)
+        start_parts[512:768, :] = jnp.concatenate([none, none, high, low], axis=1)
+        start_parts[768:1024, :] = jnp.concatenate([none, none, high, none], axis=1)
         for plane in range(EDGE):
             own[plane * 128 : (plane + 1) * 128, :] = own_plane(cotangent, mask, plane)
             source = own_plane(field, mask, plane)
             if faces:
                 source = with_faces(source, lower, upper, plane)
-            sources.append(source.T)
-        inner = jnp.concatenate(sources, axis=0)
-        groups = [(y, z) for y in STEPS for z in sides]
-        for first in range(0, count, 2):
+            sources[plane * 256 : (plane + 1) * 256, :] = source.T
+        if faces:
+            mine[...] = mine_before[...]
+            other[...] = other_before[...]
+        else:
+            put_factor(mine, other, 27, jnp.zeros((32, 256), F32))
+
+    def gather(groups):
+        for first in range(0, len(groups), 2):
             pair = groups[first : first + 2]
-            for step_x, left, where in ((-1, sources[7], 0), (0, inner, 1), (1, sources[0], 9)):
+            for step_x, left, where in (
+                (-1, sources[7 * 256 : 8 * 256, :], 0),
+                (0, sources[...], 1),
+                (1, sources[0:256, :], 9),
+            ):
                 picks = jnp.concatenate(
                     [one_hot(source_rows(slots, step_x, y, z, 1), 1, depth) for y, z in pair], axis=1
                 )
@@ -159,78 +176,64 @@
                         views[first + member, :, (where + block) * 128 : (where + block + 1) * 128] = found[
                             block * 256 : (block + 1) * 256, member * 128 : (member + 1) * 128
                         ]
-        if faces:
-            mine[...] = mine_before[...]
-            other[...] = other_before[...]
-
-    def product():
-        columns = jnp.concatenate([views[step, :, k * 128 : k * 128 + 1024] for k in range(3)], axis=0)
+
+    for index in range(len(sides) * shares):
+        chosen = STEPS[index % shares * width : index % shares * width + width]
+
+        @pl.when(step == index)
+        def _():
+            gather([(y, sides[index // shares]) for y in chosen])
+
+    parts = []
+    for member in range(width):
+        columns = jnp.concatenate([views[member, :, k * 128 : k * 128 + 1024] for k in range(3)], axis=0)
         total = lax.dot_general(columns, own[...], NN, preferred_element_type=F32)
-        total = total + error[:, 0, 0].astype(F32).reshape(768, 256)
-        corrected[:, 0, 0] = total.reshape(3, 256, 256)
-        return split(total)
-
-    def keep(parts):
-        kept_high[...], kept_low[...] = parts
-
-    def factor():
-        both = lax.dot_general(start_split[...], kept_high[...], NT, preferred_element_type=F32)
-        rest = lax.dot_general(start_split[0:32, :], kept_low[...], NT, preferred_element_type=F32)
-        return both[0:32] + both[32:64] + rest
-
-    def put(made):
-        before = step - 1
-        if faces:
-            group = before // 2 * 3 + before % 2 * 2
-        else:
-            group = before * 3 + 1
+        total = total + error[:, member, 0].astype(F32).reshape(768, 256)
+        corrected[0, :, member] = total.reshape(3, 256, 256)
+        high, low = split(total)
         for tap_x in range(3):
-            put_factor(mine, other, tap_x * 9 + group, made[:, tap_x * 256 : tap_x * 256 + 256])
-
-    @pl.when(step == 0)
-    def _():
-        keep(product())
-
-    @pl.when((step > 0) & (step < count))
-    def _():
-        made = factor()
-        parts = product()
-        put(made)
-        keep(parts)
-
-    @pl.when(step == count)
-    def _():
-        put(factor())
-        if not faces:
-            put_factor(mine, other, 27, jnp.zeros((32, 256), F32))
+            rows = slice(tap_x * 256, tap_x * 256 + 256)
+            parts.append((tap_x, member, [high[rows], low[rows]]))
+    for first in range(0, 3 * width, 2):
+        chosen = parts[first : first + 2]
+        left = jnp.concatenate([part for _, _, both in chosen for part in both], axis=1)
+        made = lax.dot_general(left, start_parts[0 : left.shape[1], :], NN, preferred_element_type=F32).T
+        for slot, (tap_x, member, _) in enumerate(chosen):
+            step_y = step % shares * width + member
+            rows = made[slot * 64 : slot * 64 + 64]
+            put_factor(mine, other, tap_x * 9 + step_y * 3 + side + 1, rows[:32] + rows[32:])
 
 
 def local_gradient(sides, slots, field, cotangent, occupancy, start, error, *more):
-    count = 3 * len(sides)
     faces = sides != (0,)
-
-    def at(step):
-        group = jnp.minimum(step, count - 1)
-        return (0, group // 2, group % 2 * 2, 0, 0) if faces else (0, group, 1, 0, 0)
-
-    taps = pl.BlockSpec((3, 1, 1, 256, 256), at)
+    width = FACES_WIDTH if faces else OWN_WIDTH
+    shares = 3 // width
+
+    def which(step):
+        return step // shares * 2 if faces else 1
+
     piece = whole(4, 28, 8, 128)
     face = whole(1, EDGE, 16, 256)
     in_specs = [
         pl.BlockSpec(memory_space=pltpu.SMEM),
         whole(2, 512, 256),
         whole(2, 512, 256),
-        whole(8, 128),
+        whole(2, 512),
         whole(32, 256),
-        taps,
+        pl.BlockSpec((3, width, 1, 256, 256), lambda step: (0, step % shares, which(step), 0, 0)),
     ]
     if faces:
         in_specs += [face, face, pl.BlockSpec(memory_space=pl.ANY), piece, piece]
+    depth = 256 if faces else 128
     return pl.pallas_call(
-        functools.partial(gradient_kernel, sides),
-        grid=(count + 1,),
+        functools.partial(gradient_kernel, sides, width),
+        grid=(len(sides) * shares,),
         in_specs=in_specs,
-        out_specs=[taps, piece, piece],
+        out_specs=[
+            pl.BlockSpec((1, 3, width, 256, 256), lambda step: (which(step), 0, step % shares, 0, 0)),
+            piece,
+            piece,
+        ],
         out_shape=[
             CORRECTED,
             jax.ShapeDtypeStruct((4, 28, 8, 128), F32),
@@ -238,15 +241,14 @@
         ],
         input_output_aliases={8: 0} if faces else {},
         scratch_shapes=[
-            pltpu.VMEM((count, 256, 1280), BF16),
+            pltpu.VMEM((width, 256, 1280), BF16),
+            pltpu.VMEM((2048, depth), BF16),
             pltpu.VMEM((1024, 256), BF16),
-            pltpu.VMEM((64, 256), BF16),
-            pltpu.VMEM((768, 256), BF16),
-            pltpu.VMEM((768, 256), BF16),
+            pltpu.VMEM((1024, 128), BF16),
         ],
         compiler_params=pltpu.CompilerParams(vmem_limit_bytes=GRAD_LIMIT),
         cost_estimate=pl.CostEstimate(
-            flops=count * 6 * 10**8, bytes_accessed=count * 15 * 10**5, transcendentals=0
+            flops=len(sides) * 2 * 10**9, bytes_accessed=len(sides) * 4 * 10**6, transcendentals=0
         ),
         name="gradient_with_faces" if faces else "gradient_own",
     )(slots, field, cotangent, occupancy, start, error, *more)
@@ -263,7 +265,7 @@
 
     @pl.when(step == 0)
     def _():
-        mask = occupancy[...].T.astype(BF16)
+        mask = voxel_mask(occupancy).astype(BF16)
         sources = [own_plane(cotangent, mask, plane) for plane in range(EDGE)]
         if side:
             sources = [with_faces(own, face, face, plane) for plane, own in enumerate(sources)]
@@ -286,20 +288,20 @@
         if not last:
             result[...] = total[...]
             return
-        mask = occupancy[...].T
+        mask = voxel_mask(occupancy)
         for plane in range(EDGE):
-            rows = total[plane * 128 : (plane + 1) * 128, :] * mask[:, plane : plane + 1]
             for brick in (0, 1):
-                result[brick, plane * PLANE : (plane + 1) * PLANE, :] = rows[
-                    brick * PLANE : (brick + 1) * PLANE
-                ].astype(BF16)
+                first = (2 * plane + brick) * PLANE
+                rows = slice(plane * PLANE, (plane + 1) * PLANE)
+                kept = total[first : first + PLANE, :] * mask[rows, brick : brick + 1]
+                result[brick, rows, :] = kept.astype(BF16)
 
 
 def input_gradient(side, last, slots, cotangent, occupancy, weight, *more, tie=None):
     in_specs = [
         pl.BlockSpec(memory_space=pltpu.SMEM),
         whole(2, 512, 256),
-        whole(8, 128),
+        whole(2, 512),
         pl.BlockSpec((3, 1, 1, 256, 256), lambda step: (0, step, side + 1, 0, 0)),
     ]
     if side:
@@ -324,6 +326,11 @@
     )(slots, cotangent, occupancy, weight, *more)
 
 
+def taps_left(mine, other, step_x, step_y):
+    first = step_x * 9 + step_y * 3
+    return jnp.concatenate([get_factor(mine, other, first + k) for k in range(3)], axis=1)
+
+
 def right_kernel(mine, other, corrected, right):
     step = pl.program_id(0)
 
@@ -331,23 +338,27 @@
     def _():
         right[...] = jnp.zeros_like(right)
 
-    left = jnp.concatenate([get_factor(mine, other, step * 3 + tap) for tap in range(3)], axis=1)
-    left_high, left_low = split(left)
-    high, low = split(corrected[...].reshape(768, 256))
-    both = lax.dot_general(jnp.concatenate([left_high, left_low], axis=0), high, NN, preferred_element_type=F32)
-    rest = lax.dot_general(left_high, low, NN, preferred_element_type=F32)
-    right[...] += both[0:32] + both[32:64] + rest
-
-
-def blocks(*shape):
-    return pl.BlockSpec((3,) + shape, lambda step: (step, 0, 0))
+    total = jnp.zeros((32, 256), F32)
+    for step_y in range(3):
+        left_high, left_low = split(taps_left(mine, other, step, step_y))
+        high, low = split(corrected[:, 0, step_y].reshape(768, 256))
+        both = lax.dot_general(
+            jnp.concatenate([left_high, left_low], axis=0), high, NN, preferred_element_type=F32
+        )
+        total += both[0:32] + both[32:64]
+        total += lax.dot_general(left_high, low, NN, preferred_element_type=F32)
+    right[...] += total
+
+
+def along_x(*shape):
+    return pl.BlockSpec((3, 1, 3) + shape, lambda step: (0, step, 0, 0, 0))
 
 
 def right_product(mine, other, corrected):
     return pl.pallas_call(
         right_kernel,
-        grid=(9,),
-        in_specs=[whole(4, 28, 8, 128), whole(4, 28, 8, 128), blocks(256, 256)],
+        grid=(3,),
+        in_specs=[whole(4, 28, 8, 128), whole(4, 28, 8, 128), along_x(256, 256)],
         out_specs=whole(32, 256),
         out_shape=jax.ShapeDtypeStruct((32, 256), F32),
         compiler_params=pltpu.CompilerParams(vmem_limit_bytes=LATE_LIMIT),
@@ -426,19 +437,27 @@
         basis[64:96, :] = low
         basis[96:128, :] = jnp.zeros((32, 256), BF16)
 
-    high, low = split(jnp.concatenate([get_factor(mine, other, step * 3 + tap) for tap in range(3)], axis=1))
-    left = jnp.concatenate([high, low, high, jnp.zeros((32, 768), BF16)], axis=0)
-    product = lax.dot_general(left, basis[...], TN, preferred_element_type=F32)
-    new_error[...] = (corrected[...] - product.reshape(3, 256, 256)).astype(BF16)
+    for step_y in range(3):
+        high, low = split(taps_left(mine, other, step, step_y))
+        left = jnp.concatenate([high, low, high, jnp.zeros((32, 768), BF16)], axis=0)
+        product = lax.dot_general(left, basis[...], TN, preferred_element_type=F32)
+        rest = corrected[:, 0, step_y] - product.reshape(3, 256, 256)
+        new_error[0, step_y] = rest.astype(BF16)
 
 
 def remaining_error(mine, other, corrected, right, inverse):
     return pl.pallas_call(
         error_kernel,
-        grid=(9,),
-        in_specs=[whole(4, 28, 8, 128), whole(4, 28, 8, 128), blocks(256, 256), whole(32, 256), whole(32, 32)],
-        out_specs=[blocks(256, 256), whole(32, 256)],
-        out_shape=[jax.ShapeDtypeStruct((27, 256, 256), BF16), jax.ShapeDtypeStruct((32, 256), F32)],
+        grid=(3,),
+        in_specs=[
+            whole(4, 28, 8, 128),
+            whole(4, 28, 8, 128),
+            along_x(256, 256),
+            whole(32, 256),
+            whole(32, 32),
+        ],
+        out_specs=[pl.BlockSpec((1, 3, 3, 256, 256), lambda step: (step, 0, 0, 0, 0)), whole(32, 256)],
+        out_shape=[jax.ShapeDtypeStruct((3, 3, 3, 256, 256), BF16), jax.ShapeDtypeStruct((32, 256), F32)],
         scratch_shapes=[pltpu.VMEM((128, 256), BF16)],
         compiler_params=pltpu.CompilerParams(vmem_limit_bytes=LATE_LIMIT),
         name="remaining_error",
@@ -447,6 +466,8 @@
 
 CORRECTED = pltpu.VMEM((3, 3, 3, 256, 256), F32)
 GRAD_LIMIT = 32 * MIB
+OWN_WIDTH = 3
+FACES_WIDTH = 3
 INPUT_LIMIT = 24 * MIB
 LATE_LIMIT = 24 * MIB
 SMALL = pltpu.CompilerParams(vmem_limit_bytes=12 * MIB)
@@ -492,34 +513,33 @@
 
 ALONG_X = [dict(x=1), dict(x=2), dict(x=3)]
 ALONG_Y = [dict(y=1), dict(y=2), dict(y=3)]
-ALONG_Z = [dict(z=2), dict(z=4), dict(z=6)]
-CORE_AND_Z = [dict(core=1), dict(z=1), dict(core=1, z=1)]
+ALONG_Z = [dict(z=1), dict(z=2), dict(z=3)]
+CORE_AND_Z = [dict(core=1), dict(z=6), dict(core=1, z=6)]
 
 
 def body(inputs, cotangent, occupancy, neighbours, weight, error_in, q_start):
-    field, gradient, occupied, slots = inputs[0], cotangent[0], occupancy[0], neighbours[0]
-    mask = occupied.reshape(2, EDGE, PLANE).transpose(1, 0, 2).reshape(EDGE, 2 * PLANE).astype(F32)
+    field, gradient = inputs[0], cotangent[0]
+    occupied, slots = in_hbm(occupancy[0]), in_hbm(neighbours[0])
     weight = weight.reshape(3, 3, 3, 256, 256)
-    up, down = brick_faces(field, gradient, mask)
+    up, down = brick_faces(field, gradient, occupied)
     lower, upper = shifted(up, 1), shifted(down, -1)
-    fixed = (slots, in_hbm(field), in_hbm(gradient), mask, q_start.T, in_hbm(error_in.reshape(3, 3, 3, 256, 256)))
+    fixed = (slots, in_hbm(field), in_hbm(gradient), occupied, in_hbm(q_start.T), in_hbm(error_in.reshape(3, 3, 3, 256, 256)))
     corrected, mine, other = local_gradient((0,), *fixed)
     corrected, mine, other = local_gradient((-1, 1), *fixed, lower, upper, in_vmem(corrected), mine, other)
-    corrected = corrected.reshape(27, 256, 256)
 
     part = mine + swapped(other, core=1)
     arrived = [swapped(part[k], x=k) for k in (1, 2, 3)]
-    total = input_gradient(0, False, slots, gradient, mask, weight, tie=part)
+    total = input_gradient(0, False, slots, gradient, occupied, weight, tie=part)
     part, total = lax.optimization_barrier((added([part[0]] + arrived), total))
     part = part.reshape(4, 7, 8, 128)
     part = added([part[0]] + [swapped(part[k], y=k) for k in (1, 2, 3)])
     arrived = [swapped(part, **bits) for bits in ALONG_Z]
-    total = input_gradient(-1, False, slots, gradient, mask, weight, upper, total, tie=part)
+    total = input_gradient(-1, False, slots, gradient, occupied, weight, upper, total, tie=part)
     part, total = lax.optimization_barrier((added([part] + arrived), total))
-    part = part + swapped(part, z=1)
+    part = part + swapped(part, z=6)
     part = jnp.concatenate([part] + [swapped(part, **bits) for bits in ALONG_Y], axis=0)
     arrived = [swapped(part, **bits) for bits in ALONG_X]
-    input_grad = input_gradient(1, True, slots, gradient, mask, weight, lower, total, tie=part)
+    input_grad = input_gradient(1, True, slots, gradient, occupied, weight, lower, total, tie=part)
     mine, input_grad = lax.optimization_barrier((jnp.stack([part] + arrived, axis=0), input_grad))
     other = swapped(mine, core=1)
 

time: 124 us -> 117 us (0.944)
  Pallas kernels: 40.9 us -> 36.4 us
  starting transfers between devices: 52.8 us -> 50.3 us
  waiting for transfers between devices: 26.7 us -> 28.8 us
  local copies, waits for them, and re-layouts: 1.65 us -> 0.04 us
    pallas_call x4, Pallas kernels: 23.8 us -> 18.8 us  [the longest x2 12.9 us: local_gradient(): pl.pallas_call(functools.partial(gradient_kernel, sides, width), grid=(le...]
    ppermute x30, starting transfers between devices: 47.3 us -> 44.8 us  [swapped(): return lax.ppermute(value, ('dp', 'space'), partners(**bits))]
    ppermute x2, waiting for transfers between devices: 0.01 us -> 2.33 us  [shifted(): lax.ppermute(value, 'space', [(i, i + by) for i in range(devices) if 0 <=...]
    unnamed x8 -> x4, local copies, waits for them, and re-layouts: 1.44 us -> 0.01 us
  transfers between devices with their start and end apart: 32 -> 32, of which waited for: 16 -> 19; matrix products, arithmetic and copies ran while one was open for 0% -> 0% of each run, Pallas kernels for 17% -> 18%
where the time goes in v3:
time: 117 us
  starting transfers between devices  50.3 us (43%)
  Pallas kernels  36.4 us (31%)
  waiting for transfers between devices  28.8 us (25%)
    ppermute x30, starting transfers between devices, swapped(): return lax.ppermute(value, ('dp', 'space'), partners(**bits))  44.8 us
    ppermute x30, waiting for transfers between devices, swapped(): return lax.ppermute(value, ('dp', 'space'), partners(**bits))  26.4 us
    pallas_call x2, Pallas kernels, local_gradient(): pl.pallas_call(functools.partial(gradient_kernel, sides, width), grid=(le...  12.9 us
    pallas_call x3, Pallas kernels, input_gradient(): pl.pallas_call(functools.partial(input_kernel, side, last), grid=(3,), in...  12.2 us
    ppermute x2, starting transfers between devices, shifted(): lax.ppermute(value, 'space', [(i, i + by) for i in range(devices) if 0 <=...  5.5 us
    pallas_call x1, Pallas kernels, remaining_error(): pl.pallas_call(error_kernel, grid=(3,), in_specs=[whole(4, 28, 8, 128), w...  3.81 us
    pallas_call x1, Pallas kernels, half_inverse(): pl.pallas_call(first_half_kernel, out_shape=[SQUARE, SQUARE], compiler_pa...  2.36 us
  transfers between devices with their start and end apart: 32, of which 19 were waited for; matrix products, arithmetic and copies ran while one was open for 0% of the time, Pallas kernels for 18%

profile of v3, /device:TPU:8, one launch (start us, length us, event | category | flops | bytes accessed | tf_op | source)
XLA Modules:
  0.0 116.5 jit_solution(3936294486339912808)
XLA Ops:
  0.6 1.6 %brick_faces.1 = (bf16[2,8,16,256]{3,2,1,0:T(8,128)(2,1)S(1)}, bf16[2,8,16,256]{3,2,1,0:T(8,128)(2,1)S(1)}) custom-call(bf16[2,512,256]{2,1,0:T(8,128)(2,1)} %bitcast.36, bf16[2,512,256]{2,1,0:T(8,128)(2,1)} %bitcast.27, s32[2,512]{1,0:T(2,128)} %bitcast.42), custom_call_target="tpu_custom_call" | custom-call | tf_op jit(solution)/shard_map/brick_faces/pallas_call | solution.py:123
  2.3 4.2 %collective-permute-start = (bf16[2,8,16,256]{3,2,1,0:T(8,128)(2,1)S(1)}, bf16[2,8,16,256]{3,2,1,0:T(8,128)(2,1)S(1)}, u32[]{:S(2)}, u32[]{:S(2)}) collective-permute-start(bf16[2,8,16,256]{3,2,1,0:T(8,128)(2,1)S(1)} %get-tuple-element.26), channel_id=1, source_target_pairs={{0,1},{1,2},{2,3},{3,4},{4,5},{5,6},{6,7},{7,8},{8,9},{9,10},{10,1... | collective-permute-start | bytes 393224 | tf_op jit(solution)/shard_map/ppermute | solution.py:486
  7.8 4.7 %gradient_own.1 = (f32[3,3,3,256,256]{4,3,2,1,0:T(8,128)S(1)}, f32[4,28,8,128]{3,2,1,0:T(8,128)S(1)}, f32[4,28,8,128]{3,2,1,0:T(8,128)S(1)}) custom-call(s32[2,27]{1,0:T(2,128)} %bitcast.54, bf16[2,512,256]{2,1,0:T(8,128)(2,1)} %bitcast.37, bf16[2,512,256]{2,1,0:T(8,128)(2,1)} %bitcast.28, s32[2,512]{1,0:T(2,128)} %bitcast.43, f32[32,256]{1,0:T(8,128)} %bitcast.51, ...), custom_call_target="tpu_custom_call" | custom-call | flops 2000000000 | bytes 4000000 | tf_op jit(solution)/shard_map/gradient_own/pallas_call | solution.py:228
  12.5 2.3 %collective-permute-done.1.refs_7_.refs_4_ = bf16[2,8,16,256]{3,2,1,0:T(8,128)(2,1)S(1)} collective-permute-done((bf16[2,8,16,256]{3,2,1,0:T(8,128)(2,1)S(1)}, bf16[2,8,16,256]{3,2,1,0:T(8,128)(2,1)S(1)}, u32[]{:S(2)}, u32[]{:S(2)}) %collective-permute-start.1) | collective-permute-done | bytes 131104 | tf_op jit(solution)/shard_map/ppermute | solution.py:486
  14.9 8.2 %gradient_with_faces.1 = (f32[3,3,3,256,256]{4,3,2,1,0:T(8,128)S(1)}, f32[4,28,8,128]{3,2,1,0:T(8,128)S(1)}, f32[4,28,8,128]{3,2,1,0:T(8,128)S(1)}) custom-call(s32[2,27]{1,0:T(2,128)} %bitcast.55, bf16[2,512,256]{2,1,0:T(8,128)(2,1)} %bitcast.38, bf16[2,512,256]{2,1,0:T(8,128)(2,1)} %bitcast.29, ...), custom_call_target="tpu_custom_call", output_to_operand_aliasing={{0}: (8, {})} | custom-call | flops 4000000000 | bytes 8000000 | tf_op jit(solution)/shard_map/gradient_with_faces/pallas_call | solution.py:228
  23.2 1.8 %collective-permute-done.2 = f32[4,28,8,128]{3,2,1,0:T(8,128)S(1)} collective-permute-done((f32[4,28,8,128]{3,2,1,0:T(8,128)S(1)}, f32[4,28,8,128]{3,2,1,0:T(8,128)S(1)}, u32[]{:S(2)}, u32[]{:S(2)}) %collective-permute-start.2) | collective-permute-done | bytes 458784 | tf_op jit(solution)/shard_map/ppermute | solution.py:503
  25.0 6.8 %collective-permute-start.5 = (f32[28,8,128]{2,1,0:T(8,128)S(1)}, f32[28,8,128]{2,1,0:T(8,128)S(1)}, u32[]{:S(2)}, u32[]{:S(2)}) collective-permute-start(f32[28,8,128]{2,1,0:T(8,128)S(1)} %get-tuple-element.49), channel_id=1, source_target_pairs={{0,48},{2,50},{4,52},{6,54},{8,56},{10,58},{12,60},{14,62},{128,17... | collective-permute-start | bytes 344072 | tf_op jit(solution)/shard_map/ppermute | solution.py:503
  32.8 3.6 %input_own.1.refs_5_ = f32[1024,256]{1,0:T(8,128)S(1)} custom-call(s32[2,27]{1,0:T(2,128)} %bitcast.56, bf16[2,512,256]{2,1,0:T(8,128)(2,1)S(1)} %bitcast.30, s32[2,512]{1,0:T(2,128)} %bitcast.45, bf16[3,3,3,256,256]{4,3,2,1,0:T(8,128)(2,1)S(1)} %bitcast.33, f32[4,28,8,128]{3,2,1,0:T(8,128)S(1)} %add.69.refs_4_), custom_call_target="tpu_custom_call" | custom-call | flops 2000000000 | bytes 4000000 | tf_op jit(solution)/shard_map/input_own/pallas_call | solution.py:316
  37.0 2.3 %collective-permute-done.4 = f32[28,8,128]{2,1,0:T(8,128)S(1)} collective-permute-done((f32[28,8,128]{2,1,0:T(8,128)S(1)}, f32[28,8,128]{2,1,0:T(8,128)S(1)}, u32[]{:S(2)}, u32[]{:S(2)}) %collective-permute-start.4) | collective-permute-done | bytes 114720 | tf_op jit(solution)/shard_map/ppermute | solution.py:503
  39.4 1.4 %collective-permute-start.6 = (f32[7,8,128]{2,1,0:T(8,128)S(1)}, f32[7,8,128]{2,1,0:T(8,128)S(1)}, u32[]{:S(2)}, u32[]{:S(2)}) collective-permute-start(f32[7,8,128]{2,1,0:T(8,128)S(1)} %get-tuple-element.54), channel_id=1, source_target_pairs={{0,128},{2,130},{4,132},{6,134},{8,136},{10,138},{12,140},{14,142}... | collective-permute-start | bytes 86024 | tf_op jit(solution)/shard_map/ppermute | solution.py:503
  40.8 2.8 %collective-permute-start.7 = (f32[7,8,128]{2,1,0:T(8,128)S(1)}, f32[7,8,128]{2,1,0:T(8,128)S(1)}, u32[]{:S(2)}, u32[]{:S(2)}) collective-permute-start(f32[7,8,128]{2,1,0:T(8,128)S(1)} %get-tuple-element.56), channel_id=1, source_target_pairs={{0,1},{2,3},{4,5},{6,7},{8,9},{10,11},{12,13},{14,15},{128,129},{1... | collective-permute-start | bytes 86024 | tf_op jit(solution)/shard_map/ppermute | solution.py:503
  44.7 1.5 %collective-permute-done.7 = f32[7,8,128]{2,1,0:T(8,128)S(1)} collective-permute-done((f32[7,8,128]{2,1,0:T(8,128)S(1)}, f32[7,8,128]{2,1,0:T(8,128)S(1)}, u32[]{:S(2)}, u32[]{:S(2)}) %collective-permute-start.7) | collective-permute-done | bytes 28704 | tf_op jit(solution)/shard_map/ppermute | solution.py:503
  46.2 5.9 %collective-permute-start.11 = (f32[7,8,128]{2,1,0:T(8,128)S(1)}, f32[7,8,128]{2,1,0:T(8,128)S(1)}, u32[]{:S(2)}, u32[]{:S(2)}) collective-permute-start(f32[7,8,128]{2,1,0:T(8,128)S(1)} %add_add_fusion.5.refs_6_), channel_id=1, source_target_pairs={{0,6},{2,4},{4,2},{6,0},{8,14},{10,12},{12,10},{14,8},{128,134},{1... | collective-permute-start | bytes 86024 | tf_op jit(solution)/shard_map/ppermute | solution.py:503
  52.8 3.8 %input_below.1.refs_5_ = f32[1024,256]{1,0:T(8,128)S(1)} custom-call(s32[2,27]{1,0:T(2,128)} %bitcast.57, bf16[2,512,256]{2,1,0:T(8,128)(2,1)S(1)} %bitcast.31, s32[2,512]{1,0:T(2,128)} %bitcast.46, bf16[3,3,3,256,256]{4,3,2,1,0:T(8,128)(2,1)S(1)} %bitcast.34, bf16[2,8,16,256]{3,2,1,0:T(8,128)(2,1)S(1)} %collective-permute-done.1.refs_7_.refs_4_, ...), custom_call_target="tpu_custom_call" | custom-call | flops 2000000000 | bytes 4000000 | tf_op jit(solution)/shard_map/input_below/pallas_call | solution.py:316
  57.9 5.1 %collective-permute-done.12 = f32[7,8,128]{2,1,0:T(8,128)S(1)} collective-permute-done((f32[7,8,128]{2,1,0:T(8,128)S(1)}, f32[7,8,128]{2,1,0:T(8,128)S(1)}, u32[]{:S(2)}, u32[]{:S(2)}) %collective-permute-start.12) | collective-permute-done | bytes 28704 | tf_op jit(solution)/shard_map/ppermute | solution.py:503
  63.0 2.7 %collective-permute-start.14 = (f32[7,8,128]{2,1,0:T(8,128)S(1)}, f32[7,8,128]{2,1,0:T(8,128)S(1)}, u32[]{:S(2)}, u32[]{:S(2)}) collective-permute-start(f32[7,8,128]{2,1,0:T(8,128)S(1)} %add.79), channel_id=1, source_target_pairs={{0,1},{2,3},{4,5},{6,7},{8,9},{10,11},{12,13},{14,15},{128,129},{1... | collective-permute-start | bytes 86024 | tf_op jit(solution)/shard_map/ppermute | solution.py:503
  67.1 1.4 %collective-permute-done.14 = f32[7,8,128]{2,1,0:T(8,128)S(1)} collective-permute-done((f32[7,8,128]{2,1,0:T(8,128)S(1)}, f32[7,8,128]{2,1,0:T(8,128)S(1)}, u32[]{:S(2)}, u32[]{:S(2)}) %collective-permute-start.14) | collective-permute-done | bytes 28704 | tf_op jit(solution)/shard_map/ppermute | solution.py:503
  69.7 2.0 %collective-permute-start.18 = (f32[28,8,128]{2,1,0:T(8,128)S(1)}, f32[28,8,128]{2,1,0:T(8,128)S(1)}, u32[]{:S(2)}, u32[]{:S(2)}) collective-permute-start(f32[28,8,128]{2,1,0:T(8,128)S(1)} %get-tuple-element.53.refs_6_), channel_id=1, source_target_pairs={{0,48},{2,50},{4,52},{6,54},{8,56},{10,58},{12,60},{14,62},{128,17... | collective-permute-start | bytes 344072 | tf_op jit(solution)/shard_map/ppermute | solution.py:503
  73.8 4.8 %input_above.1 = bf16[2,512,256]{2,1,0:T(8,128)(2,1)} custom-call(s32[2,27]{1,0:T(2,128)} %bitcast.58, bf16[2,512,256]{2,1,0:T(8,128)(2,1)S(1)} %bitcast.32, s32[2,512]{1,0:T(2,128)} %bitcast.47, bf16[3,3,3,256,256]{4,3,2,1,0:T(8,128)(2,1)S(1)} %bitcast.35, bf16[2,8,16,256]{3,2,1,0:T(8,128)(2,1)S(1)} %collective-permute-done.refs_6_.refs_4_, ...), custom_call_target="tpu_custom_call" | custom-call | flops 2000000000 | bytes 4000000 | tf_op jit(solution)/shard_map/input_above/pallas_call | solution.py:316
  78.8 1.8 %collective-permute-done.19.other = f32[4,28,8,128]{3,2,1,0:T(8,128)S(1)} collective-permute-done((f32[4,28,8,128]{3,2,1,0:T(8,128)S(1)}, f32[4,28,8,128]{3,2,1,0:T(8,128)S(1)}, u32[]{:S(2)}, u32[]{:S(2)}) %collective-permute-start.19) | collective-permute-done | bytes 458784 | tf_op jit(solution)/shard_map/ppermute | solution.py:503
  80.6 2.1 %right_product.1 = f32[32,256]{1,0:T(8,128)S(1)} custom-call(f32[4,28,8,128]{3,2,1,0:T(8,128)S(1)} %pad_maximum_fusion.mine, f32[4,28,8,128]{3,2,1,0:T(8,128)S(1)} %collective-permute-done.19.other, f32[3,3,3,256,256]{4,3,2,1,0:T(8,128)S(1)} %get-tuple-element.39.corrected), custom_call_target="tpu_custom_call" | custom-call | tf_op jit(solution)/shard_map/right_product/pallas_call | solution.py:358
  83.9 2.8 %collective-permute-start.21 = (f32[32,256]{1,0:T(8,128)S(1)}, f32[32,256]{1,0:T(8,128)S(1)}, u32[]{:S(2)}, u32[]{:S(2)}) collective-permute-start(f32[32,256]{1,0:T(8,128)S(1)} %right_product.1), channel_id=1, source_target_pairs={{0,12},{2,14},{4,8},{6,10},{8,4},{10,6},{12,0},{14,2},{128,140},{1... | collective-permute-start | bytes 98312 | tf_op jit(solution)/shard_map/ppermute | solution.py:503
  86.7 2.4 %half_inverse.1 = (f32[32,32]{1,0:T(8,128)S(1)}, f32[32,32]{1,0:T(8,128)S(1)}) custom-call(f32[4,28,8,128]{3,2,1,0:T(8,128)S(1)} %pad_maximum_fusion.mine, f32[4,28,8,128]{3,2,1,0:T(8,128)S(1)} %collective-permute-done.19.other), custom_call_target="tpu_custom_call" | custom-call | tf_op jit(solution)/shard_map/half_inverse/pallas_call | solution.py:401
  89.9 1.6 %collective-permute-start.25 = (f32[32,256]{1,0:T(8,128)S(1)}, f32[32,256]{1,0:T(8,128)S(1)}, u32[]{:S(2)}, u32[]{:S(2)}) collective-permute-start(f32[32,256]{1,0:T(8,128)S(1)} %add_add_fusion.3.refs_0_), channel_id=1, source_target_pairs={{0,48},{2,50},{4,52},{6,54},{8,56},{10,58},{12,60},{14,62},{128,17... | collective-permute-start | bytes 98312 | tf_op jit(solution)/shard_map/ppermute | solution.py:503
  91.5 2.1 %collective-permute-start.24 = (f32[32,256]{1,0:T(8,128)S(1)}, f32[32,256]{1,0:T(8,128)S(1)}, u32[]{:S(2)}, u32[]{:S(2)}) collective-permute-start(f32[32,256]{1,0:T(8,128)S(1)} %add_add_fusion.3.refs_0_), channel_id=1, source_target_pairs={{0,32},{2,34},{4,36},{6,38},{8,40},{10,42},{12,44},{14,46},{128,16... | collective-permute-start | bytes 98312 | tf_op jit(solution)/shard_map/ppermute | solution.py:503
  94.1 1.4 %whole_inverse.1.inverse = f32[32,32]{1,0:T(8,128)S(1)} custom-call(f32[32,32]{1,0:T(8,128)S(1)} %get-tuple-element.43.work, f32[32,32]{1,0:T(8,128)S(1)} %get-tuple-element.44.made, f32[32,256]{1,0:T(8,128)S(1)} %add_add_fusion.3.refs_0_), custom_call_target="tpu_custom_call" | custom-call | tf_op jit(solution)/shard_map/whole_inverse/pallas_call | solution.py:412
  95.6 1.4 %collective-permute-done.24 = f32[32,256]{1,0:T(8,128)S(1)} collective-permute-done((f32[32,256]{1,0:T(8,128)S(1)}, f32[32,256]{1,0:T(8,128)S(1)}, u32[]{:S(2)}, u32[]{:S(2)}) %collective-permute-start.24) | collective-permute-done | bytes 32800 | tf_op jit(solution)/shard_map/ppermute | solution.py:503
  98.9 2.1 %collective-permute-start.27 = (f32[32,256]{1,0:T(8,128)S(1)}, f32[32,256]{1,0:T(8,128)S(1)}, u32[]{:S(2)}, u32[]{:S(2)}) collective-permute-start(f32[32,256]{1,0:T(8,128)S(1)} %add_add_fusion.2), channel_id=1, source_target_pairs={{0,1},{2,3},{4,5},{6,7},{8,9},{10,11},{12,13},{14,15},{128,129},{1... | collective-permute-start | bytes 98312 | tf_op jit(solution)/shard_map/ppermute | solution.py:503
  101.8 2.5 %collective-permute-done.27 = f32[32,256]{1,0:T(8,128)S(1)} collective-permute-done((f32[32,256]{1,0:T(8,128)S(1)}, f32[32,256]{1,0:T(8,128)S(1)}, u32[]{:S(2)}, u32[]{:S(2)}) %collective-permute-start.27) | collective-permute-done | bytes 32800 | tf_op jit(solution)/shard_map/ppermute | solution.py:503
  104.9 2.8 %collective-permute-start.31 = (f32[32,256]{1,0:T(8,128)S(1)}, f32[32,256]{1,0:T(8,128)S(1)}, u32[]{:S(2)}, u32[]{:S(2)}) collective-permute-start(f32[32,256]{1,0:T(8,128)S(1)} %add_add_fusion.1), channel_id=1, source_target_pairs={{0,6},{2,4},{4,2},{6,0},{8,14},{10,12},{12,10},{14,8},{128,134},{1... | collective-permute-start | bytes 98312 | tf_op jit(solution)/shard_map/ppermute | solution.py:503
  110.7 1.9 %collective-permute-done.30 = f32[32,256]{1,0:T(8,128)S(1)} collective-permute-done((f32[32,256]{1,0:T(8,128)S(1)}, f32[32,256]{1,0:T(8,128)S(1)}, u32[]{:S(2)}, u32[]{:S(2)}) %collective-permute-start.30) | collective-permute-done | bytes 32800 | tf_op jit(solution)/shard_map/ppermute | solution.py:503
  112.7 3.8 %remaining_error.1 = (bf16[3,3,3,256,256]{4,3,2,1,0:T(8,128)(2,1)}, f32[32,256]{1,0:T(8,128)}) custom-call(f32[4,28,8,128]{3,2,1,0:T(8,128)S(1)} %pad_maximum_fusion.mine, f32[4,28,8,128]{3,2,1,0:T(8,128)S(1)} %collective-permute-done.19.other, f32[3,3,3,256,256]{4,3,2,1,0:T(8,128)S(1)} %get-tuple-element.39.corrected, f32[32,256]{1,0:T(8,128)S(1)} %add_add_fusion.right, ...), custom_call_target="tpu_custom_call" | custom-call | tf_op jit(solution)/shard_map/remaining_error/pallas_call | solution.py:449
  (59 shorter events, 19.9 us)
Async XLA Ops:
  2.3 10.2 %collective-permute-start = (bf16[2,8,16,256]{3,2,1,0:T(8,128)(2,1)S(1)}, bf16[2,8,16,256]{3,2,1,0:T(8,128)(2,1)S(1)}, u32[]{:S(2)}, u32[]{:S(2)}) collective-permute-start(bf16[2,8,16,256]{3,2,1,0:T(8,128)(2,1)S(1)} %get-tuple-element.26), channel_id=1, source_target_pairs={{0,1},{1,2},{2,3},{3,4},{4,5},{5,6},{6,7},{7,8},{8,9},{9,10},{10,1... | collective-permute-start | bytes 393224 | tf_op jit(solution)/shard_map/ppermute | solution.py:486
  6.5 8.4 %collective-permute-start.1 = (bf16[2,8,16,256]{3,2,1,0:T(8,128)(2,1)S(1)}, bf16[2,8,16,256]{3,2,1,0:T(8,128)(2,1)S(1)}, u32[]{:S(2)}, u32[]{:S(2)}) collective-permute-start(bf16[2,8,16,256]{3,2,1,0:T(8,128)(2,1)S(1)} %get-tuple-element.27), channel_id=1, source_target_pairs={{1,0},{2,1},{3,2},{4,3},{5,4},{6,5},{7,6},{8,7},{9,8},{10,9},{11,1... | collective-permute-start | bytes 393224 | tf_op jit(solution)/shard_map/ppermute | solution.py:486
  23.1 1.9 %collective-permute-start.2 = (f32[4,28,8,128]{3,2,1,0:T(8,128)S(1)}, f32[4,28,8,128]{3,2,1,0:T(8,128)S(1)}, u32[]{:S(2)}, u32[]{:S(2)}) collective-permute-start(f32[4,28,8,128]{3,2,1,0:T(8,128)S(1)} %get-tuple-element.32), channel_id=1, source_target_pairs={{0,64},{2,66},{4,68},{6,70},{8,72},{10,74},{12,76},{14,78},{128,19... | collective-permute-start | bytes 1376264 | tf_op jit(solution)/shard_map/ppermute | solution.py:503
  25.0 12.0 %collective-permute-start.5 = (f32[28,8,128]{2,1,0:T(8,128)S(1)}, f32[28,8,128]{2,1,0:T(8,128)S(1)}, u32[]{:S(2)}, u32[]{:S(2)}) collective-permute-start(f32[28,8,128]{2,1,0:T(8,128)S(1)} %get-tuple-element.49), channel_id=1, source_target_pairs={{0,48},{2,50},{4,52},{6,54},{8,56},{10,58},{12,60},{14,62},{128,17... | collective-permute-start | bytes 344072 | tf_op jit(solution)/shard_map/ppermute | solution.py:503
  31.8 7.5 %collective-permute-start.4 = (f32[28,8,128]{2,1,0:T(8,128)S(1)}, f32[28,8,128]{2,1,0:T(8,128)S(1)}, u32[]{:S(2)}, u32[]{:S(2)}) collective-permute-start(f32[28,8,128]{2,1,0:T(8,128)S(1)} %get-tuple-element.50), channel_id=1, source_target_pairs={{0,32},{2,34},{4,36},{6,38},{8,40},{10,42},{12,44},{14,46},{128,16... | collective-permute-start | bytes 344072 | tf_op jit(solution)/shard_map/ppermute | solution.py:503
  32.3 7.0 %collective-permute-start.3 = (f32[28,8,128]{2,1,0:T(8,128)S(1)}, f32[28,8,128]{2,1,0:T(8,128)S(1)}, u32[]{:S(2)}, u32[]{:S(2)}) collective-permute-start(f32[28,8,128]{2,1,0:T(8,128)S(1)} %get-tuple-element.51), channel_id=1, source_target_pairs={{0,16},{2,18},{4,20},{6,22},{8,24},{10,26},{12,28},{14,30},{128,14... | collective-permute-start | bytes 344072 | tf_op jit(solution)/shard_map/ppermute | solution.py:503
  39.4 4.2 %collective-permute-start.6 = (f32[7,8,128]{2,1,0:T(8,128)S(1)}, f32[7,8,128]{2,1,0:T(8,128)S(1)}, u32[]{:S(2)}, u32[]{:S(2)}) collective-permute-start(f32[7,8,128]{2,1,0:T(8,128)S(1)} %get-tuple-element.54), channel_id=1, source_target_pairs={{0,128},{2,130},{4,132},{6,134},{8,136},{10,138},{12,140},{14,142}... | collective-permute-start | bytes 86024 | tf_op jit(solution)/shard_map/ppermute | solution.py:503
  40.8 3.9 %collective-permute-start.8 = (f32[7,8,128]{2,1,0:T(8,128)S(1)}, f32[7,8,128]{2,1,0:T(8,128)S(1)}, u32[]{:S(2)}, u32[]{:S(2)}) collective-permute-start(f32[7,8,128]{2,1,0:T(8,128)S(1)} %get-tuple-element.55), channel_id=1, source_target_pairs={{0,129},{2,131},{4,133},{6,135},{8,137},{10,139},{12,141},{14,143}... | collective-permute-start | bytes 86024 | tf_op jit(solution)/shard_map/ppermute | solution.py:503
  40.8 5.4 %collective-permute-start.7 = (f32[7,8,128]{2,1,0:T(8,128)S(1)}, f32[7,8,128]{2,1,0:T(8,128)S(1)}, u32[]{:S(2)}, u32[]{:S(2)}) collective-permute-start(f32[7,8,128]{2,1,0:T(8,128)S(1)} %get-tuple-element.56), channel_id=1, source_target_pairs={{0,1},{2,3},{4,5},{6,7},{8,9},{10,11},{12,13},{14,15},{128,129},{1... | collective-permute-start | bytes 86024 | tf_op jit(solution)/shard_map/ppermute | solution.py:503
  46.2 10.4 %collective-permute-start.11 = (f32[7,8,128]{2,1,0:T(8,128)S(1)}, f32[7,8,128]{2,1,0:T(8,128)S(1)}, u32[]{:S(2)}, u32[]{:S(2)}) collective-permute-start(f32[7,8,128]{2,1,0:T(8,128)S(1)} %add_add_fusion.5.refs_6_), channel_id=1, source_target_pairs={{0,6},{2,4},{4,2},{6,0},{8,14},{10,12},{12,10},{14,8},{128,134},{1... | collective-permute-start | bytes 86024 | tf_op jit(solution)/shard_map/ppermute | solution.py:503
  52.1 4.8 %collective-permute-start.10 = (f32[7,8,128]{2,1,0:T(8,128)S(1)}, f32[7,8,128]{2,1,0:T(8,128)S(1)}, u32[]{:S(2)}, u32[]{:S(2)}) collective-permute-start(f32[7,8,128]{2,1,0:T(8,128)S(1)} %add_add_fusion.5.refs_6_), channel_id=1, source_target_pairs={{0,4},{2,6},{4,0},{6,2},{8,12},{10,14},{12,8},{14,10},{128,132},{1... | collective-permute-start | bytes 86024 | tf_op jit(solution)/shard_map/ppermute | solution.py:503
  52.1 4.8 %collective-permute-start.9 = (f32[7,8,128]{2,1,0:T(8,128)S(1)}, f32[7,8,128]{2,1,0:T(8,128)S(1)}, u32[]{:S(2)}, u32[]{:S(2)}) collective-permute-start(f32[7,8,128]{2,1,0:T(8,128)S(1)} %add_add_fusion.5.refs_6_), channel_id=1, source_target_pairs={{0,2},{2,0},{4,6},{6,4},{8,10},{10,8},{12,14},{14,12},{128,130},{1... | collective-permute-start | bytes 86024 | tf_op jit(solution)/shard_map/ppermute | solution.py:503
  56.9 6.1 %collective-permute-start.12 = (f32[7,8,128]{2,1,0:T(8,128)S(1)}, f32[7,8,128]{2,1,0:T(8,128)S(1)}, u32[]{:S(2)}, u32[]{:S(2)}) collective-permute-start(f32[7,8,128]{2,1,0:T(8,128)S(1)} %add_add_fusion.4), channel_id=1, source_target_pairs={{0,12},{2,14},{4,8},{6,10},{8,4},{10,6},{12,0},{14,2},{128,140},{1... | collective-permute-start | bytes 86024 | tf_op jit(solution)/shard_map/ppermute | solution.py:503
  63.0 4.1 %collective-permute-start.15 = (f32[7,8,128]{2,1,0:T(8,128)S(1)}, f32[7,8,128]{2,1,0:T(8,128)S(1)}, u32[]{:S(2)}, u32[]{:S(2)}) collective-permute-start(f32[7,8,128]{2,1,0:T(8,128)S(1)} %add.79), channel_id=1, source_target_pairs={{0,129},{2,131},{4,133},{6,135},{8,137},{10,139},{12,141},{14,143}... | collective-permute-start | bytes 86024 | tf_op jit(solution)/shard_map/ppermute | solution.py:503
  63.0 5.5 %collective-permute-start.14 = (f32[7,8,128]{2,1,0:T(8,128)S(1)}, f32[7,8,128]{2,1,0:T(8,128)S(1)}, u32[]{:S(2)}, u32[]{:S(2)}) collective-permute-start(f32[7,8,128]{2,1,0:T(8,128)S(1)} %add.79), channel_id=1, source_target_pairs={{0,1},{2,3},{4,5},{6,7},{8,9},{10,11},{12,13},{14,15},{128,129},{1... | collective-permute-start | bytes 86024 | tf_op jit(solution)/shard_map/ppermute | solution.py:503
  65.8 3.9 %collective-permute-start.13 = (f32[7,8,128]{2,1,0:T(8,128)S(1)}, f32[7,8,128]{2,1,0:T(8,128)S(1)}, u32[]{:S(2)}, u32[]{:S(2)}) collective-permute-start(f32[7,8,128]{2,1,0:T(8,128)S(1)} %add.79), channel_id=1, source_target_pairs={{0,128},{2,130},{4,132},{6,134},{8,136},{10,138},{12,140},{14,142}... | collective-permute-start | bytes 86024 | tf_op jit(solution)/shard_map/ppermute | solution.py:503
  69.7 9.0 %collective-permute-start.18 = (f32[28,8,128]{2,1,0:T(8,128)S(1)}, f32[28,8,128]{2,1,0:T(8,128)S(1)}, u32[]{:S(2)}, u32[]{:S(2)}) collective-permute-start(f32[28,8,128]{2,1,0:T(8,128)S(1)} %get-tuple-element.53.refs_6_), channel_id=1, source_target_pairs={{0,48},{2,50},{4,52},{6,54},{8,56},{10,58},{12,60},{14,62},{128,17... | collective-permute-start | bytes 344072 | tf_op jit(solution)/shard_map/ppermute | solution.py:503
  71.6 7.0 %collective-permute-start.17 = (f32[28,8,128]{2,1,0:T(8,128)S(1)}, f32[28,8,128]{2,1,0:T(8,128)S(1)}, u32[]{:S(2)}, u32[]{:S(2)}) collective-permute-start(f32[28,8,128]{2,1,0:T(8,128)S(1)} %get-tuple-element.53.refs_6_), channel_id=1, source_target_pairs={{0,32},{2,34},{4,36},{6,38},{8,40},{10,42},{12,44},{14,46},{128,16... | collective-permute-start | bytes 344072 | tf_op jit(solution)/shard_map/ppermute | solution.py:503
  72.5 6.2 %collective-permute-start.16 = (f32[28,8,128]{2,1,0:T(8,128)S(1)}, f32[28,8,128]{2,1,0:T(8,128)S(1)}, u32[]{:S(2)}, u32[]{:S(2)}) collective-permute-start(f32[28,8,128]{2,1,0:T(8,128)S(1)} %get-tuple-element.53.refs_6_), channel_id=1, source_target_pairs={{0,16},{2,18},{4,20},{6,22},{8,24},{10,26},{12,28},{14,30},{128,14... | collective-permute-start | bytes 344072 | tf_op jit(solution)/shard_map/ppermute | solution.py:503
  78.7 1.9 %collective-permute-start.19 = (f32[4,28,8,128]{3,2,1,0:T(8,128)S(1)}, f32[4,28,8,128]{3,2,1,0:T(8,128)S(1)}, u32[]{:S(2)}, u32[]{:S(2)}) collective-permute-start(f32[4,28,8,128]{3,2,1,0:T(8,128)S(1)} %pad_maximum_fusion.mine), channel_id=1, source_target_pairs={{0,64},{2,66},{4,68},{6,70},{8,72},{10,74},{12,76},{14,78},{128,19... | collective-permute-start | bytes 1376264 | tf_op jit(solution)/shard_map/ppermute | solution.py:503
  82.7 6.4 %collective-permute-start.22 = (f32[32,256]{1,0:T(8,128)S(1)}, f32[32,256]{1,0:T(8,128)S(1)}, u32[]{:S(2)}, u32[]{:S(2)}) collective-permute-start(f32[32,256]{1,0:T(8,128)S(1)} %right_product.1), channel_id=1, source_target_pairs={{0,76},{2,78},{4,72},{6,74},{8,68},{10,70},{12,64},{14,66},{128,20... | collective-permute-start | bytes 98312 | tf_op jit(solution)/shard_map/ppermute | solution.py:503
  83.9 6.0 %collective-permute-start.21 = (f32[32,256]{1,0:T(8,128)S(1)}, f32[32,256]{1,0:T(8,128)S(1)}, u32[]{:S(2)}, u32[]{:S(2)}) collective-permute-start(f32[32,256]{1,0:T(8,128)S(1)} %right_product.1), channel_id=1, source_target_pairs={{0,12},{2,14},{4,8},{6,10},{8,4},{10,6},{12,0},{14,2},{128,140},{1... | collective-permute-start | bytes 98312 | tf_op jit(solution)/shard_map/ppermute | solution.py:503
  86.7 3.2 %collective-permute-start.20 = (f32[32,256]{1,0:T(8,128)S(1)}, f32[32,256]{1,0:T(8,128)S(1)}, u32[]{:S(2)}, u32[]{:S(2)}) collective-permute-start(f32[32,256]{1,0:T(8,128)S(1)} %right_product.1), channel_id=1, source_target_pairs={{0,64},{2,66},{4,68},{6,70},{8,72},{10,74},{12,76},{14,78},{128,19... | collective-permute-start | bytes 98312 | tf_op jit(solution)/shard_map/ppermute | solution.py:503
  89.9 5.6 %collective-permute-start.25 = (f32[32,256]{1,0:T(8,128)S(1)}, f32[32,256]{1,0:T(8,128)S(1)}, u32[]{:S(2)}, u32[]{:S(2)}) collective-permute-start(f32[32,256]{1,0:T(8,128)S(1)} %add_add_fusion.3.refs_0_), channel_id=1, source_target_pairs={{0,48},{2,50},{4,52},{6,54},{8,56},{10,58},{12,60},{14,62},{128,17... | collective-permute-start | bytes 98312 | tf_op jit(solution)/shard_map/ppermute | solution.py:503
  91.5 5.5 %collective-permute-start.24 = (f32[32,256]{1,0:T(8,128)S(1)}, f32[32,256]{1,0:T(8,128)S(1)}, u32[]{:S(2)}, u32[]{:S(2)}) collective-permute-start(f32[32,256]{1,0:T(8,128)S(1)} %add_add_fusion.3.refs_0_), channel_id=1, source_target_pairs={{0,32},{2,34},{4,36},{6,38},{8,40},{10,42},{12,44},{14,46},{128,16... | collective-permute-start | bytes 98312 | tf_op jit(solution)/shard_map/ppermute | solution.py:503
  93.7 3.9 %collective-permute-start.23 = (f32[32,256]{1,0:T(8,128)S(1)}, f32[32,256]{1,0:T(8,128)S(1)}, u32[]{:S(2)}, u32[]{:S(2)}) collective-permute-start(f32[32,256]{1,0:T(8,128)S(1)} %add_add_fusion.3.refs_0_), channel_id=1, source_target_pairs={{0,16},{2,18},{4,20},{6,22},{8,24},{10,26},{12,28},{14,30},{128,14... | collective-permute-start | bytes 98312 | tf_op jit(solution)/shard_map/ppermute | solution.py:503
  97.6 4.2 %collective-permute-start.28 = (f32[32,256]{1,0:T(8,128)S(1)}, f32[32,256]{1,0:T(8,128)S(1)}, u32[]{:S(2)}, u32[]{:S(2)}) collective-permute-start(f32[32,256]{1,0:T(8,128)S(1)} %add_add_fusion.2), channel_id=1, source_target_pairs={{0,129},{2,131},{4,133},{6,135},{8,137},{10,139},{12,141},{14,143}... | collective-permute-start | bytes 98312 | tf_op jit(solution)/shard_map/ppermute | solution.py:503
  98.9 5.4 %collective-permute-start.27 = (f32[32,256]{1,0:T(8,128)S(1)}, f32[32,256]{1,0:T(8,128)S(1)}, u32[]{:S(2)}, u32[]{:S(2)}) collective-permute-start(f32[32,256]{1,0:T(8,128)S(1)} %add_add_fusion.2), channel_id=1, source_target_pairs={{0,1},{2,3},{4,5},{6,7},{8,9},{10,11},{12,13},{14,15},{128,129},{1... | collective-permute-start | bytes 98312 | tf_op jit(solution)/shard_map/ppermute | solution.py:503
  101.0 3.9 %collective-permute-start.26 = (f32[32,256]{1,0:T(8,128)S(1)}, f32[32,256]{1,0:T(8,128)S(1)}, u32[]{:S(2)}, u32[]{:S(2)}) collective-permute-start(f32[32,256]{1,0:T(8,128)S(1)} %add_add_fusion.2), channel_id=1, source_target_pairs={{0,128},{2,130},{4,132},{6,134},{8,136},{10,138},{12,140},{14,142}... | collective-permute-start | bytes 98312 | tf_op jit(solution)/shard_map/ppermute | solution.py:503
  104.9 5.8 %collective-permute-start.31 = (f32[32,256]{1,0:T(8,128)S(1)}, f32[32,256]{1,0:T(8,128)S(1)}, u32[]{:S(2)}, u32[]{:S(2)}) collective-permute-start(f32[32,256]{1,0:T(8,128)S(1)} %add_add_fusion.1), channel_id=1, source_target_pairs={{0,6},{2,4},{4,2},{6,0},{8,14},{10,12},{12,10},{14,8},{128,134},{1... | collective-permute-start | bytes 98312 | tf_op jit(solution)/shard_map/ppermute | solution.py:503
  107.7 4.9 %collective-permute-start.30 = (f32[32,256]{1,0:T(8,128)S(1)}, f32[32,256]{1,0:T(8,128)S(1)}, u32[]{:S(2)}, u32[]{:S(2)}) collective-permute-start(f32[32,256]{1,0:T(8,128)S(1)} %add_add_fusion.1), channel_id=1, source_target_pairs={{0,4},{2,6},{4,0},{6,2},{8,12},{10,14},{12,8},{14,10},{128,132},{1... | collective-permute-start | bytes 98312 | tf_op jit(solution)/shard_map/ppermute | solution.py:503
  108.4 4.3 %collective-permute-start.29 = (f32[32,256]{1,0:T(8,128)S(1)}, f32[32,256]{1,0:T(8,128)S(1)}, u32[]{:S(2)}, u32[]{:S(2)}) collective-permute-start(f32[32,256]{1,0:T(8,128)S(1)} %add_add_fusion.1), channel_id=1, source_target_pairs={{0,2},{2,0},{4,6},{6,4},{8,10},{10,8},{12,14},{14,12},{128,130},{1... | collective-permute-start | bytes 98312 | tf_op jit(solution)/shard_map/ppermute | solution.py:503
  (2 other events, 35.8 us)

commit v4 on v3

--- a/solution.py
+++ b/solution.py
@@ -130,9 +130,10 @@
     slots, field, cotangent, occupancy, start, error = refs[:6]
     refs = refs[6:]
     if faces:
-        lower, upper, _, mine_before, other_before = refs[:5]
-        refs = refs[5:]
-    corrected, mine, other, views, sources, own, start_parts = refs
+        lower, upper, _, _, mine_before, other_before = refs[:6]
+        refs = refs[6:]
+    kept, sent, mine, other, views, sources, own, start_parts = refs
+    core = coordinates()[0]
     step = pl.program_id(0)
     depth = 256 if faces else 128
     shares = 3 // width
@@ -189,7 +190,9 @@
         columns = jnp.concatenate([views[member, :, k * 128 : k * 128 + 1024] for k in range(3)], axis=0)
         total = lax.dot_general(columns, own[...], NN, preferred_element_type=F32)
         total = total + error[:, member, 0].astype(F32).reshape(768, 256)
-        corrected[0, :, member] = total.reshape(3, 256, 256)
+        halves = total.reshape(3, 2, 128, 256)
+        kept[0, :, member] = jnp.where(core == 0, halves[:, 0], halves[:, 1])
+        sent[0, :, member] = jnp.where(core == 0, halves[:, 1], halves[:, 0])
         high, low = split(total)
         for tap_x in range(3):
             rows = slice(tap_x * 256, tap_x * 256 + 256)
@@ -214,6 +217,8 @@
 
     piece = whole(4, 28, 8, 128)
     face = whole(1, EDGE, 16, 256)
+    anywhere = pl.BlockSpec(memory_space=pl.ANY)
+    half = pl.BlockSpec((1, 3, width, 128, 256), lambda step: (which(step), 0, step % shares, 0, 0))
     in_specs = [
         pl.BlockSpec(memory_space=pltpu.SMEM),
         whole(2, 512, 256),
@@ -223,23 +228,20 @@
         pl.BlockSpec((3, width, 1, 256, 256), lambda step: (0, step % shares, which(step), 0, 0)),
     ]
     if faces:
-        in_specs += [face, face, pl.BlockSpec(memory_space=pl.ANY), piece, piece]
+        in_specs += [face, face, anywhere, anywhere, piece, piece]
     depth = 256 if faces else 128
     return pl.pallas_call(
         functools.partial(gradient_kernel, sides, width),
         grid=(len(sides) * shares,),
         in_specs=in_specs,
-        out_specs=[
-            pl.BlockSpec((1, 3, width, 256, 256), lambda step: (which(step), 0, step % shares, 0, 0)),
-            piece,
-            piece,
-        ],
+        out_specs=[half, half, piece, piece],
         out_shape=[
-            CORRECTED,
+            HALF,
+            HALF,
             jax.ShapeDtypeStruct((4, 28, 8, 128), F32),
             jax.ShapeDtypeStruct((4, 28, 8, 128), F32),
         ],
-        input_output_aliases={8: 0} if faces else {},
+        input_output_aliases={8: 0, 9: 1} if faces else {},
         scratch_shapes=[
             pltpu.VMEM((width, 256, 1280), BF16),
             pltpu.VMEM((2048, depth), BF16),
@@ -331,8 +333,9 @@
     return jnp.concatenate([get_factor(mine, other, first + k) for k in range(3)], axis=1)
 
 
-def right_kernel(mine, other, corrected, right):
+def right_kernel(mine, kept, partner, right):
     step = pl.program_id(0)
+    _, x, y, _ = coordinates()
 
     @pl.when(step == 0)
     def _():
@@ -340,8 +343,12 @@
 
     total = jnp.zeros((32, 256), F32)
     for step_y in range(3):
-        left_high, left_low = split(taps_left(mine, other, step, step_y))
-        high, low = split(corrected[:, 0, step_y].reshape(768, 256))
+        columns = []
+        for step_z in range(3):
+            place = place_of(step * 9 + step_y * 3 + step_z, y)
+            columns.append(jnp.concatenate([mine[block ^ x, place] for block in range(4)], axis=0))
+        left_high, left_low = split(jnp.concatenate(columns, axis=1) * (1.0 / 256.0))
+        high, low = split((kept[:, 0, step_y] + partner[:, 0, step_y]).reshape(384, 256))
         both = lax.dot_general(
             jnp.concatenate([left_high, left_low], axis=0), high, NN, preferred_element_type=F32
         )
@@ -354,16 +361,16 @@
     return pl.BlockSpec((3, 1, 3) + shape, lambda step: (0, step, 0, 0, 0))
 
 
-def right_product(mine, other, corrected):
+def right_product(mine, kept, partner):
     return pl.pallas_call(
         right_kernel,
         grid=(3,),
-        in_specs=[whole(4, 28, 8, 128), whole(4, 28, 8, 128), along_x(256, 256)],
+        in_specs=[whole(4, 28, 8, 128), along_x(128, 256), along_x(128, 256)],
         out_specs=whole(32, 256),
         out_shape=jax.ShapeDtypeStruct((32, 256), F32),
         compiler_params=pltpu.CompilerParams(vmem_limit_bytes=LATE_LIMIT),
         name="right_product",
-    )(mine, other, in_vmem(corrected))
+    )(mine, in_vmem(kept), in_vmem(partner))
 
 
 def eliminate(first, work, made):
@@ -419,7 +426,7 @@
     )(work, made, *more)
 
 
-def error_kernel(mine, other, corrected, right, inverse, new_error, q_rows, basis):
+def error_kernel(mine, other, kept, sent, right, inverse, new_error, q_rows, basis):
     step = pl.program_id(0)
 
     @pl.when(step == 0)
@@ -437,22 +444,28 @@
         basis[64:96, :] = low
         basis[96:128, :] = jnp.zeros((32, 256), BF16)
 
+    core = coordinates()[0]
     for step_y in range(3):
         high, low = split(taps_left(mine, other, step, step_y))
         left = jnp.concatenate([high, low, high, jnp.zeros((32, 768), BF16)], axis=0)
         product = lax.dot_general(left, basis[...], TN, preferred_element_type=F32)
-        rest = corrected[:, 0, step_y] - product.reshape(3, 256, 256)
-        new_error[0, step_y] = rest.astype(BF16)
-
-
-def remaining_error(mine, other, corrected, right, inverse):
+        product = product.reshape(3, 2, 128, 256)
+        own, rest = kept[:, 0, step_y], sent[:, 0, step_y]
+        halves = jnp.where(core == 0, own, rest), jnp.where(core == 0, rest, own)
+        for half in (0, 1):
+            rows = slice(half * 128, half * 128 + 128)
+            new_error[0, step_y, :, rows, :] = (halves[half] - product[:, half]).astype(BF16)
+
+
+def remaining_error(mine, other, kept, sent, right, inverse):
     return pl.pallas_call(
         error_kernel,
         grid=(3,),
         in_specs=[
             whole(4, 28, 8, 128),
             whole(4, 28, 8, 128),
-            along_x(256, 256),
+            along_x(128, 256),
+            along_x(128, 256),
             whole(32, 256),
             whole(32, 32),
         ],
@@ -461,10 +474,10 @@
         scratch_shapes=[pltpu.VMEM((128, 256), BF16)],
         compiler_params=pltpu.CompilerParams(vmem_limit_bytes=LATE_LIMIT),
         name="remaining_error",
-    )(mine, other, in_vmem(corrected), right, inverse)
-
-
-CORRECTED = pltpu.VMEM((3, 3, 3, 256, 256), F32)
+    )(mine, other, in_vmem(kept), in_vmem(sent), right, inverse)
+
+
+HALF = pltpu.VMEM((3, 3, 3, 128, 256), F32)
 GRAD_LIMIT = 32 * MIB
 OWN_WIDTH = 3
 FACES_WIDTH = 3
@@ -524,34 +537,42 @@
     up, down = brick_faces(field, gradient, occupied)
     lower, upper = shifted(up, 1), shifted(down, -1)
     fixed = (slots, in_hbm(field), in_hbm(gradient), occupied, in_hbm(q_start.T), in_hbm(error_in.reshape(3, 3, 3, 256, 256)))
-    corrected, mine, other = local_gradient((0,), *fixed)
-    corrected, mine, other = local_gradient((-1, 1), *fixed, lower, upper, in_vmem(corrected), mine, other)
+    kept, sent, mine, other = local_gradient((0,), *fixed)
+    kept, sent, mine, other = local_gradient(
+        (-1, 1), *fixed, lower, upper, in_vmem(kept), in_vmem(sent), mine, other
+    )
 
     part = mine + swapped(other, core=1)
+    part, travelling = lax.optimization_barrier((part, sent))
     arrived = [swapped(part[k], x=k) for k in (1, 2, 3)]
+    partner = swapped(travelling, core=1)
     total = input_gradient(0, False, slots, gradient, occupied, weight, tie=part)
     part, total = lax.optimization_barrier((added([part[0]] + arrived), total))
     part = part.reshape(4, 7, 8, 128)
     part = added([part[0]] + [swapped(part[k], y=k) for k in (1, 2, 3)])
-    arrived = [swapped(part, **bits) for bits in ALONG_Z]
+    part = summed_among(part, ALONG_Z)
+    arrived = swapped(part, z=6)
     total = input_gradient(-1, False, slots, gradient, occupied, weight, upper, total, tie=part)
-    part, total = lax.optimization_barrier((added([part] + arrived), total))
-    part = part + swapped(part, z=6)
+    part, total = lax.optimization_barrier((part + arrived, total))
     part = jnp.concatenate([part] + [swapped(part, **bits) for bits in ALONG_Y], axis=0)
     arrived = [swapped(part, **bits) for bits in ALONG_X]
     input_grad = input_gradient(1, True, slots, gradient, occupied, weight, lower, total, tie=part)
-    mine, input_grad = lax.optimization_barrier((jnp.stack([part] + arrived, axis=0), input_grad))
+    mine, partner, input_grad = lax.optimization_barrier(
+        (jnp.stack([part] + arrived, axis=0), partner, input_grad)
+    )
+
+    right = right_product(mine, kept, partner)
+    right, mine = lax.optimization_barrier((summed_among(right, CORE_AND_Z), mine))
+    arrived = [swapped(right, **bits) for bits in ALONG_X]
     other = swapped(mine, core=1)
-
-    right = right_product(mine, other, corrected)
-    arrived = [swapped(right, **bits) for bits in CORE_AND_Z]
+    right, other = lax.optimization_barrier((added([right] + arrived), other))
+    arrived = [swapped(right, **bits) for bits in ALONG_Y]
     halves = half_inverse(mine, other)
     right, *halves = lax.optimization_barrier((added([right] + arrived), *halves))
-    arrived = [swapped(right, **bits) for bits in ALONG_X]
+    arrived = [swapped(right, **bits) for bits in ALONG_Z]
     inverse = whole_inverse(*halves, tie=right)
-    right, inverse = lax.optimization_barrier((added([right] + arrived), inverse))
-    right = summed_among(summed_among(right, ALONG_Y), ALONG_Z)
-    new_error, q_rows = remaining_error(mine, other, corrected, right, inverse)
+    right = added([right] + arrived)
+    new_error, q_rows = remaining_error(mine, other, kept, sent, right, inverse)
     return (input_grad[None], q_rows.T, new_error.reshape(1, 1, 6912, 256))
 
 

time: 117 us -> 114 us (0.974)
  waiting for transfers between devices: 28.8 us -> 24.9 us
  starting transfers between devices: 50.3 us -> 51.6 us
    ppermute x30 -> x31, waiting for transfers between devices: 26.4 us -> 22.7 us  [swapped(): return lax.ppermute(value, ('dp', 'space'), partners(**bits))]
    ppermute x30 -> x31, starting transfers between devices: 44.8 us -> 46.1 us  [swapped(): return lax.ppermute(value, ('dp', 'space'), partners(**bits))]
  transfers between devices with their start and end apart: 32 -> 33, of which waited for: 19 -> 16; matrix products, arithmetic and copies ran while one was open for 0% -> 0% of each run, Pallas kernels for 18% -> 18%
where the time goes in v4:
time: 114 us
  starting transfers between devices  51.6 us (45%)
  Pallas kernels  36.4 us (32%)
  waiting for transfers between devices  24.9 us (22%)
    ppermute x31, starting transfers between devices, swapped(): return lax.ppermute(value, ('dp', 'space'), partners(**bits))  46.1 us
    ppermute x31, waiting for transfers between devices, swapped(): return lax.ppermute(value, ('dp', 'space'), partners(**bits))  22.7 us
    pallas_call x2, Pallas kernels, local_gradient(): pl.pallas_call(functools.partial(gradient_kernel, sides, width), grid=(le...  13.2 us
    pallas_call x3, Pallas kernels, input_gradient(): pl.pallas_call(functools.partial(input_kernel, side, last), grid=(3,), in...  12.2 us
    ppermute x2, starting transfers between devices, shifted(): lax.ppermute(value, 'space', [(i, i + by) for i in range(devices) if 0 <=...  5.5 us
    pallas_call x1, Pallas kernels, remaining_error(): pl.pallas_call(error_kernel, grid=(3,), in_specs=[whole(4, 28, 8, 128), w...  3.87 us
    pallas_call x1, Pallas kernels, half_inverse(): pl.pallas_call(first_half_kernel, out_shape=[SQUARE, SQUARE], compiler_pa...  2.36 us
  transfers between devices with their start and end apart: 33, of which 16 were waited for; matrix products, arithmetic and copies ran while one was open for 0% of the time, Pallas kernels for 18%

profile of v4, /device:TPU:8, one launch (start us, length us, event | category | flops | bytes accessed | tf_op | source)
XLA Modules:
  0.0 114.0 jit_solution(16919875531644414100)
XLA Ops:
  0.6 1.6 %brick_faces.1 = (bf16[2,8,16,256]{3,2,1,0:T(8,128)(2,1)S(1)}, bf16[2,8,16,256]{3,2,1,0:T(8,128)(2,1)S(1)}) custom-call(bf16[2,512,256]{2,1,0:T(8,128)(2,1)} %bitcast.34, bf16[2,512,256]{2,1,0:T(8,128)(2,1)} %bitcast.24, s32[2,512]{1,0:T(2,128)} %bitcast.40), custom_call_target="tpu_custom_call" | custom-call | tf_op jit(solution)/shard_map/brick_faces/pallas_call | solution.py:123
  2.3 4.2 %collective-permute-start = (bf16[2,8,16,256]{3,2,1,0:T(8,128)(2,1)S(1)}, bf16[2,8,16,256]{3,2,1,0:T(8,128)(2,1)S(1)}, u32[]{:S(2)}, u32[]{:S(2)}) collective-permute-start(bf16[2,8,16,256]{3,2,1,0:T(8,128)(2,1)S(1)} %get-tuple-element.33), channel_id=1, source_target_pairs={{0,1},{1,2},{2,3},{3,4},{4,5},{5,6},{6,7},{7,8},{8,9},{9,10},{10,1... | collective-permute-start | bytes 393224 | tf_op jit(solution)/shard_map/ppermute | solution.py:499
  7.8 4.8 %gradient_own.1 = (f32[3,3,3,128,256]{4,3,2,1,0:T(8,128)S(1)}, f32[3,3,3,128,256]{4,3,2,1,0:T(8,128)S(1)}, f32[4,28,8,128]{3,2,1,0:T(8,128)S(1)}, f32[4,28,8,128]{3,2,1,0:T(8,128)S(1)}) custom-call(s32[2,27]{1,0:T(2,128)} %bitcast.52, bf16[2,512,256]{2,1,0:T(8,128)(2,1)} %bitcast.35, bf16[2,512,256]{2,1,0:T(8,128)(2,1)} %bitcast.25, s32[2,512]{1,0:T(2,128)} %bitcast.41, ...), custom_call_target="tpu_custom_call" | custom-call | flops 2000000000 | bytes 4000000 | tf_op jit(solution)/shard_map/gradient_own/pallas_call | solution.py:233
  12.6 2.3 %collective-permute-done.1.refs_7_.refs_4_ = bf16[2,8,16,256]{3,2,1,0:T(8,128)(2,1)S(1)} collective-permute-done((bf16[2,8,16,256]{3,2,1,0:T(8,128)(2,1)S(1)}, bf16[2,8,16,256]{3,2,1,0:T(8,128)(2,1)S(1)}, u32[]{:S(2)}, u32[]{:S(2)}) %collective-permute-start.1) | collective-permute-done | bytes 131104 | tf_op jit(solution)/shard_map/ppermute | solution.py:499
  14.9 8.4 %gradient_with_faces.1 = (f32[3,3,3,128,256]{4,3,2,1,0:T(8,128)S(1)}, f32[3,3,3,128,256]{4,3,2,1,0:T(8,128)S(1)}, f32[4,28,8,128]{3,2,1,0:T(8,128)S(1)}, f32[4,28,8,128]{3,2,1,0:T(8,128)S(1)}) custom-call(s32[2,27]{1,0:T(2,128)} %bitcast.53, bf16[2,512,256]{2,1,0:T(8,128)(2,1)} %bitcast.36, ...), custom_call_target="tpu_custom_call", output_to_operand_aliasing={{0}: (8, {}), {1}: (9, {})} | custom-call | flops 4000000000 | bytes 8000000 | tf_op jit(solution)/shard_map/gradient_with_faces/pallas_call | solution.py:233
  23.4 1.8 %collective-permute-done.2 = f32[4,28,8,128]{3,2,1,0:T(8,128)S(1)} collective-permute-done((f32[4,28,8,128]{3,2,1,0:T(8,128)S(1)}, f32[4,28,8,128]{3,2,1,0:T(8,128)S(1)}, u32[]{:S(2)}, u32[]{:S(2)}) %collective-permute-start.2) | collective-permute-done | bytes 458784 | tf_op jit(solution)/shard_map/ppermute | solution.py:516
  25.5 6.8 %collective-permute-start.5 = (f32[28,8,128]{2,1,0:T(8,128)S(1)}, f32[28,8,128]{2,1,0:T(8,128)S(1)}, u32[]{:S(2)}, u32[]{:S(2)}) collective-permute-start(f32[28,8,128]{2,1,0:T(8,128)S(1)} %get-tuple-element.63), channel_id=1, source_target_pairs={{0,48},{2,50},{4,52},{6,54},{8,56},{10,58},{12,60},{14,62},{128,17... | collective-permute-start | bytes 344072 | tf_op jit(solution)/shard_map/ppermute | solution.py:516
  33.3 3.6 %input_own.1.refs_5_ = f32[1024,256]{1,0:T(8,128)S(1)} custom-call(s32[2,27]{1,0:T(2,128)} %bitcast.54, bf16[2,512,256]{2,1,0:T(8,128)(2,1)S(1)} %bitcast.27, s32[2,512]{1,0:T(2,128)} %bitcast.43, bf16[3,3,3,256,256]{4,3,2,1,0:T(8,128)(2,1)S(1)} %bitcast.31, f32[4,28,8,128]{3,2,1,0:T(8,128)S(1)} %add.69.refs_4_), custom_call_target="tpu_custom_call" | custom-call | flops 2000000000 | bytes 4000000 | tf_op jit(solution)/shard_map/input_own/pallas_call | solution.py:318
  37.7 2.1 %collective-permute-done.4 = f32[28,8,128]{2,1,0:T(8,128)S(1)} collective-permute-done((f32[28,8,128]{2,1,0:T(8,128)S(1)}, f32[28,8,128]{2,1,0:T(8,128)S(1)}, u32[]{:S(2)}, u32[]{:S(2)}) %collective-permute-start.4) | collective-permute-done | bytes 114720 | tf_op jit(solution)/shard_map/ppermute | solution.py:516
  39.9 1.4 %collective-permute-start.6 = (f32[7,8,128]{2,1,0:T(8,128)S(1)}, f32[7,8,128]{2,1,0:T(8,128)S(1)}, u32[]{:S(2)}, u32[]{:S(2)}) collective-permute-start(f32[7,8,128]{2,1,0:T(8,128)S(1)} %get-tuple-element.66), channel_id=1, source_target_pairs={{0,128},{2,130},{4,132},{6,134},{8,136},{10,138},{12,140},{14,142}... | collective-permute-start | bytes 86024 | tf_op jit(solution)/shard_map/ppermute | solution.py:516
  41.3 2.7 %collective-permute-start.7 = (f32[7,8,128]{2,1,0:T(8,128)S(1)}, f32[7,8,128]{2,1,0:T(8,128)S(1)}, u32[]{:S(2)}, u32[]{:S(2)}) collective-permute-start(f32[7,8,128]{2,1,0:T(8,128)S(1)} %get-tuple-element.68), channel_id=1, source_target_pairs={{0,1},{2,3},{4,5},{6,7},{8,9},{10,11},{12,13},{14,15},{128,129},{1... | collective-permute-start | bytes 86024 | tf_op jit(solution)/shard_map/ppermute | solution.py:516
  45.2 1.5 %collective-permute-done.7 = f32[7,8,128]{2,1,0:T(8,128)S(1)} collective-permute-done((f32[7,8,128]{2,1,0:T(8,128)S(1)}, f32[7,8,128]{2,1,0:T(8,128)S(1)}, u32[]{:S(2)}, u32[]{:S(2)}) %collective-permute-start.7) | collective-permute-done | bytes 28704 | tf_op jit(solution)/shard_map/ppermute | solution.py:516
  46.7 5.9 %collective-permute-start.11 = (f32[7,8,128]{2,1,0:T(8,128)S(1)}, f32[7,8,128]{2,1,0:T(8,128)S(1)}, u32[]{:S(2)}, u32[]{:S(2)}) collective-permute-start(f32[7,8,128]{2,1,0:T(8,128)S(1)} %add_add_fusion.5), channel_id=1, source_target_pairs={{0,6},{2,4},{4,2},{6,0},{8,14},{10,12},{12,10},{14,8},{128,134},{1... | collective-permute-start | bytes 86024 | tf_op jit(solution)/shard_map/ppermute | solution.py:516
  53.2 1.3 %collective-permute-done.11 = f32[7,8,128]{2,1,0:T(8,128)S(1)} collective-permute-done((f32[7,8,128]{2,1,0:T(8,128)S(1)}, f32[7,8,128]{2,1,0:T(8,128)S(1)}, u32[]{:S(2)}, u32[]{:S(2)}) %collective-permute-start.11) | collective-permute-done | bytes 28704 | tf_op jit(solution)/shard_map/ppermute | solution.py:516
  54.5 2.8 %collective-permute-done.10 = f32[7,8,128]{2,1,0:T(8,128)S(1)} collective-permute-done((f32[7,8,128]{2,1,0:T(8,128)S(1)}, f32[7,8,128]{2,1,0:T(8,128)S(1)}, u32[]{:S(2)}, u32[]{:S(2)}) %collective-permute-start.10) | collective-permute-done | bytes 28704 | tf_op jit(solution)/shard_map/ppermute | solution.py:516
  58.4 3.7 %input_below.1.refs_5_ = f32[1024,256]{1,0:T(8,128)S(1)} custom-call(s32[2,27]{1,0:T(2,128)} %bitcast.55, bf16[2,512,256]{2,1,0:T(8,128)(2,1)S(1)} %bitcast.28, s32[2,512]{1,0:T(2,128)} %bitcast.44, bf16[3,3,3,256,256]{4,3,2,1,0:T(8,128)(2,1)S(1)} %bitcast.32, bf16[2,8,16,256]{3,2,1,0:T(8,128)(2,1)S(1)} %collective-permute-done.1.refs_7_.refs_4_, ...), custom_call_target="tpu_custom_call" | custom-call | flops 2000000000 | bytes 4000000 | tf_op jit(solution)/shard_map/input_below/pallas_call | solution.py:318
  63.4 2.9 %collective-permute-start.14 = (f32[7,8,128]{2,1,0:T(8,128)S(1)}, f32[7,8,128]{2,1,0:T(8,128)S(1)}, u32[]{:S(2)}, u32[]{:S(2)}) collective-permute-start(f32[7,8,128]{2,1,0:T(8,128)S(1)} %add.79), channel_id=1, source_target_pairs={{0,1},{2,3},{4,5},{6,7},{8,9},{10,11},{12,13},{14,15},{128,129},{1... | collective-permute-start | bytes 86024 | tf_op jit(solution)/shard_map/ppermute | solution.py:516
  67.5 2.7 %collective-permute-done.13 = f32[7,8,128]{2,1,0:T(8,128)S(1)} collective-permute-done((f32[7,8,128]{2,1,0:T(8,128)S(1)}, f32[7,8,128]{2,1,0:T(8,128)S(1)}, u32[]{:S(2)}, u32[]{:S(2)}) %collective-permute-start.13) | collective-permute-done | bytes 28704 | tf_op jit(solution)/shard_map/ppermute | solution.py:516
  70.3 2.2 %collective-permute-start.18 = (f32[28,8,128]{2,1,0:T(8,128)S(1)}, f32[28,8,128]{2,1,0:T(8,128)S(1)}, u32[]{:S(2)}, u32[]{:S(2)}) collective-permute-start(f32[28,8,128]{2,1,0:T(8,128)S(1)} %constant_dynamic-update-slice_fusion.refs_6_), channel_id=1, source_target_pairs={{0,48},{2,50},{4,52},{6,54},{8,56},{10,58},{12,60},{14,62},{128,17... | collective-permute-start | bytes 344072 | tf_op jit(solution)/shard_map/ppermute | solution.py:516
  74.5 4.8 %input_above.1 = bf16[2,512,256]{2,1,0:T(8,128)(2,1)} custom-call(s32[2,27]{1,0:T(2,128)} %bitcast.56, bf16[2,512,256]{2,1,0:T(8,128)(2,1)S(1)} %bitcast.29, s32[2,512]{1,0:T(2,128)} %bitcast.45, bf16[3,3,3,256,256]{4,3,2,1,0:T(8,128)(2,1)S(1)} %bitcast.33, bf16[2,8,16,256]{3,2,1,0:T(8,128)(2,1)S(1)} %collective-permute-done.refs_6_.refs_4_, ...), custom_call_target="tpu_custom_call" | custom-call | flops 2000000000 | bytes 4000000 | tf_op jit(solution)/shard_map/input_above/pallas_call | solution.py:318
  79.3 1.7 %right_product.1 = f32[32,256]{1,0:T(8,128)S(1)} custom-call(f32[4,28,8,128]{3,2,1,0:T(8,128)S(1)} %pad_maximum_fusion.mine, f32[3,3,3,128,256]{4,3,2,1,0:T(8,128)S(1)} %get-tuple-element.50.kept, f32[3,3,3,128,256]{4,3,2,1,0:T(8,128)S(1)} %collective-permute-done.19.partner), custom_call_target="tpu_custom_call" | custom-call | tf_op jit(solution)/shard_map/right_product/pallas_call | solution.py:365
  81.1 2.1 %collective-permute-start.21 = (f32[32,256]{1,0:T(8,128)S(1)}, f32[32,256]{1,0:T(8,128)S(1)}, u32[]{:S(2)}, u32[]{:S(2)}) collective-permute-start(f32[32,256]{1,0:T(8,128)S(1)} %right_product.1), channel_id=1, source_target_pairs={{0,12},{2,14},{4,8},{6,10},{8,4},{10,6},{12,0},{14,2},{128,140},{1... | collective-permute-start | bytes 98312 | tf_op jit(solution)/shard_map/ppermute | solution.py:516
  83.2 1.8 %collective-permute-start.20 = (f32[32,256]{1,0:T(8,128)S(1)}, f32[32,256]{1,0:T(8,128)S(1)}, u32[]{:S(2)}, u32[]{:S(2)}) collective-permute-start(f32[32,256]{1,0:T(8,128)S(1)} %right_product.1), channel_id=1, source_target_pairs={{0,64},{2,66},{4,68},{6,70},{8,72},{10,74},{12,76},{14,78},{128,19... | collective-permute-start | bytes 98312 | tf_op jit(solution)/shard_map/ppermute | solution.py:516
  85.1 1.5 %collective-permute-done.22 = f32[32,256]{1,0:T(8,128)S(1)} collective-permute-done((f32[32,256]{1,0:T(8,128)S(1)}, f32[32,256]{1,0:T(8,128)S(1)}, u32[]{:S(2)}, u32[]{:S(2)}) %collective-permute-start.22) | collective-permute-done | bytes 32800 | tf_op jit(solution)/shard_map/ppermute | solution.py:516
  88.4 2.1 %collective-permute-start.25 = (f32[32,256]{1,0:T(8,128)S(1)}, f32[32,256]{1,0:T(8,128)S(1)}, u32[]{:S(2)}, u32[]{:S(2)}) collective-permute-start(f32[32,256]{1,0:T(8,128)S(1)} %add_add_fusion.3), channel_id=1, source_target_pairs={{0,48},{2,50},{4,52},{6,54},{8,56},{10,58},{12,60},{14,62},{128,17... | collective-permute-start | bytes 98312 | tf_op jit(solution)/shard_map/ppermute | solution.py:516
  93.6 2.4 %collective-permute-done.24 = f32[32,256]{1,0:T(8,128)S(1)} collective-permute-done((f32[32,256]{1,0:T(8,128)S(1)}, f32[32,256]{1,0:T(8,128)S(1)}, u32[]{:S(2)}, u32[]{:S(2)}) %collective-permute-start.24) | collective-permute-done | bytes 32800 | tf_op jit(solution)/shard_map/ppermute | solution.py:516
  96.7 2.7 %collective-permute-start.28 = (f32[32,256]{1,0:T(8,128)S(1)}, f32[32,256]{1,0:T(8,128)S(1)}, u32[]{:S(2)}, u32[]{:S(2)}) collective-permute-start(f32[32,256]{1,0:T(8,128)S(1)} %add_add_fusion.2), channel_id=1, source_target_pairs={{0,1},{2,3},{4,5},{6,7},{8,9},{10,11},{12,13},{14,15},{128,129},{1... | collective-permute-start | bytes 98312 | tf_op jit(solution)/shard_map/ppermute | solution.py:516
  100.2 2.4 %half_inverse.1 = (f32[32,32]{1,0:T(8,128)S(1)}, f32[32,32]{1,0:T(8,128)S(1)}) custom-call(f32[4,28,8,128]{3,2,1,0:T(8,128)S(1)} %pad_maximum_fusion.mine, f32[4,28,8,128]{3,2,1,0:T(8,128)S(1)} %collective-permute-done.26.other), custom_call_target="tpu_custom_call" | custom-call | tf_op jit(solution)/shard_map/half_inverse/pallas_call | solution.py:408
  103.3 2.0 %collective-permute-start.32 = (f32[32,256]{1,0:T(8,128)S(1)}, f32[32,256]{1,0:T(8,128)S(1)}, u32[]{:S(2)}, u32[]{:S(2)}) collective-permute-start(f32[32,256]{1,0:T(8,128)S(1)} %add_add_fusion.1.refs_0_), channel_id=1, source_target_pairs={{0,6},{2,4},{4,2},{6,0},{8,14},{10,12},{12,10},{14,8},{128,134},{1... | collective-permute-start | bytes 98312 | tf_op jit(solution)/shard_map/ppermute | solution.py:516
  105.7 2.0 %collective-permute-start.30 = (f32[32,256]{1,0:T(8,128)S(1)}, f32[32,256]{1,0:T(8,128)S(1)}, u32[]{:S(2)}, u32[]{:S(2)}) collective-permute-start(f32[32,256]{1,0:T(8,128)S(1)} %add_add_fusion.1.refs_0_), channel_id=1, source_target_pairs={{0,2},{2,0},{4,6},{6,4},{8,10},{10,8},{12,14},{14,12},{128,130},{1... | collective-permute-start | bytes 98312 | tf_op jit(solution)/shard_map/ppermute | solution.py:516
  107.7 1.4 %whole_inverse.1.inverse = f32[32,32]{1,0:T(8,128)S(1)} custom-call(f32[32,32]{1,0:T(8,128)S(1)} %get-tuple-element.59.work, f32[32,32]{1,0:T(8,128)S(1)} %get-tuple-element.60.made, f32[32,256]{1,0:T(8,128)S(1)} %add_add_fusion.1.refs_0_), custom_call_target="tpu_custom_call" | custom-call | tf_op jit(solution)/shard_map/whole_inverse/pallas_call | solution.py:419
  110.1 3.9 %remaining_error.1 = (bf16[3,3,3,256,256]{4,3,2,1,0:T(8,128)(2,1)}, f32[32,256]{1,0:T(8,128)}) custom-call(f32[4,28,8,128]{3,2,1,0:T(8,128)S(1)} %pad_maximum_fusion.mine, f32[4,28,8,128]{3,2,1,0:T(8,128)S(1)} %collective-permute-done.26.other, f32[3,3,3,128,256]{4,3,2,1,0:T(8,128)S(1)} %get-tuple-element.50.kept, ...), custom_call_target="tpu_custom_call" | custom-call | tf_op jit(solution)/shard_map/remaining_error/pallas_call | solution.py:461
  (64 shorter events, 19.3 us)
Async XLA Ops:
  2.3 10.3 %collective-permute-start = (bf16[2,8,16,256]{3,2,1,0:T(8,128)(2,1)S(1)}, bf16[2,8,16,256]{3,2,1,0:T(8,128)(2,1)S(1)}, u32[]{:S(2)}, u32[]{:S(2)}) collective-permute-start(bf16[2,8,16,256]{3,2,1,0:T(8,128)(2,1)S(1)} %get-tuple-element.33), channel_id=1, source_target_pairs={{0,1},{1,2},{2,3},{3,4},{4,5},{5,6},{6,7},{7,8},{8,9},{9,10},{10,1... | collective-permute-start | bytes 393224 | tf_op jit(solution)/shard_map/ppermute | solution.py:499
  6.5 8.4 %collective-permute-start.1 = (bf16[2,8,16,256]{3,2,1,0:T(8,128)(2,1)S(1)}, bf16[2,8,16,256]{3,2,1,0:T(8,128)(2,1)S(1)}, u32[]{:S(2)}, u32[]{:S(2)}) collective-permute-start(bf16[2,8,16,256]{3,2,1,0:T(8,128)(2,1)S(1)} %get-tuple-element.34), channel_id=1, source_target_pairs={{1,0},{2,1},{3,2},{4,3},{5,4},{6,5},{7,6},{8,7},{9,8},{10,9},{11,1... | collective-permute-start | bytes 393224 | tf_op jit(solution)/shard_map/ppermute | solution.py:499
  25.2 54.1 %collective-permute-start.19 = (f32[3,3,3,128,256]{4,3,2,1,0:T(8,128)S(1)}, f32[3,3,3,128,256]{4,3,2,1,0:T(8,128)S(1)}, u32[]{:S(2)}, u32[]{:S(2)}) collective-permute-start(f32[3,3,3,128,256]{4,3,2,1,0:T(8,128)S(1)} %get-tuple-element.46.sent), channel_id=1, source_target_pairs={{0,64},{2,66},{4,68},{6,70},{8,72},{10,74},{12,76},{14,78},{128,19... | collective-permute-start | bytes 10616840 | tf_op jit(solution)/shard_map/ppermute | solution.py:516
  25.5 12.2 %collective-permute-start.5 = (f32[28,8,128]{2,1,0:T(8,128)S(1)}, f32[28,8,128]{2,1,0:T(8,128)S(1)}, u32[]{:S(2)}, u32[]{:S(2)}) collective-permute-start(f32[28,8,128]{2,1,0:T(8,128)S(1)} %get-tuple-element.63), channel_id=1, source_target_pairs={{0,48},{2,50},{4,52},{6,54},{8,56},{10,58},{12,60},{14,62},{128,17... | collective-permute-start | bytes 344072 | tf_op jit(solution)/shard_map/ppermute | solution.py:516
  32.3 7.5 %collective-permute-start.4 = (f32[28,8,128]{2,1,0:T(8,128)S(1)}, f32[28,8,128]{2,1,0:T(8,128)S(1)}, u32[]{:S(2)}, u32[]{:S(2)}) collective-permute-start(f32[28,8,128]{2,1,0:T(8,128)S(1)} %get-tuple-element.64), channel_id=1, source_target_pairs={{0,32},{2,34},{4,36},{6,38},{8,40},{10,42},{12,44},{14,46},{128,16... | collective-permute-start | bytes 344072 | tf_op jit(solution)/shard_map/ppermute | solution.py:516
  32.8 7.0 %collective-permute-start.3 = (f32[28,8,128]{2,1,0:T(8,128)S(1)}, f32[28,8,128]{2,1,0:T(8,128)S(1)}, u32[]{:S(2)}, u32[]{:S(2)}) collective-permute-start(f32[28,8,128]{2,1,0:T(8,128)S(1)} %get-tuple-element.65), channel_id=1, source_target_pairs={{0,16},{2,18},{4,20},{6,22},{8,24},{10,26},{12,28},{14,30},{128,14... | collective-permute-start | bytes 344072 | tf_op jit(solution)/shard_map/ppermute | solution.py:516
  39.9 4.2 %collective-permute-start.6 = (f32[7,8,128]{2,1,0:T(8,128)S(1)}, f32[7,8,128]{2,1,0:T(8,128)S(1)}, u32[]{:S(2)}, u32[]{:S(2)}) collective-permute-start(f32[7,8,128]{2,1,0:T(8,128)S(1)} %get-tuple-element.66), channel_id=1, source_target_pairs={{0,128},{2,130},{4,132},{6,134},{8,136},{10,138},{12,140},{14,142}... | collective-permute-start | bytes 86024 | tf_op jit(solution)/shard_map/ppermute | solution.py:516
  41.3 3.9 %collective-permute-start.8 = (f32[7,8,128]{2,1,0:T(8,128)S(1)}, f32[7,8,128]{2,1,0:T(8,128)S(1)}, u32[]{:S(2)}, u32[]{:S(2)}) collective-permute-start(f32[7,8,128]{2,1,0:T(8,128)S(1)} %get-tuple-element.67), channel_id=1, source_target_pairs={{0,129},{2,131},{4,133},{6,135},{8,137},{10,139},{12,141},{14,143}... | collective-permute-start | bytes 86024 | tf_op jit(solution)/shard_map/ppermute | solution.py:516
  41.3 5.4 %collective-permute-start.7 = (f32[7,8,128]{2,1,0:T(8,128)S(1)}, f32[7,8,128]{2,1,0:T(8,128)S(1)}, u32[]{:S(2)}, u32[]{:S(2)}) collective-permute-start(f32[7,8,128]{2,1,0:T(8,128)S(1)} %get-tuple-element.68), channel_id=1, source_target_pairs={{0,1},{2,3},{4,5},{6,7},{8,9},{10,11},{12,13},{14,15},{128,129},{1... | collective-permute-start | bytes 86024 | tf_op jit(solution)/shard_map/ppermute | solution.py:516
  46.7 7.8 %collective-permute-start.11 = (f32[7,8,128]{2,1,0:T(8,128)S(1)}, f32[7,8,128]{2,1,0:T(8,128)S(1)}, u32[]{:S(2)}, u32[]{:S(2)}) collective-permute-start(f32[7,8,128]{2,1,0:T(8,128)S(1)} %add_add_fusion.5), channel_id=1, source_target_pairs={{0,6},{2,4},{4,2},{6,0},{8,14},{10,12},{12,10},{14,8},{128,134},{1... | collective-permute-start | bytes 86024 | tf_op jit(solution)/shard_map/ppermute | solution.py:516
  52.6 4.8 %collective-permute-start.10 = (f32[7,8,128]{2,1,0:T(8,128)S(1)}, f32[7,8,128]{2,1,0:T(8,128)S(1)}, u32[]{:S(2)}, u32[]{:S(2)}) collective-permute-start(f32[7,8,128]{2,1,0:T(8,128)S(1)} %add_add_fusion.5), channel_id=1, source_target_pairs={{0,4},{2,6},{4,0},{6,2},{8,12},{10,14},{12,8},{14,10},{128,132},{1... | collective-permute-start | bytes 86024 | tf_op jit(solution)/shard_map/ppermute | solution.py:516
  52.6 4.8 %collective-permute-start.9 = (f32[7,8,128]{2,1,0:T(8,128)S(1)}, f32[7,8,128]{2,1,0:T(8,128)S(1)}, u32[]{:S(2)}, u32[]{:S(2)}) collective-permute-start(f32[7,8,128]{2,1,0:T(8,128)S(1)} %add_add_fusion.5), channel_id=1, source_target_pairs={{0,2},{2,0},{4,6},{6,4},{8,10},{10,8},{12,14},{14,12},{128,130},{1... | collective-permute-start | bytes 86024 | tf_op jit(solution)/shard_map/ppermute | solution.py:516
  57.3 6.1 %collective-permute-start.12 = (f32[7,8,128]{2,1,0:T(8,128)S(1)}, f32[7,8,128]{2,1,0:T(8,128)S(1)}, u32[]{:S(2)}, u32[]{:S(2)}) collective-permute-start(f32[7,8,128]{2,1,0:T(8,128)S(1)} %add_add_fusion.4.refs_6_), channel_id=1, source_target_pairs={{0,12},{2,14},{4,8},{6,10},{8,4},{10,6},{12,0},{14,2},{128,140},{1... | collective-permute-start | bytes 86024 | tf_op jit(solution)/shard_map/ppermute | solution.py:516
  63.4 6.8 %collective-permute-start.15 = (f32[7,8,128]{2,1,0:T(8,128)S(1)}, f32[7,8,128]{2,1,0:T(8,128)S(1)}, u32[]{:S(2)}, u32[]{:S(2)}) collective-permute-start(f32[7,8,128]{2,1,0:T(8,128)S(1)} %add.79), channel_id=1, source_target_pairs={{0,129},{2,131},{4,133},{6,135},{8,137},{10,139},{12,141},{14,143}... | collective-permute-start | bytes 86024 | tf_op jit(solution)/shard_map/ppermute | solution.py:516
  63.4 6.8 %collective-permute-start.14 = (f32[7,8,128]{2,1,0:T(8,128)S(1)}, f32[7,8,128]{2,1,0:T(8,128)S(1)}, u32[]{:S(2)}, u32[]{:S(2)}) collective-permute-start(f32[7,8,128]{2,1,0:T(8,128)S(1)} %add.79), channel_id=1, source_target_pairs={{0,1},{2,3},{4,5},{6,7},{8,9},{10,11},{12,13},{14,15},{128,129},{1... | collective-permute-start | bytes 86024 | tf_op jit(solution)/shard_map/ppermute | solution.py:516
  66.4 3.9 %collective-permute-start.13 = (f32[7,8,128]{2,1,0:T(8,128)S(1)}, f32[7,8,128]{2,1,0:T(8,128)S(1)}, u32[]{:S(2)}, u32[]{:S(2)}) collective-permute-start(f32[7,8,128]{2,1,0:T(8,128)S(1)} %add.79), channel_id=1, source_target_pairs={{0,128},{2,130},{4,132},{6,134},{8,136},{10,138},{12,140},{14,142}... | collective-permute-start | bytes 86024 | tf_op jit(solution)/shard_map/ppermute | solution.py:516
  70.3 9.0 %collective-permute-start.18 = (f32[28,8,128]{2,1,0:T(8,128)S(1)}, f32[28,8,128]{2,1,0:T(8,128)S(1)}, u32[]{:S(2)}, u32[]{:S(2)}) collective-permute-start(f32[28,8,128]{2,1,0:T(8,128)S(1)} %constant_dynamic-update-slice_fusion.refs_6_), channel_id=1, source_target_pairs={{0,48},{2,50},{4,52},{6,54},{8,56},{10,58},{12,60},{14,62},{128,17... | collective-permute-start | bytes 344072 | tf_op jit(solution)/shard_map/ppermute | solution.py:516
  72.5 6.8 %collective-permute-start.17 = (f32[28,8,128]{2,1,0:T(8,128)S(1)}, f32[28,8,128]{2,1,0:T(8,128)S(1)}, u32[]{:S(2)}, u32[]{:S(2)}) collective-permute-start(f32[28,8,128]{2,1,0:T(8,128)S(1)} %constant_dynamic-update-slice_fusion.refs_6_), channel_id=1, source_target_pairs={{0,32},{2,34},{4,36},{6,38},{8,40},{10,42},{12,44},{14,46},{128,16... | collective-permute-start | bytes 344072 | tf_op jit(solution)/shard_map/ppermute | solution.py:516
  73.4 5.9 %collective-permute-start.16 = (f32[28,8,128]{2,1,0:T(8,128)S(1)}, f32[28,8,128]{2,1,0:T(8,128)S(1)}, u32[]{:S(2)}, u32[]{:S(2)}) collective-permute-start(f32[28,8,128]{2,1,0:T(8,128)S(1)} %constant_dynamic-update-slice_fusion.refs_6_), channel_id=1, source_target_pairs={{0,16},{2,18},{4,20},{6,22},{8,24},{10,26},{12,28},{14,30},{128,14... | collective-permute-start | bytes 344072 | tf_op jit(solution)/shard_map/ppermute | solution.py:516
  81.0 5.6 %collective-permute-start.22 = (f32[32,256]{1,0:T(8,128)S(1)}, f32[32,256]{1,0:T(8,128)S(1)}, u32[]{:S(2)}, u32[]{:S(2)}) collective-permute-start(f32[32,256]{1,0:T(8,128)S(1)} %right_product.1), channel_id=1, source_target_pairs={{0,76},{2,78},{4,72},{6,74},{8,68},{10,70},{12,64},{14,66},{128,20... | collective-permute-start | bytes 98312 | tf_op jit(solution)/shard_map/ppermute | solution.py:516
  81.1 6.1 %collective-permute-start.21 = (f32[32,256]{1,0:T(8,128)S(1)}, f32[32,256]{1,0:T(8,128)S(1)}, u32[]{:S(2)}, u32[]{:S(2)}) collective-permute-start(f32[32,256]{1,0:T(8,128)S(1)} %right_product.1), channel_id=1, source_target_pairs={{0,12},{2,14},{4,8},{6,10},{8,4},{10,6},{12,0},{14,2},{128,140},{1... | collective-permute-start | bytes 98312 | tf_op jit(solution)/shard_map/ppermute | solution.py:516
  83.2 4.0 %collective-permute-start.20 = (f32[32,256]{1,0:T(8,128)S(1)}, f32[32,256]{1,0:T(8,128)S(1)}, u32[]{:S(2)}, u32[]{:S(2)}) collective-permute-start(f32[32,256]{1,0:T(8,128)S(1)} %right_product.1), channel_id=1, source_target_pairs={{0,64},{2,66},{4,68},{6,70},{8,72},{10,74},{12,76},{14,78},{128,19... | collective-permute-start | bytes 98312 | tf_op jit(solution)/shard_map/ppermute | solution.py:516
  87.2 8.8 %collective-permute-start.26 = (f32[4,28,8,128]{3,2,1,0:T(8,128)S(1)}, f32[4,28,8,128]{3,2,1,0:T(8,128)S(1)}, u32[]{:S(2)}, u32[]{:S(2)}) collective-permute-start(f32[4,28,8,128]{3,2,1,0:T(8,128)S(1)} %pad_maximum_fusion.mine), channel_id=1, source_target_pairs={{0,64},{2,66},{4,68},{6,70},{8,72},{10,74},{12,76},{14,78},{128,19... | collective-permute-start | bytes 1376264 | tf_op jit(solution)/shard_map/ppermute | solution.py:516
  88.4 5.1 %collective-permute-start.25 = (f32[32,256]{1,0:T(8,128)S(1)}, f32[32,256]{1,0:T(8,128)S(1)}, u32[]{:S(2)}, u32[]{:S(2)}) collective-permute-start(f32[32,256]{1,0:T(8,128)S(1)} %add_add_fusion.3), channel_id=1, source_target_pairs={{0,48},{2,50},{4,52},{6,54},{8,56},{10,58},{12,60},{14,62},{128,17... | collective-permute-start | bytes 98312 | tf_op jit(solution)/shard_map/ppermute | solution.py:516
  90.6 5.4 %collective-permute-start.24 = (f32[32,256]{1,0:T(8,128)S(1)}, f32[32,256]{1,0:T(8,128)S(1)}, u32[]{:S(2)}, u32[]{:S(2)}) collective-permute-start(f32[32,256]{1,0:T(8,128)S(1)} %add_add_fusion.3), channel_id=1, source_target_pairs={{0,32},{2,34},{4,36},{6,38},{8,40},{10,42},{12,44},{14,46},{128,16... | collective-permute-start | bytes 98312 | tf_op jit(solution)/shard_map/ppermute | solution.py:516
  91.4 4.6 %collective-permute-start.23 = (f32[32,256]{1,0:T(8,128)S(1)}, f32[32,256]{1,0:T(8,128)S(1)}, u32[]{:S(2)}, u32[]{:S(2)}) collective-permute-start(f32[32,256]{1,0:T(8,128)S(1)} %add_add_fusion.3), channel_id=1, source_target_pairs={{0,16},{2,18},{4,20},{6,22},{8,24},{10,26},{12,28},{14,30},{128,14... | collective-permute-start | bytes 98312 | tf_op jit(solution)/shard_map/ppermute | solution.py:516
  96.0 6.5 %collective-permute-start.29 = (f32[32,256]{1,0:T(8,128)S(1)}, f32[32,256]{1,0:T(8,128)S(1)}, u32[]{:S(2)}, u32[]{:S(2)}) collective-permute-start(f32[32,256]{1,0:T(8,128)S(1)} %add_add_fusion.2), channel_id=1, source_target_pairs={{0,129},{2,131},{4,133},{6,135},{8,137},{10,139},{12,141},{14,143}... | collective-permute-start | bytes 98312 | tf_op jit(solution)/shard_map/ppermute | solution.py:516
  96.7 5.9 %collective-permute-start.28 = (f32[32,256]{1,0:T(8,128)S(1)}, f32[32,256]{1,0:T(8,128)S(1)}, u32[]{:S(2)}, u32[]{:S(2)}) collective-permute-start(f32[32,256]{1,0:T(8,128)S(1)} %add_add_fusion.2), channel_id=1, source_target_pairs={{0,1},{2,3},{4,5},{6,7},{8,9},{10,11},{12,13},{14,15},{128,129},{1... | collective-permute-start | bytes 98312 | tf_op jit(solution)/shard_map/ppermute | solution.py:516
  99.3 3.9 %collective-permute-start.27 = (f32[32,256]{1,0:T(8,128)S(1)}, f32[32,256]{1,0:T(8,128)S(1)}, u32[]{:S(2)}, u32[]{:S(2)}) collective-permute-start(f32[32,256]{1,0:T(8,128)S(1)} %add_add_fusion.2), channel_id=1, source_target_pairs={{0,128},{2,130},{4,132},{6,134},{8,136},{10,138},{12,140},{14,142}... | collective-permute-start | bytes 98312 | tf_op jit(solution)/shard_map/ppermute | solution.py:516
  103.3 5.9 %collective-permute-start.32 = (f32[32,256]{1,0:T(8,128)S(1)}, f32[32,256]{1,0:T(8,128)S(1)}, u32[]{:S(2)}, u32[]{:S(2)}) collective-permute-start(f32[32,256]{1,0:T(8,128)S(1)} %add_add_fusion.1.refs_0_), channel_id=1, source_target_pairs={{0,6},{2,4},{4,2},{6,0},{8,14},{10,12},{12,10},{14,8},{128,134},{1... | collective-permute-start | bytes 98312 | tf_op jit(solution)/shard_map/ppermute | solution.py:516
  105.3 4.8 %collective-permute-start.31 = (f32[32,256]{1,0:T(8,128)S(1)}, f32[32,256]{1,0:T(8,128)S(1)}, u32[]{:S(2)}, u32[]{:S(2)}) collective-permute-start(f32[32,256]{1,0:T(8,128)S(1)} %add_add_fusion.1.refs_0_), channel_id=1, source_target_pairs={{0,4},{2,6},{4,0},{6,2},{8,12},{10,14},{12,8},{14,10},{128,132},{1... | collective-permute-start | bytes 98312 | tf_op jit(solution)/shard_map/ppermute | solution.py:516
  105.7 4.4 %collective-permute-start.30 = (f32[32,256]{1,0:T(8,128)S(1)}, f32[32,256]{1,0:T(8,128)S(1)}, u32[]{:S(2)}, u32[]{:S(2)}) collective-permute-start(f32[32,256]{1,0:T(8,128)S(1)} %add_add_fusion.1.refs_0_), channel_id=1, source_target_pairs={{0,2},{2,0},{4,6},{6,4},{8,10},{10,8},{12,14},{14,12},{128,130},{1... | collective-permute-start | bytes 98312 | tf_op jit(solution)/shard_map/ppermute | solution.py:516
  (3 other events, 38.7 us)

commit v5 on v3

--- a/solution.py
+++ b/solution.py
@@ -80,29 +80,33 @@
     return ((tap // 7) ^ y) * 7 + tap % 7
 
 
-def put_factor(mine, other, tap, value):
-    core, x, y, _ = coordinates()
+def put_factor(part, tap, value):
+    _, x, y, _ = coordinates()
     place = place_of(tap, y)
-    halves = value[:, :128], value[:, 128:]
-    kept = jnp.where(core == 0, halves[0], halves[1])
-    sent = jnp.where(core == 0, halves[1], halves[0])
     for block in range(4):
-        rows = slice(block * 8, block * 8 + 8)
-        mine[block ^ x, place] = kept[rows]
-        other[block ^ x, place] = sent[rows]
-
-
-def get_factor(mine, other, tap):
-    core, x, y, _ = coordinates()
+        part[block ^ x, place] = value[block * 8 : block * 8 + 8]
+
+
+def get_factor(part, tap):
+    _, x, y, _ = coordinates()
     place = place_of(tap, y)
-    own = jnp.concatenate([mine[block ^ x, place] for block in range(4)], axis=0)
-    rest = jnp.concatenate([other[block ^ x, place] for block in range(4)], axis=0)
-    both = jnp.concatenate([jnp.where(core == 0, own, rest), jnp.where(core == 0, rest, own)], axis=1)
-    return both * (1.0 / 256.0)
+    return jnp.concatenate([part[block ^ x, place] for block in range(4)], axis=0) * (1.0 / 256.0)
+
+
+def taps_left(part, step_x, step_y):
+    first = step_x * 9 + step_y * 3
+    return jnp.concatenate([get_factor(part, first + k) for k in range(3)], axis=1)
+
+
+def on_core(own, given):
+    return jnp.where(coordinates()[0] == 0, given, own)
 
 
 def whole(*shape):
     return pl.BlockSpec(shape, lambda *step: (0,) * len(shape))
+
+
+FACTOR_SPEC = whole(4, 28, 8, 256)
 
 
 def faces_kernel(field, cotangent, occupancy, up, down):
@@ -130,9 +134,9 @@
     slots, field, cotangent, occupancy, start, error = refs[:6]
     refs = refs[6:]
     if faces:
-        lower, upper, _, mine_before, other_before = refs[:5]
-        refs = refs[5:]
-    corrected, mine, other, views, sources, own, start_parts = refs
+        lower, upper, _, before = refs[:4]
+        refs = refs[4:]
+    corrected, factor, views, sources, own, start_parts = refs
     step = pl.program_id(0)
     depth = 256 if faces else 128
     shares = 3 // width
@@ -154,10 +158,9 @@
                 source = with_faces(source, lower, upper, plane)
             sources[plane * 256 : (plane + 1) * 256, :] = source.T
         if faces:
-            mine[...] = mine_before[...]
-            other[...] = other_before[...]
+            factor[...] = before[...]
         else:
-            put_factor(mine, other, 27, jnp.zeros((32, 256), F32))
+            put_factor(factor, 27, jnp.zeros((32, 256), F32))
 
     def gather(groups):
         for first in range(0, len(groups), 2):
@@ -201,7 +204,7 @@
         for slot, (tap_x, member, _) in enumerate(chosen):
             step_y = step % shares * width + member
             rows = made[slot * 64 : slot * 64 + 64]
-            put_factor(mine, other, tap_x * 9 + step_y * 3 + side + 1, rows[:32] + rows[32:])
+            put_factor(factor, tap_x * 9 + step_y * 3 + side + 1, rows[:32] + rows[32:])
 
 
 def local_gradient(sides, slots, field, cotangent, occupancy, start, error, *more):
@@ -212,7 +215,6 @@
     def which(step):
         return step // shares * 2 if faces else 1
 
-    piece = whole(4, 28, 8, 128)
     face = whole(1, EDGE, 16, 256)
     in_specs = [
         pl.BlockSpec(memory_space=pltpu.SMEM),
@@ -223,7 +225,7 @@
         pl.BlockSpec((3, width, 1, 256, 256), lambda step: (0, step % shares, which(step), 0, 0)),
     ]
     if faces:
-        in_specs += [face, face, pl.BlockSpec(memory_space=pl.ANY), piece, piece]
+        in_specs += [face, face, pl.BlockSpec(memory_space=pl.ANY), FACTOR_SPEC]
     depth = 256 if faces else 128
     return pl.pallas_call(
         functools.partial(gradient_kernel, sides, width),
@@ -231,14 +233,9 @@
         in_specs=in_specs,
         out_specs=[
             pl.BlockSpec((1, 3, width, 256, 256), lambda step: (which(step), 0, step % shares, 0, 0)),
-            piece,
-            piece,
+            FACTOR_SPEC,
         ],
-        out_shape=[
-            CORRECTED,
-            jax.ShapeDtypeStruct((4, 28, 8, 128), F32),
-            jax.ShapeDtypeStruct((4, 28, 8, 128), F32),
-        ],
+        out_shape=[CORRECTED, jax.ShapeDtypeStruct((4, 28, 8, 256), F32)],
         input_output_aliases={8: 0} if faces else {},
         scratch_shapes=[
             pltpu.VMEM((width, 256, 1280), BF16),
@@ -326,12 +323,7 @@
     )(slots, cotangent, occupancy, weight, *more)
 
 
-def taps_left(mine, other, step_x, step_y):
-    first = step_x * 9 + step_y * 3
-    return jnp.concatenate([get_factor(mine, other, first + k) for k in range(3)], axis=1)
-
-
-def right_kernel(mine, other, corrected, right):
+def right_kernel(part, corrected, partner, right):
     step = pl.program_id(0)
 
     @pl.when(step == 0)
@@ -340,8 +332,8 @@
 
     total = jnp.zeros((32, 256), F32)
     for step_y in range(3):
-        left_high, left_low = split(taps_left(mine, other, step, step_y))
-        high, low = split(corrected[:, 0, step_y].reshape(768, 256))
+        left_high, left_low = split(taps_left(part, step, step_y))
+        high, low = split((corrected[:, 0, step_y] + partner[:, 0, step_y]).reshape(768, 256))
         both = lax.dot_general(
             jnp.concatenate([left_high, left_low], axis=0), high, NN, preferred_element_type=F32
         )
@@ -354,16 +346,16 @@
     return pl.BlockSpec((3, 1, 3) + shape, lambda step: (0, step, 0, 0, 0))
 
 
-def right_product(mine, other, corrected):
+def right_product(part, corrected, partner):
     return pl.pallas_call(
         right_kernel,
         grid=(3,),
-        in_specs=[whole(4, 28, 8, 128), whole(4, 28, 8, 128), along_x(256, 256)],
+        in_specs=[FACTOR_SPEC, along_x(256, 256), along_x(256, 256)],
         out_specs=whole(32, 256),
         out_shape=jax.ShapeDtypeStruct((32, 256), F32),
         compiler_params=pltpu.CompilerParams(vmem_limit_bytes=LATE_LIMIT),
         name="right_product",
-    )(mine, other, in_vmem(corrected))
+    )(part, in_vmem(corrected), in_vmem(partner))
 
 
 def eliminate(first, work, made):
@@ -380,10 +372,10 @@
     return work, made
 
 
-def first_half_kernel(mine, other, work, made):
+def first_half_kernel(part, given, work, made):
     gram = jnp.zeros((32, 32), F32)
     for step in range(9):
-        left = jnp.concatenate([get_factor(mine, other, step * 3 + tap) for tap in range(3)], axis=1)
+        left = on_core(taps_left(part, step // 3, step % 3), taps_left(given, step // 3, step % 3))
         gram += lax.dot_general(left, left, NT, precision=lax.Precision.HIGHEST, preferred_element_type=F32)
     row = lax.broadcasted_iota(jnp.int32, (32, 32), 0)
     column = lax.broadcasted_iota(jnp.int32, (32, 32), 1)
@@ -397,9 +389,9 @@
 SQUARE = jax.ShapeDtypeStruct((32, 32), F32)
 
 
-def half_inverse(mine, other):
+def half_inverse(part, given):
     return pl.pallas_call(first_half_kernel, out_shape=[SQUARE, SQUARE], compiler_params=SMALL, name="half_inverse")(
-        mine, other
+        part, given
     )
 
 
@@ -419,13 +411,13 @@
     )(work, made, *more)
 
 
-def error_kernel(mine, other, corrected, right, inverse, new_error, q_rows, basis):
+def error_kernel(part, given, corrected, right, right_given, inverse, new_error, q_rows, basis):
     step = pl.program_id(0)
 
     @pl.when(step == 0)
     def _():
         rows = lax.dot_general(
-            inverse[...], right[...], NN, precision=lax.Precision.HIGHEST, preferred_element_type=F32
+            inverse[...], on_core(right[...], right_given[...]), NN, precision=lax.Precision.HIGHEST, preferred_element_type=F32
         ) * (1.0 / 256.0)
         q_rows[...] = rows
         back = lax.dot_general(
@@ -438,21 +430,22 @@
         basis[96:128, :] = jnp.zeros((32, 256), BF16)
 
     for step_y in range(3):
-        high, low = split(taps_left(mine, other, step, step_y))
+        high, low = split(on_core(taps_left(part, step, step_y), taps_left(given, step, step_y)))
         left = jnp.concatenate([high, low, high, jnp.zeros((32, 768), BF16)], axis=0)
         product = lax.dot_general(left, basis[...], TN, preferred_element_type=F32)
         rest = corrected[:, 0, step_y] - product.reshape(3, 256, 256)
         new_error[0, step_y] = rest.astype(BF16)
 
 
-def remaining_error(mine, other, corrected, right, inverse):
+def remaining_error(part, given, corrected, right, right_given, inverse):
     return pl.pallas_call(
         error_kernel,
         grid=(3,),
         in_specs=[
-            whole(4, 28, 8, 128),
-            whole(4, 28, 8, 128),
+            FACTOR_SPEC,
+            FACTOR_SPEC,
             along_x(256, 256),
+            whole(32, 256),
             whole(32, 256),
             whole(32, 32),
         ],
@@ -461,7 +454,7 @@
         scratch_shapes=[pltpu.VMEM((128, 256), BF16)],
         compiler_params=pltpu.CompilerParams(vmem_limit_bytes=LATE_LIMIT),
         name="remaining_error",
-    )(mine, other, in_vmem(corrected), right, inverse)
+    )(part, given, in_vmem(corrected), right, right_given, inverse)
 
 
 CORRECTED = pltpu.VMEM((3, 3, 3, 256, 256), F32)
@@ -486,21 +479,20 @@
     return lax.ppermute(value, "space", [(i, i + by) for i in range(devices) if 0 <= i + by < devices])
 
 
-def partners(core=0, x=0, y=0, z=0):
-    def place(at_core, at_x, at_y, at_z):
-        return (at_y % 2 * 2 + at_core) * 64 + (at_x * 8 + at_z) * 2 + at_y // 2
-
-    return [
-        (place(c, i, j, l), place(c ^ core, i ^ x, j ^ y, l ^ z))
-        for c in range(2)
-        for i in range(4)
-        for j in range(4)
-        for l in range(8)
-    ]
-
-
-def swapped(value, **bits):
-    return lax.ppermute(value, ("dp", "space"), partners(**bits))
+def place(core, x, y, z):
+    return (y % 2 * 2 + core) * 64 + (x * 8 + z) * 2 + y // 2
+
+
+def swapped(value, x=0, y=0, z=0):
+    chips = [(i, j, k) for i in range(4) for j in range(4) for k in range(8)]
+    pairs = [(place(1, i, j, k), place(1, i ^ x, j ^ y, k ^ z)) for i, j, k in chips]
+    return lax.ppermute(value, ("dp", "space"), pairs)
+
+
+def handed(value, to):
+    chips = [(i, j, k) for i in range(4) for j in range(4) for k in range(8)]
+    pairs = [(place(1 - to, *chip), place(to, *chip)) for chip in chips]
+    return lax.ppermute(value, ("dp", "space"), pairs)
 
 
 def added(values):
@@ -514,7 +506,6 @@
 ALONG_X = [dict(x=1), dict(x=2), dict(x=3)]
 ALONG_Y = [dict(y=1), dict(y=2), dict(y=3)]
 ALONG_Z = [dict(z=1), dict(z=2), dict(z=3)]
-CORE_AND_Z = [dict(core=1), dict(z=6), dict(core=1, z=6)]
 
 
 def body(inputs, cotangent, occupancy, neighbours, weight, error_in, q_start):
@@ -524,34 +515,41 @@
     up, down = brick_faces(field, gradient, occupied)
     lower, upper = shifted(up, 1), shifted(down, -1)
     fixed = (slots, in_hbm(field), in_hbm(gradient), occupied, in_hbm(q_start.T), in_hbm(error_in.reshape(3, 3, 3, 256, 256)))
-    corrected, mine, other = local_gradient((0,), *fixed)
-    corrected, mine, other = local_gradient((-1, 1), *fixed, lower, upper, in_vmem(corrected), mine, other)
-
-    part = mine + swapped(other, core=1)
+    corrected, factor = local_gradient((0,), *fixed)
+    corrected, factor = local_gradient((-1, 1), *fixed, lower, upper, in_vmem(corrected), factor)
+
+    part = factor + handed(factor, to=1)
+    part, travelling = lax.optimization_barrier((part, corrected))
     arrived = [swapped(part[k], x=k) for k in (1, 2, 3)]
+    partner = handed(travelling, to=1)
     total = input_gradient(0, False, slots, gradient, occupied, weight, tie=part)
     part, total = lax.optimization_barrier((added([part[0]] + arrived), total))
-    part = part.reshape(4, 7, 8, 128)
+    part = part.reshape(4, 7, 8, 256)
     part = added([part[0]] + [swapped(part[k], y=k) for k in (1, 2, 3)])
-    arrived = [swapped(part, **bits) for bits in ALONG_Z]
+    part = summed_among(part, ALONG_Z)
+    arrived = swapped(part, z=6)
     total = input_gradient(-1, False, slots, gradient, occupied, weight, upper, total, tie=part)
-    part, total = lax.optimization_barrier((added([part] + arrived), total))
-    part = part + swapped(part, z=6)
+    part, total = lax.optimization_barrier((part + arrived, total))
     part = jnp.concatenate([part] + [swapped(part, **bits) for bits in ALONG_Y], axis=0)
     arrived = [swapped(part, **bits) for bits in ALONG_X]
     input_grad = input_gradient(1, True, slots, gradient, occupied, weight, lower, total, tie=part)
-    mine, input_grad = lax.optimization_barrier((jnp.stack([part] + arrived, axis=0), input_grad))
-    other = swapped(mine, core=1)
-
-    right = right_product(mine, other, corrected)
-    arrived = [swapped(right, **bits) for bits in CORE_AND_Z]
-    halves = half_inverse(mine, other)
+    part, partner, input_grad = lax.optimization_barrier(
+        (jnp.stack([part] + arrived, axis=0), partner, input_grad)
+    )
+
+    right = right_product(part, corrected, partner)
+    right, part = lax.optimization_barrier((summed_among(right, ALONG_X), part))
+    arrived = [swapped(right, **bits) for bits in ALONG_Y]
+    given = handed(part, to=0)
+    right, given = lax.optimization_barrier((added([right] + arrived), given))
+    arrived = [swapped(right, **bits) for bits in ALONG_Z]
+    halves = half_inverse(part, given)
     right, *halves = lax.optimization_barrier((added([right] + arrived), *halves))
-    arrived = [swapped(right, **bits) for bits in ALONG_X]
+    arrived = swapped(right, z=6)
     inverse = whole_inverse(*halves, tie=right)
-    right, inverse = lax.optimization_barrier((added([right] + arrived), inverse))
-    right = summed_among(summed_among(right, ALONG_Y), ALONG_Z)
-    new_error, q_rows = remaining_error(mine, other, corrected, right, inverse)
+    right, inverse = lax.optimization_barrier((right + arrived, inverse))
+    right_given = handed(right, to=0)
+    new_error, q_rows = remaining_error(part, given, corrected, right, right_given, inverse)
     return (input_grad[None], q_rows.T, new_error.reshape(1, 1, 6912, 256))
 
 

time: 117 us -> 158 us (1.35); the launches traced: 117 us -> 154 us
  waiting for transfers between devices: 28.8 us -> 86.1 us
  starting transfers between devices: 50.3 us -> 29.7 us
    ppermute x30, waiting for transfers between devices: 26.4 us -> 83.7 us  [the longest x4 83.6 us: handed(): return lax.ppermute(value, ('dp', 'space'), pairs)]
    ppermute x30, starting transfers between devices: 44.8 us -> 24.2 us  [the longest x26 17.5 us: swapped(): return lax.ppermute(value, ('dp', 'space'), pairs)]
  transfers between devices with their start and end apart: 32 -> 32, of which waited for: 19 -> 4; matrix products, arithmetic and copies ran while one was open for 0% -> 0% of each run, Pallas kernels for 18% -> 13%
where the time goes in v5:
time: 158 us; the launch traced here: 154 us
  waiting for transfers between devices  86.1 us (54%)
  Pallas kernels  37.1 us (23%)
  starting transfers between devices  29.7 us (19%)
    ppermute x4, waiting for transfers between devices, handed(): return lax.ppermute(value, ('dp', 'space'), pairs)  83.6 us
    ppermute x26, starting transfers between devices, swapped(): return lax.ppermute(value, ('dp', 'space'), pairs)  17.5 us
    pallas_call x2, Pallas kernels, local_gradient(): pl.pallas_call(functools.partial(gradient_kernel, sides, width), grid=(le...  12.9 us
    pallas_call x3, Pallas kernels, input_gradient(): pl.pallas_call(functools.partial(input_kernel, side, last), grid=(3,), in...  12.2 us
    ppermute x4, starting transfers between devices, handed(): return lax.ppermute(value, ('dp', 'space'), pairs)  6.67 us
    ppermute x2, starting transfers between devices, shifted(): lax.ppermute(value, 'space', [(i, i + by) for i in range(devices) if 0 <=...  5.5 us
    pallas_call x1, Pallas kernels, remaining_error(): pl.pallas_call(error_kernel, grid=(3,), in_specs=[FACTOR_SPEC, FACTOR_SPE...  3.8 us
  transfers between devices with their start and end apart: 32, of which 4 were waited for; matrix products, arithmetic and copies ran while one was open for 0% of the time, Pallas kernels for 13%

profile of v5, /device:TPU:8, one launch (start us, length us, event | category | flops | bytes accessed | tf_op | source)
XLA Modules:
  0.0 154.4 jit_solution(13989220036942468860)
XLA Ops:
  0.6 1.6 %brick_faces.1 = (bf16[2,8,16,256]{3,2,1,0:T(8,128)(2,1)S(1)}, bf16[2,8,16,256]{3,2,1,0:T(8,128)(2,1)S(1)}) custom-call(bf16[2,512,256]{2,1,0:T(8,128)(2,1)} %bitcast.34, bf16[2,512,256]{2,1,0:T(8,128)(2,1)} %bitcast.24, s32[2,512]{1,0:T(2,128)} %bitcast.40), custom_call_target="tpu_custom_call" | custom-call | tf_op jit(solution)/shard_map/brick_faces/pallas_call | solution.py:127
  2.3 4.2 %collective-permute-start = (bf16[2,8,16,256]{3,2,1,0:T(8,128)(2,1)S(1)}, bf16[2,8,16,256]{3,2,1,0:T(8,128)(2,1)S(1)}, u32[]{:S(2)}, u32[]{:S(2)}) collective-permute-start(bf16[2,8,16,256]{3,2,1,0:T(8,128)(2,1)S(1)} %get-tuple-element.31), channel_id=1, source_target_pairs={{0,1},{1,2},{2,3},{3,4},{4,5},{5,6},{6,7},{7,8},{8,9},{9,10},{10,1... | collective-permute-start | bytes 393224 | tf_op jit(solution)/shard_map/ppermute | solution.py:479
  6.5 1.3 collective-permute-start.1
  7.8 4.7 %gradient_own.1 = (f32[3,3,3,256,256]{4,3,2,1,0:T(8,128)S(1)}, f32[4,28,8,256]{3,2,1,0:T(8,128)S(1)}) custom-call(s32[2,27]{1,0:T(2,128)} %bitcast.52, bf16[2,512,256]{2,1,0:T(8,128)(2,1)} %bitcast.35, bf16[2,512,256]{2,1,0:T(8,128)(2,1)} %bitcast.25, s32[2,512]{1,0:T(2,128)} %bitcast.41, f32[32,256]{1,0:T(8,128)} %bitcast.49, ...), custom_call_target="tpu_custom_call" | custom-call | flops 2000000000 | bytes 4000000 | tf_op jit(solution)/shard_map/gradient_own/pallas_call | solution.py:230
  12.5 2.3 %collective-permute-done.1.refs_7_.refs_4_ = bf16[2,8,16,256]{3,2,1,0:T(8,128)(2,1)S(1)} collective-permute-done((bf16[2,8,16,256]{3,2,1,0:T(8,128)(2,1)S(1)}, bf16[2,8,16,256]{3,2,1,0:T(8,128)(2,1)S(1)}, u32[]{:S(2)}, u32[]{:S(2)}) %collective-permute-start.1) | collective-permute-done | bytes 131104 | tf_op jit(solution)/shard_map/ppermute | solution.py:479
  14.9 8.2 %gradient_with_faces.1 = (f32[3,3,3,256,256]{4,3,2,1,0:T(8,128)S(1)}, f32[4,28,8,256]{3,2,1,0:T(8,128)S(1)}) custom-call(s32[2,27]{1,0:T(2,128)} %bitcast.53, bf16[2,512,256]{2,1,0:T(8,128)(2,1)} %bitcast.36, bf16[2,512,256]{2,1,0:T(8,128)(2,1)} %bitcast.26, s32[2,512]{1,0:T(2,128)} %bitcast.42, ...), custom_call_target="tpu_custom_call", output_to_operand_aliasing={{0}: (8, {})} | custom-call | flops 4000000000 | bytes 8000000 | tf_op jit(solution)/shard_map/gradient_with_faces/pallas_call | solution.py:230
  23.1 1.3 collective-permute-start.2
  24.4 2.0 %collective-permute-done.2 = f32[4,28,8,256]{3,2,1,0:T(8,128)S(1)} collective-permute-done((f32[4,28,8,256]{3,2,1,0:T(8,128)S(1)}, f32[4,28,8,256]{3,2,1,0:T(8,128)S(1)}, u32[]{:S(2)}, u32[]{:S(2)}) %collective-permute-start.2) | collective-permute-done | bytes 917536 | tf_op jit(solution)/shard_map/ppermute | solution.py:495
  26.6 2.7 %collective-permute-start.19 = (f32[3,3,3,256,256]{4,3,2,1,0:T(8,128)S(1)}, f32[3,3,3,256,256]{4,3,2,1,0:T(8,128)S(1)}, u32[]{:S(2)}, u32[]{:S(2)}) collective-permute-start(f32[3,3,3,256,256]{4,3,2,1,0:T(8,128)S(1)} %get-tuple-element.41.corrected), channel_id=1, source_target_pairs={{0,64},{2,66},{4,68},{6,70},{8,72},{10,74},{12,76},{14,78},{128,19... | collective-permute-start | bytes 21233672 | tf_op jit(solution)/shard_map/ppermute | solution.py:495
  29.4 0.7 collective-permute-start.5
  30.0 0.7 collective-permute-start.4
  30.7 0.7 collective-permute-start.3
  31.4 3.6 %input_own.1.refs_5_ = f32[1024,256]{1,0:T(8,128)S(1)} custom-call(s32[2,27]{1,0:T(2,128)} %bitcast.54, bf16[2,512,256]{2,1,0:T(8,128)(2,1)S(1)} %bitcast.27, s32[2,512]{1,0:T(2,128)} %bitcast.43, bf16[3,3,3,256,256]{4,3,2,1,0:T(8,128)(2,1)S(1)} %bitcast.31, f32[4,28,8,256]{3,2,1,0:T(8,128)S(1)} %add.63.refs_4_), custom_call_target="tpu_custom_call" | custom-call | flops 2000000000 | bytes 4000000 | tf_op jit(solution)/shard_map/input_own/pallas_call | solution.py:313
  35.2 0.7 collective-permute-start.6
  35.9 0.7 collective-permute-start.8
  37.9 0.7 collective-permute-start.10
  38.6 0.7 collective-permute-start.9
  39.3 0.8 collective-permute-start.12
  40.2 3.8 %input_below.1.refs_5_ = f32[1024,256]{1,0:T(8,128)S(1)} custom-call(s32[2,27]{1,0:T(2,128)} %bitcast.55, bf16[2,512,256]{2,1,0:T(8,128)(2,1)S(1)} %bitcast.28, s32[2,512]{1,0:T(2,128)} %bitcast.44, bf16[3,3,3,256,256]{4,3,2,1,0:T(8,128)(2,1)S(1)} %bitcast.32, bf16[2,8,16,256]{3,2,1,0:T(8,128)(2,1)S(1)} %collective-permute-done.1.refs_7_.refs_4_, ...), custom_call_target="tpu_custom_call" | custom-call | flops 2000000000 | bytes 4000000 | tf_op jit(solution)/shard_map/input_below/pallas_call | solution.py:313
  44.7 0.7 collective-permute-start.14
  46.1 0.7 collective-permute-start.18
  46.8 0.7 collective-permute-start.17
  47.5 0.7 collective-permute-start.16
  48.1 4.8 %input_above.1 = bf16[2,512,256]{2,1,0:T(8,128)(2,1)} custom-call(s32[2,27]{1,0:T(2,128)} %bitcast.56, bf16[2,512,256]{2,1,0:T(8,128)(2,1)S(1)} %bitcast.29, s32[2,512]{1,0:T(2,128)} %bitcast.45, bf16[3,3,3,256,256]{4,3,2,1,0:T(8,128)(2,1)S(1)} %bitcast.33, bf16[2,8,16,256]{3,2,1,0:T(8,128)(2,1)S(1)} %collective-permute-done.refs_6_.refs_4_, ...), custom_call_target="tpu_custom_call" | custom-call | flops 2000000000 | bytes 4000000 | tf_op jit(solution)/shard_map/input_above/pallas_call | solution.py:313
  53.1 2.6 %right_product.1 = f32[32,256]{1,0:T(8,128)S(1)} custom-call(f32[4,28,8,256]{3,2,1,0:T(8,128)S(1)} %pad_maximum_fusion.part, f32[3,3,3,256,256]{4,3,2,1,0:T(8,128)S(1)} %get-tuple-element.41.corrected, f32[3,3,3,256,256]{4,3,2,1,0:T(8,128)S(1)} %collective-permute-done.19.partner), custom_call_target="tpu_custom_call" | custom-call | tf_op jit(solution)/shard_map/right_product/pallas_call | solution.py:350
  57.8 1.3 collective-permute-start.26
  61.1 60.2 %collective-permute-done.26.given = f32[4,28,8,256]{3,2,1,0:T(8,128)S(1)} collective-permute-done((f32[4,28,8,256]{3,2,1,0:T(8,128)S(1)}, f32[4,28,8,256]{3,2,1,0:T(8,128)S(1)}, u32[]{:S(2)}, u32[]{:S(2)}) %collective-permute-start.26) | collective-permute-done | bytes 917536 | tf_op jit(solution)/shard_map/ppermute | solution.py:495
  123.4 2.4 %half_inverse.1 = (f32[32,32]{1,0:T(8,128)S(1)}, f32[32,32]{1,0:T(8,128)S(1)}) custom-call(f32[4,28,8,256]{3,2,1,0:T(8,128)S(1)} %pad_maximum_fusion.part, f32[4,28,8,256]{3,2,1,0:T(8,128)S(1)} %collective-permute-done.26.given), custom_call_target="tpu_custom_call" | custom-call | tf_op jit(solution)/shard_map/half_inverse/pallas_call | solution.py:393
  126.5 1.4 whole_inverse.1.inverse
  127.9 1.3 collective-permute-start.31
  129.2 21.4 %collective-permute-done.31.right_given = f32[32,256]{1,0:T(8,128)S(1)} collective-permute-done((f32[32,256]{1,0:T(8,128)S(1)}, f32[32,256]{1,0:T(8,128)S(1)}, u32[]{:S(2)}, u32[]{:S(2)}) %collective-permute-start.31) | collective-permute-done | bytes 32800 | tf_op jit(solution)/shard_map/ppermute | solution.py:495
  150.6 3.8 %remaining_error.1 = (bf16[3,3,3,256,256]{4,3,2,1,0:T(8,128)(2,1)}, f32[32,256]{1,0:T(8,128)}) custom-call(f32[4,28,8,256]{3,2,1,0:T(8,128)S(1)} %pad_maximum_fusion.part, f32[4,28,8,256]{3,2,1,0:T(8,128)S(1)} %collective-permute-done.26.given, f32[3,3,3,256,256]{4,3,2,1,0:T(8,128)S(1)} %get-tuple-element.41.corrected, f32[32,256]{1,0:T(8,128)S(1)} %add.83.right, ...), custom_call_target="tpu_custom_call" | custom-call | tf_op jit(solution)/shard_map/remaining_error/pallas_call | solution.py:441
  (62 shorter events, 9.8 us)
Async XLA Ops:
  2.3 10.2 %collective-permute-start = (bf16[2,8,16,256]{3,2,1,0:T(8,128)(2,1)S(1)}, bf16[2,8,16,256]{3,2,1,0:T(8,128)(2,1)S(1)}, u32[]{:S(2)}, u32[]{:S(2)}) collective-permute-start(bf16[2,8,16,256]{3,2,1,0:T(8,128)(2,1)S(1)} %get-tuple-element.31), channel_id=1, source_target_pairs={{0,1},{1,2},{2,3},{3,4},{4,5},{5,6},{6,7},{7,8},{8,9},{9,10},{10,1... | collective-permute-start | bytes 393224 | tf_op jit(solution)/shard_map/ppermute | solution.py:479
  6.5 8.4 %collective-permute-start.1 = (bf16[2,8,16,256]{3,2,1,0:T(8,128)(2,1)S(1)}, bf16[2,8,16,256]{3,2,1,0:T(8,128)(2,1)S(1)}, u32[]{:S(2)}, u32[]{:S(2)}) collective-permute-start(bf16[2,8,16,256]{3,2,1,0:T(8,128)(2,1)S(1)} %get-tuple-element.32), channel_id=1, source_target_pairs={{1,0},{2,1},{3,2},{4,3},{5,4},{6,5},{7,6},{8,7},{9,8},{10,9},{11,1... | collective-permute-start | bytes 393224 | tf_op jit(solution)/shard_map/ppermute | solution.py:479
  23.1 3.4 %collective-permute-start.2 = (f32[4,28,8,256]{3,2,1,0:T(8,128)S(1)}, f32[4,28,8,256]{3,2,1,0:T(8,128)S(1)}, u32[]{:S(2)}, u32[]{:S(2)}) collective-permute-start(f32[4,28,8,256]{3,2,1,0:T(8,128)S(1)} %get-tuple-element.35), channel_id=1, source_target_pairs={{0,64},{2,66},{4,68},{6,70},{8,72},{10,74},{12,76},{14,78},{128,19... | collective-permute-start | bytes 2752520 | tf_op jit(solution)/shard_map/ppermute | solution.py:495
  26.6 26.5 %collective-permute-start.19 = (f32[3,3,3,256,256]{4,3,2,1,0:T(8,128)S(1)}, f32[3,3,3,256,256]{4,3,2,1,0:T(8,128)S(1)}, u32[]{:S(2)}, u32[]{:S(2)}) collective-permute-start(f32[3,3,3,256,256]{4,3,2,1,0:T(8,128)S(1)} %get-tuple-element.41.corrected), channel_id=1, source_target_pairs={{0,64},{2,66},{4,68},{6,70},{8,72},{10,74},{12,76},{14,78},{128,19... | collective-permute-start | bytes 21233672 | tf_op jit(solution)/shard_map/ppermute | solution.py:495
  29.4 5.7 %collective-permute-start.5 = (f32[28,8,256]{2,1,0:T(8,128)S(1)}, f32[28,8,256]{2,1,0:T(8,128)S(1)}, u32[]{:S(2)}, u32[]{:S(2)}) collective-permute-start(f32[28,8,256]{2,1,0:T(8,128)S(1)} %get-tuple-element.59), channel_id=1, source_target_pairs={{64,112},{66,114},{68,116},{70,118},{72,120},{74,122},{76,124},{78... | collective-permute-start | bytes 688136 | tf_op jit(solution)/shard_map/ppermute | solution.py:489
  30.0 5.1 %collective-permute-start.4 = (f32[28,8,256]{2,1,0:T(8,128)S(1)}, f32[28,8,256]{2,1,0:T(8,128)S(1)}, u32[]{:S(2)}, u32[]{:S(2)}) collective-permute-start(f32[28,8,256]{2,1,0:T(8,128)S(1)} %get-tuple-element.60), channel_id=1, source_target_pairs={{64,96},{66,98},{68,100},{70,102},{72,104},{74,106},{76,108},{78,1... | collective-permute-start | bytes 688136 | tf_op jit(solution)/shard_map/ppermute | solution.py:489
  30.7 4.4 %collective-permute-start.3 = (f32[28,8,256]{2,1,0:T(8,128)S(1)}, f32[28,8,256]{2,1,0:T(8,128)S(1)}, u32[]{:S(2)}, u32[]{:S(2)}) collective-permute-start(f32[28,8,256]{2,1,0:T(8,128)S(1)} %get-tuple-element.61), channel_id=1, source_target_pairs={{64,80},{66,82},{68,84},{70,86},{72,88},{74,90},{76,92},{78,94},{1... | collective-permute-start | bytes 688136 | tf_op jit(solution)/shard_map/ppermute | solution.py:489
  35.2 2.0 %collective-permute-start.6 = (f32[7,8,256]{2,1,0:T(8,128)S(1)}, f32[7,8,256]{2,1,0:T(8,128)S(1)}, u32[]{:S(2)}, u32[]{:S(2)}) collective-permute-start(f32[7,8,256]{2,1,0:T(8,128)S(1)} %get-tuple-element.62), channel_id=1, source_target_pairs={{64,192},{66,194},{68,196},{70,198},{72,200},{74,202},{76,204},{78... | collective-permute-start | bytes 172040 | tf_op jit(solution)/shard_map/ppermute | solution.py:489
  35.9 1.4 collective-permute-start.8
  36.5 0.7 collective-permute-start.7
  37.3 2.0 %collective-permute-start.11 = (f32[7,8,256]{2,1,0:T(8,128)S(1)}, f32[7,8,256]{2,1,0:T(8,128)S(1)}, u32[]{:S(2)}, u32[]{:S(2)}) collective-permute-start(f32[7,8,256]{2,1,0:T(8,128)S(1)} %add_add_fusion.1), channel_id=1, source_target_pairs={{64,70},{66,68},{68,66},{70,64},{72,78},{74,76},{76,74},{78,72},{1... | collective-permute-start | bytes 172040 | tf_op jit(solution)/shard_map/ppermute | solution.py:489
  37.9 1.4 collective-permute-start.10
  38.6 0.7 collective-permute-start.9
  39.3 4.6 %collective-permute-start.12 = (f32[7,8,256]{2,1,0:T(8,128)S(1)}, f32[7,8,256]{2,1,0:T(8,128)S(1)}, u32[]{:S(2)}, u32[]{:S(2)}) collective-permute-start(f32[7,8,256]{2,1,0:T(8,128)S(1)} %add_add_fusion.refs_6_), channel_id=1, source_target_pairs={{64,76},{66,78},{68,72},{70,74},{72,68},{74,70},{76,64},{78,66},{1... | collective-permute-start | bytes 172040 | tf_op jit(solution)/shard_map/ppermute | solution.py:489
  44.0 2.1 %collective-permute-start.15 = (f32[7,8,256]{2,1,0:T(8,128)S(1)}, f32[7,8,256]{2,1,0:T(8,128)S(1)}, u32[]{:S(2)}, u32[]{:S(2)}) collective-permute-start(f32[7,8,256]{2,1,0:T(8,128)S(1)} %add.73), channel_id=1, source_target_pairs={{64,193},{66,195},{68,197},{70,199},{72,201},{74,203},{76,205},{78... | collective-permute-start | bytes 172040 | tf_op jit(solution)/shard_map/ppermute | solution.py:489
  44.7 1.4 collective-permute-start.14
  45.3 0.7 collective-permute-start.13
  46.1 6.9 %collective-permute-start.18 = (f32[28,8,256]{2,1,0:T(8,128)S(1)}, f32[28,8,256]{2,1,0:T(8,128)S(1)}, u32[]{:S(2)}, u32[]{:S(2)}) collective-permute-start(f32[28,8,256]{2,1,0:T(8,128)S(1)} %constant_dynamic-update-slice_fusion.refs_6_), channel_id=1, source_target_pairs={{64,112},{66,114},{68,116},{70,118},{72,120},{74,122},{76,124},{78... | collective-permute-start | bytes 688136 | tf_op jit(solution)/shard_map/ppermute | solution.py:489
  46.8 6.2 %collective-permute-start.17 = (f32[28,8,256]{2,1,0:T(8,128)S(1)}, f32[28,8,256]{2,1,0:T(8,128)S(1)}, u32[]{:S(2)}, u32[]{:S(2)}) collective-permute-start(f32[28,8,256]{2,1,0:T(8,128)S(1)} %constant_dynamic-update-slice_fusion.refs_6_), channel_id=1, source_target_pairs={{64,96},{66,98},{68,100},{70,102},{72,104},{74,106},{76,108},{78,1... | collective-permute-start | bytes 688136 | tf_op jit(solution)/shard_map/ppermute | solution.py:489
  47.5 5.5 %collective-permute-start.16 = (f32[28,8,256]{2,1,0:T(8,128)S(1)}, f32[28,8,256]{2,1,0:T(8,128)S(1)}, u32[]{:S(2)}, u32[]{:S(2)}) collective-permute-start(f32[28,8,256]{2,1,0:T(8,128)S(1)} %constant_dynamic-update-slice_fusion.refs_6_), channel_id=1, source_target_pairs={{64,80},{66,82},{68,84},{70,86},{72,88},{74,90},{76,92},{78,94},{1... | collective-permute-start | bytes 688136 | tf_op jit(solution)/shard_map/ppermute | solution.py:489
  55.7 2.0 %collective-permute-start.22 = (f32[32,256]{1,0:T(8,128)S(1)}, f32[32,256]{1,0:T(8,128)S(1)}, u32[]{:S(2)}, u32[]{:S(2)}) collective-permute-start(f32[32,256]{1,0:T(8,128)S(1)} %right_product.1), channel_id=1, source_target_pairs={{64,112},{66,114},{68,116},{70,118},{72,120},{74,122},{76,124},{78... | collective-permute-start | bytes 98312 | tf_op jit(solution)/shard_map/ppermute | solution.py:489
  56.4 1.4 collective-permute-start.21
  57.1 0.7 collective-permute-start.20
  57.8 63.6 %collective-permute-start.26 = (f32[4,28,8,256]{3,2,1,0:T(8,128)S(1)}, f32[4,28,8,256]{3,2,1,0:T(8,128)S(1)}, u32[]{:S(2)}, u32[]{:S(2)}) collective-permute-start(f32[4,28,8,256]{3,2,1,0:T(8,128)S(1)} %pad_maximum_fusion.part), channel_id=1, source_target_pairs={{64,0},{66,2},{68,4},{70,6},{72,8},{74,10},{76,12},{78,14},{192,12... | collective-permute-start | bytes 2752520 | tf_op jit(solution)/shard_map/ppermute | solution.py:495
  59.1 2.0 %collective-permute-start.25 = (f32[32,256]{1,0:T(8,128)S(1)}, f32[32,256]{1,0:T(8,128)S(1)}, u32[]{:S(2)}, u32[]{:S(2)}) collective-permute-start(f32[32,256]{1,0:T(8,128)S(1)} %add_add_fusion.4), channel_id=1, source_target_pairs={{64,193},{66,195},{68,197},{70,199},{72,201},{74,203},{76,205},{78... | collective-permute-start | bytes 98312 | tf_op jit(solution)/shard_map/ppermute | solution.py:489
  59.8 1.4 collective-permute-start.24
  60.4 0.7 collective-permute-start.23
  121.4 4.4 %collective-permute-start.29 = (f32[32,256]{1,0:T(8,128)S(1)}, f32[32,256]{1,0:T(8,128)S(1)}, u32[]{:S(2)}, u32[]{:S(2)}) collective-permute-start(f32[32,256]{1,0:T(8,128)S(1)} %add_add_fusion.3), channel_id=1, source_target_pairs={{64,70},{66,68},{68,66},{70,64},{72,78},{74,76},{76,74},{78,72},{1... | collective-permute-start | bytes 98312 | tf_op jit(solution)/shard_map/ppermute | solution.py:489
  122.0 3.7 %collective-permute-start.28 = (f32[32,256]{1,0:T(8,128)S(1)}, f32[32,256]{1,0:T(8,128)S(1)}, u32[]{:S(2)}, u32[]{:S(2)}) collective-permute-start(f32[32,256]{1,0:T(8,128)S(1)} %add_add_fusion.3), channel_id=1, source_target_pairs={{64,68},{66,70},{68,64},{70,66},{72,76},{74,78},{76,72},{78,74},{1... | collective-permute-start | bytes 98312 | tf_op jit(solution)/shard_map/ppermute | solution.py:489
  122.7 3.1 %collective-permute-start.27 = (f32[32,256]{1,0:T(8,128)S(1)}, f32[32,256]{1,0:T(8,128)S(1)}, u32[]{:S(2)}, u32[]{:S(2)}) collective-permute-start(f32[32,256]{1,0:T(8,128)S(1)} %add_add_fusion.3), channel_id=1, source_target_pairs={{64,66},{66,64},{68,70},{70,68},{72,74},{74,72},{76,78},{78,76},{1... | collective-permute-start | bytes 98312 | tf_op jit(solution)/shard_map/ppermute | solution.py:489
  125.8 2.1 %collective-permute-start.30 = (f32[32,256]{1,0:T(8,128)S(1)}, f32[32,256]{1,0:T(8,128)S(1)}, u32[]{:S(2)}, u32[]{:S(2)}) collective-permute-start(f32[32,256]{1,0:T(8,128)S(1)} %add_add_fusion.2.refs_0_), channel_id=1, source_target_pairs={{64,76},{66,78},{68,72},{70,74},{72,68},{74,70},{76,64},{78,66},{1... | collective-permute-start | bytes 98312 | tf_op jit(solution)/shard_map/ppermute | solution.py:489
  127.9 22.7 %collective-permute-start.31 = (f32[32,256]{1,0:T(8,128)S(1)}, f32[32,256]{1,0:T(8,128)S(1)}, u32[]{:S(2)}, u32[]{:S(2)}) collective-permute-start(f32[32,256]{1,0:T(8,128)S(1)} %add.83.right), channel_id=1, source_target_pairs={{64,0},{66,2},{68,4},{70,6},{72,8},{74,10},{76,12},{78,14},{192,12... | collective-permute-start | bytes 98312 | tf_op jit(solution)/shard_map/ppermute | solution.py:495
  (2 other events, 33.1 us)

commit v6 on v5

--- a/solution.py
+++ b/solution.py
@@ -45,6 +45,9 @@
                 first, stride = (128 if side_z < 0 else 144), EDGE
             for which in (0, 1):
                 slot = slots[which, (step_x + 1) * 9 + (side_y + 1) * 3 + side_z + 1]
+                if side_z:
+                    end = 0 if side_z < 0 else lax.axis_size("space") - 1
+                    slot = jnp.where(lax.axis_index("space") == end, -1, slot)
                 base = jnp.where(slot < 0, -4096, slot * stride + first)
                 rows = jnp.where(in_y & in_z & (brick == which), base + offset, rows)
     return rows
@@ -476,22 +479,24 @@
 
 def shifted(value, by):
     devices = lax.axis_size("space")
-    return lax.ppermute(value, "space", [(i, i + by) for i in range(devices) if 0 <= i + by < devices])
+    return lax.ppermute(value, "space", [(i, (i + by) % devices) for i in range(devices)])
 
 
 def place(core, x, y, z):
     return (y % 2 * 2 + core) * 64 + (x * 8 + z) * 2 + y // 2
 
 
+CHIPS = [(x, y, z) for x in range(4) for y in range(4) for z in range(8)]
+
+
 def swapped(value, x=0, y=0, z=0):
-    chips = [(i, j, k) for i in range(4) for j in range(4) for k in range(8)]
-    pairs = [(place(1, i, j, k), place(1, i ^ x, j ^ y, k ^ z)) for i, j, k in chips]
+    pairs = [(place(1, i, j, k), place(1, i ^ x, j ^ y, k ^ z)) for i, j, k in CHIPS]
+    pairs += [(place(0, *chip), place(0, *chip)) for chip in CHIPS]
     return lax.ppermute(value, ("dp", "space"), pairs)
 
 
-def handed(value, to):
-    chips = [(i, j, k) for i in range(4) for j in range(4) for k in range(8)]
-    pairs = [(place(1 - to, *chip), place(to, *chip)) for chip in chips]
+def handed(value):
+    pairs = [(place(core, *chip), place(1 - core, *chip)) for chip in CHIPS for core in (0, 1)]
     return lax.ppermute(value, ("dp", "space"), pairs)
 
 
@@ -518,10 +523,10 @@
     corrected, factor = local_gradient((0,), *fixed)
     corrected, factor = local_gradient((-1, 1), *fixed, lower, upper, in_vmem(corrected), factor)
 
-    part = factor + handed(factor, to=1)
+    part = factor + handed(factor)
     part, travelling = lax.optimization_barrier((part, corrected))
     arrived = [swapped(part[k], x=k) for k in (1, 2, 3)]
-    partner = handed(travelling, to=1)
+    partner = handed(travelling)
     total = input_gradient(0, False, slots, gradient, occupied, weight, tie=part)
     part, total = lax.optimization_barrier((added([part[0]] + arrived), total))
     part = part.reshape(4, 7, 8, 256)
@@ -540,7 +545,7 @@
     right = right_product(part, corrected, partner)
     right, part = lax.optimization_barrier((summed_among(right, ALONG_X), part))
     arrived = [swapped(right, **bits) for bits in ALONG_Y]
-    given = handed(part, to=0)
+    given = handed(part)
     right, given = lax.optimization_barrier((added([right] + arrived), given))
     arrived = [swapped(right, **bits) for bits in ALONG_Z]
     halves = half_inverse(part, given)
@@ -548,7 +553,7 @@
     arrived = swapped(right, z=6)
     inverse = whole_inverse(*halves, tie=right)
     right, inverse = lax.optimization_barrier((right + arrived, inverse))
-    right_given = handed(right, to=0)
+    right_given = handed(right)
     new_error, q_rows = remaining_error(part, given, corrected, right, right_given, inverse)
     return (input_grad[None], q_rows.T, new_error.reshape(1, 1, 6912, 256))
 

time: 158 us -> 151 us (0.956)
  the two profiles are of different devices: /device:TPU:8 before, /device:TPU:1 now
where the time goes in v6:
time: 151 us; the launch traced here: 150 us
  starting transfers between devices  94 us (62%)
  Pallas kernels  37.1 us (25%)
  waiting for transfers between devices  17.5 us (12%)
    ppermute x26, starting transfers between devices, swapped(): return lax.ppermute(value, ('dp', 'space'), pairs)  81 us
    ppermute x26, waiting for transfers between devices, swapped(): return lax.ppermute(value, ('dp', 'space'), pairs)  14.2 us
    pallas_call x2, Pallas kernels, local_gradient(): pl.pallas_call(functools.partial(gradient_kernel, sides, width), grid=(le...  12.9 us
    pallas_call x3, Pallas kernels, input_gradient(): pl.pallas_call(functools.partial(input_kernel, side, last), grid=(3,), in...  12.2 us
    ppermute x2, starting transfers between devices, shifted(): lax.ppermute(value, 'space', [(i, (i + by) % devices) for i in range(devi...  11.4 us
    pallas_call x1, Pallas kernels, remaining_error(): pl.pallas_call(error_kernel, grid=(3,), in_specs=[FACTOR_SPEC, FACTOR_SPE...  3.8 us
    ppermute x4, waiting for transfers between devices, handed(): return lax.ppermute(value, ('dp', 'space'), pairs)  3.3 us
  transfers between devices with their start and end apart: 32, of which 11 were waited for; matrix products, arithmetic and copies ran while one was open for 0% of the time, Pallas kernels for 14%

profile of v6, /device:TPU:1, one launch (start us, length us, event | category | flops | bytes accessed | tf_op | source)
XLA Modules:
  0.0 150.1 jit_solution(12610130624346915174)
XLA Ops:
  2.3 3.8 %collective-permute-start = (bf16[2,8,16,256]{3,2,1,0:T(8,128)(2,1)S(1)}, bf16[2,8,16,256]{3,2,1,0:T(8,128)(2,1)S(1)}, u32[]{:S(2)}, u32[]{:S(2)}) collective-permute-start(bf16[2,8,16,256]{3,2,1,0:T(8,128)(2,1)S(1)} %get-tuple-element.31), channel_id=1, source_target_pairs={{0,1},{1,2},{2,3},{3,4},{4,5},{5,6},{6,7},{7,8},{8,9},{9,10},{10,1... | collective-permute-start | bytes 393224 | tf_op jit(solution)/shard_map/ppermute | solution.py:482
  6.1 7.6 %collective-permute-start.1 = (bf16[2,8,16,256]{3,2,1,0:T(8,128)(2,1)S(1)}, bf16[2,8,16,256]{3,2,1,0:T(8,128)(2,1)S(1)}, u32[]{:S(2)}, u32[]{:S(2)}) collective-permute-start(bf16[2,8,16,256]{3,2,1,0:T(8,128)(2,1)S(1)} %get-tuple-element.32), channel_id=1, source_target_pairs={{0,63},{1,0},{2,1},{3,2},{4,3},{5,4},{6,5},{7,6},{8,7},{9,8},{10,9... | collective-permute-start | bytes 393224 | tf_op jit(solution)/shard_map/ppermute | solution.py:482
  13.7 4.7 %gradient_own.1 = (f32[3,3,3,256,256]{4,3,2,1,0:T(8,128)S(1)}, f32[4,28,8,256]{3,2,1,0:T(8,128)S(1)}) custom-call(s32[2,27]{1,0:T(2,128)} %bitcast.52, bf16[2,512,256]{2,1,0:T(8,128)(2,1)} %bitcast.35, bf16[2,512,256]{2,1,0:T(8,128)(2,1)} %bitcast.25, s32[2,512]{1,0:T(2,128)} %bitcast.41, f32[32,256]{1,0:T(8,128)} %bitcast.49, ...), custom_call_target="tpu_custom_call" | custom-call | flops 2000000000 | bytes 4000000 | tf_op jit(solution)/shard_map/gradient_own/pallas_call | solution.py:233
  18.5 8.2 %gradient_with_faces.1 = (f32[3,3,3,256,256]{4,3,2,1,0:T(8,128)S(1)}, f32[4,28,8,256]{3,2,1,0:T(8,128)S(1)}) custom-call(s32[2,27]{1,0:T(2,128)} %bitcast.53, bf16[2,512,256]{2,1,0:T(8,128)(2,1)} %bitcast.36, bf16[2,512,256]{2,1,0:T(8,128)(2,1)} %bitcast.26, s32[2,512]{1,0:T(2,128)} %bitcast.42, ...), custom_call_target="tpu_custom_call", output_to_operand_aliasing={{0}: (8, {})} | custom-call | flops 4000000000 | bytes 8000000 | tf_op jit(solution)/shard_map/gradient_with_faces/pallas_call | solution.py:233
  30.5 2.5 %collective-permute-start.5 = (f32[28,8,256]{2,1,0:T(8,128)S(1)}, f32[28,8,256]{2,1,0:T(8,128)S(1)}, u32[]{:S(2)}, u32[]{:S(2)}) collective-permute-start(f32[28,8,256]{2,1,0:T(8,128)S(1)} %get-tuple-element.59), channel_id=1, source_target_pairs={{64,112},{66,114},{68,116},{70,118},{72,120},{74,122},{76,124},{78... | collective-permute-start | bytes 688136 | tf_op jit(solution)/shard_map/ppermute | solution.py:495
  35.1 4.4 %collective-permute-start.3 = (f32[28,8,256]{2,1,0:T(8,128)S(1)}, f32[28,8,256]{2,1,0:T(8,128)S(1)}, u32[]{:S(2)}, u32[]{:S(2)}) collective-permute-start(f32[28,8,256]{2,1,0:T(8,128)S(1)} %get-tuple-element.61), channel_id=1, source_target_pairs={{64,80},{66,82},{68,84},{70,86},{72,88},{74,90},{76,92},{78,94},{1... | collective-permute-start | bytes 688136 | tf_op jit(solution)/shard_map/ppermute | solution.py:495
  39.5 3.6 %input_own.1.refs_5_ = f32[1024,256]{1,0:T(8,128)S(1)} custom-call(s32[2,27]{1,0:T(2,128)} %bitcast.54, bf16[2,512,256]{2,1,0:T(8,128)(2,1)S(1)} %bitcast.27, s32[2,512]{1,0:T(2,128)} %bitcast.43, bf16[3,3,3,256,256]{4,3,2,1,0:T(8,128)(2,1)S(1)} %bitcast.31, f32[4,28,8,256]{3,2,1,0:T(8,128)S(1)} %add.63.refs_4_), custom_call_target="tpu_custom_call" | custom-call | flops 2000000000 | bytes 4000000 | tf_op jit(solution)/shard_map/input_own/pallas_call | solution.py:316
  43.5 2.3 %collective-permute-start.6 = (f32[7,8,256]{2,1,0:T(8,128)S(1)}, f32[7,8,256]{2,1,0:T(8,128)S(1)}, u32[]{:S(2)}, u32[]{:S(2)}) collective-permute-start(f32[7,8,256]{2,1,0:T(8,128)S(1)} %get-tuple-element.62), channel_id=1, source_target_pairs={{64,192},{66,194},{68,196},{70,198},{72,200},{74,202},{76,204},{78... | collective-permute-start | bytes 172040 | tf_op jit(solution)/shard_map/ppermute | solution.py:495
  47.7 4.8 %collective-permute-start.7 = (f32[7,8,256]{2,1,0:T(8,128)S(1)}, f32[7,8,256]{2,1,0:T(8,128)S(1)}, u32[]{:S(2)}, u32[]{:S(2)}) collective-permute-start(f32[7,8,256]{2,1,0:T(8,128)S(1)} %get-tuple-element.64), channel_id=1, source_target_pairs={{64,65},{66,67},{68,69},{70,71},{72,73},{74,75},{76,77},{78,79},{1... | collective-permute-start | bytes 172040 | tf_op jit(solution)/shard_map/ppermute | solution.py:495
  54.2 6.1 %collective-permute-start.11 = (f32[7,8,256]{2,1,0:T(8,128)S(1)}, f32[7,8,256]{2,1,0:T(8,128)S(1)}, u32[]{:S(2)}, u32[]{:S(2)}) collective-permute-start(f32[7,8,256]{2,1,0:T(8,128)S(1)} %add_add_fusion.1), channel_id=1, source_target_pairs={{64,70},{66,68},{68,66},{70,64},{72,78},{74,76},{76,74},{78,72},{1... | collective-permute-start | bytes 172040 | tf_op jit(solution)/shard_map/ppermute | solution.py:495
  67.1 5.2 %collective-permute-start.12 = (f32[7,8,256]{2,1,0:T(8,128)S(1)}, f32[7,8,256]{2,1,0:T(8,128)S(1)}, u32[]{:S(2)}, u32[]{:S(2)}) collective-permute-start(f32[7,8,256]{2,1,0:T(8,128)S(1)} %add_add_fusion.refs_6_), channel_id=1, source_target_pairs={{64,76},{66,78},{68,72},{70,74},{72,68},{74,70},{76,64},{78,66},{1... | collective-permute-start | bytes 172040 | tf_op jit(solution)/shard_map/ppermute | solution.py:495
  72.3 3.8 %input_below.1.refs_5_ = f32[1024,256]{1,0:T(8,128)S(1)} custom-call(s32[2,27]{1,0:T(2,128)} %bitcast.55, bf16[2,512,256]{2,1,0:T(8,128)(2,1)S(1)} %bitcast.28, s32[2,512]{1,0:T(2,128)} %bitcast.44, bf16[3,3,3,256,256]{4,3,2,1,0:T(8,128)(2,1)S(1)} %bitcast.32, bf16[2,8,16,256]{3,2,1,0:T(8,128)(2,1)S(1)} %collective-permute-done.1.refs_7_.refs_4_, ...), custom_call_target="tpu_custom_call" | custom-call | flops 2000000000 | bytes 4000000 | tf_op jit(solution)/shard_map/input_below/pallas_call | solution.py:316
  76.1 2.6 %collective-permute-start.15 = (f32[7,8,256]{2,1,0:T(8,128)S(1)}, f32[7,8,256]{2,1,0:T(8,128)S(1)}, u32[]{:S(2)}, u32[]{:S(2)}) collective-permute-start(f32[7,8,256]{2,1,0:T(8,128)S(1)} %add.73), channel_id=1, source_target_pairs={{64,193},{66,195},{68,197},{70,199},{72,201},{74,203},{76,205},{78... | collective-permute-start | bytes 172040 | tf_op jit(solution)/shard_map/ppermute | solution.py:495
  78.7 3.4 %collective-permute-start.14 = (f32[7,8,256]{2,1,0:T(8,128)S(1)}, f32[7,8,256]{2,1,0:T(8,128)S(1)}, u32[]{:S(2)}, u32[]{:S(2)}) collective-permute-start(f32[7,8,256]{2,1,0:T(8,128)S(1)} %add.73), channel_id=1, source_target_pairs={{64,65},{66,67},{68,69},{70,71},{72,73},{74,75},{76,77},{78,79},{1... | collective-permute-start | bytes 172040 | tf_op jit(solution)/shard_map/ppermute | solution.py:495
  82.1 3.0 %collective-permute-start.13 = (f32[7,8,256]{2,1,0:T(8,128)S(1)}, f32[7,8,256]{2,1,0:T(8,128)S(1)}, u32[]{:S(2)}, u32[]{:S(2)}) collective-permute-start(f32[7,8,256]{2,1,0:T(8,128)S(1)} %add.73), channel_id=1, source_target_pairs={{64,192},{66,194},{68,196},{70,198},{72,200},{74,202},{76,204},{78... | collective-permute-start | bytes 172040 | tf_op jit(solution)/shard_map/ppermute | solution.py:495
  87.1 4.2 %collective-permute-start.18 = (f32[28,8,256]{2,1,0:T(8,128)S(1)}, f32[28,8,256]{2,1,0:T(8,128)S(1)}, u32[]{:S(2)}, u32[]{:S(2)}) collective-permute-start(f32[28,8,256]{2,1,0:T(8,128)S(1)} %constant_dynamic-update-slice_fusion.refs_6_), channel_id=1, source_target_pairs={{64,112},{66,114},{68,116},{70,118},{72,120},{74,122},{76,124},{78... | collective-permute-start | bytes 688136 | tf_op jit(solution)/shard_map/ppermute | solution.py:495
  91.3 2.6 %collective-permute-start.17 = (f32[28,8,256]{2,1,0:T(8,128)S(1)}, f32[28,8,256]{2,1,0:T(8,128)S(1)}, u32[]{:S(2)}, u32[]{:S(2)}) collective-permute-start(f32[28,8,256]{2,1,0:T(8,128)S(1)} %constant_dynamic-update-slice_fusion.refs_6_), channel_id=1, source_target_pairs={{64,96},{66,98},{68,100},{70,102},{72,104},{74,106},{76,108},{78,1... | collective-permute-start | bytes 688136 | tf_op jit(solution)/shard_map/ppermute | solution.py:495
  96.1 4.8 %input_above.1 = bf16[2,512,256]{2,1,0:T(8,128)(2,1)} custom-call(s32[2,27]{1,0:T(2,128)} %bitcast.56, bf16[2,512,256]{2,1,0:T(8,128)(2,1)S(1)} %bitcast.29, s32[2,512]{1,0:T(2,128)} %bitcast.45, bf16[3,3,3,256,256]{4,3,2,1,0:T(8,128)(2,1)S(1)} %bitcast.33, bf16[2,8,16,256]{3,2,1,0:T(8,128)(2,1)S(1)} %collective-permute-done.refs_6_.refs_4_, ...), custom_call_target="tpu_custom_call" | custom-call | flops 2000000000 | bytes 4000000 | tf_op jit(solution)/shard_map/input_above/pallas_call | solution.py:316
  101.0 2.6 %right_product.1 = f32[32,256]{1,0:T(8,128)S(1)} custom-call(f32[4,28,8,256]{3,2,1,0:T(8,128)S(1)} %pad_maximum_fusion.part, f32[3,3,3,256,256]{4,3,2,1,0:T(8,128)S(1)} %get-tuple-element.41.corrected, f32[3,3,3,256,256]{4,3,2,1,0:T(8,128)S(1)} %collective-permute-done.19.partner), custom_call_target="tpu_custom_call" | custom-call | tf_op jit(solution)/shard_map/right_product/pallas_call | solution.py:353
  103.7 4.2 %collective-permute-start.22 = (f32[32,256]{1,0:T(8,128)S(1)}, f32[32,256]{1,0:T(8,128)S(1)}, u32[]{:S(2)}, u32[]{:S(2)}) collective-permute-start(f32[32,256]{1,0:T(8,128)S(1)} %right_product.1), channel_id=1, source_target_pairs={{64,112},{66,114},{68,116},{70,118},{72,120},{74,122},{76,124},{78... | collective-permute-start | bytes 98312 | tf_op jit(solution)/shard_map/ppermute | solution.py:495
  107.9 2.6 %collective-permute-start.21 = (f32[32,256]{1,0:T(8,128)S(1)}, f32[32,256]{1,0:T(8,128)S(1)}, u32[]{:S(2)}, u32[]{:S(2)}) collective-permute-start(f32[32,256]{1,0:T(8,128)S(1)} %right_product.1), channel_id=1, source_target_pairs={{64,96},{66,98},{68,100},{70,102},{72,104},{74,106},{76,108},{78,1... | collective-permute-start | bytes 98312 | tf_op jit(solution)/shard_map/ppermute | solution.py:495
  115.2 2.5 %collective-permute-start.25 = (f32[32,256]{1,0:T(8,128)S(1)}, f32[32,256]{1,0:T(8,128)S(1)}, u32[]{:S(2)}, u32[]{:S(2)}) collective-permute-start(f32[32,256]{1,0:T(8,128)S(1)} %add_add_fusion.4), channel_id=1, source_target_pairs={{64,193},{66,195},{68,197},{70,199},{72,201},{74,203},{76,205},{78... | collective-permute-start | bytes 98312 | tf_op jit(solution)/shard_map/ppermute | solution.py:495
  117.8 4.2 %collective-permute-start.24 = (f32[32,256]{1,0:T(8,128)S(1)}, f32[32,256]{1,0:T(8,128)S(1)}, u32[]{:S(2)}, u32[]{:S(2)}) collective-permute-start(f32[32,256]{1,0:T(8,128)S(1)} %add_add_fusion.4), channel_id=1, source_target_pairs={{64,65},{66,67},{68,69},{70,71},{72,73},{74,75},{76,77},{78,79},{1... | collective-permute-start | bytes 98312 | tf_op jit(solution)/shard_map/ppermute | solution.py:495
  121.9 2.3 %collective-permute-start.23 = (f32[32,256]{1,0:T(8,128)S(1)}, f32[32,256]{1,0:T(8,128)S(1)}, u32[]{:S(2)}, u32[]{:S(2)}) collective-permute-start(f32[32,256]{1,0:T(8,128)S(1)} %add_add_fusion.4), channel_id=1, source_target_pairs={{64,192},{66,194},{68,196},{70,198},{72,200},{74,202},{76,204},{78... | collective-permute-start | bytes 98312 | tf_op jit(solution)/shard_map/ppermute | solution.py:495
  124.3 2.3 %collective-permute-done.23 = f32[32,256]{1,0:T(8,128)S(1)} collective-permute-done((f32[32,256]{1,0:T(8,128)S(1)}, f32[32,256]{1,0:T(8,128)S(1)}, u32[]{:S(2)}, u32[]{:S(2)}) %collective-permute-start.23) | collective-permute-done | bytes 32800 | tf_op jit(solution)/shard_map/ppermute | solution.py:495
  126.6 2.8 %collective-permute-start.29 = (f32[32,256]{1,0:T(8,128)S(1)}, f32[32,256]{1,0:T(8,128)S(1)}, u32[]{:S(2)}, u32[]{:S(2)}) collective-permute-start(f32[32,256]{1,0:T(8,128)S(1)} %add_add_fusion.3), channel_id=1, source_target_pairs={{64,70},{66,68},{68,66},{70,64},{72,78},{74,76},{76,74},{78,72},{1... | collective-permute-start | bytes 98312 | tf_op jit(solution)/shard_map/ppermute | solution.py:495
  129.4 2.3 %collective-permute-start.28 = (f32[32,256]{1,0:T(8,128)S(1)}, f32[32,256]{1,0:T(8,128)S(1)}, u32[]{:S(2)}, u32[]{:S(2)}) collective-permute-start(f32[32,256]{1,0:T(8,128)S(1)} %add_add_fusion.3), channel_id=1, source_target_pairs={{64,68},{66,70},{68,64},{70,66},{72,76},{74,78},{76,72},{78,74},{1... | collective-permute-start | bytes 98312 | tf_op jit(solution)/shard_map/ppermute | solution.py:495
  131.6 4.3 %collective-permute-start.27 = (f32[32,256]{1,0:T(8,128)S(1)}, f32[32,256]{1,0:T(8,128)S(1)}, u32[]{:S(2)}, u32[]{:S(2)}) collective-permute-start(f32[32,256]{1,0:T(8,128)S(1)} %add_add_fusion.3), channel_id=1, source_target_pairs={{64,66},{66,64},{68,70},{70,68},{72,74},{74,72},{76,78},{78,76},{1... | collective-permute-start | bytes 98312 | tf_op jit(solution)/shard_map/ppermute | solution.py:495
  135.9 2.4 %half_inverse.1 = (f32[32,32]{1,0:T(8,128)S(1)}, f32[32,32]{1,0:T(8,128)S(1)}) custom-call(f32[4,28,8,256]{3,2,1,0:T(8,128)S(1)} %pad_maximum_fusion.part, f32[4,28,8,256]{3,2,1,0:T(8,128)S(1)} %collective-permute-done.26.given), custom_call_target="tpu_custom_call" | custom-call | tf_op jit(solution)/shard_map/half_inverse/pallas_call | solution.py:396
  138.4 2.5 %collective-permute-start.30 = (f32[32,256]{1,0:T(8,128)S(1)}, f32[32,256]{1,0:T(8,128)S(1)}, u32[]{:S(2)}, u32[]{:S(2)}) collective-permute-start(f32[32,256]{1,0:T(8,128)S(1)} %add_add_fusion.2.refs_0_), channel_id=1, source_target_pairs={{64,76},{66,78},{68,72},{70,74},{72,68},{74,70},{76,64},{78,66},{1... | collective-permute-start | bytes 98312 | tf_op jit(solution)/shard_map/ppermute | solution.py:495
  142.3 2.8 %collective-permute-done.30 = f32[32,256]{1,0:T(8,128)S(1)} collective-permute-done((f32[32,256]{1,0:T(8,128)S(1)}, f32[32,256]{1,0:T(8,128)S(1)}, u32[]{:S(2)}, u32[]{:S(2)}) %collective-permute-start.30) | collective-permute-done | bytes 32800 | tf_op jit(solution)/shard_map/ppermute | solution.py:495
  146.3 3.8 %remaining_error.1 = (bf16[3,3,3,256,256]{4,3,2,1,0:T(8,128)(2,1)}, f32[32,256]{1,0:T(8,128)}) custom-call(f32[4,28,8,256]{3,2,1,0:T(8,128)S(1)} %pad_maximum_fusion.part, f32[4,28,8,256]{3,2,1,0:T(8,128)S(1)} %collective-permute-done.26.given, f32[3,3,3,256,256]{4,3,2,1,0:T(8,128)S(1)} %get-tuple-element.41.corrected, f32[32,256]{1,0:T(8,128)S(1)} %add.83.right, ...), custom_call_target="tpu_custom_call" | custom-call | tf_op jit(solution)/shard_map/remaining_error/pallas_call | solution.py:444
  (62 shorter events, 30.0 us)
Async XLA Ops:
  2.3 16.1 %collective-permute-start = (bf16[2,8,16,256]{3,2,1,0:T(8,128)(2,1)S(1)}, bf16[2,8,16,256]{3,2,1,0:T(8,128)(2,1)S(1)}, u32[]{:S(2)}, u32[]{:S(2)}) collective-permute-start(bf16[2,8,16,256]{3,2,1,0:T(8,128)(2,1)S(1)} %get-tuple-element.31), channel_id=1, source_target_pairs={{0,1},{1,2},{2,3},{3,4},{4,5},{5,6},{6,7},{7,8},{8,9},{9,10},{10,1... | collective-permute-start | bytes 393224 | tf_op jit(solution)/shard_map/ppermute | solution.py:482
  6.1 12.3 %collective-permute-start.1 = (bf16[2,8,16,256]{3,2,1,0:T(8,128)(2,1)S(1)}, bf16[2,8,16,256]{3,2,1,0:T(8,128)(2,1)S(1)}, u32[]{:S(2)}, u32[]{:S(2)}) collective-permute-start(bf16[2,8,16,256]{3,2,1,0:T(8,128)(2,1)S(1)} %get-tuple-element.32), channel_id=1, source_target_pairs={{0,63},{1,0},{2,1},{3,2},{4,3},{5,4},{6,5},{7,6},{8,7},{9,8},{10,9... | collective-permute-start | bytes 393224 | tf_op jit(solution)/shard_map/ppermute | solution.py:482
  26.7 3.1 %collective-permute-start.2 = (f32[4,28,8,256]{3,2,1,0:T(8,128)S(1)}, f32[4,28,8,256]{3,2,1,0:T(8,128)S(1)}, u32[]{:S(2)}, u32[]{:S(2)}) collective-permute-start(f32[4,28,8,256]{3,2,1,0:T(8,128)S(1)} %get-tuple-element.35), channel_id=1, source_target_pairs={{0,64},{64,0},{2,66},{66,2},{4,68},{68,4},{6,70},{70,6},{8,72},{72... | collective-permute-start | bytes 2752520 | tf_op jit(solution)/shard_map/ppermute | solution.py:500
  29.9 71.1 %collective-permute-start.19 = (f32[3,3,3,256,256]{4,3,2,1,0:T(8,128)S(1)}, f32[3,3,3,256,256]{4,3,2,1,0:T(8,128)S(1)}, u32[]{:S(2)}, u32[]{:S(2)}) collective-permute-start(f32[3,3,3,256,256]{4,3,2,1,0:T(8,128)S(1)} %get-tuple-element.41.corrected), channel_id=1, source_target_pairs={{0,64},{64,0},{2,66},{66,2},{4,68},{68,4},{6,70},{70,6},{8,72},{72... | collective-permute-start | bytes 21233672 | tf_op jit(solution)/shard_map/ppermute | solution.py:500
  30.5 12.7 %collective-permute-start.5 = (f32[28,8,256]{2,1,0:T(8,128)S(1)}, f32[28,8,256]{2,1,0:T(8,128)S(1)}, u32[]{:S(2)}, u32[]{:S(2)}) collective-permute-start(f32[28,8,256]{2,1,0:T(8,128)S(1)} %get-tuple-element.59), channel_id=1, source_target_pairs={{64,112},{66,114},{68,116},{70,118},{72,120},{74,122},{76,124},{78... | collective-permute-start | bytes 688136 | tf_op jit(solution)/shard_map/ppermute | solution.py:495
  32.9 10.2 %collective-permute-start.4 = (f32[28,8,256]{2,1,0:T(8,128)S(1)}, f32[28,8,256]{2,1,0:T(8,128)S(1)}, u32[]{:S(2)}, u32[]{:S(2)}) collective-permute-start(f32[28,8,256]{2,1,0:T(8,128)S(1)} %get-tuple-element.60), channel_id=1, source_target_pairs={{64,96},{66,98},{68,100},{70,102},{72,104},{74,106},{76,108},{78,1... | collective-permute-start | bytes 688136 | tf_op jit(solution)/shard_map/ppermute | solution.py:495
  35.1 8.3 %collective-permute-start.3 = (f32[28,8,256]{2,1,0:T(8,128)S(1)}, f32[28,8,256]{2,1,0:T(8,128)S(1)}, u32[]{:S(2)}, u32[]{:S(2)}) collective-permute-start(f32[28,8,256]{2,1,0:T(8,128)S(1)} %get-tuple-element.61), channel_id=1, source_target_pairs={{64,80},{66,82},{68,84},{70,86},{72,88},{74,90},{76,92},{78,94},{1... | collective-permute-start | bytes 688136 | tf_op jit(solution)/shard_map/ppermute | solution.py:495
  43.5 9.0 %collective-permute-start.6 = (f32[7,8,256]{2,1,0:T(8,128)S(1)}, f32[7,8,256]{2,1,0:T(8,128)S(1)}, u32[]{:S(2)}, u32[]{:S(2)}) collective-permute-start(f32[7,8,256]{2,1,0:T(8,128)S(1)} %get-tuple-element.62), channel_id=1, source_target_pairs={{64,192},{66,194},{68,196},{70,198},{72,200},{74,202},{76,204},{78... | collective-permute-start | bytes 172040 | tf_op jit(solution)/shard_map/ppermute | solution.py:495
  45.8 6.7 %collective-permute-start.8 = (f32[7,8,256]{2,1,0:T(8,128)S(1)}, f32[7,8,256]{2,1,0:T(8,128)S(1)}, u32[]{:S(2)}, u32[]{:S(2)}) collective-permute-start(f32[7,8,256]{2,1,0:T(8,128)S(1)} %get-tuple-element.63), channel_id=1, source_target_pairs={{64,193},{66,195},{68,197},{70,199},{72,201},{74,203},{76,205},{78... | collective-permute-start | bytes 172040 | tf_op jit(solution)/shard_map/ppermute | solution.py:495
  47.7 6.4 %collective-permute-start.7 = (f32[7,8,256]{2,1,0:T(8,128)S(1)}, f32[7,8,256]{2,1,0:T(8,128)S(1)}, u32[]{:S(2)}, u32[]{:S(2)}) collective-permute-start(f32[7,8,256]{2,1,0:T(8,128)S(1)} %get-tuple-element.64), channel_id=1, source_target_pairs={{64,65},{66,67},{68,69},{70,71},{72,73},{74,75},{76,77},{78,79},{1... | collective-permute-start | bytes 172040 | tf_op jit(solution)/shard_map/ppermute | solution.py:495
  54.2 10.2 %collective-permute-start.11 = (f32[7,8,256]{2,1,0:T(8,128)S(1)}, f32[7,8,256]{2,1,0:T(8,128)S(1)}, u32[]{:S(2)}, u32[]{:S(2)}) collective-permute-start(f32[7,8,256]{2,1,0:T(8,128)S(1)} %add_add_fusion.1), channel_id=1, source_target_pairs={{64,70},{66,68},{68,66},{70,64},{72,78},{74,76},{76,74},{78,72},{1... | collective-permute-start | bytes 172040 | tf_op jit(solution)/shard_map/ppermute | solution.py:495
  60.3 5.8 %collective-permute-start.10 = (f32[7,8,256]{2,1,0:T(8,128)S(1)}, f32[7,8,256]{2,1,0:T(8,128)S(1)}, u32[]{:S(2)}, u32[]{:S(2)}) collective-permute-start(f32[7,8,256]{2,1,0:T(8,128)S(1)} %add_add_fusion.1), channel_id=1, source_target_pairs={{64,68},{66,70},{68,64},{70,66},{72,76},{74,78},{76,72},{78,74},{1... | collective-permute-start | bytes 172040 | tf_op jit(solution)/shard_map/ppermute | solution.py:495
  62.2 4.9 %collective-permute-start.9 = (f32[7,8,256]{2,1,0:T(8,128)S(1)}, f32[7,8,256]{2,1,0:T(8,128)S(1)}, u32[]{:S(2)}, u32[]{:S(2)}) collective-permute-start(f32[7,8,256]{2,1,0:T(8,128)S(1)} %add_add_fusion.1), channel_id=1, source_target_pairs={{64,66},{66,64},{68,70},{70,68},{72,74},{74,72},{76,78},{78,76},{1... | collective-permute-start | bytes 172040 | tf_op jit(solution)/shard_map/ppermute | solution.py:495
  67.1 9.0 %collective-permute-start.12 = (f32[7,8,256]{2,1,0:T(8,128)S(1)}, f32[7,8,256]{2,1,0:T(8,128)S(1)}, u32[]{:S(2)}, u32[]{:S(2)}) collective-permute-start(f32[7,8,256]{2,1,0:T(8,128)S(1)} %add_add_fusion.refs_6_), channel_id=1, source_target_pairs={{64,76},{66,78},{68,72},{70,74},{72,68},{74,70},{76,64},{78,66},{1... | collective-permute-start | bytes 172040 | tf_op jit(solution)/shard_map/ppermute | solution.py:495
  76.1 11.0 %collective-permute-start.15 = (f32[7,8,256]{2,1,0:T(8,128)S(1)}, f32[7,8,256]{2,1,0:T(8,128)S(1)}, u32[]{:S(2)}, u32[]{:S(2)}) collective-permute-start(f32[7,8,256]{2,1,0:T(8,128)S(1)} %add.73), channel_id=1, source_target_pairs={{64,193},{66,195},{68,197},{70,199},{72,201},{74,203},{76,205},{78... | collective-permute-start | bytes 172040 | tf_op jit(solution)/shard_map/ppermute | solution.py:495
  78.7 8.4 %collective-permute-start.14 = (f32[7,8,256]{2,1,0:T(8,128)S(1)}, f32[7,8,256]{2,1,0:T(8,128)S(1)}, u32[]{:S(2)}, u32[]{:S(2)}) collective-permute-start(f32[7,8,256]{2,1,0:T(8,128)S(1)} %add.73), channel_id=1, source_target_pairs={{64,65},{66,67},{68,69},{70,71},{72,73},{74,75},{76,77},{78,79},{1... | collective-permute-start | bytes 172040 | tf_op jit(solution)/shard_map/ppermute | solution.py:495
  82.1 4.9 %collective-permute-start.13 = (f32[7,8,256]{2,1,0:T(8,128)S(1)}, f32[7,8,256]{2,1,0:T(8,128)S(1)}, u32[]{:S(2)}, u32[]{:S(2)}) collective-permute-start(f32[7,8,256]{2,1,0:T(8,128)S(1)} %add.73), channel_id=1, source_target_pairs={{64,192},{66,194},{68,196},{70,198},{72,200},{74,202},{76,204},{78... | collective-permute-start | bytes 172040 | tf_op jit(solution)/shard_map/ppermute | solution.py:495
  87.1 13.8 %collective-permute-start.18 = (f32[28,8,256]{2,1,0:T(8,128)S(1)}, f32[28,8,256]{2,1,0:T(8,128)S(1)}, u32[]{:S(2)}, u32[]{:S(2)}) collective-permute-start(f32[28,8,256]{2,1,0:T(8,128)S(1)} %constant_dynamic-update-slice_fusion.refs_6_), channel_id=1, source_target_pairs={{64,112},{66,114},{68,116},{70,118},{72,120},{74,122},{76,124},{78... | collective-permute-start | bytes 688136 | tf_op jit(solution)/shard_map/ppermute | solution.py:495
  91.3 9.6 %collective-permute-start.17 = (f32[28,8,256]{2,1,0:T(8,128)S(1)}, f32[28,8,256]{2,1,0:T(8,128)S(1)}, u32[]{:S(2)}, u32[]{:S(2)}) collective-permute-start(f32[28,8,256]{2,1,0:T(8,128)S(1)} %constant_dynamic-update-slice_fusion.refs_6_), channel_id=1, source_target_pairs={{64,96},{66,98},{68,100},{70,102},{72,104},{74,106},{76,108},{78,1... | collective-permute-start | bytes 688136 | tf_op jit(solution)/shard_map/ppermute | solution.py:495
  93.9 7.0 %collective-permute-start.16 = (f32[28,8,256]{2,1,0:T(8,128)S(1)}, f32[28,8,256]{2,1,0:T(8,128)S(1)}, u32[]{:S(2)}, u32[]{:S(2)}) collective-permute-start(f32[28,8,256]{2,1,0:T(8,128)S(1)} %constant_dynamic-update-slice_fusion.refs_6_), channel_id=1, source_target_pairs={{64,80},{66,82},{68,84},{70,86},{72,88},{74,90},{76,92},{78,94},{1... | collective-permute-start | bytes 688136 | tf_op jit(solution)/shard_map/ppermute | solution.py:495
  103.7 9.0 %collective-permute-start.22 = (f32[32,256]{1,0:T(8,128)S(1)}, f32[32,256]{1,0:T(8,128)S(1)}, u32[]{:S(2)}, u32[]{:S(2)}) collective-permute-start(f32[32,256]{1,0:T(8,128)S(1)} %right_product.1), channel_id=1, source_target_pairs={{64,112},{66,114},{68,116},{70,118},{72,120},{74,122},{76,124},{78... | collective-permute-start | bytes 98312 | tf_op jit(solution)/shard_map/ppermute | solution.py:495
  107.9 6.2 %collective-permute-start.21 = (f32[32,256]{1,0:T(8,128)S(1)}, f32[32,256]{1,0:T(8,128)S(1)}, u32[]{:S(2)}, u32[]{:S(2)}) collective-permute-start(f32[32,256]{1,0:T(8,128)S(1)} %right_product.1), channel_id=1, source_target_pairs={{64,96},{66,98},{68,100},{70,102},{72,104},{74,106},{76,108},{78,1... | collective-permute-start | bytes 98312 | tf_op jit(solution)/shard_map/ppermute | solution.py:495
  110.5 4.7 %collective-permute-start.20 = (f32[32,256]{1,0:T(8,128)S(1)}, f32[32,256]{1,0:T(8,128)S(1)}, u32[]{:S(2)}, u32[]{:S(2)}) collective-permute-start(f32[32,256]{1,0:T(8,128)S(1)} %right_product.1), channel_id=1, source_target_pairs={{64,80},{66,82},{68,84},{70,86},{72,88},{74,90},{76,92},{78,94},{1... | collective-permute-start | bytes 98312 | tf_op jit(solution)/shard_map/ppermute | solution.py:495
  115.1 11.5 %collective-permute-start.26 = (f32[4,28,8,256]{3,2,1,0:T(8,128)S(1)}, f32[4,28,8,256]{3,2,1,0:T(8,128)S(1)}, u32[]{:S(2)}, u32[]{:S(2)}) collective-permute-start(f32[4,28,8,256]{3,2,1,0:T(8,128)S(1)} %pad_maximum_fusion.part), channel_id=1, source_target_pairs={{0,64},{64,0},{2,66},{66,2},{4,68},{68,4},{6,70},{70,6},{8,72},{72... | collective-permute-start | bytes 2752520 | tf_op jit(solution)/shard_map/ppermute | solution.py:500
  115.2 9.0 %collective-permute-start.25 = (f32[32,256]{1,0:T(8,128)S(1)}, f32[32,256]{1,0:T(8,128)S(1)}, u32[]{:S(2)}, u32[]{:S(2)}) collective-permute-start(f32[32,256]{1,0:T(8,128)S(1)} %add_add_fusion.4), channel_id=1, source_target_pairs={{64,193},{66,195},{68,197},{70,199},{72,201},{74,203},{76,205},{78... | collective-permute-start | bytes 98312 | tf_op jit(solution)/shard_map/ppermute | solution.py:495
  117.8 6.5 %collective-permute-start.24 = (f32[32,256]{1,0:T(8,128)S(1)}, f32[32,256]{1,0:T(8,128)S(1)}, u32[]{:S(2)}, u32[]{:S(2)}) collective-permute-start(f32[32,256]{1,0:T(8,128)S(1)} %add_add_fusion.4), channel_id=1, source_target_pairs={{64,65},{66,67},{68,69},{70,71},{72,73},{74,75},{76,77},{78,79},{1... | collective-permute-start | bytes 98312 | tf_op jit(solution)/shard_map/ppermute | solution.py:495
  121.9 4.7 %collective-permute-start.23 = (f32[32,256]{1,0:T(8,128)S(1)}, f32[32,256]{1,0:T(8,128)S(1)}, u32[]{:S(2)}, u32[]{:S(2)}) collective-permute-start(f32[32,256]{1,0:T(8,128)S(1)} %add_add_fusion.4), channel_id=1, source_target_pairs={{64,192},{66,194},{68,196},{70,198},{72,200},{74,202},{76,204},{78... | collective-permute-start | bytes 98312 | tf_op jit(solution)/shard_map/ppermute | solution.py:495
  126.6 11.7 %collective-permute-start.29 = (f32[32,256]{1,0:T(8,128)S(1)}, f32[32,256]{1,0:T(8,128)S(1)}, u32[]{:S(2)}, u32[]{:S(2)}) collective-permute-start(f32[32,256]{1,0:T(8,128)S(1)} %add_add_fusion.3), channel_id=1, source_target_pairs={{64,70},{66,68},{68,66},{70,64},{72,78},{74,76},{76,74},{78,72},{1... | collective-permute-start | bytes 98312 | tf_op jit(solution)/shard_map/ppermute | solution.py:495
  129.4 8.9 %collective-permute-start.28 = (f32[32,256]{1,0:T(8,128)S(1)}, f32[32,256]{1,0:T(8,128)S(1)}, u32[]{:S(2)}, u32[]{:S(2)}) collective-permute-start(f32[32,256]{1,0:T(8,128)S(1)} %add_add_fusion.3), channel_id=1, source_target_pairs={{64,68},{66,70},{68,64},{70,66},{72,76},{74,78},{76,72},{78,74},{1... | collective-permute-start | bytes 98312 | tf_op jit(solution)/shard_map/ppermute | solution.py:495
  131.6 6.7 %collective-permute-start.27 = (f32[32,256]{1,0:T(8,128)S(1)}, f32[32,256]{1,0:T(8,128)S(1)}, u32[]{:S(2)}, u32[]{:S(2)}) collective-permute-start(f32[32,256]{1,0:T(8,128)S(1)} %add_add_fusion.3), channel_id=1, source_target_pairs={{64,66},{66,64},{68,70},{70,68},{72,74},{74,72},{76,78},{78,76},{1... | collective-permute-start | bytes 98312 | tf_op jit(solution)/shard_map/ppermute | solution.py:495
  138.4 6.8 %collective-permute-start.30 = (f32[32,256]{1,0:T(8,128)S(1)}, f32[32,256]{1,0:T(8,128)S(1)}, u32[]{:S(2)}, u32[]{:S(2)}) collective-permute-start(f32[32,256]{1,0:T(8,128)S(1)} %add_add_fusion.2.refs_0_), channel_id=1, source_target_pairs={{64,76},{66,78},{68,72},{70,74},{72,68},{74,70},{76,64},{78,66},{1... | collective-permute-start | bytes 98312 | tf_op jit(solution)/shard_map/ppermute | solution.py:495
  145.1 1.2 collective-permute-start.31
  (2 other events, 42.1 us)

commit v7 on v4

--- a/solution.py
+++ b/solution.py
@@ -45,6 +45,9 @@
                 first, stride = (128 if side_z < 0 else 144), EDGE
             for which in (0, 1):
                 slot = slots[which, (step_x + 1) * 9 + (side_y + 1) * 3 + side_z + 1]
+                if side_z:
+                    end = 0 if side_z < 0 else lax.axis_size("space") - 1
+                    slot = jnp.where(lax.axis_index("space") == end, -1, slot)
                 base = jnp.where(slot < 0, -4096, slot * stride + first)
                 rows = jnp.where(in_y & in_z & (brick == which), base + offset, rows)
     return rows
@@ -496,7 +499,7 @@
 
 def shifted(value, by):
     devices = lax.axis_size("space")
-    return lax.ppermute(value, "space", [(i, i + by) for i in range(devices) if 0 <= i + by < devices])
+    return lax.ppermute(value, "space", [(i, (i + by) % devices) for i in range(devices)])
 
 
 def partners(core=0, x=0, y=0, z=0):

time: 114 us -> 112 us (0.982)
  waiting for transfers between devices: 24.9 us -> 20.8 us
  starting transfers between devices: 51.6 us -> 52.8 us
    ppermute x2, starting transfers between devices: 5.5 us -> 9.95 us  [shifted(): lax.ppermute(value, 'space', [(i, (i + by) % devices) for i in range(devi...]
    ppermute x31, starting transfers between devices: 46.1 us -> 42.9 us  [swapped(): return lax.ppermute(value, ('dp', 'space'), partners(**bits))]
    ppermute x2, waiting for transfers between devices: 2.26 us -> 0.01 us  [shifted(): lax.ppermute(value, 'space', [(i, (i + by) % devices) for i in range(devi...]
    ppermute x31, waiting for transfers between devices: 22.7 us -> 20.8 us  [swapped(): return lax.ppermute(value, ('dp', 'space'), partners(**bits))]
  transfers between devices with their start and end apart: 33 -> 33, of which waited for: 16 -> 14; matrix products, arithmetic and copies ran while one was open for 0% -> 0% of each run, Pallas kernels for 18% -> 19%
where the time goes in v7:
time: 112 us; the launch traced here: 111 us
  starting transfers between devices  52.8 us (47%)
  Pallas kernels  36.4 us (32%)
  waiting for transfers between devices  20.8 us (19%)
    ppermute x31, starting transfers between devices, swapped(): return lax.ppermute(value, ('dp', 'space'), partners(**bits))  42.9 us
    ppermute x31, waiting for transfers between devices, swapped(): return lax.ppermute(value, ('dp', 'space'), partners(**bits))  20.8 us
    pallas_call x2, Pallas kernels, local_gradient(): pl.pallas_call(functools.partial(gradient_kernel, sides, width), grid=(le...  13.2 us
    pallas_call x3, Pallas kernels, input_gradient(): pl.pallas_call(functools.partial(input_kernel, side, last), grid=(3,), in...  12.2 us
    ppermute x2, starting transfers between devices, shifted(): lax.ppermute(value, 'space', [(i, (i + by) % devices) for i in range(devi...  9.95 us
    pallas_call x1, Pallas kernels, remaining_error(): pl.pallas_call(error_kernel, grid=(3,), in_specs=[whole(4, 28, 8, 128), w...  3.87 us
    pallas_call x1, Pallas kernels, half_inverse(): pl.pallas_call(first_half_kernel, out_shape=[SQUARE, SQUARE], compiler_pa...  2.36 us
  transfers between devices with their start and end apart: 33, of which 14 were waited for; matrix products, arithmetic and copies ran while one was open for 0% of the time, Pallas kernels for 19%

profile of v7, /device:TPU:8, one launch (start us, length us, event | category | flops | bytes accessed | tf_op | source)
XLA Modules:
  0.0 111.1 jit_solution(3661157637949582111)
XLA Ops:
  0.6 1.6 %brick_faces.1 = (bf16[2,8,16,256]{3,2,1,0:T(8,128)(2,1)S(1)}, bf16[2,8,16,256]{3,2,1,0:T(8,128)(2,1)S(1)}) custom-call(bf16[2,512,256]{2,1,0:T(8,128)(2,1)} %bitcast.34, bf16[2,512,256]{2,1,0:T(8,128)(2,1)} %bitcast.24, s32[2,512]{1,0:T(2,128)} %bitcast.40), custom_call_target="tpu_custom_call" | custom-call | tf_op jit(solution)/shard_map/brick_faces/pallas_call | solution.py:126
  2.3 2.4 %collective-permute-start = (bf16[2,8,16,256]{3,2,1,0:T(8,128)(2,1)S(1)}, bf16[2,8,16,256]{3,2,1,0:T(8,128)(2,1)S(1)}, u32[]{:S(2)}, u32[]{:S(2)}) collective-permute-start(bf16[2,8,16,256]{3,2,1,0:T(8,128)(2,1)S(1)} %get-tuple-element.33), channel_id=1, source_target_pairs={{0,1},{1,2},{2,3},{3,4},{4,5},{5,6},{6,7},{7,8},{8,9},{9,10},{10,1... | collective-permute-start | bytes 393224 | tf_op jit(solution)/shard_map/ppermute | solution.py:502
  4.7 7.6 %collective-permute-start.1 = (bf16[2,8,16,256]{3,2,1,0:T(8,128)(2,1)S(1)}, bf16[2,8,16,256]{3,2,1,0:T(8,128)(2,1)S(1)}, u32[]{:S(2)}, u32[]{:S(2)}) collective-permute-start(bf16[2,8,16,256]{3,2,1,0:T(8,128)(2,1)S(1)} %get-tuple-element.34), channel_id=1, source_target_pairs={{0,63},{1,0},{2,1},{3,2},{4,3},{5,4},{6,5},{7,6},{8,7},{9,8},{10,9... | collective-permute-start | bytes 393224 | tf_op jit(solution)/shard_map/ppermute | solution.py:502
  12.2 4.8 %gradient_own.1 = (f32[3,3,3,128,256]{4,3,2,1,0:T(8,128)S(1)}, f32[3,3,3,128,256]{4,3,2,1,0:T(8,128)S(1)}, f32[4,28,8,128]{3,2,1,0:T(8,128)S(1)}, f32[4,28,8,128]{3,2,1,0:T(8,128)S(1)}) custom-call(s32[2,27]{1,0:T(2,128)} %bitcast.52, bf16[2,512,256]{2,1,0:T(8,128)(2,1)} %bitcast.35, bf16[2,512,256]{2,1,0:T(8,128)(2,1)} %bitcast.25, s32[2,512]{1,0:T(2,128)} %bitcast.41, ...), custom_call_target="tpu_custom_call" | custom-call | flops 2000000000 | bytes 4000000 | tf_op jit(solution)/shard_map/gradient_own/pallas_call | solution.py:236
  17.1 8.4 %gradient_with_faces.1 = (f32[3,3,3,128,256]{4,3,2,1,0:T(8,128)S(1)}, f32[3,3,3,128,256]{4,3,2,1,0:T(8,128)S(1)}, f32[4,28,8,128]{3,2,1,0:T(8,128)S(1)}, f32[4,28,8,128]{3,2,1,0:T(8,128)S(1)}) custom-call(s32[2,27]{1,0:T(2,128)} %bitcast.53, bf16[2,512,256]{2,1,0:T(8,128)(2,1)} %bitcast.36, ...), custom_call_target="tpu_custom_call", output_to_operand_aliasing={{0}: (8, {}), {1}: (9, {})} | custom-call | flops 4000000000 | bytes 8000000 | tf_op jit(solution)/shard_map/gradient_with_faces/pallas_call | solution.py:236
  25.6 1.8 %collective-permute-done.2 = f32[4,28,8,128]{3,2,1,0:T(8,128)S(1)} collective-permute-done((f32[4,28,8,128]{3,2,1,0:T(8,128)S(1)}, f32[4,28,8,128]{3,2,1,0:T(8,128)S(1)}, u32[]{:S(2)}, u32[]{:S(2)}) %collective-permute-start.2) | collective-permute-done | bytes 458784 | tf_op jit(solution)/shard_map/ppermute | solution.py:519
  29.2 2.8 %collective-permute-start.3 = (f32[28,8,128]{2,1,0:T(8,128)S(1)}, f32[28,8,128]{2,1,0:T(8,128)S(1)}, u32[]{:S(2)}, u32[]{:S(2)}) collective-permute-start(f32[28,8,128]{2,1,0:T(8,128)S(1)} %get-tuple-element.65), channel_id=1, source_target_pairs={{0,16},{2,18},{4,20},{6,22},{8,24},{10,26},{12,28},{14,30},{128,14... | collective-permute-start | bytes 344072 | tf_op jit(solution)/shard_map/ppermute | solution.py:519
  31.9 3.6 %input_own.1.refs_5_ = f32[1024,256]{1,0:T(8,128)S(1)} custom-call(s32[2,27]{1,0:T(2,128)} %bitcast.54, bf16[2,512,256]{2,1,0:T(8,128)(2,1)S(1)} %bitcast.27, s32[2,512]{1,0:T(2,128)} %bitcast.43, bf16[3,3,3,256,256]{4,3,2,1,0:T(8,128)(2,1)S(1)} %bitcast.31, f32[4,28,8,128]{3,2,1,0:T(8,128)S(1)} %add.69.refs_4_), custom_call_target="tpu_custom_call" | custom-call | flops 2000000000 | bytes 4000000 | tf_op jit(solution)/shard_map/input_own/pallas_call | solution.py:321
  39.0 2.7 %collective-permute-start.7 = (f32[7,8,128]{2,1,0:T(8,128)S(1)}, f32[7,8,128]{2,1,0:T(8,128)S(1)}, u32[]{:S(2)}, u32[]{:S(2)}) collective-permute-start(f32[7,8,128]{2,1,0:T(8,128)S(1)} %get-tuple-element.68), channel_id=1, source_target_pairs={{0,1},{2,3},{4,5},{6,7},{8,9},{10,11},{12,13},{14,15},{128,129},{1... | collective-permute-start | bytes 86024 | tf_op jit(solution)/shard_map/ppermute | solution.py:519
  42.8 1.5 %collective-permute-done.7 = f32[7,8,128]{2,1,0:T(8,128)S(1)} collective-permute-done((f32[7,8,128]{2,1,0:T(8,128)S(1)}, f32[7,8,128]{2,1,0:T(8,128)S(1)}, u32[]{:S(2)}, u32[]{:S(2)}) %collective-permute-start.7) | collective-permute-done | bytes 28704 | tf_op jit(solution)/shard_map/ppermute | solution.py:519
  44.4 4.5 %collective-permute-start.11 = (f32[7,8,128]{2,1,0:T(8,128)S(1)}, f32[7,8,128]{2,1,0:T(8,128)S(1)}, u32[]{:S(2)}, u32[]{:S(2)}) collective-permute-start(f32[7,8,128]{2,1,0:T(8,128)S(1)} %add_add_fusion.5), channel_id=1, source_target_pairs={{0,6},{2,4},{4,2},{6,0},{8,14},{10,12},{12,10},{14,8},{128,134},{1... | collective-permute-start | bytes 86024 | tf_op jit(solution)/shard_map/ppermute | solution.py:519
  50.8 2.8 %collective-permute-done.10 = f32[7,8,128]{2,1,0:T(8,128)S(1)} collective-permute-done((f32[7,8,128]{2,1,0:T(8,128)S(1)}, f32[7,8,128]{2,1,0:T(8,128)S(1)}, u32[]{:S(2)}, u32[]{:S(2)}) %collective-permute-start.10) | collective-permute-done | bytes 28704 | tf_op jit(solution)/shard_map/ppermute | solution.py:519
  53.6 2.9 %collective-permute-start.12 = (f32[7,8,128]{2,1,0:T(8,128)S(1)}, f32[7,8,128]{2,1,0:T(8,128)S(1)}, u32[]{:S(2)}, u32[]{:S(2)}) collective-permute-start(f32[7,8,128]{2,1,0:T(8,128)S(1)} %add_add_fusion.4.refs_6_), channel_id=1, source_target_pairs={{0,12},{2,14},{4,8},{6,10},{8,4},{10,6},{12,0},{14,2},{128,140},{1... | collective-permute-start | bytes 86024 | tf_op jit(solution)/shard_map/ppermute | solution.py:519
  56.5 3.7 %input_below.1.refs_5_ = f32[1024,256]{1,0:T(8,128)S(1)} custom-call(s32[2,27]{1,0:T(2,128)} %bitcast.55, bf16[2,512,256]{2,1,0:T(8,128)(2,1)S(1)} %bitcast.28, s32[2,512]{1,0:T(2,128)} %bitcast.44, bf16[3,3,3,256,256]{4,3,2,1,0:T(8,128)(2,1)S(1)} %bitcast.32, bf16[2,8,16,256]{3,2,1,0:T(8,128)(2,1)S(1)} %collective-permute-done.1.refs_7_.refs_4_, ...), custom_call_target="tpu_custom_call" | custom-call | flops 2000000000 | bytes 4000000 | tf_op jit(solution)/shard_map/input_below/pallas_call | solution.py:321
  60.4 3.4 %collective-permute-start.14 = (f32[7,8,128]{2,1,0:T(8,128)S(1)}, f32[7,8,128]{2,1,0:T(8,128)S(1)}, u32[]{:S(2)}, u32[]{:S(2)}) collective-permute-start(f32[7,8,128]{2,1,0:T(8,128)S(1)} %add.79), channel_id=1, source_target_pairs={{0,1},{2,3},{4,5},{6,7},{8,9},{10,11},{12,13},{14,15},{128,129},{1... | collective-permute-start | bytes 86024 | tf_op jit(solution)/shard_map/ppermute | solution.py:519
  64.5 3.2 %collective-permute-done.13 = f32[7,8,128]{2,1,0:T(8,128)S(1)} collective-permute-done((f32[7,8,128]{2,1,0:T(8,128)S(1)}, f32[7,8,128]{2,1,0:T(8,128)S(1)}, u32[]{:S(2)}, u32[]{:S(2)}) %collective-permute-start.13) | collective-permute-done | bytes 28704 | tf_op jit(solution)/shard_map/ppermute | solution.py:519
  67.7 2.2 %collective-permute-start.18 = (f32[28,8,128]{2,1,0:T(8,128)S(1)}, f32[28,8,128]{2,1,0:T(8,128)S(1)}, u32[]{:S(2)}, u32[]{:S(2)}) collective-permute-start(f32[28,8,128]{2,1,0:T(8,128)S(1)} %constant_dynamic-update-slice_fusion.refs_6_), channel_id=1, source_target_pairs={{0,48},{2,50},{4,52},{6,54},{8,56},{10,58},{12,60},{14,62},{128,17... | collective-permute-start | bytes 344072 | tf_op jit(solution)/shard_map/ppermute | solution.py:519
  70.2 1.7 %collective-permute-start.16 = (f32[28,8,128]{2,1,0:T(8,128)S(1)}, f32[28,8,128]{2,1,0:T(8,128)S(1)}, u32[]{:S(2)}, u32[]{:S(2)}) collective-permute-start(f32[28,8,128]{2,1,0:T(8,128)S(1)} %constant_dynamic-update-slice_fusion.refs_6_), channel_id=1, source_target_pairs={{0,16},{2,18},{4,20},{6,22},{8,24},{10,26},{12,28},{14,30},{128,14... | collective-permute-start | bytes 344072 | tf_op jit(solution)/shard_map/ppermute | solution.py:519
  71.9 4.8 %input_above.1 = bf16[2,512,256]{2,1,0:T(8,128)(2,1)} custom-call(s32[2,27]{1,0:T(2,128)} %bitcast.56, bf16[2,512,256]{2,1,0:T(8,128)(2,1)S(1)} %bitcast.29, s32[2,512]{1,0:T(2,128)} %bitcast.45, bf16[3,3,3,256,256]{4,3,2,1,0:T(8,128)(2,1)S(1)} %bitcast.33, bf16[2,8,16,256]{3,2,1,0:T(8,128)(2,1)S(1)} %collective-permute-done.refs_6_.refs_4_, ...), custom_call_target="tpu_custom_call" | custom-call | flops 2000000000 | bytes 4000000 | tf_op jit(solution)/shard_map/input_above/pallas_call | solution.py:321
  76.8 1.7 %right_product.1 = f32[32,256]{1,0:T(8,128)S(1)} custom-call(f32[4,28,8,128]{3,2,1,0:T(8,128)S(1)} %pad_maximum_fusion.mine, f32[3,3,3,128,256]{4,3,2,1,0:T(8,128)S(1)} %get-tuple-element.50.kept, f32[3,3,3,128,256]{4,3,2,1,0:T(8,128)S(1)} %collective-permute-done.19.partner), custom_call_target="tpu_custom_call" | custom-call | tf_op jit(solution)/shard_map/right_product/pallas_call | solution.py:368
  78.6 2.2 %collective-permute-start.21 = (f32[32,256]{1,0:T(8,128)S(1)}, f32[32,256]{1,0:T(8,128)S(1)}, u32[]{:S(2)}, u32[]{:S(2)}) collective-permute-start(f32[32,256]{1,0:T(8,128)S(1)} %right_product.1), channel_id=1, source_target_pairs={{0,12},{2,14},{4,8},{6,10},{8,4},{10,6},{12,0},{14,2},{128,140},{1... | collective-permute-start | bytes 98312 | tf_op jit(solution)/shard_map/ppermute | solution.py:519
  80.8 1.8 %collective-permute-start.20 = (f32[32,256]{1,0:T(8,128)S(1)}, f32[32,256]{1,0:T(8,128)S(1)}, u32[]{:S(2)}, u32[]{:S(2)}) collective-permute-start(f32[32,256]{1,0:T(8,128)S(1)} %right_product.1), channel_id=1, source_target_pairs={{0,64},{2,66},{4,68},{6,70},{8,72},{10,74},{12,76},{14,78},{128,19... | collective-permute-start | bytes 98312 | tf_op jit(solution)/shard_map/ppermute | solution.py:519
  82.5 1.5 %collective-permute-done.22 = f32[32,256]{1,0:T(8,128)S(1)} collective-permute-done((f32[32,256]{1,0:T(8,128)S(1)}, f32[32,256]{1,0:T(8,128)S(1)}, u32[]{:S(2)}, u32[]{:S(2)}) %collective-permute-start.22) | collective-permute-done | bytes 32800 | tf_op jit(solution)/shard_map/ppermute | solution.py:519
  85.8 2.2 %collective-permute-start.25 = (f32[32,256]{1,0:T(8,128)S(1)}, f32[32,256]{1,0:T(8,128)S(1)}, u32[]{:S(2)}, u32[]{:S(2)}) collective-permute-start(f32[32,256]{1,0:T(8,128)S(1)} %add_add_fusion.3), channel_id=1, source_target_pairs={{0,48},{2,50},{4,52},{6,54},{8,56},{10,58},{12,60},{14,62},{128,17... | collective-permute-start | bytes 98312 | tf_op jit(solution)/shard_map/ppermute | solution.py:519
  88.2 1.7 %collective-permute-start.23 = (f32[32,256]{1,0:T(8,128)S(1)}, f32[32,256]{1,0:T(8,128)S(1)}, u32[]{:S(2)}, u32[]{:S(2)}) collective-permute-start(f32[32,256]{1,0:T(8,128)S(1)} %add_add_fusion.3), channel_id=1, source_target_pairs={{0,16},{2,18},{4,20},{6,22},{8,24},{10,26},{12,28},{14,30},{128,14... | collective-permute-start | bytes 98312 | tf_op jit(solution)/shard_map/ppermute | solution.py:519
  90.9 2.5 %collective-permute-done.24 = f32[32,256]{1,0:T(8,128)S(1)} collective-permute-done((f32[32,256]{1,0:T(8,128)S(1)}, f32[32,256]{1,0:T(8,128)S(1)}, u32[]{:S(2)}, u32[]{:S(2)}) %collective-permute-start.24) | collective-permute-done | bytes 32800 | tf_op jit(solution)/shard_map/ppermute | solution.py:519
  93.5 2.7 %collective-permute-start.28 = (f32[32,256]{1,0:T(8,128)S(1)}, f32[32,256]{1,0:T(8,128)S(1)}, u32[]{:S(2)}, u32[]{:S(2)}) collective-permute-start(f32[32,256]{1,0:T(8,128)S(1)} %add_add_fusion.2), channel_id=1, source_target_pairs={{0,1},{2,3},{4,5},{6,7},{8,9},{10,11},{12,13},{14,15},{128,129},{1... | collective-permute-start | bytes 98312 | tf_op jit(solution)/shard_map/ppermute | solution.py:519
  97.5 2.4 %half_inverse.1 = (f32[32,32]{1,0:T(8,128)S(1)}, f32[32,32]{1,0:T(8,128)S(1)}) custom-call(f32[4,28,8,128]{3,2,1,0:T(8,128)S(1)} %pad_maximum_fusion.mine, f32[4,28,8,128]{3,2,1,0:T(8,128)S(1)} %collective-permute-done.26.other), custom_call_target="tpu_custom_call" | custom-call | tf_op jit(solution)/shard_map/half_inverse/pallas_call | solution.py:411
  100.1 2.3 %collective-permute-start.32 = (f32[32,256]{1,0:T(8,128)S(1)}, f32[32,256]{1,0:T(8,128)S(1)}, u32[]{:S(2)}, u32[]{:S(2)}) collective-permute-start(f32[32,256]{1,0:T(8,128)S(1)} %add_add_fusion.1.refs_0_), channel_id=1, source_target_pairs={{0,6},{2,4},{4,2},{6,0},{8,14},{10,12},{12,10},{14,8},{128,134},{1... | collective-permute-start | bytes 98312 | tf_op jit(solution)/shard_map/ppermute | solution.py:519
  102.4 2.2 %collective-permute-start.30 = (f32[32,256]{1,0:T(8,128)S(1)}, f32[32,256]{1,0:T(8,128)S(1)}, u32[]{:S(2)}, u32[]{:S(2)}) collective-permute-start(f32[32,256]{1,0:T(8,128)S(1)} %add_add_fusion.1.refs_0_), channel_id=1, source_target_pairs={{0,2},{2,0},{4,6},{6,4},{8,10},{10,8},{12,14},{14,12},{128,130},{1... | collective-permute-start | bytes 98312 | tf_op jit(solution)/shard_map/ppermute | solution.py:519
  104.6 1.4 %whole_inverse.1.inverse = f32[32,32]{1,0:T(8,128)S(1)} custom-call(f32[32,32]{1,0:T(8,128)S(1)} %get-tuple-element.59.work, f32[32,32]{1,0:T(8,128)S(1)} %get-tuple-element.60.made, f32[32,256]{1,0:T(8,128)S(1)} %add_add_fusion.1.refs_0_), custom_call_target="tpu_custom_call" | custom-call | tf_op jit(solution)/shard_map/whole_inverse/pallas_call | solution.py:422
  107.2 3.9 %remaining_error.1 = (bf16[3,3,3,256,256]{4,3,2,1,0:T(8,128)(2,1)}, f32[32,256]{1,0:T(8,128)}) custom-call(f32[4,28,8,128]{3,2,1,0:T(8,128)S(1)} %pad_maximum_fusion.mine, f32[4,28,8,128]{3,2,1,0:T(8,128)S(1)} %collective-permute-done.26.other, f32[3,3,3,128,256]{4,3,2,1,0:T(8,128)S(1)} %get-tuple-element.50.kept, ...), custom_call_target="tpu_custom_call" | custom-call | tf_op jit(solution)/shard_map/remaining_error/pallas_call | solution.py:464
  (64 shorter events, 15.6 us)
Async XLA Ops:
  2.3 14.7 %collective-permute-start = (bf16[2,8,16,256]{3,2,1,0:T(8,128)(2,1)S(1)}, bf16[2,8,16,256]{3,2,1,0:T(8,128)(2,1)S(1)}, u32[]{:S(2)}, u32[]{:S(2)}) collective-permute-start(bf16[2,8,16,256]{3,2,1,0:T(8,128)(2,1)S(1)} %get-tuple-element.33), channel_id=1, source_target_pairs={{0,1},{1,2},{2,3},{3,4},{4,5},{5,6},{6,7},{7,8},{8,9},{9,10},{10,1... | collective-permute-start | bytes 393224 | tf_op jit(solution)/shard_map/ppermute | solution.py:502
  4.7 12.4 %collective-permute-start.1 = (bf16[2,8,16,256]{3,2,1,0:T(8,128)(2,1)S(1)}, bf16[2,8,16,256]{3,2,1,0:T(8,128)(2,1)S(1)}, u32[]{:S(2)}, u32[]{:S(2)}) collective-permute-start(bf16[2,8,16,256]{3,2,1,0:T(8,128)(2,1)S(1)} %get-tuple-element.34), channel_id=1, source_target_pairs={{0,63},{1,0},{2,1},{3,2},{4,3},{5,4},{6,5},{7,6},{8,7},{9,8},{10,9... | collective-permute-start | bytes 393224 | tf_op jit(solution)/shard_map/ppermute | solution.py:502
  27.5 49.3 %collective-permute-start.19 = (f32[3,3,3,128,256]{4,3,2,1,0:T(8,128)S(1)}, f32[3,3,3,128,256]{4,3,2,1,0:T(8,128)S(1)}, u32[]{:S(2)}, u32[]{:S(2)}) collective-permute-start(f32[3,3,3,128,256]{4,3,2,1,0:T(8,128)S(1)} %get-tuple-element.46.sent), channel_id=1, source_target_pairs={{0,64},{2,66},{4,68},{6,70},{8,72},{10,74},{12,76},{14,78},{128,19... | collective-permute-start | bytes 10616840 | tf_op jit(solution)/shard_map/ppermute | solution.py:519
  27.7 9.2 %collective-permute-start.5 = (f32[28,8,128]{2,1,0:T(8,128)S(1)}, f32[28,8,128]{2,1,0:T(8,128)S(1)}, u32[]{:S(2)}, u32[]{:S(2)}) collective-permute-start(f32[28,8,128]{2,1,0:T(8,128)S(1)} %get-tuple-element.63), channel_id=1, source_target_pairs={{0,48},{2,50},{4,52},{6,54},{8,56},{10,58},{12,60},{14,62},{128,17... | collective-permute-start | bytes 344072 | tf_op jit(solution)/shard_map/ppermute | solution.py:519
  28.7 8.3 %collective-permute-start.4 = (f32[28,8,128]{2,1,0:T(8,128)S(1)}, f32[28,8,128]{2,1,0:T(8,128)S(1)}, u32[]{:S(2)}, u32[]{:S(2)}) collective-permute-start(f32[28,8,128]{2,1,0:T(8,128)S(1)} %get-tuple-element.64), channel_id=1, source_target_pairs={{0,32},{2,34},{4,36},{6,38},{8,40},{10,42},{12,44},{14,46},{128,16... | collective-permute-start | bytes 344072 | tf_op jit(solution)/shard_map/ppermute | solution.py:519
  29.2 8.3 %collective-permute-start.3 = (f32[28,8,128]{2,1,0:T(8,128)S(1)}, f32[28,8,128]{2,1,0:T(8,128)S(1)}, u32[]{:S(2)}, u32[]{:S(2)}) collective-permute-start(f32[28,8,128]{2,1,0:T(8,128)S(1)} %get-tuple-element.65), channel_id=1, source_target_pairs={{0,16},{2,18},{4,20},{6,22},{8,24},{10,26},{12,28},{14,30},{128,14... | collective-permute-start | bytes 344072 | tf_op jit(solution)/shard_map/ppermute | solution.py:519
  37.5 4.2 %collective-permute-start.6 = (f32[7,8,128]{2,1,0:T(8,128)S(1)}, f32[7,8,128]{2,1,0:T(8,128)S(1)}, u32[]{:S(2)}, u32[]{:S(2)}) collective-permute-start(f32[7,8,128]{2,1,0:T(8,128)S(1)} %get-tuple-element.66), channel_id=1, source_target_pairs={{0,128},{2,130},{4,132},{6,134},{8,136},{10,138},{12,140},{14,142}... | collective-permute-start | bytes 86024 | tf_op jit(solution)/shard_map/ppermute | solution.py:519
  39.0 3.9 %collective-permute-start.8 = (f32[7,8,128]{2,1,0:T(8,128)S(1)}, f32[7,8,128]{2,1,0:T(8,128)S(1)}, u32[]{:S(2)}, u32[]{:S(2)}) collective-permute-start(f32[7,8,128]{2,1,0:T(8,128)S(1)} %get-tuple-element.67), channel_id=1, source_target_pairs={{0,129},{2,131},{4,133},{6,135},{8,137},{10,139},{12,141},{14,143}... | collective-permute-start | bytes 86024 | tf_op jit(solution)/shard_map/ppermute | solution.py:519
  39.0 5.4 %collective-permute-start.7 = (f32[7,8,128]{2,1,0:T(8,128)S(1)}, f32[7,8,128]{2,1,0:T(8,128)S(1)}, u32[]{:S(2)}, u32[]{:S(2)}) collective-permute-start(f32[7,8,128]{2,1,0:T(8,128)S(1)} %get-tuple-element.68), channel_id=1, source_target_pairs={{0,1},{2,3},{4,5},{6,7},{8,9},{10,11},{12,13},{14,15},{128,129},{1... | collective-permute-start | bytes 86024 | tf_op jit(solution)/shard_map/ppermute | solution.py:519
  44.4 6.5 %collective-permute-start.11 = (f32[7,8,128]{2,1,0:T(8,128)S(1)}, f32[7,8,128]{2,1,0:T(8,128)S(1)}, u32[]{:S(2)}, u32[]{:S(2)}) collective-permute-start(f32[7,8,128]{2,1,0:T(8,128)S(1)} %add_add_fusion.5), channel_id=1, source_target_pairs={{0,6},{2,4},{4,2},{6,0},{8,14},{10,12},{12,10},{14,8},{128,134},{1... | collective-permute-start | bytes 86024 | tf_op jit(solution)/shard_map/ppermute | solution.py:519
  48.8 4.8 %collective-permute-start.10 = (f32[7,8,128]{2,1,0:T(8,128)S(1)}, f32[7,8,128]{2,1,0:T(8,128)S(1)}, u32[]{:S(2)}, u32[]{:S(2)}) collective-permute-start(f32[7,8,128]{2,1,0:T(8,128)S(1)} %add_add_fusion.5), channel_id=1, source_target_pairs={{0,4},{2,6},{4,0},{6,2},{8,12},{10,14},{12,8},{14,10},{128,132},{1... | collective-permute-start | bytes 86024 | tf_op jit(solution)/shard_map/ppermute | solution.py:519
  48.9 4.8 %collective-permute-start.9 = (f32[7,8,128]{2,1,0:T(8,128)S(1)}, f32[7,8,128]{2,1,0:T(8,128)S(1)}, u32[]{:S(2)}, u32[]{:S(2)}) collective-permute-start(f32[7,8,128]{2,1,0:T(8,128)S(1)} %add_add_fusion.5), channel_id=1, source_target_pairs={{0,2},{2,0},{4,6},{6,4},{8,10},{10,8},{12,14},{14,12},{128,130},{1... | collective-permute-start | bytes 86024 | tf_op jit(solution)/shard_map/ppermute | solution.py:519
  53.6 6.7 %collective-permute-start.12 = (f32[7,8,128]{2,1,0:T(8,128)S(1)}, f32[7,8,128]{2,1,0:T(8,128)S(1)}, u32[]{:S(2)}, u32[]{:S(2)}) collective-permute-start(f32[7,8,128]{2,1,0:T(8,128)S(1)} %add_add_fusion.4.refs_6_), channel_id=1, source_target_pairs={{0,12},{2,14},{4,8},{6,10},{8,4},{10,6},{12,0},{14,2},{128,140},{1... | collective-permute-start | bytes 86024 | tf_op jit(solution)/shard_map/ppermute | solution.py:519
  60.3 7.4 %collective-permute-start.15 = (f32[7,8,128]{2,1,0:T(8,128)S(1)}, f32[7,8,128]{2,1,0:T(8,128)S(1)}, u32[]{:S(2)}, u32[]{:S(2)}) collective-permute-start(f32[7,8,128]{2,1,0:T(8,128)S(1)} %add.79), channel_id=1, source_target_pairs={{0,129},{2,131},{4,133},{6,135},{8,137},{10,139},{12,141},{14,143}... | collective-permute-start | bytes 86024 | tf_op jit(solution)/shard_map/ppermute | solution.py:519
  60.4 7.3 %collective-permute-start.14 = (f32[7,8,128]{2,1,0:T(8,128)S(1)}, f32[7,8,128]{2,1,0:T(8,128)S(1)}, u32[]{:S(2)}, u32[]{:S(2)}) collective-permute-start(f32[7,8,128]{2,1,0:T(8,128)S(1)} %add.79), channel_id=1, source_target_pairs={{0,1},{2,3},{4,5},{6,7},{8,9},{10,11},{12,13},{14,15},{128,129},{1... | collective-permute-start | bytes 86024 | tf_op jit(solution)/shard_map/ppermute | solution.py:519
  63.8 3.9 %collective-permute-start.13 = (f32[7,8,128]{2,1,0:T(8,128)S(1)}, f32[7,8,128]{2,1,0:T(8,128)S(1)}, u32[]{:S(2)}, u32[]{:S(2)}) collective-permute-start(f32[7,8,128]{2,1,0:T(8,128)S(1)} %add.79), channel_id=1, source_target_pairs={{0,128},{2,130},{4,132},{6,134},{8,136},{10,138},{12,140},{14,142}... | collective-permute-start | bytes 86024 | tf_op jit(solution)/shard_map/ppermute | solution.py:519
  67.7 9.0 %collective-permute-start.18 = (f32[28,8,128]{2,1,0:T(8,128)S(1)}, f32[28,8,128]{2,1,0:T(8,128)S(1)}, u32[]{:S(2)}, u32[]{:S(2)}) collective-permute-start(f32[28,8,128]{2,1,0:T(8,128)S(1)} %constant_dynamic-update-slice_fusion.refs_6_), channel_id=1, source_target_pairs={{0,48},{2,50},{4,52},{6,54},{8,56},{10,58},{12,60},{14,62},{128,17... | collective-permute-start | bytes 344072 | tf_op jit(solution)/shard_map/ppermute | solution.py:519
  70.0 6.8 %collective-permute-start.17 = (f32[28,8,128]{2,1,0:T(8,128)S(1)}, f32[28,8,128]{2,1,0:T(8,128)S(1)}, u32[]{:S(2)}, u32[]{:S(2)}) collective-permute-start(f32[28,8,128]{2,1,0:T(8,128)S(1)} %constant_dynamic-update-slice_fusion.refs_6_), channel_id=1, source_target_pairs={{0,32},{2,34},{4,36},{6,38},{8,40},{10,42},{12,44},{14,46},{128,16... | collective-permute-start | bytes 344072 | tf_op jit(solution)/shard_map/ppermute | solution.py:519
  70.2 6.5 %collective-permute-start.16 = (f32[28,8,128]{2,1,0:T(8,128)S(1)}, f32[28,8,128]{2,1,0:T(8,128)S(1)}, u32[]{:S(2)}, u32[]{:S(2)}) collective-permute-start(f32[28,8,128]{2,1,0:T(8,128)S(1)} %constant_dynamic-update-slice_fusion.refs_6_), channel_id=1, source_target_pairs={{0,16},{2,18},{4,20},{6,22},{8,24},{10,26},{12,28},{14,30},{128,14... | collective-permute-start | bytes 344072 | tf_op jit(solution)/shard_map/ppermute | solution.py:519
  78.5 5.5 %collective-permute-start.22 = (f32[32,256]{1,0:T(8,128)S(1)}, f32[32,256]{1,0:T(8,128)S(1)}, u32[]{:S(2)}, u32[]{:S(2)}) collective-permute-start(f32[32,256]{1,0:T(8,128)S(1)} %right_product.1), channel_id=1, source_target_pairs={{0,76},{2,78},{4,72},{6,74},{8,68},{10,70},{12,64},{14,66},{128,20... | collective-permute-start | bytes 98312 | tf_op jit(solution)/shard_map/ppermute | solution.py:519
  78.6 6.2 %collective-permute-start.21 = (f32[32,256]{1,0:T(8,128)S(1)}, f32[32,256]{1,0:T(8,128)S(1)}, u32[]{:S(2)}, u32[]{:S(2)}) collective-permute-start(f32[32,256]{1,0:T(8,128)S(1)} %right_product.1), channel_id=1, source_target_pairs={{0,12},{2,14},{4,8},{6,10},{8,4},{10,6},{12,0},{14,2},{128,140},{1... | collective-permute-start | bytes 98312 | tf_op jit(solution)/shard_map/ppermute | solution.py:519
  80.8 4.0 %collective-permute-start.20 = (f32[32,256]{1,0:T(8,128)S(1)}, f32[32,256]{1,0:T(8,128)S(1)}, u32[]{:S(2)}, u32[]{:S(2)}) collective-permute-start(f32[32,256]{1,0:T(8,128)S(1)} %right_product.1), channel_id=1, source_target_pairs={{0,64},{2,66},{4,68},{6,70},{8,72},{10,74},{12,76},{14,78},{128,19... | collective-permute-start | bytes 98312 | tf_op jit(solution)/shard_map/ppermute | solution.py:519
  84.8 8.6 %collective-permute-start.26 = (f32[4,28,8,128]{3,2,1,0:T(8,128)S(1)}, f32[4,28,8,128]{3,2,1,0:T(8,128)S(1)}, u32[]{:S(2)}, u32[]{:S(2)}) collective-permute-start(f32[4,28,8,128]{3,2,1,0:T(8,128)S(1)} %pad_maximum_fusion.mine), channel_id=1, source_target_pairs={{0,64},{2,66},{4,68},{6,70},{8,72},{10,74},{12,76},{14,78},{128,19... | collective-permute-start | bytes 1376264 | tf_op jit(solution)/shard_map/ppermute | solution.py:519
  85.8 5.1 %collective-permute-start.25 = (f32[32,256]{1,0:T(8,128)S(1)}, f32[32,256]{1,0:T(8,128)S(1)}, u32[]{:S(2)}, u32[]{:S(2)}) collective-permute-start(f32[32,256]{1,0:T(8,128)S(1)} %add_add_fusion.3), channel_id=1, source_target_pairs={{0,48},{2,50},{4,52},{6,54},{8,56},{10,58},{12,60},{14,62},{128,17... | collective-permute-start | bytes 98312 | tf_op jit(solution)/shard_map/ppermute | solution.py:519
  87.9 5.4 %collective-permute-start.24 = (f32[32,256]{1,0:T(8,128)S(1)}, f32[32,256]{1,0:T(8,128)S(1)}, u32[]{:S(2)}, u32[]{:S(2)}) collective-permute-start(f32[32,256]{1,0:T(8,128)S(1)} %add_add_fusion.3), channel_id=1, source_target_pairs={{0,32},{2,34},{4,36},{6,38},{8,40},{10,42},{12,44},{14,46},{128,16... | collective-permute-start | bytes 98312 | tf_op jit(solution)/shard_map/ppermute | solution.py:519
  88.2 5.1 %collective-permute-start.23 = (f32[32,256]{1,0:T(8,128)S(1)}, f32[32,256]{1,0:T(8,128)S(1)}, u32[]{:S(2)}, u32[]{:S(2)}) collective-permute-start(f32[32,256]{1,0:T(8,128)S(1)} %add_add_fusion.3), channel_id=1, source_target_pairs={{0,16},{2,18},{4,20},{6,22},{8,24},{10,26},{12,28},{14,30},{128,14... | collective-permute-start | bytes 98312 | tf_op jit(solution)/shard_map/ppermute | solution.py:519
  93.4 6.5 %collective-permute-start.29 = (f32[32,256]{1,0:T(8,128)S(1)}, f32[32,256]{1,0:T(8,128)S(1)}, u32[]{:S(2)}, u32[]{:S(2)}) collective-permute-start(f32[32,256]{1,0:T(8,128)S(1)} %add_add_fusion.2), channel_id=1, source_target_pairs={{0,129},{2,131},{4,133},{6,135},{8,137},{10,139},{12,141},{14,143}... | collective-permute-start | bytes 98312 | tf_op jit(solution)/shard_map/ppermute | solution.py:519
  93.5 6.4 %collective-permute-start.28 = (f32[32,256]{1,0:T(8,128)S(1)}, f32[32,256]{1,0:T(8,128)S(1)}, u32[]{:S(2)}, u32[]{:S(2)}) collective-permute-start(f32[32,256]{1,0:T(8,128)S(1)} %add_add_fusion.2), channel_id=1, source_target_pairs={{0,1},{2,3},{4,5},{6,7},{8,9},{10,11},{12,13},{14,15},{128,129},{1... | collective-permute-start | bytes 98312 | tf_op jit(solution)/shard_map/ppermute | solution.py:519
  96.2 3.9 %collective-permute-start.27 = (f32[32,256]{1,0:T(8,128)S(1)}, f32[32,256]{1,0:T(8,128)S(1)}, u32[]{:S(2)}, u32[]{:S(2)}) collective-permute-start(f32[32,256]{1,0:T(8,128)S(1)} %add_add_fusion.2), channel_id=1, source_target_pairs={{0,128},{2,130},{4,132},{6,134},{8,136},{10,138},{12,140},{14,142}... | collective-permute-start | bytes 98312 | tf_op jit(solution)/shard_map/ppermute | solution.py:519
  100.1 5.9 %collective-permute-start.32 = (f32[32,256]{1,0:T(8,128)S(1)}, f32[32,256]{1,0:T(8,128)S(1)}, u32[]{:S(2)}, u32[]{:S(2)}) collective-permute-start(f32[32,256]{1,0:T(8,128)S(1)} %add_add_fusion.1.refs_0_), channel_id=1, source_target_pairs={{0,6},{2,4},{4,2},{6,0},{8,14},{10,12},{12,10},{14,8},{128,134},{1... | collective-permute-start | bytes 98312 | tf_op jit(solution)/shard_map/ppermute | solution.py:519
  102.4 4.8 %collective-permute-start.31 = (f32[32,256]{1,0:T(8,128)S(1)}, f32[32,256]{1,0:T(8,128)S(1)}, u32[]{:S(2)}, u32[]{:S(2)}) collective-permute-start(f32[32,256]{1,0:T(8,128)S(1)} %add_add_fusion.1.refs_0_), channel_id=1, source_target_pairs={{0,4},{2,6},{4,0},{6,2},{8,12},{10,14},{12,8},{14,10},{128,132},{1... | collective-permute-start | bytes 98312 | tf_op jit(solution)/shard_map/ppermute | solution.py:519
  102.4 4.8 %collective-permute-start.30 = (f32[32,256]{1,0:T(8,128)S(1)}, f32[32,256]{1,0:T(8,128)S(1)}, u32[]{:S(2)}, u32[]{:S(2)}) collective-permute-start(f32[32,256]{1,0:T(8,128)S(1)} %add_add_fusion.1.refs_0_), channel_id=1, source_target_pairs={{0,2},{2,0},{4,6},{6,4},{8,10},{10,8},{12,14},{14,12},{128,130},{1... | collective-permute-start | bytes 98312 | tf_op jit(solution)/shard_map/ppermute | solution.py:519
  (3 other events, 31.7 us)

commit v8 on v7

--- a/solution.py
+++ b/solution.py
@@ -564,17 +564,16 @@
         (jnp.stack([part] + arrived, axis=0), partner, input_grad)
     )
 
+    other = swapped(mine, core=1)
     right = right_product(mine, kept, partner)
-    right, mine = lax.optimization_barrier((summed_among(right, CORE_AND_Z), mine))
+    right, other = lax.optimization_barrier((summed_among(right, CORE_AND_Z), other))
     arrived = [swapped(right, **bits) for bits in ALONG_X]
-    other = swapped(mine, core=1)
-    right, other = lax.optimization_barrier((added([right] + arrived), other))
-    arrived = [swapped(right, **bits) for bits in ALONG_Y]
     halves = half_inverse(mine, other)
     right, *halves = lax.optimization_barrier((added([right] + arrived), *halves))
-    arrived = [swapped(right, **bits) for bits in ALONG_Z]
+    arrived = [swapped(right, **bits) for bits in ALONG_Y]
     inverse = whole_inverse(*halves, tie=right)
-    right = added([right] + arrived)
+    right, inverse = lax.optimization_barrier((added([right] + arrived), inverse))
+    right = summed_among(right, ALONG_Z)
     new_error, q_rows = remaining_error(mine, other, kept, sent, right, inverse)
     return (input_grad[None], q_rows.T, new_error.reshape(1, 1, 6912, 256))
 

time: 112 us -> 113 us (level)
  waiting for transfers between devices: 20.8 us -> 22.5 us
    ppermute x31, waiting for transfers between devices: 20.8 us -> 22.5 us  [swapped(): return lax.ppermute(value, ('dp', 'space'), partners(**bits))]
  transfers between devices with their start and end apart: 33 -> 33, of which waited for: 14 -> 14; matrix products, arithmetic and copies ran while one was open for 0% -> 0% of each run, Pallas kernels for 19% -> 20%
where the time goes in v8:
time: 113 us
  starting transfers between devices  52.5 us (46%)
  Pallas kernels  36.4 us (32%)
  waiting for transfers between devices  22.5 us (20%)
    ppermute x31, starting transfers between devices, swapped(): return lax.ppermute(value, ('dp', 'space'), partners(**bits))  42.6 us
    ppermute x31, waiting for transfers between devices, swapped(): return lax.ppermute(value, ('dp', 'space'), partners(**bits))  22.5 us
    pallas_call x2, Pallas kernels, local_gradient(): pl.pallas_call(functools.partial(gradient_kernel, sides, width), grid=(le...  13.2 us
    pallas_call x3, Pallas kernels, input_gradient(): pl.pallas_call(functools.partial(input_kernel, side, last), grid=(3,), in...  12.2 us
    ppermute x2, starting transfers between devices, shifted(): lax.ppermute(value, 'space', [(i, (i + by) % devices) for i in range(devi...  9.95 us
    pallas_call x1, Pallas kernels, remaining_error(): pl.pallas_call(error_kernel, grid=(3,), in_specs=[whole(4, 28, 8, 128), w...  3.87 us
    pallas_call x1, Pallas kernels, half_inverse(): pl.pallas_call(first_half_kernel, out_shape=[SQUARE, SQUARE], compiler_pa...  2.36 us
  transfers between devices with their start and end apart: 33, of which 14 were waited for; matrix products, arithmetic and copies ran while one was open for 0% of the time, Pallas kernels for 20%

profile of v8, /device:TPU:8, one launch (start us, length us, event | category | flops | bytes accessed | tf_op | source)
XLA Modules:
  0.0 112.6 jit_solution(6454702561713243982)
XLA Ops:
  0.6 1.6 %brick_faces.1 = (bf16[2,8,16,256]{3,2,1,0:T(8,128)(2,1)S(1)}, bf16[2,8,16,256]{3,2,1,0:T(8,128)(2,1)S(1)}) custom-call(bf16[2,512,256]{2,1,0:T(8,128)(2,1)} %bitcast.34, bf16[2,512,256]{2,1,0:T(8,128)(2,1)} %bitcast.24, s32[2,512]{1,0:T(2,128)} %bitcast.40), custom_call_target="tpu_custom_call" | custom-call | tf_op jit(solution)/shard_map/brick_faces/pallas_call | solution.py:126
  2.3 2.4 %collective-permute-start = (bf16[2,8,16,256]{3,2,1,0:T(8,128)(2,1)S(1)}, bf16[2,8,16,256]{3,2,1,0:T(8,128)(2,1)S(1)}, u32[]{:S(2)}, u32[]{:S(2)}) collective-permute-start(bf16[2,8,16,256]{3,2,1,0:T(8,128)(2,1)S(1)} %get-tuple-element.33), channel_id=1, source_target_pairs={{0,1},{1,2},{2,3},{3,4},{4,5},{5,6},{6,7},{7,8},{8,9},{9,10},{10,1... | collective-permute-start | bytes 393224 | tf_op jit(solution)/shard_map/ppermute | solution.py:502
  4.7 7.6 %collective-permute-start.1 = (bf16[2,8,16,256]{3,2,1,0:T(8,128)(2,1)S(1)}, bf16[2,8,16,256]{3,2,1,0:T(8,128)(2,1)S(1)}, u32[]{:S(2)}, u32[]{:S(2)}) collective-permute-start(bf16[2,8,16,256]{3,2,1,0:T(8,128)(2,1)S(1)} %get-tuple-element.34), channel_id=1, source_target_pairs={{0,63},{1,0},{2,1},{3,2},{4,3},{5,4},{6,5},{7,6},{8,7},{9,8},{10,9... | collective-permute-start | bytes 393224 | tf_op jit(solution)/shard_map/ppermute | solution.py:502
  12.2 4.8 %gradient_own.1 = (f32[3,3,3,128,256]{4,3,2,1,0:T(8,128)S(1)}, f32[3,3,3,128,256]{4,3,2,1,0:T(8,128)S(1)}, f32[4,28,8,128]{3,2,1,0:T(8,128)S(1)}, f32[4,28,8,128]{3,2,1,0:T(8,128)S(1)}) custom-call(s32[2,27]{1,0:T(2,128)} %bitcast.52, bf16[2,512,256]{2,1,0:T(8,128)(2,1)} %bitcast.35, bf16[2,512,256]{2,1,0:T(8,128)(2,1)} %bitcast.25, s32[2,512]{1,0:T(2,128)} %bitcast.41, ...), custom_call_target="tpu_custom_call" | custom-call | flops 2000000000 | bytes 4000000 | tf_op jit(solution)/shard_map/gradient_own/pallas_call | solution.py:236
  17.1 8.4 %gradient_with_faces.1 = (f32[3,3,3,128,256]{4,3,2,1,0:T(8,128)S(1)}, f32[3,3,3,128,256]{4,3,2,1,0:T(8,128)S(1)}, f32[4,28,8,128]{3,2,1,0:T(8,128)S(1)}, f32[4,28,8,128]{3,2,1,0:T(8,128)S(1)}) custom-call(s32[2,27]{1,0:T(2,128)} %bitcast.53, bf16[2,512,256]{2,1,0:T(8,128)(2,1)} %bitcast.36, ...), custom_call_target="tpu_custom_call", output_to_operand_aliasing={{0}: (8, {}), {1}: (9, {})} | custom-call | flops 4000000000 | bytes 8000000 | tf_op jit(solution)/shard_map/gradient_with_faces/pallas_call | solution.py:236
  25.6 1.8 %collective-permute-done.2 = f32[4,28,8,128]{3,2,1,0:T(8,128)S(1)} collective-permute-done((f32[4,28,8,128]{3,2,1,0:T(8,128)S(1)}, f32[4,28,8,128]{3,2,1,0:T(8,128)S(1)}, u32[]{:S(2)}, u32[]{:S(2)}) %collective-permute-start.2) | collective-permute-done | bytes 458784 | tf_op jit(solution)/shard_map/ppermute | solution.py:519
  29.2 2.8 %collective-permute-start.3 = (f32[28,8,128]{2,1,0:T(8,128)S(1)}, f32[28,8,128]{2,1,0:T(8,128)S(1)}, u32[]{:S(2)}, u32[]{:S(2)}) collective-permute-start(f32[28,8,128]{2,1,0:T(8,128)S(1)} %get-tuple-element.65), channel_id=1, source_target_pairs={{0,16},{2,18},{4,20},{6,22},{8,24},{10,26},{12,28},{14,30},{128,14... | collective-permute-start | bytes 344072 | tf_op jit(solution)/shard_map/ppermute | solution.py:519
  31.9 3.6 %input_own.1.refs_5_ = f32[1024,256]{1,0:T(8,128)S(1)} custom-call(s32[2,27]{1,0:T(2,128)} %bitcast.54, bf16[2,512,256]{2,1,0:T(8,128)(2,1)S(1)} %bitcast.27, s32[2,512]{1,0:T(2,128)} %bitcast.43, bf16[3,3,3,256,256]{4,3,2,1,0:T(8,128)(2,1)S(1)} %bitcast.31, f32[4,28,8,128]{3,2,1,0:T(8,128)S(1)} %add.69.refs_4_), custom_call_target="tpu_custom_call" | custom-call | flops 2000000000 | bytes 4000000 | tf_op jit(solution)/shard_map/input_own/pallas_call | solution.py:321
  37.5 1.4 %collective-permute-start.6 = (f32[7,8,128]{2,1,0:T(8,128)S(1)}, f32[7,8,128]{2,1,0:T(8,128)S(1)}, u32[]{:S(2)}, u32[]{:S(2)}) collective-permute-start(f32[7,8,128]{2,1,0:T(8,128)S(1)} %get-tuple-element.66), channel_id=1, source_target_pairs={{0,128},{2,130},{4,132},{6,134},{8,136},{10,138},{12,140},{14,142}... | collective-permute-start | bytes 86024 | tf_op jit(solution)/shard_map/ppermute | solution.py:519
  39.0 2.7 %collective-permute-start.7 = (f32[7,8,128]{2,1,0:T(8,128)S(1)}, f32[7,8,128]{2,1,0:T(8,128)S(1)}, u32[]{:S(2)}, u32[]{:S(2)}) collective-permute-start(f32[7,8,128]{2,1,0:T(8,128)S(1)} %get-tuple-element.68), channel_id=1, source_target_pairs={{0,1},{2,3},{4,5},{6,7},{8,9},{10,11},{12,13},{14,15},{128,129},{1... | collective-permute-start | bytes 86024 | tf_op jit(solution)/shard_map/ppermute | solution.py:519
  42.8 1.5 %collective-permute-done.7 = f32[7,8,128]{2,1,0:T(8,128)S(1)} collective-permute-done((f32[7,8,128]{2,1,0:T(8,128)S(1)}, f32[7,8,128]{2,1,0:T(8,128)S(1)}, u32[]{:S(2)}, u32[]{:S(2)}) %collective-permute-start.7) | collective-permute-done | bytes 28704 | tf_op jit(solution)/shard_map/ppermute | solution.py:519
  44.4 4.5 %collective-permute-start.11 = (f32[7,8,128]{2,1,0:T(8,128)S(1)}, f32[7,8,128]{2,1,0:T(8,128)S(1)}, u32[]{:S(2)}, u32[]{:S(2)}) collective-permute-start(f32[7,8,128]{2,1,0:T(8,128)S(1)} %add_add_fusion.5), channel_id=1, source_target_pairs={{0,6},{2,4},{4,2},{6,0},{8,14},{10,12},{12,10},{14,8},{128,134},{1... | collective-permute-start | bytes 86024 | tf_op jit(solution)/shard_map/ppermute | solution.py:519
  50.8 2.8 %collective-permute-done.10 = f32[7,8,128]{2,1,0:T(8,128)S(1)} collective-permute-done((f32[7,8,128]{2,1,0:T(8,128)S(1)}, f32[7,8,128]{2,1,0:T(8,128)S(1)}, u32[]{:S(2)}, u32[]{:S(2)}) %collective-permute-start.10) | collective-permute-done | bytes 28704 | tf_op jit(solution)/shard_map/ppermute | solution.py:519
  53.6 2.9 %collective-permute-start.12 = (f32[7,8,128]{2,1,0:T(8,128)S(1)}, f32[7,8,128]{2,1,0:T(8,128)S(1)}, u32[]{:S(2)}, u32[]{:S(2)}) collective-permute-start(f32[7,8,128]{2,1,0:T(8,128)S(1)} %add_add_fusion.4.refs_6_), channel_id=1, source_target_pairs={{0,12},{2,14},{4,8},{6,10},{8,4},{10,6},{12,0},{14,2},{128,140},{1... | collective-permute-start | bytes 86024 | tf_op jit(solution)/shard_map/ppermute | solution.py:519
  56.5 3.7 %input_below.1.refs_5_ = f32[1024,256]{1,0:T(8,128)S(1)} custom-call(s32[2,27]{1,0:T(2,128)} %bitcast.55, bf16[2,512,256]{2,1,0:T(8,128)(2,1)S(1)} %bitcast.28, s32[2,512]{1,0:T(2,128)} %bitcast.44, bf16[3,3,3,256,256]{4,3,2,1,0:T(8,128)(2,1)S(1)} %bitcast.32, bf16[2,8,16,256]{3,2,1,0:T(8,128)(2,1)S(1)} %collective-permute-done.1.refs_7_.refs_4_, ...), custom_call_target="tpu_custom_call" | custom-call | flops 2000000000 | bytes 4000000 | tf_op jit(solution)/shard_map/input_below/pallas_call | solution.py:321
  60.4 3.4 %collective-permute-start.14 = (f32[7,8,128]{2,1,0:T(8,128)S(1)}, f32[7,8,128]{2,1,0:T(8,128)S(1)}, u32[]{:S(2)}, u32[]{:S(2)}) collective-permute-start(f32[7,8,128]{2,1,0:T(8,128)S(1)} %add.79), channel_id=1, source_target_pairs={{0,1},{2,3},{4,5},{6,7},{8,9},{10,11},{12,13},{14,15},{128,129},{1... | collective-permute-start | bytes 86024 | tf_op jit(solution)/shard_map/ppermute | solution.py:519
  64.5 3.2 %collective-permute-done.13 = f32[7,8,128]{2,1,0:T(8,128)S(1)} collective-permute-done((f32[7,8,128]{2,1,0:T(8,128)S(1)}, f32[7,8,128]{2,1,0:T(8,128)S(1)}, u32[]{:S(2)}, u32[]{:S(2)}) %collective-permute-start.13) | collective-permute-done | bytes 28704 | tf_op jit(solution)/shard_map/ppermute | solution.py:519
  67.7 2.2 %collective-permute-start.18 = (f32[28,8,128]{2,1,0:T(8,128)S(1)}, f32[28,8,128]{2,1,0:T(8,128)S(1)}, u32[]{:S(2)}, u32[]{:S(2)}) collective-permute-start(f32[28,8,128]{2,1,0:T(8,128)S(1)} %constant_dynamic-update-slice_fusion.refs_6_), channel_id=1, source_target_pairs={{0,48},{2,50},{4,52},{6,54},{8,56},{10,58},{12,60},{14,62},{128,17... | collective-permute-start | bytes 344072 | tf_op jit(solution)/shard_map/ppermute | solution.py:519
  70.2 1.7 %collective-permute-start.16 = (f32[28,8,128]{2,1,0:T(8,128)S(1)}, f32[28,8,128]{2,1,0:T(8,128)S(1)}, u32[]{:S(2)}, u32[]{:S(2)}) collective-permute-start(f32[28,8,128]{2,1,0:T(8,128)S(1)} %constant_dynamic-update-slice_fusion.refs_6_), channel_id=1, source_target_pairs={{0,16},{2,18},{4,20},{6,22},{8,24},{10,26},{12,28},{14,30},{128,14... | collective-permute-start | bytes 344072 | tf_op jit(solution)/shard_map/ppermute | solution.py:519
  71.9 4.8 %input_above.1 = bf16[2,512,256]{2,1,0:T(8,128)(2,1)} custom-call(s32[2,27]{1,0:T(2,128)} %bitcast.56, bf16[2,512,256]{2,1,0:T(8,128)(2,1)S(1)} %bitcast.29, s32[2,512]{1,0:T(2,128)} %bitcast.45, bf16[3,3,3,256,256]{4,3,2,1,0:T(8,128)(2,1)S(1)} %bitcast.33, bf16[2,8,16,256]{3,2,1,0:T(8,128)(2,1)S(1)} %collective-permute-done.refs_6_.refs_4_, ...), custom_call_target="tpu_custom_call" | custom-call | flops 2000000000 | bytes 4000000 | tf_op jit(solution)/shard_map/input_above/pallas_call | solution.py:321
  77.1 1.7 %right_product.1 = f32[32,256]{1,0:T(8,128)S(1)} custom-call(f32[4,28,8,128]{3,2,1,0:T(8,128)S(1)} %pad_maximum_fusion.mine, f32[3,3,3,128,256]{4,3,2,1,0:T(8,128)S(1)} %get-tuple-element.50.kept, f32[3,3,3,128,256]{4,3,2,1,0:T(8,128)S(1)} %collective-permute-done.19.partner), custom_call_target="tpu_custom_call" | custom-call | tf_op jit(solution)/shard_map/right_product/pallas_call | solution.py:368
  78.8 2.3 %collective-permute-start.22 = (f32[32,256]{1,0:T(8,128)S(1)}, f32[32,256]{1,0:T(8,128)S(1)}, u32[]{:S(2)}, u32[]{:S(2)}) collective-permute-start(f32[32,256]{1,0:T(8,128)S(1)} %right_product.1), channel_id=1, source_target_pairs={{0,76},{2,78},{4,72},{6,74},{8,68},{10,70},{12,64},{14,66},{128,20... | collective-permute-start | bytes 98312 | tf_op jit(solution)/shard_map/ppermute | solution.py:519
  81.1 2.0 %collective-permute-start.21 = (f32[32,256]{1,0:T(8,128)S(1)}, f32[32,256]{1,0:T(8,128)S(1)}, u32[]{:S(2)}, u32[]{:S(2)}) collective-permute-start(f32[32,256]{1,0:T(8,128)S(1)} %right_product.1), channel_id=1, source_target_pairs={{0,12},{2,14},{4,8},{6,10},{8,4},{10,6},{12,0},{14,2},{128,140},{1... | collective-permute-start | bytes 98312 | tf_op jit(solution)/shard_map/ppermute | solution.py:519
  84.3 2.8 %collective-permute-done.21 = f32[32,256]{1,0:T(8,128)S(1)} collective-permute-done((f32[32,256]{1,0:T(8,128)S(1)}, f32[32,256]{1,0:T(8,128)S(1)}, u32[]{:S(2)}, u32[]{:S(2)}) %collective-permute-start.21) | collective-permute-done | bytes 32800 | tf_op jit(solution)/shard_map/ppermute | solution.py:519
  87.1 2.2 %collective-permute-start.26 = (f32[32,256]{1,0:T(8,128)S(1)}, f32[32,256]{1,0:T(8,128)S(1)}, u32[]{:S(2)}, u32[]{:S(2)}) collective-permute-start(f32[32,256]{1,0:T(8,128)S(1)} %add_add_fusion.3), channel_id=1, source_target_pairs={{0,48},{2,50},{4,52},{6,54},{8,56},{10,58},{12,60},{14,62},{128,17... | collective-permute-start | bytes 98312 | tf_op jit(solution)/shard_map/ppermute | solution.py:519
  89.7 1.7 %collective-permute-start.24 = (f32[32,256]{1,0:T(8,128)S(1)}, f32[32,256]{1,0:T(8,128)S(1)}, u32[]{:S(2)}, u32[]{:S(2)}) collective-permute-start(f32[32,256]{1,0:T(8,128)S(1)} %add_add_fusion.3), channel_id=1, source_target_pairs={{0,16},{2,18},{4,20},{6,22},{8,24},{10,26},{12,28},{14,30},{128,14... | collective-permute-start | bytes 98312 | tf_op jit(solution)/shard_map/ppermute | solution.py:519
  91.3 2.4 %half_inverse.1 = (f32[32,32]{1,0:T(8,128)S(1)}, f32[32,32]{1,0:T(8,128)S(1)}) custom-call(f32[4,28,8,128]{3,2,1,0:T(8,128)S(1)} %pad_maximum_fusion.mine, f32[4,28,8,128]{3,2,1,0:T(8,128)S(1)} %collective-permute-done.23.other), custom_call_target="tpu_custom_call" | custom-call | tf_op jit(solution)/shard_map/half_inverse/pallas_call | solution.py:411
  95.0 2.7 %collective-permute-start.28 = (f32[32,256]{1,0:T(8,128)S(1)}, f32[32,256]{1,0:T(8,128)S(1)}, u32[]{:S(2)}, u32[]{:S(2)}) collective-permute-start(f32[32,256]{1,0:T(8,128)S(1)} %add_add_fusion.2.refs_0_), channel_id=1, source_target_pairs={{0,1},{2,3},{4,5},{6,7},{8,9},{10,11},{12,13},{14,15},{128,129},{1... | collective-permute-start | bytes 98312 | tf_op jit(solution)/shard_map/ppermute | solution.py:519
  99.0 1.4 %whole_inverse.1.inverse = f32[32,32]{1,0:T(8,128)S(1)} custom-call(f32[32,32]{1,0:T(8,128)S(1)} %get-tuple-element.57.work, f32[32,32]{1,0:T(8,128)S(1)} %get-tuple-element.58.made, f32[32,256]{1,0:T(8,128)S(1)} %add_add_fusion.2.refs_0_), custom_call_target="tpu_custom_call" | custom-call | tf_op jit(solution)/shard_map/whole_inverse/pallas_call | solution.py:422
  101.6 2.3 %collective-permute-start.32 = (f32[32,256]{1,0:T(8,128)S(1)}, f32[32,256]{1,0:T(8,128)S(1)}, u32[]{:S(2)}, u32[]{:S(2)}) collective-permute-start(f32[32,256]{1,0:T(8,128)S(1)} %add_add_fusion.1), channel_id=1, source_target_pairs={{0,6},{2,4},{4,2},{6,0},{8,14},{10,12},{12,10},{14,8},{128,134},{1... | collective-permute-start | bytes 98312 | tf_op jit(solution)/shard_map/ppermute | solution.py:519
  104.0 2.1 %collective-permute-start.30 = (f32[32,256]{1,0:T(8,128)S(1)}, f32[32,256]{1,0:T(8,128)S(1)}, u32[]{:S(2)}, u32[]{:S(2)}) collective-permute-start(f32[32,256]{1,0:T(8,128)S(1)} %add_add_fusion.1), channel_id=1, source_target_pairs={{0,2},{2,0},{4,6},{6,4},{8,10},{10,8},{12,14},{14,12},{128,130},{1... | collective-permute-start | bytes 98312 | tf_op jit(solution)/shard_map/ppermute | solution.py:519
  108.7 3.9 %remaining_error.1 = (bf16[3,3,3,256,256]{4,3,2,1,0:T(8,128)(2,1)}, f32[32,256]{1,0:T(8,128)}) custom-call(f32[4,28,8,128]{3,2,1,0:T(8,128)S(1)} %pad_maximum_fusion.mine, f32[4,28,8,128]{3,2,1,0:T(8,128)S(1)} %collective-permute-done.23.other, f32[3,3,3,128,256]{4,3,2,1,0:T(8,128)S(1)} %get-tuple-element.50.kept, ...), custom_call_target="tpu_custom_call" | custom-call | tf_op jit(solution)/shard_map/remaining_error/pallas_call | solution.py:464
  (64 shorter events, 16.4 us)
Async XLA Ops:
  2.3 14.7 %collective-permute-start = (bf16[2,8,16,256]{3,2,1,0:T(8,128)(2,1)S(1)}, bf16[2,8,16,256]{3,2,1,0:T(8,128)(2,1)S(1)}, u32[]{:S(2)}, u32[]{:S(2)}) collective-permute-start(bf16[2,8,16,256]{3,2,1,0:T(8,128)(2,1)S(1)} %get-tuple-element.33), channel_id=1, source_target_pairs={{0,1},{1,2},{2,3},{3,4},{4,5},{5,6},{6,7},{7,8},{8,9},{9,10},{10,1... | collective-permute-start | bytes 393224 | tf_op jit(solution)/shard_map/ppermute | solution.py:502
  4.7 12.4 %collective-permute-start.1 = (bf16[2,8,16,256]{3,2,1,0:T(8,128)(2,1)S(1)}, bf16[2,8,16,256]{3,2,1,0:T(8,128)(2,1)S(1)}, u32[]{:S(2)}, u32[]{:S(2)}) collective-permute-start(bf16[2,8,16,256]{3,2,1,0:T(8,128)(2,1)S(1)} %get-tuple-element.34), channel_id=1, source_target_pairs={{0,63},{1,0},{2,1},{3,2},{4,3},{5,4},{6,5},{7,6},{8,7},{9,8},{10,9... | collective-permute-start | bytes 393224 | tf_op jit(solution)/shard_map/ppermute | solution.py:502
  27.5 49.3 %collective-permute-start.19 = (f32[3,3,3,128,256]{4,3,2,1,0:T(8,128)S(1)}, f32[3,3,3,128,256]{4,3,2,1,0:T(8,128)S(1)}, u32[]{:S(2)}, u32[]{:S(2)}) collective-permute-start(f32[3,3,3,128,256]{4,3,2,1,0:T(8,128)S(1)} %get-tuple-element.46.sent), channel_id=1, source_target_pairs={{0,64},{2,66},{4,68},{6,70},{8,72},{10,74},{12,76},{14,78},{128,19... | collective-permute-start | bytes 10616840 | tf_op jit(solution)/shard_map/ppermute | solution.py:519
  27.7 9.2 %collective-permute-start.5 = (f32[28,8,128]{2,1,0:T(8,128)S(1)}, f32[28,8,128]{2,1,0:T(8,128)S(1)}, u32[]{:S(2)}, u32[]{:S(2)}) collective-permute-start(f32[28,8,128]{2,1,0:T(8,128)S(1)} %get-tuple-element.63), channel_id=1, source_target_pairs={{0,48},{2,50},{4,52},{6,54},{8,56},{10,58},{12,60},{14,62},{128,17... | collective-permute-start | bytes 344072 | tf_op jit(solution)/shard_map/ppermute | solution.py:519
  28.7 8.3 %collective-permute-start.4 = (f32[28,8,128]{2,1,0:T(8,128)S(1)}, f32[28,8,128]{2,1,0:T(8,128)S(1)}, u32[]{:S(2)}, u32[]{:S(2)}) collective-permute-start(f32[28,8,128]{2,1,0:T(8,128)S(1)} %get-tuple-element.64), channel_id=1, source_target_pairs={{0,32},{2,34},{4,36},{6,38},{8,40},{10,42},{12,44},{14,46},{128,16... | collective-permute-start | bytes 344072 | tf_op jit(solution)/shard_map/ppermute | solution.py:519
  29.2 8.3 %collective-permute-start.3 = (f32[28,8,128]{2,1,0:T(8,128)S(1)}, f32[28,8,128]{2,1,0:T(8,128)S(1)}, u32[]{:S(2)}, u32[]{:S(2)}) collective-permute-start(f32[28,8,128]{2,1,0:T(8,128)S(1)} %get-tuple-element.65), channel_id=1, source_target_pairs={{0,16},{2,18},{4,20},{6,22},{8,24},{10,26},{12,28},{14,30},{128,14... | collective-permute-start | bytes 344072 | tf_op jit(solution)/shard_map/ppermute | solution.py:519
  37.5 4.2 %collective-permute-start.6 = (f32[7,8,128]{2,1,0:T(8,128)S(1)}, f32[7,8,128]{2,1,0:T(8,128)S(1)}, u32[]{:S(2)}, u32[]{:S(2)}) collective-permute-start(f32[7,8,128]{2,1,0:T(8,128)S(1)} %get-tuple-element.66), channel_id=1, source_target_pairs={{0,128},{2,130},{4,132},{6,134},{8,136},{10,138},{12,140},{14,142}... | collective-permute-start | bytes 86024 | tf_op jit(solution)/shard_map/ppermute | solution.py:519
  39.0 3.9 %collective-permute-start.8 = (f32[7,8,128]{2,1,0:T(8,128)S(1)}, f32[7,8,128]{2,1,0:T(8,128)S(1)}, u32[]{:S(2)}, u32[]{:S(2)}) collective-permute-start(f32[7,8,128]{2,1,0:T(8,128)S(1)} %get-tuple-element.67), channel_id=1, source_target_pairs={{0,129},{2,131},{4,133},{6,135},{8,137},{10,139},{12,141},{14,143}... | collective-permute-start | bytes 86024 | tf_op jit(solution)/shard_map/ppermute | solution.py:519
  39.0 5.4 %collective-permute-start.7 = (f32[7,8,128]{2,1,0:T(8,128)S(1)}, f32[7,8,128]{2,1,0:T(8,128)S(1)}, u32[]{:S(2)}, u32[]{:S(2)}) collective-permute-start(f32[7,8,128]{2,1,0:T(8,128)S(1)} %get-tuple-element.68), channel_id=1, source_target_pairs={{0,1},{2,3},{4,5},{6,7},{8,9},{10,11},{12,13},{14,15},{128,129},{1... | collective-permute-start | bytes 86024 | tf_op jit(solution)/shard_map/ppermute | solution.py:519
  44.4 6.5 %collective-permute-start.11 = (f32[7,8,128]{2,1,0:T(8,128)S(1)}, f32[7,8,128]{2,1,0:T(8,128)S(1)}, u32[]{:S(2)}, u32[]{:S(2)}) collective-permute-start(f32[7,8,128]{2,1,0:T(8,128)S(1)} %add_add_fusion.5), channel_id=1, source_target_pairs={{0,6},{2,4},{4,2},{6,0},{8,14},{10,12},{12,10},{14,8},{128,134},{1... | collective-permute-start | bytes 86024 | tf_op jit(solution)/shard_map/ppermute | solution.py:519
  48.8 4.8 %collective-permute-start.10 = (f32[7,8,128]{2,1,0:T(8,128)S(1)}, f32[7,8,128]{2,1,0:T(8,128)S(1)}, u32[]{:S(2)}, u32[]{:S(2)}) collective-permute-start(f32[7,8,128]{2,1,0:T(8,128)S(1)} %add_add_fusion.5), channel_id=1, source_target_pairs={{0,4},{2,6},{4,0},{6,2},{8,12},{10,14},{12,8},{14,10},{128,132},{1... | collective-permute-start | bytes 86024 | tf_op jit(solution)/shard_map/ppermute | solution.py:519
  48.9 4.8 %collective-permute-start.9 = (f32[7,8,128]{2,1,0:T(8,128)S(1)}, f32[7,8,128]{2,1,0:T(8,128)S(1)}, u32[]{:S(2)}, u32[]{:S(2)}) collective-permute-start(f32[7,8,128]{2,1,0:T(8,128)S(1)} %add_add_fusion.5), channel_id=1, source_target_pairs={{0,2},{2,0},{4,6},{6,4},{8,10},{10,8},{12,14},{14,12},{128,130},{1... | collective-permute-start | bytes 86024 | tf_op jit(solution)/shard_map/ppermute | solution.py:519
  53.6 6.7 %collective-permute-start.12 = (f32[7,8,128]{2,1,0:T(8,128)S(1)}, f32[7,8,128]{2,1,0:T(8,128)S(1)}, u32[]{:S(2)}, u32[]{:S(2)}) collective-permute-start(f32[7,8,128]{2,1,0:T(8,128)S(1)} %add_add_fusion.4.refs_6_), channel_id=1, source_target_pairs={{0,12},{2,14},{4,8},{6,10},{8,4},{10,6},{12,0},{14,2},{128,140},{1... | collective-permute-start | bytes 86024 | tf_op jit(solution)/shard_map/ppermute | solution.py:519
  60.3 7.4 %collective-permute-start.15 = (f32[7,8,128]{2,1,0:T(8,128)S(1)}, f32[7,8,128]{2,1,0:T(8,128)S(1)}, u32[]{:S(2)}, u32[]{:S(2)}) collective-permute-start(f32[7,8,128]{2,1,0:T(8,128)S(1)} %add.79), channel_id=1, source_target_pairs={{0,129},{2,131},{4,133},{6,135},{8,137},{10,139},{12,141},{14,143}... | collective-permute-start | bytes 86024 | tf_op jit(solution)/shard_map/ppermute | solution.py:519
  60.4 7.3 %collective-permute-start.14 = (f32[7,8,128]{2,1,0:T(8,128)S(1)}, f32[7,8,128]{2,1,0:T(8,128)S(1)}, u32[]{:S(2)}, u32[]{:S(2)}) collective-permute-start(f32[7,8,128]{2,1,0:T(8,128)S(1)} %add.79), channel_id=1, source_target_pairs={{0,1},{2,3},{4,5},{6,7},{8,9},{10,11},{12,13},{14,15},{128,129},{1... | collective-permute-start | bytes 86024 | tf_op jit(solution)/shard_map/ppermute | solution.py:519
  63.8 3.9 %collective-permute-start.13 = (f32[7,8,128]{2,1,0:T(8,128)S(1)}, f32[7,8,128]{2,1,0:T(8,128)S(1)}, u32[]{:S(2)}, u32[]{:S(2)}) collective-permute-start(f32[7,8,128]{2,1,0:T(8,128)S(1)} %add.79), channel_id=1, source_target_pairs={{0,128},{2,130},{4,132},{6,134},{8,136},{10,138},{12,140},{14,142}... | collective-permute-start | bytes 86024 | tf_op jit(solution)/shard_map/ppermute | solution.py:519
  67.7 9.0 %collective-permute-start.18 = (f32[28,8,128]{2,1,0:T(8,128)S(1)}, f32[28,8,128]{2,1,0:T(8,128)S(1)}, u32[]{:S(2)}, u32[]{:S(2)}) collective-permute-start(f32[28,8,128]{2,1,0:T(8,128)S(1)} %constant_dynamic-update-slice_fusion.refs_6_), channel_id=1, source_target_pairs={{0,48},{2,50},{4,52},{6,54},{8,56},{10,58},{12,60},{14,62},{128,17... | collective-permute-start | bytes 344072 | tf_op jit(solution)/shard_map/ppermute | solution.py:519
  70.0 6.8 %collective-permute-start.17 = (f32[28,8,128]{2,1,0:T(8,128)S(1)}, f32[28,8,128]{2,1,0:T(8,128)S(1)}, u32[]{:S(2)}, u32[]{:S(2)}) collective-permute-start(f32[28,8,128]{2,1,0:T(8,128)S(1)} %constant_dynamic-update-slice_fusion.refs_6_), channel_id=1, source_target_pairs={{0,32},{2,34},{4,36},{6,38},{8,40},{10,42},{12,44},{14,46},{128,16... | collective-permute-start | bytes 344072 | tf_op jit(solution)/shard_map/ppermute | solution.py:519
  70.2 6.5 %collective-permute-start.16 = (f32[28,8,128]{2,1,0:T(8,128)S(1)}, f32[28,8,128]{2,1,0:T(8,128)S(1)}, u32[]{:S(2)}, u32[]{:S(2)}) collective-permute-start(f32[28,8,128]{2,1,0:T(8,128)S(1)} %constant_dynamic-update-slice_fusion.refs_6_), channel_id=1, source_target_pairs={{0,16},{2,18},{4,20},{6,22},{8,24},{10,26},{12,28},{14,30},{128,14... | collective-permute-start | bytes 344072 | tf_op jit(solution)/shard_map/ppermute | solution.py:519
  76.8 10.3 %collective-permute-start.23 = (f32[4,28,8,128]{3,2,1,0:T(8,128)S(1)}, f32[4,28,8,128]{3,2,1,0:T(8,128)S(1)}, u32[]{:S(2)}, u32[]{:S(2)}) collective-permute-start(f32[4,28,8,128]{3,2,1,0:T(8,128)S(1)} %pad_maximum_fusion.mine), channel_id=1, source_target_pairs={{0,64},{2,66},{4,68},{6,70},{8,72},{10,74},{12,76},{14,78},{128,19... | collective-permute-start | bytes 1376264 | tf_op jit(solution)/shard_map/ppermute | solution.py:519
  78.8 5.5 %collective-permute-start.22 = (f32[32,256]{1,0:T(8,128)S(1)}, f32[32,256]{1,0:T(8,128)S(1)}, u32[]{:S(2)}, u32[]{:S(2)}) collective-permute-start(f32[32,256]{1,0:T(8,128)S(1)} %right_product.1), channel_id=1, source_target_pairs={{0,76},{2,78},{4,72},{6,74},{8,68},{10,70},{12,64},{14,66},{128,20... | collective-permute-start | bytes 98312 | tf_op jit(solution)/shard_map/ppermute | solution.py:519
  81.1 6.0 %collective-permute-start.21 = (f32[32,256]{1,0:T(8,128)S(1)}, f32[32,256]{1,0:T(8,128)S(1)}, u32[]{:S(2)}, u32[]{:S(2)}) collective-permute-start(f32[32,256]{1,0:T(8,128)S(1)} %right_product.1), channel_id=1, source_target_pairs={{0,12},{2,14},{4,8},{6,10},{8,4},{10,6},{12,0},{14,2},{128,140},{1... | collective-permute-start | bytes 98312 | tf_op jit(solution)/shard_map/ppermute | solution.py:519
  83.1 4.0 %collective-permute-start.20 = (f32[32,256]{1,0:T(8,128)S(1)}, f32[32,256]{1,0:T(8,128)S(1)}, u32[]{:S(2)}, u32[]{:S(2)}) collective-permute-start(f32[32,256]{1,0:T(8,128)S(1)} %right_product.1), channel_id=1, source_target_pairs={{0,64},{2,66},{4,68},{6,70},{8,72},{10,74},{12,76},{14,78},{128,19... | collective-permute-start | bytes 98312 | tf_op jit(solution)/shard_map/ppermute | solution.py:519
  87.1 6.5 %collective-permute-start.26 = (f32[32,256]{1,0:T(8,128)S(1)}, f32[32,256]{1,0:T(8,128)S(1)}, u32[]{:S(2)}, u32[]{:S(2)}) collective-permute-start(f32[32,256]{1,0:T(8,128)S(1)} %add_add_fusion.3), channel_id=1, source_target_pairs={{0,48},{2,50},{4,52},{6,54},{8,56},{10,58},{12,60},{14,62},{128,17... | collective-permute-start | bytes 98312 | tf_op jit(solution)/shard_map/ppermute | solution.py:519
  89.4 5.4 %collective-permute-start.25 = (f32[32,256]{1,0:T(8,128)S(1)}, f32[32,256]{1,0:T(8,128)S(1)}, u32[]{:S(2)}, u32[]{:S(2)}) collective-permute-start(f32[32,256]{1,0:T(8,128)S(1)} %add_add_fusion.3), channel_id=1, source_target_pairs={{0,32},{2,34},{4,36},{6,38},{8,40},{10,42},{12,44},{14,46},{128,16... | collective-permute-start | bytes 98312 | tf_op jit(solution)/shard_map/ppermute | solution.py:519
  89.7 5.1 %collective-permute-start.24 = (f32[32,256]{1,0:T(8,128)S(1)}, f32[32,256]{1,0:T(8,128)S(1)}, u32[]{:S(2)}, u32[]{:S(2)}) collective-permute-start(f32[32,256]{1,0:T(8,128)S(1)} %add_add_fusion.3), channel_id=1, source_target_pairs={{0,16},{2,18},{4,20},{6,22},{8,24},{10,26},{12,28},{14,30},{128,14... | collective-permute-start | bytes 98312 | tf_op jit(solution)/shard_map/ppermute | solution.py:519
  94.8 5.6 %collective-permute-start.29 = (f32[32,256]{1,0:T(8,128)S(1)}, f32[32,256]{1,0:T(8,128)S(1)}, u32[]{:S(2)}, u32[]{:S(2)}) collective-permute-start(f32[32,256]{1,0:T(8,128)S(1)} %add_add_fusion.2.refs_0_), channel_id=1, source_target_pairs={{0,129},{2,131},{4,133},{6,135},{8,137},{10,139},{12,141},{14,143}... | collective-permute-start | bytes 98312 | tf_op jit(solution)/shard_map/ppermute | solution.py:519
  95.0 5.5 %collective-permute-start.28 = (f32[32,256]{1,0:T(8,128)S(1)}, f32[32,256]{1,0:T(8,128)S(1)}, u32[]{:S(2)}, u32[]{:S(2)}) collective-permute-start(f32[32,256]{1,0:T(8,128)S(1)} %add_add_fusion.2.refs_0_), channel_id=1, source_target_pairs={{0,1},{2,3},{4,5},{6,7},{8,9},{10,11},{12,13},{14,15},{128,129},{1... | collective-permute-start | bytes 98312 | tf_op jit(solution)/shard_map/ppermute | solution.py:519
  97.6 3.9 %collective-permute-start.27 = (f32[32,256]{1,0:T(8,128)S(1)}, f32[32,256]{1,0:T(8,128)S(1)}, u32[]{:S(2)}, u32[]{:S(2)}) collective-permute-start(f32[32,256]{1,0:T(8,128)S(1)} %add_add_fusion.2.refs_0_), channel_id=1, source_target_pairs={{0,128},{2,130},{4,132},{6,134},{8,136},{10,138},{12,140},{14,142}... | collective-permute-start | bytes 98312 | tf_op jit(solution)/shard_map/ppermute | solution.py:519
  101.6 5.8 %collective-permute-start.32 = (f32[32,256]{1,0:T(8,128)S(1)}, f32[32,256]{1,0:T(8,128)S(1)}, u32[]{:S(2)}, u32[]{:S(2)}) collective-permute-start(f32[32,256]{1,0:T(8,128)S(1)} %add_add_fusion.1), channel_id=1, source_target_pairs={{0,6},{2,4},{4,2},{6,0},{8,14},{10,12},{12,10},{14,8},{128,134},{1... | collective-permute-start | bytes 98312 | tf_op jit(solution)/shard_map/ppermute | solution.py:519
  103.9 4.8 %collective-permute-start.31 = (f32[32,256]{1,0:T(8,128)S(1)}, f32[32,256]{1,0:T(8,128)S(1)}, u32[]{:S(2)}, u32[]{:S(2)}) collective-permute-start(f32[32,256]{1,0:T(8,128)S(1)} %add_add_fusion.1), channel_id=1, source_target_pairs={{0,4},{2,6},{4,0},{6,2},{8,12},{10,14},{12,8},{14,10},{128,132},{1... | collective-permute-start | bytes 98312 | tf_op jit(solution)/shard_map/ppermute | solution.py:519
  104.0 4.7 %collective-permute-start.30 = (f32[32,256]{1,0:T(8,128)S(1)}, f32[32,256]{1,0:T(8,128)S(1)}, u32[]{:S(2)}, u32[]{:S(2)}) collective-permute-start(f32[32,256]{1,0:T(8,128)S(1)} %add_add_fusion.1), channel_id=1, source_target_pairs={{0,2},{2,0},{4,6},{6,4},{8,10},{10,8},{12,14},{14,12},{128,130},{1... | collective-permute-start | bytes 98312 | tf_op jit(solution)/shard_map/ppermute | solution.py:519
  (3 other events, 31.7 us)

commit v9 on v7

--- a/solution.py
+++ b/solution.py
@@ -566,13 +566,13 @@
 
     right = right_product(mine, kept, partner)
     right, mine = lax.optimization_barrier((summed_among(right, CORE_AND_Z), mine))
-    arrived = [swapped(right, **bits) for bits in ALONG_X]
+    arrived = [swapped(right, **bits) for bits in ALONG_Z]
     other = swapped(mine, core=1)
     right, other = lax.optimization_barrier((added([right] + arrived), other))
-    arrived = [swapped(right, **bits) for bits in ALONG_Y]
+    arrived = [swapped(right, **bits) for bits in ALONG_X]
     halves = half_inverse(mine, other)
     right, *halves = lax.optimization_barrier((added([right] + arrived), *halves))
-    arrived = [swapped(right, **bits) for bits in ALONG_Z]
+    arrived = [swapped(right, **bits) for bits in ALONG_Y]
     inverse = whole_inverse(*halves, tie=right)
     right = added([right] + arrived)
     new_error, q_rows = remaining_error(mine, other, kept, sent, right, inverse)

time: 112 us -> 112 us (level)
  transfers between devices with their start and end apart: 33 -> 33, of which waited for: 14 -> 15; matrix products, arithmetic and copies ran while one was open for 0% -> 0% of each run, Pallas kernels for 19% -> 19%
where the time goes in v9:
time: 112 us; the launch traced here: 111 us
  starting transfers between devices  52.8 us (47%)
  Pallas kernels  36.4 us (32%)
  waiting for transfers between devices  20.8 us (19%)
    ppermute x31, starting transfers between devices, swapped(): return lax.ppermute(value, ('dp', 'space'), partners(**bits))  42.9 us
    ppermute x31, waiting for transfers between devices, swapped(): return lax.ppermute(value, ('dp', 'space'), partners(**bits))  20.8 us
    pallas_call x2, Pallas kernels, local_gradient(): pl.pallas_call(functools.partial(gradient_kernel, sides, width), grid=(le...  13.2 us
    pallas_call x3, Pallas kernels, input_gradient(): pl.pallas_call(functools.partial(input_kernel, side, last), grid=(3,), in...  12.2 us
    ppermute x2, starting transfers between devices, shifted(): lax.ppermute(value, 'space', [(i, (i + by) % devices) for i in range(devi...  9.95 us
    pallas_call x1, Pallas kernels, remaining_error(): pl.pallas_call(error_kernel, grid=(3,), in_specs=[whole(4, 28, 8, 128), w...  3.87 us
    pallas_call x1, Pallas kernels, half_inverse(): pl.pallas_call(first_half_kernel, out_shape=[SQUARE, SQUARE], compiler_pa...  2.36 us
  transfers between devices with their start and end apart: 33, of which 15 were waited for; matrix products, arithmetic and copies ran while one was open for 0% of the time, Pallas kernels for 19%

profile of v9, /device:TPU:8, one launch (start us, length us, event | category | flops | bytes accessed | tf_op | source)
XLA Modules:
  0.0 111.1 jit_solution(14444115937093290503)
XLA Ops:
  0.6 1.6 %brick_faces.1 = (bf16[2,8,16,256]{3,2,1,0:T(8,128)(2,1)S(1)}, bf16[2,8,16,256]{3,2,1,0:T(8,128)(2,1)S(1)}) custom-call(bf16[2,512,256]{2,1,0:T(8,128)(2,1)} %bitcast.34, bf16[2,512,256]{2,1,0:T(8,128)(2,1)} %bitcast.24, s32[2,512]{1,0:T(2,128)} %bitcast.40), custom_call_target="tpu_custom_call" | custom-call | tf_op jit(solution)/shard_map/brick_faces/pallas_call | solution.py:126
  2.3 2.4 %collective-permute-start = (bf16[2,8,16,256]{3,2,1,0:T(8,128)(2,1)S(1)}, bf16[2,8,16,256]{3,2,1,0:T(8,128)(2,1)S(1)}, u32[]{:S(2)}, u32[]{:S(2)}) collective-permute-start(bf16[2,8,16,256]{3,2,1,0:T(8,128)(2,1)S(1)} %get-tuple-element.33), channel_id=1, source_target_pairs={{0,1},{1,2},{2,3},{3,4},{4,5},{5,6},{6,7},{7,8},{8,9},{9,10},{10,1... | collective-permute-start | bytes 393224 | tf_op jit(solution)/shard_map/ppermute | solution.py:502
  4.7 7.6 %collective-permute-start.1 = (bf16[2,8,16,256]{3,2,1,0:T(8,128)(2,1)S(1)}, bf16[2,8,16,256]{3,2,1,0:T(8,128)(2,1)S(1)}, u32[]{:S(2)}, u32[]{:S(2)}) collective-permute-start(bf16[2,8,16,256]{3,2,1,0:T(8,128)(2,1)S(1)} %get-tuple-element.34), channel_id=1, source_target_pairs={{0,63},{1,0},{2,1},{3,2},{4,3},{5,4},{6,5},{7,6},{8,7},{9,8},{10,9... | collective-permute-start | bytes 393224 | tf_op jit(solution)/shard_map/ppermute | solution.py:502
  12.2 4.8 %gradient_own.1 = (f32[3,3,3,128,256]{4,3,2,1,0:T(8,128)S(1)}, f32[3,3,3,128,256]{4,3,2,1,0:T(8,128)S(1)}, f32[4,28,8,128]{3,2,1,0:T(8,128)S(1)}, f32[4,28,8,128]{3,2,1,0:T(8,128)S(1)}) custom-call(s32[2,27]{1,0:T(2,128)} %bitcast.52, bf16[2,512,256]{2,1,0:T(8,128)(2,1)} %bitcast.35, bf16[2,512,256]{2,1,0:T(8,128)(2,1)} %bitcast.25, s32[2,512]{1,0:T(2,128)} %bitcast.41, ...), custom_call_target="tpu_custom_call" | custom-call | flops 2000000000 | bytes 4000000 | tf_op jit(solution)/shard_map/gradient_own/pallas_call | solution.py:236
  17.1 8.4 %gradient_with_faces.1 = (f32[3,3,3,128,256]{4,3,2,1,0:T(8,128)S(1)}, f32[3,3,3,128,256]{4,3,2,1,0:T(8,128)S(1)}, f32[4,28,8,128]{3,2,1,0:T(8,128)S(1)}, f32[4,28,8,128]{3,2,1,0:T(8,128)S(1)}) custom-call(s32[2,27]{1,0:T(2,128)} %bitcast.53, bf16[2,512,256]{2,1,0:T(8,128)(2,1)} %bitcast.36, ...), custom_call_target="tpu_custom_call", output_to_operand_aliasing={{0}: (8, {}), {1}: (9, {})} | custom-call | flops 4000000000 | bytes 8000000 | tf_op jit(solution)/shard_map/gradient_with_faces/pallas_call | solution.py:236
  25.6 1.8 %collective-permute-done.2 = f32[4,28,8,128]{3,2,1,0:T(8,128)S(1)} collective-permute-done((f32[4,28,8,128]{3,2,1,0:T(8,128)S(1)}, f32[4,28,8,128]{3,2,1,0:T(8,128)S(1)}, u32[]{:S(2)}, u32[]{:S(2)}) %collective-permute-start.2) | collective-permute-done | bytes 458784 | tf_op jit(solution)/shard_map/ppermute | solution.py:519
  29.2 2.8 %collective-permute-start.3 = (f32[28,8,128]{2,1,0:T(8,128)S(1)}, f32[28,8,128]{2,1,0:T(8,128)S(1)}, u32[]{:S(2)}, u32[]{:S(2)}) collective-permute-start(f32[28,8,128]{2,1,0:T(8,128)S(1)} %get-tuple-element.65), channel_id=1, source_target_pairs={{0,16},{2,18},{4,20},{6,22},{8,24},{10,26},{12,28},{14,30},{128,14... | collective-permute-start | bytes 344072 | tf_op jit(solution)/shard_map/ppermute | solution.py:519
  31.9 3.6 %input_own.1.refs_5_ = f32[1024,256]{1,0:T(8,128)S(1)} custom-call(s32[2,27]{1,0:T(2,128)} %bitcast.54, bf16[2,512,256]{2,1,0:T(8,128)(2,1)S(1)} %bitcast.27, s32[2,512]{1,0:T(2,128)} %bitcast.43, bf16[3,3,3,256,256]{4,3,2,1,0:T(8,128)(2,1)S(1)} %bitcast.31, f32[4,28,8,128]{3,2,1,0:T(8,128)S(1)} %add.69.refs_4_), custom_call_target="tpu_custom_call" | custom-call | flops 2000000000 | bytes 4000000 | tf_op jit(solution)/shard_map/input_own/pallas_call | solution.py:321
  39.0 2.7 %collective-permute-start.7 = (f32[7,8,128]{2,1,0:T(8,128)S(1)}, f32[7,8,128]{2,1,0:T(8,128)S(1)}, u32[]{:S(2)}, u32[]{:S(2)}) collective-permute-start(f32[7,8,128]{2,1,0:T(8,128)S(1)} %get-tuple-element.68), channel_id=1, source_target_pairs={{0,1},{2,3},{4,5},{6,7},{8,9},{10,11},{12,13},{14,15},{128,129},{1... | collective-permute-start | bytes 86024 | tf_op jit(solution)/shard_map/ppermute | solution.py:519
  42.8 1.5 %collective-permute-done.7 = f32[7,8,128]{2,1,0:T(8,128)S(1)} collective-permute-done((f32[7,8,128]{2,1,0:T(8,128)S(1)}, f32[7,8,128]{2,1,0:T(8,128)S(1)}, u32[]{:S(2)}, u32[]{:S(2)}) %collective-permute-start.7) | collective-permute-done | bytes 28704 | tf_op jit(solution)/shard_map/ppermute | solution.py:519
  44.4 4.5 %collective-permute-start.11 = (f32[7,8,128]{2,1,0:T(8,128)S(1)}, f32[7,8,128]{2,1,0:T(8,128)S(1)}, u32[]{:S(2)}, u32[]{:S(2)}) collective-permute-start(f32[7,8,128]{2,1,0:T(8,128)S(1)} %add_add_fusion.5), channel_id=1, source_target_pairs={{0,6},{2,4},{4,2},{6,0},{8,14},{10,12},{12,10},{14,8},{128,134},{1... | collective-permute-start | bytes 86024 | tf_op jit(solution)/shard_map/ppermute | solution.py:519
  50.8 2.8 %collective-permute-done.10 = f32[7,8,128]{2,1,0:T(8,128)S(1)} collective-permute-done((f32[7,8,128]{2,1,0:T(8,128)S(1)}, f32[7,8,128]{2,1,0:T(8,128)S(1)}, u32[]{:S(2)}, u32[]{:S(2)}) %collective-permute-start.10) | collective-permute-done | bytes 28704 | tf_op jit(solution)/shard_map/ppermute | solution.py:519
  53.6 2.9 %collective-permute-start.12 = (f32[7,8,128]{2,1,0:T(8,128)S(1)}, f32[7,8,128]{2,1,0:T(8,128)S(1)}, u32[]{:S(2)}, u32[]{:S(2)}) collective-permute-start(f32[7,8,128]{2,1,0:T(8,128)S(1)} %add_add_fusion.4.refs_6_), channel_id=1, source_target_pairs={{0,12},{2,14},{4,8},{6,10},{8,4},{10,6},{12,0},{14,2},{128,140},{1... | collective-permute-start | bytes 86024 | tf_op jit(solution)/shard_map/ppermute | solution.py:519
  56.5 3.7 %input_below.1.refs_5_ = f32[1024,256]{1,0:T(8,128)S(1)} custom-call(s32[2,27]{1,0:T(2,128)} %bitcast.55, bf16[2,512,256]{2,1,0:T(8,128)(2,1)S(1)} %bitcast.28, s32[2,512]{1,0:T(2,128)} %bitcast.44, bf16[3,3,3,256,256]{4,3,2,1,0:T(8,128)(2,1)S(1)} %bitcast.32, bf16[2,8,16,256]{3,2,1,0:T(8,128)(2,1)S(1)} %collective-permute-done.1.refs_7_.refs_4_, ...), custom_call_target="tpu_custom_call" | custom-call | flops 2000000000 | bytes 4000000 | tf_op jit(solution)/shard_map/input_below/pallas_call | solution.py:321
  60.4 3.4 %collective-permute-start.14 = (f32[7,8,128]{2,1,0:T(8,128)S(1)}, f32[7,8,128]{2,1,0:T(8,128)S(1)}, u32[]{:S(2)}, u32[]{:S(2)}) collective-permute-start(f32[7,8,128]{2,1,0:T(8,128)S(1)} %add.79), channel_id=1, source_target_pairs={{0,1},{2,3},{4,5},{6,7},{8,9},{10,11},{12,13},{14,15},{128,129},{1... | collective-permute-start | bytes 86024 | tf_op jit(solution)/shard_map/ppermute | solution.py:519
  64.5 3.2 %collective-permute-done.13 = f32[7,8,128]{2,1,0:T(8,128)S(1)} collective-permute-done((f32[7,8,128]{2,1,0:T(8,128)S(1)}, f32[7,8,128]{2,1,0:T(8,128)S(1)}, u32[]{:S(2)}, u32[]{:S(2)}) %collective-permute-start.13) | collective-permute-done | bytes 28704 | tf_op jit(solution)/shard_map/ppermute | solution.py:519
  67.7 2.2 %collective-permute-start.18 = (f32[28,8,128]{2,1,0:T(8,128)S(1)}, f32[28,8,128]{2,1,0:T(8,128)S(1)}, u32[]{:S(2)}, u32[]{:S(2)}) collective-permute-start(f32[28,8,128]{2,1,0:T(8,128)S(1)} %constant_dynamic-update-slice_fusion.refs_6_), channel_id=1, source_target_pairs={{0,48},{2,50},{4,52},{6,54},{8,56},{10,58},{12,60},{14,62},{128,17... | collective-permute-start | bytes 344072 | tf_op jit(solution)/shard_map/ppermute | solution.py:519
  70.2 1.7 %collective-permute-start.16 = (f32[28,8,128]{2,1,0:T(8,128)S(1)}, f32[28,8,128]{2,1,0:T(8,128)S(1)}, u32[]{:S(2)}, u32[]{:S(2)}) collective-permute-start(f32[28,8,128]{2,1,0:T(8,128)S(1)} %constant_dynamic-update-slice_fusion.refs_6_), channel_id=1, source_target_pairs={{0,16},{2,18},{4,20},{6,22},{8,24},{10,26},{12,28},{14,30},{128,14... | collective-permute-start | bytes 344072 | tf_op jit(solution)/shard_map/ppermute | solution.py:519
  71.9 4.8 %input_above.1 = bf16[2,512,256]{2,1,0:T(8,128)(2,1)} custom-call(s32[2,27]{1,0:T(2,128)} %bitcast.56, bf16[2,512,256]{2,1,0:T(8,128)(2,1)S(1)} %bitcast.29, s32[2,512]{1,0:T(2,128)} %bitcast.45, bf16[3,3,3,256,256]{4,3,2,1,0:T(8,128)(2,1)S(1)} %bitcast.33, bf16[2,8,16,256]{3,2,1,0:T(8,128)(2,1)S(1)} %collective-permute-done.refs_6_.refs_4_, ...), custom_call_target="tpu_custom_call" | custom-call | flops 2000000000 | bytes 4000000 | tf_op jit(solution)/shard_map/input_above/pallas_call | solution.py:321
  76.8 1.7 %right_product.1 = f32[32,256]{1,0:T(8,128)S(1)} custom-call(f32[4,28,8,128]{3,2,1,0:T(8,128)S(1)} %pad_maximum_fusion.mine, f32[3,3,3,128,256]{4,3,2,1,0:T(8,128)S(1)} %get-tuple-element.50.kept, f32[3,3,3,128,256]{4,3,2,1,0:T(8,128)S(1)} %collective-permute-done.19.partner), custom_call_target="tpu_custom_call" | custom-call | tf_op jit(solution)/shard_map/right_product/pallas_call | solution.py:368
  78.6 2.2 %collective-permute-start.21 = (f32[32,256]{1,0:T(8,128)S(1)}, f32[32,256]{1,0:T(8,128)S(1)}, u32[]{:S(2)}, u32[]{:S(2)}) collective-permute-start(f32[32,256]{1,0:T(8,128)S(1)} %right_product.1), channel_id=1, source_target_pairs={{0,12},{2,14},{4,8},{6,10},{8,4},{10,6},{12,0},{14,2},{128,140},{1... | collective-permute-start | bytes 98312 | tf_op jit(solution)/shard_map/ppermute | solution.py:519
  80.8 1.8 %collective-permute-start.20 = (f32[32,256]{1,0:T(8,128)S(1)}, f32[32,256]{1,0:T(8,128)S(1)}, u32[]{:S(2)}, u32[]{:S(2)}) collective-permute-start(f32[32,256]{1,0:T(8,128)S(1)} %right_product.1), channel_id=1, source_target_pairs={{0,64},{2,66},{4,68},{6,70},{8,72},{10,74},{12,76},{14,78},{128,19... | collective-permute-start | bytes 98312 | tf_op jit(solution)/shard_map/ppermute | solution.py:519
  82.5 1.5 %collective-permute-done.22 = f32[32,256]{1,0:T(8,128)S(1)} collective-permute-done((f32[32,256]{1,0:T(8,128)S(1)}, f32[32,256]{1,0:T(8,128)S(1)}, u32[]{:S(2)}, u32[]{:S(2)}) %collective-permute-start.22) | collective-permute-done | bytes 32800 | tf_op jit(solution)/shard_map/ppermute | solution.py:519
  87.3 2.9 %collective-permute-start.23 = (f32[32,256]{1,0:T(8,128)S(1)}, f32[32,256]{1,0:T(8,128)S(1)}, u32[]{:S(2)}, u32[]{:S(2)}) collective-permute-start(f32[32,256]{1,0:T(8,128)S(1)} %add_add_fusion.3), channel_id=1, source_target_pairs={{0,2},{2,0},{4,6},{6,4},{8,10},{10,8},{12,14},{14,12},{128,130},{1... | collective-permute-start | bytes 98312 | tf_op jit(solution)/shard_map/ppermute | solution.py:519
  90.1 1.5 %collective-permute-done.25 = f32[32,256]{1,0:T(8,128)S(1)} collective-permute-done((f32[32,256]{1,0:T(8,128)S(1)}, f32[32,256]{1,0:T(8,128)S(1)}, u32[]{:S(2)}, u32[]{:S(2)}) %collective-permute-start.25) | collective-permute-done | bytes 32800 | tf_op jit(solution)/shard_map/ppermute | solution.py:519
  92.1 2.2 %collective-permute-start.29 = (f32[32,256]{1,0:T(8,128)S(1)}, f32[32,256]{1,0:T(8,128)S(1)}, u32[]{:S(2)}, u32[]{:S(2)}) collective-permute-start(f32[32,256]{1,0:T(8,128)S(1)} %add_add_fusion.2), channel_id=1, source_target_pairs={{0,48},{2,50},{4,52},{6,54},{8,56},{10,58},{12,60},{14,62},{128,17... | collective-permute-start | bytes 98312 | tf_op jit(solution)/shard_map/ppermute | solution.py:519
  94.8 1.5 %collective-permute-start.27 = (f32[32,256]{1,0:T(8,128)S(1)}, f32[32,256]{1,0:T(8,128)S(1)}, u32[]{:S(2)}, u32[]{:S(2)}) collective-permute-start(f32[32,256]{1,0:T(8,128)S(1)} %add_add_fusion.2), channel_id=1, source_target_pairs={{0,16},{2,18},{4,20},{6,22},{8,24},{10,26},{12,28},{14,30},{128,14... | collective-permute-start | bytes 98312 | tf_op jit(solution)/shard_map/ppermute | solution.py:519
  96.2 2.4 %half_inverse.1 = (f32[32,32]{1,0:T(8,128)S(1)}, f32[32,32]{1,0:T(8,128)S(1)}) custom-call(f32[4,28,8,128]{3,2,1,0:T(8,128)S(1)} %pad_maximum_fusion.mine, f32[4,28,8,128]{3,2,1,0:T(8,128)S(1)} %collective-permute-done.26.other), custom_call_target="tpu_custom_call" | custom-call | tf_op jit(solution)/shard_map/half_inverse/pallas_call | solution.py:411
  99.7 1.5 %collective-permute-start.32 = (f32[32,256]{1,0:T(8,128)S(1)}, f32[32,256]{1,0:T(8,128)S(1)}, u32[]{:S(2)}, u32[]{:S(2)}) collective-permute-start(f32[32,256]{1,0:T(8,128)S(1)} %add_add_fusion.1.refs_0_), channel_id=1, source_target_pairs={{0,129},{2,131},{4,133},{6,135},{8,137},{10,139},{12,141},{14,143}... | collective-permute-start | bytes 98312 | tf_op jit(solution)/shard_map/ppermute | solution.py:519
  101.2 2.1 %collective-permute-start.31 = (f32[32,256]{1,0:T(8,128)S(1)}, f32[32,256]{1,0:T(8,128)S(1)}, u32[]{:S(2)}, u32[]{:S(2)}) collective-permute-start(f32[32,256]{1,0:T(8,128)S(1)} %add_add_fusion.1.refs_0_), channel_id=1, source_target_pairs={{0,1},{2,3},{4,5},{6,7},{8,9},{10,11},{12,13},{14,15},{128,129},{1... | collective-permute-start | bytes 98312 | tf_op jit(solution)/shard_map/ppermute | solution.py:519
  103.9 1.4 %whole_inverse.1.inverse = f32[32,32]{1,0:T(8,128)S(1)} custom-call(f32[32,32]{1,0:T(8,128)S(1)} %get-tuple-element.59.work, f32[32,32]{1,0:T(8,128)S(1)} %get-tuple-element.60.made, f32[32,256]{1,0:T(8,128)S(1)} %add_add_fusion.1.refs_0_), custom_call_target="tpu_custom_call" | custom-call | tf_op jit(solution)/shard_map/whole_inverse/pallas_call | solution.py:422
  107.2 3.9 %remaining_error.1 = (bf16[3,3,3,256,256]{4,3,2,1,0:T(8,128)(2,1)}, f32[32,256]{1,0:T(8,128)}) custom-call(f32[4,28,8,128]{3,2,1,0:T(8,128)S(1)} %pad_maximum_fusion.mine, f32[4,28,8,128]{3,2,1,0:T(8,128)S(1)} %collective-permute-done.26.other, f32[3,3,3,128,256]{4,3,2,1,0:T(8,128)S(1)} %get-tuple-element.50.kept, ...), custom_call_target="tpu_custom_call" | custom-call | tf_op jit(solution)/shard_map/remaining_error/pallas_call | solution.py:464
  (64 shorter events, 17.3 us)
Async XLA Ops:
  2.3 14.7 %collective-permute-start = (bf16[2,8,16,256]{3,2,1,0:T(8,128)(2,1)S(1)}, bf16[2,8,16,256]{3,2,1,0:T(8,128)(2,1)S(1)}, u32[]{:S(2)}, u32[]{:S(2)}) collective-permute-start(bf16[2,8,16,256]{3,2,1,0:T(8,128)(2,1)S(1)} %get-tuple-element.33), channel_id=1, source_target_pairs={{0,1},{1,2},{2,3},{3,4},{4,5},{5,6},{6,7},{7,8},{8,9},{9,10},{10,1... | collective-permute-start | bytes 393224 | tf_op jit(solution)/shard_map/ppermute | solution.py:502
  4.7 12.4 %collective-permute-start.1 = (bf16[2,8,16,256]{3,2,1,0:T(8,128)(2,1)S(1)}, bf16[2,8,16,256]{3,2,1,0:T(8,128)(2,1)S(1)}, u32[]{:S(2)}, u32[]{:S(2)}) collective-permute-start(bf16[2,8,16,256]{3,2,1,0:T(8,128)(2,1)S(1)} %get-tuple-element.34), channel_id=1, source_target_pairs={{0,63},{1,0},{2,1},{3,2},{4,3},{5,4},{6,5},{7,6},{8,7},{9,8},{10,9... | collective-permute-start | bytes 393224 | tf_op jit(solution)/shard_map/ppermute | solution.py:502
  27.5 49.3 %collective-permute-start.19 = (f32[3,3,3,128,256]{4,3,2,1,0:T(8,128)S(1)}, f32[3,3,3,128,256]{4,3,2,1,0:T(8,128)S(1)}, u32[]{:S(2)}, u32[]{:S(2)}) collective-permute-start(f32[3,3,3,128,256]{4,3,2,1,0:T(8,128)S(1)} %get-tuple-element.46.sent), channel_id=1, source_target_pairs={{0,64},{2,66},{4,68},{6,70},{8,72},{10,74},{12,76},{14,78},{128,19... | collective-permute-start | bytes 10616840 | tf_op jit(solution)/shard_map/ppermute | solution.py:519
  27.7 9.2 %collective-permute-start.5 = (f32[28,8,128]{2,1,0:T(8,128)S(1)}, f32[28,8,128]{2,1,0:T(8,128)S(1)}, u32[]{:S(2)}, u32[]{:S(2)}) collective-permute-start(f32[28,8,128]{2,1,0:T(8,128)S(1)} %get-tuple-element.63), channel_id=1, source_target_pairs={{0,48},{2,50},{4,52},{6,54},{8,56},{10,58},{12,60},{14,62},{128,17... | collective-permute-start | bytes 344072 | tf_op jit(solution)/shard_map/ppermute | solution.py:519
  28.7 8.3 %collective-permute-start.4 = (f32[28,8,128]{2,1,0:T(8,128)S(1)}, f32[28,8,128]{2,1,0:T(8,128)S(1)}, u32[]{:S(2)}, u32[]{:S(2)}) collective-permute-start(f32[28,8,128]{2,1,0:T(8,128)S(1)} %get-tuple-element.64), channel_id=1, source_target_pairs={{0,32},{2,34},{4,36},{6,38},{8,40},{10,42},{12,44},{14,46},{128,16... | collective-permute-start | bytes 344072 | tf_op jit(solution)/shard_map/ppermute | solution.py:519
  29.2 8.3 %collective-permute-start.3 = (f32[28,8,128]{2,1,0:T(8,128)S(1)}, f32[28,8,128]{2,1,0:T(8,128)S(1)}, u32[]{:S(2)}, u32[]{:S(2)}) collective-permute-start(f32[28,8,128]{2,1,0:T(8,128)S(1)} %get-tuple-element.65), channel_id=1, source_target_pairs={{0,16},{2,18},{4,20},{6,22},{8,24},{10,26},{12,28},{14,30},{128,14... | collective-permute-start | bytes 344072 | tf_op jit(solution)/shard_map/ppermute | solution.py:519
  37.5 4.2 %collective-permute-start.6 = (f32[7,8,128]{2,1,0:T(8,128)S(1)}, f32[7,8,128]{2,1,0:T(8,128)S(1)}, u32[]{:S(2)}, u32[]{:S(2)}) collective-permute-start(f32[7,8,128]{2,1,0:T(8,128)S(1)} %get-tuple-element.66), channel_id=1, source_target_pairs={{0,128},{2,130},{4,132},{6,134},{8,136},{10,138},{12,140},{14,142}... | collective-permute-start | bytes 86024 | tf_op jit(solution)/shard_map/ppermute | solution.py:519
  39.0 3.9 %collective-permute-start.8 = (f32[7,8,128]{2,1,0:T(8,128)S(1)}, f32[7,8,128]{2,1,0:T(8,128)S(1)}, u32[]{:S(2)}, u32[]{:S(2)}) collective-permute-start(f32[7,8,128]{2,1,0:T(8,128)S(1)} %get-tuple-element.67), channel_id=1, source_target_pairs={{0,129},{2,131},{4,133},{6,135},{8,137},{10,139},{12,141},{14,143}... | collective-permute-start | bytes 86024 | tf_op jit(solution)/shard_map/ppermute | solution.py:519
  39.0 5.4 %collective-permute-start.7 = (f32[7,8,128]{2,1,0:T(8,128)S(1)}, f32[7,8,128]{2,1,0:T(8,128)S(1)}, u32[]{:S(2)}, u32[]{:S(2)}) collective-permute-start(f32[7,8,128]{2,1,0:T(8,128)S(1)} %get-tuple-element.68), channel_id=1, source_target_pairs={{0,1},{2,3},{4,5},{6,7},{8,9},{10,11},{12,13},{14,15},{128,129},{1... | collective-permute-start | bytes 86024 | tf_op jit(solution)/shard_map/ppermute | solution.py:519
  44.4 6.5 %collective-permute-start.11 = (f32[7,8,128]{2,1,0:T(8,128)S(1)}, f32[7,8,128]{2,1,0:T(8,128)S(1)}, u32[]{:S(2)}, u32[]{:S(2)}) collective-permute-start(f32[7,8,128]{2,1,0:T(8,128)S(1)} %add_add_fusion.5), channel_id=1, source_target_pairs={{0,6},{2,4},{4,2},{6,0},{8,14},{10,12},{12,10},{14,8},{128,134},{1... | collective-permute-start | bytes 86024 | tf_op jit(solution)/shard_map/ppermute | solution.py:519
  48.8 4.8 %collective-permute-start.10 = (f32[7,8,128]{2,1,0:T(8,128)S(1)}, f32[7,8,128]{2,1,0:T(8,128)S(1)}, u32[]{:S(2)}, u32[]{:S(2)}) collective-permute-start(f32[7,8,128]{2,1,0:T(8,128)S(1)} %add_add_fusion.5), channel_id=1, source_target_pairs={{0,4},{2,6},{4,0},{6,2},{8,12},{10,14},{12,8},{14,10},{128,132},{1... | collective-permute-start | bytes 86024 | tf_op jit(solution)/shard_map/ppermute | solution.py:519
  48.9 4.8 %collective-permute-start.9 = (f32[7,8,128]{2,1,0:T(8,128)S(1)}, f32[7,8,128]{2,1,0:T(8,128)S(1)}, u32[]{:S(2)}, u32[]{:S(2)}) collective-permute-start(f32[7,8,128]{2,1,0:T(8,128)S(1)} %add_add_fusion.5), channel_id=1, source_target_pairs={{0,2},{2,0},{4,6},{6,4},{8,10},{10,8},{12,14},{14,12},{128,130},{1... | collective-permute-start | bytes 86024 | tf_op jit(solution)/shard_map/ppermute | solution.py:519
  53.6 6.7 %collective-permute-start.12 = (f32[7,8,128]{2,1,0:T(8,128)S(1)}, f32[7,8,128]{2,1,0:T(8,128)S(1)}, u32[]{:S(2)}, u32[]{:S(2)}) collective-permute-start(f32[7,8,128]{2,1,0:T(8,128)S(1)} %add_add_fusion.4.refs_6_), channel_id=1, source_target_pairs={{0,12},{2,14},{4,8},{6,10},{8,4},{10,6},{12,0},{14,2},{128,140},{1... | collective-permute-start | bytes 86024 | tf_op jit(solution)/shard_map/ppermute | solution.py:519
  60.3 7.4 %collective-permute-start.15 = (f32[7,8,128]{2,1,0:T(8,128)S(1)}, f32[7,8,128]{2,1,0:T(8,128)S(1)}, u32[]{:S(2)}, u32[]{:S(2)}) collective-permute-start(f32[7,8,128]{2,1,0:T(8,128)S(1)} %add.79), channel_id=1, source_target_pairs={{0,129},{2,131},{4,133},{6,135},{8,137},{10,139},{12,141},{14,143}... | collective-permute-start | bytes 86024 | tf_op jit(solution)/shard_map/ppermute | solution.py:519
  60.4 7.3 %collective-permute-start.14 = (f32[7,8,128]{2,1,0:T(8,128)S(1)}, f32[7,8,128]{2,1,0:T(8,128)S(1)}, u32[]{:S(2)}, u32[]{:S(2)}) collective-permute-start(f32[7,8,128]{2,1,0:T(8,128)S(1)} %add.79), channel_id=1, source_target_pairs={{0,1},{2,3},{4,5},{6,7},{8,9},{10,11},{12,13},{14,15},{128,129},{1... | collective-permute-start | bytes 86024 | tf_op jit(solution)/shard_map/ppermute | solution.py:519
  63.8 3.9 %collective-permute-start.13 = (f32[7,8,128]{2,1,0:T(8,128)S(1)}, f32[7,8,128]{2,1,0:T(8,128)S(1)}, u32[]{:S(2)}, u32[]{:S(2)}) collective-permute-start(f32[7,8,128]{2,1,0:T(8,128)S(1)} %add.79), channel_id=1, source_target_pairs={{0,128},{2,130},{4,132},{6,134},{8,136},{10,138},{12,140},{14,142}... | collective-permute-start | bytes 86024 | tf_op jit(solution)/shard_map/ppermute | solution.py:519
  67.7 9.0 %collective-permute-start.18 = (f32[28,8,128]{2,1,0:T(8,128)S(1)}, f32[28,8,128]{2,1,0:T(8,128)S(1)}, u32[]{:S(2)}, u32[]{:S(2)}) collective-permute-start(f32[28,8,128]{2,1,0:T(8,128)S(1)} %constant_dynamic-update-slice_fusion.refs_6_), channel_id=1, source_target_pairs={{0,48},{2,50},{4,52},{6,54},{8,56},{10,58},{12,60},{14,62},{128,17... | collective-permute-start | bytes 344072 | tf_op jit(solution)/shard_map/ppermute | solution.py:519
  70.0 6.8 %collective-permute-start.17 = (f32[28,8,128]{2,1,0:T(8,128)S(1)}, f32[28,8,128]{2,1,0:T(8,128)S(1)}, u32[]{:S(2)}, u32[]{:S(2)}) collective-permute-start(f32[28,8,128]{2,1,0:T(8,128)S(1)} %constant_dynamic-update-slice_fusion.refs_6_), channel_id=1, source_target_pairs={{0,32},{2,34},{4,36},{6,38},{8,40},{10,42},{12,44},{14,46},{128,16... | collective-permute-start | bytes 344072 | tf_op jit(solution)/shard_map/ppermute | solution.py:519
  70.2 6.5 %collective-permute-start.16 = (f32[28,8,128]{2,1,0:T(8,128)S(1)}, f32[28,8,128]{2,1,0:T(8,128)S(1)}, u32[]{:S(2)}, u32[]{:S(2)}) collective-permute-start(f32[28,8,128]{2,1,0:T(8,128)S(1)} %constant_dynamic-update-slice_fusion.refs_6_), channel_id=1, source_target_pairs={{0,16},{2,18},{4,20},{6,22},{8,24},{10,26},{12,28},{14,30},{128,14... | collective-permute-start | bytes 344072 | tf_op jit(solution)/shard_map/ppermute | solution.py:519
  78.5 5.5 %collective-permute-start.22 = (f32[32,256]{1,0:T(8,128)S(1)}, f32[32,256]{1,0:T(8,128)S(1)}, u32[]{:S(2)}, u32[]{:S(2)}) collective-permute-start(f32[32,256]{1,0:T(8,128)S(1)} %right_product.1), channel_id=1, source_target_pairs={{0,76},{2,78},{4,72},{6,74},{8,68},{10,70},{12,64},{14,66},{128,20... | collective-permute-start | bytes 98312 | tf_op jit(solution)/shard_map/ppermute | solution.py:519
  78.6 6.2 %collective-permute-start.21 = (f32[32,256]{1,0:T(8,128)S(1)}, f32[32,256]{1,0:T(8,128)S(1)}, u32[]{:S(2)}, u32[]{:S(2)}) collective-permute-start(f32[32,256]{1,0:T(8,128)S(1)} %right_product.1), channel_id=1, source_target_pairs={{0,12},{2,14},{4,8},{6,10},{8,4},{10,6},{12,0},{14,2},{128,140},{1... | collective-permute-start | bytes 98312 | tf_op jit(solution)/shard_map/ppermute | solution.py:519
  80.8 4.0 %collective-permute-start.20 = (f32[32,256]{1,0:T(8,128)S(1)}, f32[32,256]{1,0:T(8,128)S(1)}, u32[]{:S(2)}, u32[]{:S(2)}) collective-permute-start(f32[32,256]{1,0:T(8,128)S(1)} %right_product.1), channel_id=1, source_target_pairs={{0,64},{2,66},{4,68},{6,70},{8,72},{10,74},{12,76},{14,78},{128,19... | collective-permute-start | bytes 98312 | tf_op jit(solution)/shard_map/ppermute | solution.py:519
  84.8 7.3 %collective-permute-start.26 = (f32[4,28,8,128]{3,2,1,0:T(8,128)S(1)}, f32[4,28,8,128]{3,2,1,0:T(8,128)S(1)}, u32[]{:S(2)}, u32[]{:S(2)}) collective-permute-start(f32[4,28,8,128]{3,2,1,0:T(8,128)S(1)} %pad_maximum_fusion.mine), channel_id=1, source_target_pairs={{0,64},{2,66},{4,68},{6,70},{8,72},{10,74},{12,76},{14,78},{128,19... | collective-permute-start | bytes 1376264 | tf_op jit(solution)/shard_map/ppermute | solution.py:519
  85.8 5.9 %collective-permute-start.25 = (f32[32,256]{1,0:T(8,128)S(1)}, f32[32,256]{1,0:T(8,128)S(1)}, u32[]{:S(2)}, u32[]{:S(2)}) collective-permute-start(f32[32,256]{1,0:T(8,128)S(1)} %add_add_fusion.3), channel_id=1, source_target_pairs={{0,6},{2,4},{4,2},{6,0},{8,14},{10,12},{12,10},{14,8},{128,134},{1... | collective-permute-start | bytes 98312 | tf_op jit(solution)/shard_map/ppermute | solution.py:519
  86.2 5.5 %collective-permute-start.24 = (f32[32,256]{1,0:T(8,128)S(1)}, f32[32,256]{1,0:T(8,128)S(1)}, u32[]{:S(2)}, u32[]{:S(2)}) collective-permute-start(f32[32,256]{1,0:T(8,128)S(1)} %add_add_fusion.3), channel_id=1, source_target_pairs={{0,4},{2,6},{4,0},{6,2},{8,12},{10,14},{12,8},{14,10},{128,132},{1... | collective-permute-start | bytes 98312 | tf_op jit(solution)/shard_map/ppermute | solution.py:519
  87.3 4.8 %collective-permute-start.23 = (f32[32,256]{1,0:T(8,128)S(1)}, f32[32,256]{1,0:T(8,128)S(1)}, u32[]{:S(2)}, u32[]{:S(2)}) collective-permute-start(f32[32,256]{1,0:T(8,128)S(1)} %add_add_fusion.3), channel_id=1, source_target_pairs={{0,2},{2,0},{4,6},{6,4},{8,10},{10,8},{12,14},{14,12},{128,130},{1... | collective-permute-start | bytes 98312 | tf_op jit(solution)/shard_map/ppermute | solution.py:519
  92.1 6.5 %collective-permute-start.29 = (f32[32,256]{1,0:T(8,128)S(1)}, f32[32,256]{1,0:T(8,128)S(1)}, u32[]{:S(2)}, u32[]{:S(2)}) collective-permute-start(f32[32,256]{1,0:T(8,128)S(1)} %add_add_fusion.2), channel_id=1, source_target_pairs={{0,48},{2,50},{4,52},{6,54},{8,56},{10,58},{12,60},{14,62},{128,17... | collective-permute-start | bytes 98312 | tf_op jit(solution)/shard_map/ppermute | solution.py:519
  94.3 5.4 %collective-permute-start.28 = (f32[32,256]{1,0:T(8,128)S(1)}, f32[32,256]{1,0:T(8,128)S(1)}, u32[]{:S(2)}, u32[]{:S(2)}) collective-permute-start(f32[32,256]{1,0:T(8,128)S(1)} %add_add_fusion.2), channel_id=1, source_target_pairs={{0,32},{2,34},{4,36},{6,38},{8,40},{10,42},{12,44},{14,46},{128,16... | collective-permute-start | bytes 98312 | tf_op jit(solution)/shard_map/ppermute | solution.py:519
  94.8 5.0 %collective-permute-start.27 = (f32[32,256]{1,0:T(8,128)S(1)}, f32[32,256]{1,0:T(8,128)S(1)}, u32[]{:S(2)}, u32[]{:S(2)}) collective-permute-start(f32[32,256]{1,0:T(8,128)S(1)} %add_add_fusion.2), channel_id=1, source_target_pairs={{0,16},{2,18},{4,20},{6,22},{8,24},{10,26},{12,28},{14,30},{128,14... | collective-permute-start | bytes 98312 | tf_op jit(solution)/shard_map/ppermute | solution.py:519
  99.7 5.6 %collective-permute-start.32 = (f32[32,256]{1,0:T(8,128)S(1)}, f32[32,256]{1,0:T(8,128)S(1)}, u32[]{:S(2)}, u32[]{:S(2)}) collective-permute-start(f32[32,256]{1,0:T(8,128)S(1)} %add_add_fusion.1.refs_0_), channel_id=1, source_target_pairs={{0,129},{2,131},{4,133},{6,135},{8,137},{10,139},{12,141},{14,143}... | collective-permute-start | bytes 98312 | tf_op jit(solution)/shard_map/ppermute | solution.py:519
  101.2 5.4 %collective-permute-start.31 = (f32[32,256]{1,0:T(8,128)S(1)}, f32[32,256]{1,0:T(8,128)S(1)}, u32[]{:S(2)}, u32[]{:S(2)}) collective-permute-start(f32[32,256]{1,0:T(8,128)S(1)} %add_add_fusion.1.refs_0_), channel_id=1, source_target_pairs={{0,1},{2,3},{4,5},{6,7},{8,9},{10,11},{12,13},{14,15},{128,129},{1... | collective-permute-start | bytes 98312 | tf_op jit(solution)/shard_map/ppermute | solution.py:519
  103.3 3.9 %collective-permute-start.30 = (f32[32,256]{1,0:T(8,128)S(1)}, f32[32,256]{1,0:T(8,128)S(1)}, u32[]{:S(2)}, u32[]{:S(2)}) collective-permute-start(f32[32,256]{1,0:T(8,128)S(1)} %add_add_fusion.1.refs_0_), channel_id=1, source_target_pairs={{0,128},{2,130},{4,132},{6,134},{8,136},{10,138},{12,140},{14,142}... | collective-permute-start | bytes 98312 | tf_op jit(solution)/shard_map/ppermute | solution.py:519
  (3 other events, 31.7 us)
